TPU v7x, 128 devices: a whole 4x4x4 slice. The times are simulated.
128 devices in a mesh: seq: 8 (over y, core), tp: 16 (over x, z).
Axes of the slice: x: 4, y: 4, z: 4, core: 2. Of those that a mesh axis runs over, the one named last changes fastest.
Arguments:
- tokens: bfloat16 [8192, 5376], P('seq'), may hold values from -6 to 6
- pre_gain: float32 [5376], replicated, may hold values from 0.5 to 2
- w_query: bfloat16 [5376, 4096], P(None, 'tp'), may hold values from -0.078125 to 0.078125
- key_weight_matrix: bfloat16 [5376, 2048], P(None, 'tp'), may hold values from -0.078125 to 0.078125
- value_weight_matrix: bfloat16 [5376, 2048], P(None, 'tp'), may hold values from -0.078125 to 0.078125
- query_gain: float32 [128], replicated, may hold values from 0.5 to 9
- key_norm_gain: float32 [128], replicated, may hold values from 0.5 to 9
- prior_key_cache: bfloat16 [1024, 2048], P(None, 'tp'), may hold values from -6 to 6
- prior_value_cache: bfloat16 [1024, 2048], P(None, 'tp'), may hold values from -6 to 6
- w_out: bfloat16 [4096, 5376], P('tp'), may hold values from -0.09375 to 0.09375
- post_gain: float32 [5376], replicated, may hold values from 0.5 to 2
Outputs:
- updated: bfloat16 [8192, 5376], P(('seq', 'tp'))
All inputs are finite; a program needn't handle non-finite values.
Results may differ from a plain program's by a relative error of at most 0.015.
The roundings to bfloat16 on the way count: a program that leaves them out, or rounds other values in their place, can miss the bound.
Values may be sent and summed in bfloat16 or wider, within the bound.
No kernel may reach another device: no remote copies, remote signals or barrier semaphores. Data moves between devices by JAX's collectives and lax.ppermute only.
A program may use at most 128 MiB of HBM per device.

v0:
```python
import jax
import jax.numpy as jnp
from jax import lax
from jax.sharding import PartitionSpec as P

MODEL_WIDTH = 5376
HQ = 32
WINDOW_SPAN = 1024


EPSILON = 1e-06


def in_one_piece(arrays, axis, dim, along):
    both = jnp.concatenate(arrays, axis=along)
    filled, at, gathered = (lax.all_gather(both, axis, axis=dim, tiled=True), 0, [])
    for a in arrays:
        gathered.append(lax.slice_in_dim(filled, at, at + a.shape[along], axis=along))
        at += a.shape[along]
    return tuple(gathered)


def root_mean_norm(values, gain):
    mean_square = jnp.mean(values * values, axis=-1, keepdims=True)
    return values * lax.rsqrt(mean_square + EPSILON) * gain


def rotary_embed_pairs(values, token_positions):
    half = values.shape[-1] // 2
    exponent = jnp.arange(half, dtype=jnp.float32) * (-2.0 / values.shape[-1])
    frequency = jnp.power(jnp.float32(10000.0), exponent)
    angles = token_positions.astype(jnp.float32)[:, None] * frequency[None, :]
    cosine = jnp.cos(angles)[:, None, :]
    sine = jnp.sin(angles)[:, None, :]
    first = values[..., :half]
    second = values[..., half:]
    return jnp.concatenate(
        [first * cosine - second * sine, second * cosine + first * sine], axis=-1
    )


def attend_block(query_rows, key_rows, value_rows, scale):
    count = query_rows.shape[0]
    heads = query_rows.shape[1]
    kv_heads = key_rows.shape[1]
    grouped = query_rows.reshape(count, kv_heads, heads // kv_heads, -1)
    scores = (
        jnp.einsum("bkgd,mkd->kgbm", grouped, key_rows, preferred_element_type=jnp.float32) * scale
    )
    row_ids = lax.broadcasted_iota(jnp.int32, (count, key_rows.shape[0]), 0)
    col_ids = lax.broadcasted_iota(jnp.int32, (count, key_rows.shape[0]), 1)
    allowed = (col_ids > row_ids) & (col_ids <= row_ids + WINDOW_SPAN)
    scores = jnp.where(allowed, scores, -jnp.inf)
    highest = jnp.max(scores, axis=-1, keepdims=True)
    weights = jnp.exp(scores - highest)
    weights = (weights / jnp.sum(weights, axis=-1, keepdims=True)).astype(jnp.bfloat16)
    mixed = jnp.einsum("kgbm,mkd->bkgd", weights, value_rows, preferred_element_type=jnp.float32)
    return mixed.astype(jnp.bfloat16).reshape(count, heads, -1)


def per_device(
    tokens,
    pre_gain,
    w_query,
    key_weight_matrix,
    value_weight_matrix,
    query_gain,
    key_norm_gain,
    prior_key_cache,
    prior_value_cache,
    w_out,
    post_gain,
):
    seq_tokens = tokens.shape[0]
    local_rows = seq_tokens // lax.axis_size("tp")
    head_size = query_gain.shape[0]
    query_cols = w_query.shape[1]
    key_cols = key_weight_matrix.shape[1]
    normed = root_mean_norm(tokens.astype(jnp.float32), pre_gain).astype(jnp.bfloat16)
    query_raw = jnp.dot(normed, w_query, preferred_element_type=jnp.float32)
    unnormed_keys = jnp.dot(normed, key_weight_matrix, preferred_element_type=jnp.float32)
    projected_values = jnp.dot(normed, value_weight_matrix, preferred_element_type=jnp.float32)
    seq_index = lax.axis_index("seq")
    token_positions = WINDOW_SPAN + seq_index * seq_tokens + jnp.arange(seq_tokens, dtype=jnp.int32)
    queries = rotary_embed_pairs(
        root_mean_norm(query_raw.reshape(seq_tokens, -1, head_size), query_gain), token_positions
    ).astype(jnp.bfloat16)
    block_keys = rotary_embed_pairs(
        root_mean_norm(unnormed_keys.reshape(seq_tokens, -1, head_size), key_norm_gain),
        token_positions,
    ).astype(jnp.bfloat16)
    key_flat = block_keys.reshape(seq_tokens, key_cols)
    value_flat = projected_values.astype(jnp.bfloat16)
    all_keys, all_values = in_one_piece((key_flat, value_flat), "seq", 0, 1)
    joined_keys = jnp.concatenate([prior_key_cache, all_keys], axis=0)
    joined_values = jnp.concatenate([prior_value_cache, all_values], axis=0)
    begin = seq_index * seq_tokens
    context_keys = lax.dynamic_slice_in_dim(joined_keys, begin, WINDOW_SPAN + seq_tokens, 0)
    context_values = lax.dynamic_slice_in_dim(joined_values, begin, WINDOW_SPAN + seq_tokens, 0)
    context_keys = context_keys.reshape(WINDOW_SPAN + seq_tokens, -1, head_size)
    context_values = context_values.reshape(WINDOW_SPAN + seq_tokens, -1, head_size)
    size = min(512, seq_tokens)
    scale = float(MODEL_WIDTH // HQ) ** (-0.5)
    outputs = []
    for number in range(seq_tokens // size):
        first_row = number * size
        outputs.append(
            attend_block(
                queries[first_row : first_row + size],
                context_keys[first_row : first_row + size + WINDOW_SPAN],
                context_values[first_row : first_row + size + WINDOW_SPAN],
                scale,
            )
        )
    attended = jnp.concatenate(outputs, axis=0).reshape(seq_tokens, query_cols)
    partial_value = jnp.dot(attended, w_out, preferred_element_type=jnp.float32)
    summed = lax.psum_scatter(
        partial_value.astype(jnp.bfloat16), "tp", scatter_dimension=0, tiled=True
    ).astype(jnp.float32)
    own_start = lax.axis_index("tp") * local_rows
    own_rows = lax.dynamic_slice_in_dim(tokens, own_start, local_rows, 0).astype(jnp.float32)
    return (own_rows + root_mean_norm(summed, post_gain)).astype(jnp.bfloat16)


def solution(mesh):
    return jax.shard_map(
        per_device,
        mesh=mesh,
        in_specs=(
            P("seq", None),
            P(),
            P(None, "tp"),
            P(None, "tp"),
            P(None, "tp"),
            P(),
            P(),
            P(None, "tp"),
            P(None, "tp"),
            P("tp", None),
            P(),
        ),
        out_specs=P(("seq", "tp"), None),
        check_vma=False,
    )
```

profile of v0, /device:TPU:0, one launch (start us, length us, event | category | flops | bytes accessed | tf_op | source)
XLA Modules:
  0.0 185.9 jit_solution(5513251860041485242)
XLA Ops:
  6.6 6.5 %fusion = f32[1024]{0:T(1024)S(1)} fusion(bf16[1024,5376]{1,0:T(8,128)(2,1)} %param.11), kind=kLoop, calls=%fused_computation.2 | loop fusion | flops 16514048 | bytes 11014144 | tf_op jit(solution)/shard_map/reduce_sum | solution.py:24
  13.1 0.0 copy-start.3
  13.1 6.8 %fusion.2 = bf16[1024,5376]{1,0:T(8,128)(2,1)S(1)} fusion(bf16[1024,5376]{1,0:T(8,128)(2,1)} %param.11, f32[5376]{0:T(1024)S(1)} %copy-done.10, f32[1024]{0:T(1024)S(1)} %add_rsqrt_fusion.2), kind=kLoop, calls=%fused_computation.4 | loop fusion | flops 22020096 | bytes 22045696 | tf_op jit(solution)/shard_map/convert_element_type | solution.py:79
  19.9 3.7 %convolution_convert_fusion.1 = bf16[1024,128]{0,1:T(8,128)(2,1)S(1)} fusion(bf16[1024,5376]{1,0:T(8,128)(2,1)S(1)} %fusion.2, bf16[5376,128]{1,0:T(8,128)(2,1)S(1)} %copy-done.3), kind=kOutput, calls=%fused_computation.35 | convolution fusion | flops 1409417216 | bytes 12648448 | tf_op jit(solution)/shard_map/dot_general | solution.py:82
  23.7 0.4 copy-done.1
  24.1 3.7 %multiply_reduce_fusion.1 = (f32[1024]{0:T(1024)S(1)}, f32[1024,128]{0,1:T(8,128)S(1)}) fusion(bf16[1024,5376]{1,0:T(8,128)(2,1)S(1)} %fusion.2, bf16[5376,128]{1,0:T(8,128)(2,1)S(1)} %copy-done.2), kind=kOutput, calls=%fused_computation.51 | convolution fusion | flops 1409547264 | bytes 12914688 | tf_op jit(solution)/shard_map/dot_general | solution.py:81
  27.9 0.1 multiply_bitcast_fusion
  28.0 1.2 fusion.41
  29.1 0.9 pad_maximum_fusion
  30.0 0.0 all-gather.2.cloned.1.call-update
  30.0 0.2 reduce-scatter.2.cloned.1.call-start
  30.3 0.8 copy.13
  31.1 0.8 copy.12
  32.0 9.0 %multiply_reduce_fusion = (f32[1024,2]{0,1:T(2,128)S(1)}, f32[1024,256]{0,1:T(8,128)}) fusion(bf16[1024,5376]{1,0:T(8,128)(2,1)} %copy-done.1, bf16[5376,256]{1,0:T(8,128)(2,1)} %param.13), kind=kOutput, calls=%fused_computation.39 | convolution fusion | flops 2819094528 | bytes 14819328 | tf_op jit(solution)/shard_map/dot_general | solution.py:80
  40.9 2.6 %copy.14 = f32[1024,2,128]{2,0,1:T(8,128)} copy(f32[1024,2,128]{0,2,1:T(8,128)} %bitcast.81) | data formatting | bytes 2097152 | tf_op jit(solution)/shard_map/reshape | solution.py:86
  43.5 1.9 %multiply_cosine_fusion = (f32[1024,64]{1,0:T(8,128)S(1)}, f32[1024,64]{1,0:T(8,128)S(1)}) fusion(f32[64]{0:T(128)S(1)} %multiply_power_fusion, f32[1024]{0:T(1024)S(1)} %add_convert_fusion.1), kind=kLoop, calls=%fused_computation.41 | loop fusion | flops 65536 | bytes 528640 | tf_op jit(solution)/shard_map/cos | solution.py:33
  45.4 1.6 multiply_multiply_fusion
  47.0 1.5 subtract_convert_fusion
  48.5 0.6 fusion.11
  49.0 15.7 %all-gather.2.cloned.1.call-done = bf16[8192,256]{0,1:T(8,128)(2,1)} async-done(((bf16[1024,256]{0,1:T(8,128)(2,1)}), bf16[8192,256]{0,1:T(8,128)(2,1)}) %all-gather.2.cloned.1.call-update) | async-done | bytes 4194320 | tf_op jit(solution)/shard_map/all_gather | solution.py:16
  64.8 2.8 %fusion.49 = (bf16[8192,128]{0,1:T(8,128)(2,1)S(1)}, bf16[8192,128]{0,1:T(8,128)(2,1)S(1)}) fusion(bf16[8192,256]{0,1:T(8,128)(2,1)} %all-gather.2.cloned.1.call-done), kind=kLoop, calls=%fused_computation.87 | loop fusion | bytes 8388608 | tf_op jit(solution)/shard_map/slice | solution.py:18
  67.6 0.3 fusion.22
  67.9 1.5 fusion.5
  69.5 2.9 %fusion.3 = (f32[2,512]{1,0:T(2,128)S(1)}, f32[2,512]{1,0:T(2,128)S(1)}, f32[1536,512,2]{1,0,2:T(8,128)S(1)}) fusion(f32[1536,512,2]{1,0,2:T(8,128)S(1)} %get-tuple-element.20, f32[2,512]{1,0:T(2,128)S(1)} %get-tuple-element.19, pred[512,1536]{0,1:T(8,128)(4,1)S(1)} %fusion.11, bf16[1024,2,64]{2,0,1:T(8,128)(2,1)S(1)} %copy-done.7, ...), kind=kOutput, calls=%fused_computation.12 | convolution fusion | flops 414185472 | bytes 14823424 | tf_op jit(solution)/shard_map/bkgd,mkd->kgbm/dot_general | solution.py:48
  72.4 2.4 %fusion.16 = bf16[128,2,512]{2,0,1:T(8,128)(2,1)S(1)} fusion(f32[2,512]{1,0:T(2,128)S(1)} %get-tuple-element.5, f32[2,512]{1,0:T(2,128)S(1)} %get-tuple-element.19, f32[1536,512,2]{1,0,2:T(8,128)S(1)} %get-tuple-element.20, pred[512,1536]{0,1:T(8,128)(4,1)S(1)} %fusion.11, bf16[2048,128]{0,1:T(8,128)(2,1)S(1)} %get-tuple-element.23), kind=kOutput, calls=%fused_computation.33 | convolution fusion | flops 410648576 | bytes 7741440 | tf_op jit(solution)/shard_map/kgbm,mkd->bkgd/dot_general | solution.py:57
  74.8 1.5 fusion.4
  76.2 2.2 %fusion.19 = bf16[128,2,512]{2,0,1:T(8,128)(2,1)S(1)} fusion(f32[2,512]{1,0:T(2,128)S(1)} %fusion.4, f32[2,512]{1,0:T(2,128)S(1)} %get-tuple-element.6, f32[1536,512,2]{1,0,2:T(8,128)S(1)} %get-tuple-element.21, pred[512,1536]{0,1:T(8,128)(4,1)S(1)} %fusion.11, bf16[2048,128]{0,1:T(8,128)(2,1)S(1)} %get-tuple-element.23), kind=kOutput, calls=%fused_computation.34 | convolution fusion | flops 410648576 | bytes 7741440 | tf_op jit(solution)/shard_map/kgbm,mkd->bkgd/dot_general | solution.py:57
  78.4 5.9 %convolution_convert_fusion = bf16[1024,5376]{1,0:T(8,128)(2,1)} fusion(bf16[256,5376]{1,0:T(8,128)(2,1)S(1)} %copy-done, bf16[512,256]{0,1:T(8,128)(2,1)S(1)} %bitcast.83, bf16[512,256]{0,1:T(8,128)(2,1)S(1)} %bitcast.82), kind=kOutput, calls=%fused_computation.5 | convolution fusion | flops 2825125888 | bytes 14286848 | tf_op jit(solution)/shard_map/dot_general | solution.py:116
  84.3 0.0 reduce-scatter.2.cloned.1.call-update
  84.3 90.9 %reduce-scatter.2.cloned.1.call-done = bf16[64,5376]{1,0:T(8,128)(2,1)} async-done(((bf16[1024,5376]{1,0:T(8,128)(2,1)}), bf16[64,5376]{1,0:T(8,128)(2,1)}) %reduce-scatter.2.cloned.1.call-update) | async-done | bytes 688144 | tf_op jit(solution)/shard_map/reduce_scatter | solution.py:117
  175.2 1.3 fusion.12
  176.6 2.5 %fusion.15 = bf16[64,5376]{1,0:T(8,128)(2,1)} fusion(bf16[64,5376]{1,0:T(8,128)(2,1)} %reduce-scatter.2.cloned.1.call-done, f32[5376]{0:T(1024)S(1)} %copy-done.11, f32[64]{0:T(128)S(1)} %add_rsqrt_fusion.3, bf16[1024,5376]{1,0:T(8,128)(2,1)} %param.11, s32[]{:T(128)S(6)} %select_n.14), kind=kLoop, calls=%fused_computation.32 | loop fusion | flops 2064384 | bytes 2086148 | tf_op jit(solution)/shard_map/convert_element_type | solution.py:122
  (34 shorter events, 0.1 us)
Async XLA Ops:
  6.5 71.9 %copy-start = (bf16[256,5376]{1,0:T(8,128)(2,1)S(1)}, bf16[256,5376]{1,0:T(8,128)(2,1)}, u32[]{:S(2)}) copy-start(bf16[256,5376]{1,0:T(8,128)(2,1)} %param.20) | copy-start | bytes 8257540
  6.5 6.5 %copy-start.10 = (f32[5376]{0:T(1024)S(1)}, f32[5376]{0:T(1024)}, u32[]{:S(2)}) copy-start(f32[5376]{0:T(1024)} %param.12) | copy-start | bytes 64516
  6.5 58.2 %all-gather.2.cloned.1.call-start = ((), (), s32[]{:S(2)}) async-start(), calls=%async_computation.1 | async-start | bytes 4718592 | tf_op jit(solution)/shard_map/all_gather | solution.py:16
  13.1 6.8 %copy-start.3 = (bf16[5376,128]{1,0:T(8,128)(2,1)S(1)}, bf16[5376,128]{1,0:T(8,128)(2,1)}, u32[]{:S(2)}) copy-start(bf16[5376,128]{1,0:T(8,128)(2,1)} %param.15) | copy-start | bytes 4128772
  19.9 4.2 %copy-start.1 = (bf16[1024,5376]{1,0:T(8,128)(2,1)}, bf16[1024,5376]{1,0:T(8,128)(2,1)S(1)}, u32[]{:S(2)}) copy-start(bf16[1024,5376]{1,0:T(8,128)(2,1)S(1)} %fusion.2) | copy-start | bytes 33030148
  19.9 4.2 %copy-start.2 = (bf16[5376,128]{1,0:T(8,128)(2,1)S(1)}, bf16[5376,128]{1,0:T(8,128)(2,1)}, u32[]{:S(2)}) copy-start(bf16[5376,128]{1,0:T(8,128)(2,1)} %param.14) | copy-start | bytes 4128772
  24.1 3.8 %copy-start.12 = (f32[128]{0:T(128)S(1)}, f32[128]{0:T(128)}, u32[]{:S(2)}) copy-start(f32[128]{0:T(128)} %param.17) | copy-start | bytes 1540
  24.1 6.2 %copy-start.8 = (bf16[1024,128]{1,0:T(8,128)(2,1)S(1)}, bf16[1024,128]{1,0:T(8,128)(2,1)}, u32[]{:S(2)}) copy-start(bf16[1024,128]{1,0:T(8,128)(2,1)} %param.18) | copy-start | bytes 786436
  24.1 7.0 %copy-start.9 = (bf16[1024,128]{1,0:T(8,128)(2,1)S(1)}, bf16[1024,128]{1,0:T(8,128)(2,1)}, u32[]{:S(2)}) copy-start(bf16[1024,128]{1,0:T(8,128)(2,1)} %param.19) | copy-start | bytes 786436
  30.0 145.2 %reduce-scatter.2.cloned.1.call-start = ((), (), s32[]{:S(2)}) async-start(), calls=%async_computation.2 | async-start | bytes 11698176 | tf_op jit(solution)/shard_map/reduce_scatter | solution.py:117
  32.0 13.5 %copy-start.13 = (f32[128]{0:T(128)S(1)}, f32[128]{0:T(128)}, u32[]{:S(2)}) copy-start(f32[128]{0:T(128)} %param.16) | copy-start | bytes 1540
  64.8 2.8 %copy-start.4 = (bf16[1024,128]{0,1:T(8,128)(2,1)S(1)}, bf16[1024,128]{0,1:T(8,128)(2,1)}, u32[]{:S(2)}) copy-start(bf16[1024,128]{0,1:T(8,128)(2,1)} %copy.13) | copy-start | bytes 786436
  64.8 2.8 %copy-start.5 = (bf16[1024,128]{0,1:T(8,128)(2,1)S(1)}, bf16[1024,128]{0,1:T(8,128)(2,1)}, u32[]{:S(2)}) copy-start(bf16[1024,128]{0,1:T(8,128)(2,1)} %copy.12) | copy-start | bytes 786436
  64.8 3.1 %copy-start.6 = (bf16[1024,2,64]{2,0,1:T(8,128)(2,1)S(1)}, bf16[1024,2,64]{2,0,1:T(8,128)(2,1)}, u32[]{:S(2)}) copy-start(bf16[1024,2,64]{2,0,1:T(8,128)(2,1)} %get-tuple-element.9) | copy-start | bytes 786436
  64.8 3.1 %copy-start.7 = (bf16[1024,2,64]{2,0,1:T(8,128)(2,1)S(1)}, bf16[1024,2,64]{2,0,1:T(8,128)(2,1)}, u32[]{:S(2)}) copy-start(bf16[1024,2,64]{2,0,1:T(8,128)(2,1)} %get-tuple-element.10) | copy-start | bytes 786436
  84.3 92.3 %copy-start.11 = (f32[5376]{0:T(1024)S(1)}, f32[5376]{0:T(1024)}, u32[]{:S(2)}) copy-start(f32[5376]{0:T(1024)} %param.21) | copy-start | bytes 64516
Sparse Core Ops, SparseCore 0:
  30.1 34.5 all-gather.1
  84.5 90.7 reduce-scatter.1
where the time goes:
time: 186 us
  waiting for transfers between devices  107 us (58%)
  matrix products  31.3 us (17%)
  other arithmetic  26.5 us (14%)
  between operations  13.6 us (7%)
  local copies, waits for them, and re-layouts  7.52 us (4%)
    reduce_scatter x1, waiting for transfers between devices, per_device(): lax.psum_scatter(partial_value.astype(jnp.bfloat16), 'tp', scatter_dimens...  90.9 us
    all_gather x1, waiting for transfers between devices, in_one_piece(): lax.all_gather(both, axis, axis=dim, tiled=True)  15.7 us
    dot_general x1, matrix products, per_device(): query_raw = jnp.dot(normed, w_query, preferred_element_type=jnp.float32)  8.96 us
    reduce_sum x2, other arithmetic, root_mean_norm(): mean_square = jnp.mean(values * values, axis=-1, keepdims=True)  7.81 us
    convert_element_type x1, other arithmetic, per_device(): root_mean_norm(tokens.astype(jnp.float32), pre_gain).astype(jnp.bfloat16)  6.82 us
    dot_general x1, matrix products, per_device(): partial_value = jnp.dot(attended, w_out, preferred_element_type=jnp.float32)  5.88 us
    dot_general x2, matrix products, attend_block(): jnp.einsum('kgbm,mkd->bkgd', weights, value_rows, preferred_element_type=...  4.53 us
    dot_general x2, matrix products, attend_block(): jnp.einsum('bkgd,mkd->kgbm', grouped, key_rows, preferred_element_type=jn...  4.45 us
  transfers between devices with their start and end apart: 2, of which 2 were waited for; matrix products, arithmetic and copies ran while one was open for 10% of the time, Pallas kernels for 0%

commit v1 on v0

v1 whole, which is shorter than its diff:
```python
import functools

import jax
import jax.numpy as jnp
import numpy as np
from jax import lax
from jax.experimental import pallas as pl
from jax.experimental.pallas import tpu as pltpu
from jax.sharding import Mesh
from jax.sharding import PartitionSpec as P

MODEL_WIDTH = 5376
HQ = 32
HEAD = 128
WINDOW_SPAN = 1024
BLOCK_TOKENS = 8192
SHARD = 1024
EPSILON = 1e-06
LOG2E = 1.4426950408889634
SCORE_SCALE = float(MODEL_WIDTH // HQ) ** (-0.5)

F32 = jnp.float32
BF16 = jnp.bfloat16

ROWS = 256
GROUP = 16
HALF = 128


def rotary_table():
    half = HEAD // 2
    exponent = np.arange(half, dtype=np.float32) * np.float32(-2.0 / HEAD)
    frequency = np.power(np.float64(10000.0), exponent.astype(np.float64)).astype(np.float32)
    position = (WINDOW_SPAN + np.arange(BLOCK_TOKENS)).astype(np.float32)
    angle = (position[:, None] * frequency[None, :]).astype(np.float64)
    return np.concatenate([np.cos(angle), np.sin(angle)], axis=1).astype(np.float32)


def project_kernel(
    seq_ref, tok_ref, g_ref, wq_ref, wk_ref, wv_ref, qg_ref, kg_ref, tab_ref,
    q_ref, kv_ref, w_all, g_all, normed,
):
    @pl.when(pl.program_id(0) == 0)
    def _():
        w_all[:, 0:256] = wq_ref[...]
        w_all[:, 256:384] = wk_ref[...]
        w_all[:, 384:512] = wv_ref[...]
        g_all[...] = jnp.broadcast_to(g_ref[...], g_all.shape)

    blocks = MODEL_WIDTH // 128

    def norm_group(i, carry):
        rows = pl.ds(pl.multiple_of(i * GROUP, GROUP), GROUP)
        parts = [jnp.zeros((GROUP, 128), F32) for _ in range(2)]
        for b in range(blocks):
            v = tok_ref[rows, b * 128 : (b + 1) * 128].astype(F32)
            parts[b % 2] = parts[b % 2] + v * v
        mean = jnp.sum(parts[0] + parts[1], axis=-1, keepdims=True) * (1.0 / MODEL_WIDTH)
        r = lax.rsqrt(mean + EPSILON)
        for b in range(blocks):
            cols = slice(b * 128, (b + 1) * 128)
            v = tok_ref[rows, cols].astype(F32)
            normed[rows, cols] = (v * r * g_all[:, cols]).astype(BF16)
        return carry

    lax.fori_loop(0, ROWS // GROUP, norm_group, 0)
    raw = jnp.dot(normed[...], w_all[...], preferred_element_type=F32)

    table = tab_ref[...]
    swapped = pltpu.roll(table, 64, 1)
    low = lax.broadcasted_iota(jnp.int32, table.shape, 1) < 64
    cosine = jnp.where(low, table, swapped)
    sine = jnp.where(low, -swapped, table)

    def rotate(u, gain):
        mean = jnp.sum(u * u, axis=-1, keepdims=True) * (1.0 / HEAD)
        u = u * lax.rsqrt(mean + EPSILON) * gain
        return (u * cosine + pltpu.roll(u, 64, 1) * sine).astype(BF16)

    q_ref[:, 0:128] = rotate(raw[:, 0:128], qg_ref[...])
    q_ref[:, 128:256] = rotate(raw[:, 128:256], qg_ref[...])
    kv_ref[:, 0:128] = rotate(raw[:, 256:384], kg_ref[...])
    kv_ref[:, 128:256] = raw[:, 384:512].astype(BF16)


def project(seq, tokens, pre_gain, wq, wk, wv, q_gain, k_gain, table):
    whole = lambda shape: pl.BlockSpec(shape, lambda i, s: (0, 0))
    return pl.pallas_call(
        project_kernel,
        grid_spec=pltpu.PrefetchScalarGridSpec(
            num_scalar_prefetch=1,
            grid=(SHARD // ROWS,),
            in_specs=[
                pl.BlockSpec((ROWS, MODEL_WIDTH), lambda i, s: (i, 0)),
                whole((1, MODEL_WIDTH)),
                whole((MODEL_WIDTH, 256)),
                whole((MODEL_WIDTH, 128)),
                whole((MODEL_WIDTH, 128)),
                whole((1, 128)),
                whole((1, 128)),
                pl.BlockSpec((ROWS, 128), lambda i, s: (s[0] * (SHARD // ROWS) + i, 0)),
            ],
            out_specs=[
                pl.BlockSpec((ROWS, 256), lambda i, s: (i, 0)),
                pl.BlockSpec((ROWS, 256), lambda i, s: (i, 0)),
            ],
            scratch_shapes=[
                pltpu.VMEM((MODEL_WIDTH, 512), BF16),
                pltpu.VMEM((GROUP, MODEL_WIDTH), F32),
                pltpu.VMEM((ROWS, MODEL_WIDTH), BF16),
            ],
        ),
        out_shape=[
            jax.ShapeDtypeStruct((SHARD, 256), BF16),
            jax.ShapeDtypeStruct((SHARD, 256), BF16),
        ],
        compiler_params=pltpu.CompilerParams(vmem_limit_bytes=48 << 20),
        cost_estimate=pl.CostEstimate(
            flops=2 * SHARD * MODEL_WIDTH * 512, bytes_accessed=18 << 20, transcendentals=0
        ),
        name="project",
    )(
        seq, tokens, pre_gain.reshape(1, -1), wq, wk, wv,
        q_gain.reshape(1, -1), k_gain.reshape(1, -1), table,
    )


def attend_kernel(pos_ref, q_ref, kv_ref, got_ref, pk_ref, pv_ref, out_ref, keys, values):
    @pl.when(pos_ref[0] == 0)
    def _():
        keys[0:SHARD] = pk_ref[...]
        values[0:SHARD, 0:128] = pv_ref[...]

    @pl.when(pos_ref[0] != 0)
    def _():
        keys[0:SHARD] = got_ref[:, 0:128]
        values[0:SHARD, 0:128] = got_ref[:, 128:256]

    keys[SHARD:] = kv_ref[:, 0:128]
    values[SHARD:, 0:128] = kv_ref[:, 128:256]
    values[:, 128:256] = jnp.ones((2 * SHARD, 128), BF16)

    span = HALF + WINDOW_SPAN
    row = lax.broadcasted_iota(jnp.int32, (2 * HALF, HALF), 0) % HALF
    col = lax.broadcasted_iota(jnp.int32, (2 * HALF, HALF), 1)
    lowest = jnp.float32(-jnp.inf)
    for part in range(out_ref.shape[0] // HALF):
        first = pl.multiple_of(pos_ref[1 + part], HALF)
        q = q_ref[pl.ds(first, HALF), :]
        q = jnp.concatenate([q[:, 0:128], q[:, 128:256]], axis=0)
        k = keys[pl.ds(first, span), :]
        scores = lax.dot_general(q, k, (((1,), (1,)), ((), ())), preferred_element_type=F32)
        scores = jnp.concatenate(
            [
                jnp.where(col > row, scores[:, 0:HALF], lowest),
                scores[:, HALF:WINDOW_SPAN],
                jnp.where(col <= row, scores[:, WINDOW_SPAN:], lowest),
            ],
            axis=1,
        )
        top = jnp.max(scores, axis=-1, keepdims=True)
        weights = jnp.exp2((scores - top) * (SCORE_SCALE * LOG2E)).astype(BF16)
        mixed = jnp.dot(weights, values[pl.ds(first, span), :], preferred_element_type=F32)
        mixed = (mixed[:, 0:128] / mixed[:, 128:256]).astype(BF16)
        out_ref[part * HALF : (part + 1) * HALF, 0:128] = mixed[0:HALF]
        out_ref[part * HALF : (part + 1) * HALF, 128:256] = mixed[HALF:]


def attend(pos, q, kv, got, prior_k, prior_v, parts):
    vmem = pl.BlockSpec(memory_space=pltpu.VMEM)
    return pl.pallas_call(
        attend_kernel,
        in_specs=[pl.BlockSpec(memory_space=pltpu.SMEM)] + [vmem] * 5,
        out_specs=vmem,
        out_shape=jax.ShapeDtypeStruct((parts * HALF, 256), BF16),
        scratch_shapes=[
            pltpu.VMEM((2 * SHARD, 128), BF16),
            pltpu.VMEM((2 * SHARD, 256), BF16),
        ],
        compiler_params=pltpu.CompilerParams(vmem_limit_bytes=32 << 20),
        cost_estimate=pl.CostEstimate(
            flops=8 * parts * HALF * 1152 * 256, bytes_accessed=2 << 20,
            transcendentals=parts * 2 * HALF * 1152,
        ),
        name="attend",
    )(pos, q, kv, got, prior_k, prior_v)


def per_device(
    tokens, pre_gain, w_query, key_weight, value_weight, query_gain, key_gain,
    prior_key, prior_value, w_out, post_gain, table,
):
    seq = lax.axis_index("y") * 2 + lax.axis_index("c")
    tp = lax.axis_index("x") * 4 + lax.axis_index("z")
    q, kv = project(
        seq.reshape(1), tokens, pre_gain, w_query, key_weight, value_weight,
        query_gain, key_gain, table,
    )
    got = lax.ppermute(kv, ("y", "c"), [(i, i + 1) for i in range(7)])
    steps = []
    for step in range(4):
        pos = jnp.stack([seq, jnp.int32(step * 256), jnp.int32(step * 256 + 128)])
        steps.append(attend(pos, q, kv, got, prior_key, prior_value, 2))
    attended = jnp.concatenate(steps, axis=0)
    partial = jnp.dot(attended, w_out, preferred_element_type=F32)
    summed = lax.psum_scatter(
        partial.astype(BF16), ("x", "z"), scatter_dimension=0, tiled=True
    ).astype(F32)
    own = lax.dynamic_slice_in_dim(tokens, tp * 64, 64, 0).astype(F32)
    mean = jnp.mean(summed * summed, axis=-1, keepdims=True)
    return (own + summed * lax.rsqrt(mean + EPSILON) * post_gain).astype(BF16)


def solution(mesh):
    fine = Mesh(mesh.devices.reshape(4, 2, 4, 4), ("y", "c", "x", "z"))
    seq, tp = ("y", "c"), ("x", "z")
    inner = jax.shard_map(
        per_device,
        mesh=fine,
        in_specs=(
            P(seq, None), P(), P(None, tp), P(None, tp), P(None, tp), P(), P(),
            P(None, tp), P(None, tp), P(tp, None), P(), P(),
        ),
        out_specs=P(seq + tp, None),
        check_vma=False,
    )

    def run(*args):
        return inner(*args, jnp.asarray(rotary_table()))

    return run
```

time: 186 us -> 162 us (0.87)
  Pallas kernels: 0 us -> 27.9 us
  matrix products: 31.3 us -> 7.06 us
  other arithmetic: 26.5 us -> 3.97 us
  waiting for transfers between devices: 107 us -> 103 us
  local copies, waits for them, and re-layouts: 7.52 us -> 4.9 us
    pallas_call x0 -> x5, Pallas kernels: none -> 27.9 us  [the longest x1 20.2 us: project(): pl.pallas_call(project_kernel, grid_spec=pltpu.PrefetchScalarGridSpec(num...]
    dot_general x8 -> x1, matrix products: 31.3 us -> 7.06 us  [per_device(): partial = jnp.dot(attended, w_out, preferred_element_type=F32)]
    all_gather x1 -> x0, waiting for transfers between devices: 15.7 us -> none  [in_one_piece(): lax.all_gather(both, axis, axis=dim, tiled=True)]
    reduce_scatter x1, waiting for transfers between devices: 90.9 us -> 101 us  [per_device(): lax.psum_scatter(partial.astype(BF16), ('x', 'z'), scatter_dimension=0, t...]
    reduce_sum x3 -> x1, other arithmetic: 9.3 us -> 1.33 us  [per_device(): mean = jnp.mean(summed * summed, axis=-1, keepdims=True)]
    convert_element_type x3 -> x1, other arithmetic: 9.3 us -> 2.48 us  [per_device(): return (own + summed * lax.rsqrt(mean + EPSILON) * post_gain).astype(BF16)]
    slice x1 -> x0, local copies, waits for them, and re-layouts: 2.77 us -> none  [in_one_piece(): lax.slice_in_dim(filled, at, at + a.shape[along], axis=along)]
    concatenate x3 -> x0, other arithmetic: 2.33 us -> none  [the longest x1 1.16 us: rotary_embed_pairs(): jnp.concatenate([first * cosine - second * sine, second * cosine + first...]
  transfers between devices with their start and end apart: 2 -> 2, of which waited for: 2 -> 2; matrix products, arithmetic and copies ran while one was open for 10% -> 0% of each run, Pallas kernels for 0% -> 0%
where the time goes in v1:
time: 162 us; the launch traced here: 161 us
  waiting for transfers between devices  103 us (64%)
  Pallas kernels  27.9 us (17%)
  between operations  13.5 us (8%)
  matrix products  7.06 us (4%)
  local copies, waits for them, and re-layouts  4.9 us (3%)
  other arithmetic  3.97 us (2%)
    reduce_scatter x1, waiting for transfers between devices, per_device(): lax.psum_scatter(partial.astype(BF16), ('x', 'z'), scatter_dimension=0, t...  101 us
    pallas_call x1, Pallas kernels, project(): pl.pallas_call(project_kernel, grid_spec=pltpu.PrefetchScalarGridSpec(num...  20.2 us
    pallas_call x4, Pallas kernels, attend(): pl.pallas_call(attend_kernel, in_specs=[pl.BlockSpec(memory_space=pltpu.S...  7.7 us
    dot_general x1, matrix products, per_device(): partial = jnp.dot(attended, w_out, preferred_element_type=F32)  7.06 us
    unnamed x16, local copies, waits for them, and re-layouts  4 us
  transfers between devices with their start and end apart: 2, of which 2 were waited for; matrix products, arithmetic and copies ran while one was open for 0% of the time, Pallas kernels for 0%

profile of v1, /device:TPU:0, one launch (start us, length us, event | category | flops | bytes accessed | tf_op | source)
XLA Modules:
  0.0 161.5 jit_solution(15709416916929950361)
XLA Ops:
  6.5 0.0 copy-start
  6.5 0.0 reduce-scatter.2.cloned.1.call-start
  6.5 0.9 reshape.19.g_ref
  7.5 0.0 copy-start.1
  7.5 1.3 copy-done.1
  8.8 0.0 copy-start.2
  8.8 1.3 copy-done.2
  10.1 0.0 copy-start.5
  10.1 0.7 copy-done.5
  10.8 0.0 copy-start.6
  10.8 0.7 copy-done.6
  11.4 0.0 copy-start.3
  11.4 0.0 copy-start.4
  11.5 20.2 %project.1 = (bf16[1024,256]{1,0:T(8,128)(2,1)S(1)}, bf16[1024,256]{1,0:T(8,128)(2,1)S(1)}) custom-call(s32[1]{0:T(128)} %bitcast.seq_ref, bf16[1024,5376]{1,0:T(8,128)(2,1)} %tok_ref.1, f32[1,5376]{1,0:T(1,128)S(1)} %reshape.19.g_ref, bf16[5376,256]{1,0:T(8,128)(2,1)} %wq_ref.1, bf16[5376,128]{1,0:T(8,128)(2,1)S(1)} %copy-done.1, ...), custom_call_target="tpu_custom_call" | custom-call | flops 5637144576 | bytes 18874368 | tf_op jit(solution)/shard_map/project/pallas_call | solution.py:88
  31.7 1.3 collective-permute-start
  33.0 0.1 pad_add_fusion.2
  33.1 0.1 pad_add_fusion
  33.2 1.3 collective-permute-done.got_ref
  34.5 0.0 copy-done.3
  34.5 0.0 copy-done.4
  34.5 1.9 %attend.7 = bf16[256,256]{1,0:T(8,128)(2,1)S(1)} custom-call(s32[3]{0:T(128)S(1)} %get-tuple-element.12.pos_ref, bf16[1024,256]{1,0:T(8,128)(2,1)S(1)} %get-tuple-element.7.q_ref, bf16[1024,256]{1,0:T(8,128)(2,1)S(1)} %get-tuple-element.8.kv_ref, bf16[1024,256]{1,0:T(8,128)(2,1)S(1)} %collective-permute-done.got_ref, bf16[1024,128]{1,0:T(8,128)(2,1)S(1)} %copy-done.3, ...), custom_call_target="tpu_custom_call" | custom-call | flops 603979776 | bytes 2097152 | tf_op jit(solution)/shard_map/attend/pallas_call | solution.py:171
  36.5 1.9 %attend.6 = bf16[256,256]{1,0:T(8,128)(2,1)S(1)} custom-call(s32[3]{0:T(128)S(1)} %get-tuple-element.11.pos_ref, bf16[1024,256]{1,0:T(8,128)(2,1)S(1)} %get-tuple-element.7.q_ref, bf16[1024,256]{1,0:T(8,128)(2,1)S(1)} %get-tuple-element.8.kv_ref, bf16[1024,256]{1,0:T(8,128)(2,1)S(1)} %collective-permute-done.got_ref, bf16[1024,128]{1,0:T(8,128)(2,1)S(1)} %copy-done.3, ...), custom_call_target="tpu_custom_call" | custom-call | flops 603979776 | bytes 2097152 | tf_op jit(solution)/shard_map/attend/pallas_call | solution.py:171
  38.4 1.9 %attend.5 = bf16[256,256]{1,0:T(8,128)(2,1)S(1)} custom-call(s32[3]{0:T(128)S(1)} %get-tuple-element.10.pos_ref, bf16[1024,256]{1,0:T(8,128)(2,1)S(1)} %get-tuple-element.7.q_ref, bf16[1024,256]{1,0:T(8,128)(2,1)S(1)} %get-tuple-element.8.kv_ref, bf16[1024,256]{1,0:T(8,128)(2,1)S(1)} %collective-permute-done.got_ref, bf16[1024,128]{1,0:T(8,128)(2,1)S(1)} %copy-done.3, ...), custom_call_target="tpu_custom_call" | custom-call | flops 603979776 | bytes 2097152 | tf_op jit(solution)/shard_map/attend/pallas_call | solution.py:171
  40.3 1.9 %attend.4 = bf16[256,256]{1,0:T(8,128)(2,1)S(1)} custom-call(s32[3]{0:T(128)S(1)} %get-tuple-element.9.pos_ref, bf16[1024,256]{1,0:T(8,128)(2,1)S(1)} %get-tuple-element.7.q_ref, bf16[1024,256]{1,0:T(8,128)(2,1)S(1)} %get-tuple-element.8.kv_ref, bf16[1024,256]{1,0:T(8,128)(2,1)S(1)} %collective-permute-done.got_ref, bf16[1024,128]{1,0:T(8,128)(2,1)S(1)} %copy-done.3, ...), custom_call_target="tpu_custom_call" | custom-call | flops 603979776 | bytes 2097152 | tf_op jit(solution)/shard_map/attend/pallas_call | solution.py:171
  42.2 0.0 copy-done
  42.3 7.1 %convolution_convert_fusion = bf16[1024,5376]{1,0:T(8,128)(2,1)} fusion(bf16[256,5376]{1,0:T(8,128)(2,1)S(1)} %copy-done, bf16[256,256]{1,0:T(8,128)(2,1)S(1)} %attend.7, bf16[256,256]{1,0:T(8,128)(2,1)S(1)} %attend.6, bf16[256,256]{1,0:T(8,128)(2,1)S(1)} %attend.5, bf16[256,256]{1,0:T(8,128)(2,1)S(1)} %attend.4), kind=kOutput, calls=%fused_computation | convolution fusion | flops 2826174464 | bytes 14286848 | tf_op jit(solution)/shard_map/dot_general | solution.py:205
  49.3 0.0 copy-start.7
  49.3 0.0 reduce-scatter.2.cloned.1.call-update
  49.3 101.5 %reduce-scatter.2.cloned.1.call-done = bf16[64,5376]{1,0:T(8,128)(2,1)} async-done(((bf16[1024,5376]{1,0:T(8,128)(2,1)}), bf16[64,5376]{1,0:T(8,128)(2,1)}) %reduce-scatter.2.cloned.1.call-update) | async-done | bytes 688144 | tf_op jit(solution)/shard_map/reduce_scatter | solution.py:206
  150.8 1.3 fusion
  152.2 0.0 copy-done.7
  152.2 2.5 %fusion.3 = bf16[64,5376]{1,0:T(8,128)(2,1)} fusion(bf16[64,5376]{1,0:T(8,128)(2,1)} %reduce-scatter.2.cloned.1.call-done, f32[5376]{0:T(1024)S(1)} %copy-done.7, f32[64]{0:T(128)S(1)} %add_rsqrt_fusion, bf16[1024,5376]{1,0:T(8,128)(2,1)} %tok_ref.1, s32[]{:T(128)S(6)} %select_n.3), kind=kLoop, calls=%fused_computation.6 | loop fusion | flops 2064384 | bytes 2086148 | tf_op jit(solution)/shard_map/convert_element_type | solution.py:211
  (1 shorter events, 0.0 us)
Async XLA Ops:
  6.5 35.7 %copy-start = (bf16[256,5376]{1,0:T(8,128)(2,1)S(1)}, bf16[256,5376]{1,0:T(8,128)(2,1)}, u32[]{:S(2)}) copy-start(bf16[256,5376]{1,0:T(8,128)(2,1)} %param.21) | copy-start | bytes 8257540
  6.5 144.3 %reduce-scatter.2.cloned.1.call-start = ((), (), s32[]{:S(2)}) async-start(), calls=%async_computation.1 | async-start | bytes 11698176 | tf_op jit(solution)/shard_map/reduce_scatter | solution.py:206
  7.5 1.3 copy-start.1
  8.8 1.3 copy-start.2
  10.1 0.7 copy-start.5
  10.8 0.7 copy-start.6
  11.4 23.1 %copy-start.3 = (bf16[1024,128]{1,0:T(8,128)(2,1)S(1)}, bf16[1024,128]{1,0:T(8,128)(2,1)}, u32[]{:S(2)}) copy-start(bf16[1024,128]{1,0:T(8,128)(2,1)} %pk_ref.7) | copy-start | bytes 786436
  11.4 23.1 %copy-start.4 = (bf16[1024,128]{1,0:T(8,128)(2,1)S(1)}, bf16[1024,128]{1,0:T(8,128)(2,1)}, u32[]{:S(2)}) copy-start(bf16[1024,128]{1,0:T(8,128)(2,1)} %pv_ref.7) | copy-start | bytes 786436
  31.7 2.8 %collective-permute-start = (bf16[1024,256]{1,0:T(8,128)(2,1)S(1)}, bf16[1024,256]{1,0:T(8,128)(2,1)S(1)}, u32[]{:S(2)}, u32[]{:S(2)}) collective-permute-start(bf16[1024,256]{1,0:T(8,128)(2,1)S(1)} %get-tuple-element.8.kv_ref), channel_id=1, source_target_pairs={{0,16},{16,32},{32,48},{48,64},{64,80},{80,96},{96,112},{1,17},{17... | collective-permute-start | bytes 1572872 | tf_op jit(solution)/shard_map/ppermute | solution.py:199
  49.3 102.8 %copy-start.7 = (f32[5376]{0:T(1024)S(1)}, f32[5376]{0:T(1024)}, u32[]{:S(2)}) copy-start(f32[5376]{0:T(1024)} %param.22) | copy-start | bytes 64516
Sparse Core Ops, SparseCore 0:
  49.5 101.2 reduce-scatter.1

commit v2 on v1

--- a/solution.py
+++ b/solution.py
@@ -25,6 +25,8 @@
 ROWS = 256
 GROUP = 16
 HALF = 128
+QUARTER = 1408
+ROW_AT = 3
 
 
 def rotary_table():
@@ -34,6 +36,18 @@
     position = (WINDOW_SPAN + np.arange(BLOCK_TOKENS)).astype(np.float32)
     angle = (position[:, None] * frequency[None, :]).astype(np.float64)
     return np.concatenate([np.cos(angle), np.sin(angle)], axis=1).astype(np.float32)
+
+
+def places():
+    rows = []
+    for device in range(128):
+        seq, x, z = device // 16, device // 4 % 4, device % 4
+        far, up, down = ((x + by) % 4 * 256 for by in (2, 1, 3))
+        rows.append(
+            [seq, z, seq % 2, far, far + 128, up + 128, down, up, down + 128, x * 256,
+             x * 256 + 128, x * 256 + z * 64]
+        )
+    return np.array(rows, np.int32)
 
 
 def project_kernel(
@@ -125,7 +139,7 @@
     )
 
 
-def attend_kernel(pos_ref, q_ref, kv_ref, got_ref, pk_ref, pv_ref, out_ref, keys, values):
+def attend_kernel(step, pos_ref, q_ref, kv_ref, got_ref, pk_ref, pv_ref, out_ref, keys, values):
     @pl.when(pos_ref[0] == 0)
     def _():
         keys[0:SHARD] = pk_ref[...]
@@ -144,8 +158,8 @@
     row = lax.broadcasted_iota(jnp.int32, (2 * HALF, HALF), 0) % HALF
     col = lax.broadcasted_iota(jnp.int32, (2 * HALF, HALF), 1)
     lowest = jnp.float32(-jnp.inf)
-    for part in range(out_ref.shape[0] // HALF):
-        first = pl.multiple_of(pos_ref[1 + part], HALF)
+    for part in range(2):
+        first = pl.multiple_of(pos_ref[ROW_AT + 2 * step + part], HALF)
         q = q_ref[pl.ds(first, HALF), :]
         q = jnp.concatenate([q[:, 0:128], q[:, 128:256]], axis=0)
         k = keys[pl.ds(first, span), :]
@@ -166,10 +180,11 @@
         out_ref[part * HALF : (part + 1) * HALF, 128:256] = mixed[HALF:]
 
 
-def attend(pos, q, kv, got, prior_k, prior_v, parts):
+def attend(step, pos, q, kv, got, prior_k, prior_v):
+    parts = 2
     vmem = pl.BlockSpec(memory_space=pltpu.VMEM)
     return pl.pallas_call(
-        attend_kernel,
+        functools.partial(attend_kernel, step),
         in_specs=[pl.BlockSpec(memory_space=pltpu.SMEM)] + [vmem] * 5,
         out_specs=vmem,
         out_shape=jax.ShapeDtypeStruct((parts * HALF, 256), BF16),
@@ -186,29 +201,227 @@
     )(pos, q, kv, got, prior_k, prior_v)
 
 
+ANY = pl.BlockSpec(memory_space=pl.ANY)
+VMEM = pl.BlockSpec(memory_space=pltpu.VMEM)
+SMEM = pl.BlockSpec(memory_space=pltpu.SMEM)
+
+
+def quarter_start(number):
+    return pl.multiple_of((number * 21 // 2) * 128, 128)
+
+
+def pick_kernel(pos_ref, w_ref, own_ref, next_ref, last_ref, far_ref, sems):
+    z, c = pos_ref[1], pos_ref[2]
+    rows = pl.ds(pl.multiple_of(c * 128, 128), 128)
+    copies = [
+        pltpu.make_async_copy(
+            w_ref.at[:, pl.ds(quarter_start(z), QUARTER)], own_ref, sems.at[3]
+        )
+    ]
+    for i, (shift, ref) in enumerate(((1, next_ref), (3, last_ref), (2, far_ref))):
+        cols = pl.ds(quarter_start((z + shift) % 4), QUARTER)
+        copies.append(pltpu.make_async_copy(w_ref.at[rows, cols], ref, sems.at[i]))
+    for copy in copies:
+        copy.start()
+    for copy in copies:
+        copy.wait()
+
+
+def pick(pos, w_out):
+    part = jax.ShapeDtypeStruct((128, QUARTER), BF16)
+    return pl.pallas_call(
+        pick_kernel,
+        in_specs=[SMEM, ANY],
+        out_specs=[ANY] * 4,
+        out_shape=[jax.ShapeDtypeStruct((256, QUARTER), BF16), part, part, part],
+        scratch_shapes=[pltpu.SemaphoreType.DMA((4,))],
+        cost_estimate=pl.CostEstimate(flops=0, bytes_accessed=4 << 20, transcendentals=0),
+        name="pick",
+    )(pos, w_out)
+
+
+def product(pos_ref, a_refs, w_refs, a_all, w_all, sems):
+    c = pos_ref[2]
+    copies = [pltpu.make_async_copy(w_refs[0], w_all.at[0:256], sems.at[0])]
+    for i in range(3):
+        for j, side in enumerate((c, 1 - c)):
+            at = pl.multiple_of(256 * (i + 1) + side * 128, 128)
+            copies.append(
+                pltpu.make_async_copy(
+                    w_refs[1 + i + 3 * j], w_all.at[pl.ds(at, 128)], sems.at[1 + 2 * i + j]
+                )
+            )
+    for copy in copies:
+        copy.start()
+    for i in range(4):
+        a_all[:, 256 * i : 256 * (i + 1)] = a_refs[i][...]
+    for copy in copies:
+        copy.wait()
+    return jnp.dot(a_all[...], w_all[...], preferred_element_type=F32)
+
+
+def send_kernel(has_relay, *refs):
+    pos_ref, a_refs, w_refs = refs[0], refs[1:5], refs[5:12]
+    relay_refs = refs[12:14] if has_relay else ()
+    up_ref, down_ref, a_all, w_all, sems = refs[-5:]
+    out = product(pos_ref, a_refs, w_refs, a_all, w_all, sems)
+    up, down = out[0:HALF], out[HALF:]
+    if has_relay:
+        up = up + relay_refs[0][...].astype(F32)
+        down = down + relay_refs[1][...].astype(F32)
+    up_ref[...] = up.astype(BF16)
+    down_ref[...] = down.astype(BF16)
+
+
+def keep_kernel(*refs):
+    pos_ref, a_refs, w_refs = refs[0], refs[1:5], refs[5:12]
+    first_ref, second_ref, out_ref, a_all, w_all, sems = refs[12:]
+    out = product(pos_ref, a_refs, w_refs, a_all, w_all, sems)
+    out_ref[0:HALF] = out[0:HALF] + first_ref[...].astype(F32)
+    out_ref[HALF:] = out[HALF:] + second_ref[...].astype(F32)
+
+
+PRODUCT_SCRATCH = [
+    pltpu.VMEM((256, 1024), BF16),
+    pltpu.VMEM((1024, QUARTER), BF16),
+    pltpu.SemaphoreType.DMA((7,)),
+]
+PRODUCT_COST = pl.CostEstimate(
+    flops=2 * 256 * 1024 * QUARTER, bytes_accessed=5 << 20, transcendentals=0
+)
+
+
+def send_step(pos, pieces, weights, relays):
+    half = jax.ShapeDtypeStruct((HALF, QUARTER), BF16)
+    return pl.pallas_call(
+        functools.partial(send_kernel, bool(relays)),
+        in_specs=[SMEM] + [VMEM] * 4 + [ANY] * 7 + [VMEM] * len(relays),
+        out_specs=[VMEM] * 2,
+        out_shape=[half, half],
+        scratch_shapes=PRODUCT_SCRATCH,
+        compiler_params=pltpu.CompilerParams(vmem_limit_bytes=32 << 20),
+        cost_estimate=PRODUCT_COST,
+        name="send_step",
+    )(pos, *pieces, *weights, *relays)
+
+
+def keep_step(pos, pieces, weights, first, second):
+    return pl.pallas_call(
+        keep_kernel,
+        in_specs=[SMEM] + [VMEM] * 4 + [ANY] * 7 + [VMEM] * 2,
+        out_specs=VMEM,
+        out_shape=jax.ShapeDtypeStruct((256, QUARTER), F32),
+        scratch_shapes=PRODUCT_SCRATCH,
+        compiler_params=pltpu.CompilerParams(vmem_limit_bytes=32 << 20),
+        cost_estimate=PRODUCT_COST,
+        name="keep_step",
+    )(pos, *pieces, *weights, first, second)
+
+
+def total_kernel(pos_ref, kept_ref, up_ref, down_ref, own_ref, next_ref, last_ref, far_ref, total):
+    z = pos_ref[1]
+    total[0:HALF] = kept_ref[0:HALF] + up_ref[...].astype(F32)
+    total[HALF:] = kept_ref[HALF:] + down_ref[...].astype(F32)
+
+    def rows(shift):
+        return total[pl.ds(pl.multiple_of(((z + shift) % 4) * 64, 64), 64), :]
+
+    own_ref[...] = rows(0)
+    next_ref[...] = rows(1).astype(BF16)
+    last_ref[...] = rows(3).astype(BF16)
+    far_ref[...] = rows(2).astype(BF16)
+
+
+def total_step(pos, kept, up, down):
+    part = jax.ShapeDtypeStruct((64, QUARTER), BF16)
+    return pl.pallas_call(
+        total_kernel,
+        in_specs=[SMEM] + [VMEM] * 3,
+        out_specs=[VMEM] * 4,
+        out_shape=[jax.ShapeDtypeStruct((64, QUARTER), F32), part, part, part],
+        scratch_shapes=[pltpu.VMEM((256, QUARTER), F32)],
+        compiler_params=pltpu.CompilerParams(vmem_limit_bytes=32 << 20),
+        cost_estimate=pl.CostEstimate(flops=1 << 20, bytes_accessed=4 << 20, transcendentals=0),
+        name="total_step",
+    )(pos, kept, up, down)
+
+
+def finish_kernel(pos_ref, own_ref, next_ref, last_ref, far_ref, tok_ref, g_ref, out_ref, line, tok, sem):
+    z = pos_ref[1]
+    at = pl.multiple_of(pos_ref[ROW_AT + 8], 64)
+    copy = pltpu.make_async_copy(tok_ref.at[pl.ds(at, 64)], tok, sem)
+    copy.start()
+    for shift, ref in ((0, own_ref), (3, next_ref), (1, last_ref), (2, far_ref)):
+        line[:, pl.ds(quarter_start((z + shift) % 4), QUARTER)] = ref[...].astype(F32)
+    copy.wait()
+
+    def group(i, carry):
+        rows = pl.ds(pl.multiple_of(i * 16, 16), 16)
+        summed = line[rows, :]
+        mean = jnp.sum(summed * summed, axis=-1, keepdims=True) * (1.0 / MODEL_WIDTH)
+        normed = summed * lax.rsqrt(mean + EPSILON) * g_ref[...]
+        out_ref[rows, :] = (tok[rows, :].astype(F32) + normed).astype(BF16)
+        return carry
+
+    lax.fori_loop(0, 4, group, 0)
+
+
+def finish(pos, own, nxt, last, far, tokens, gain):
+    return pl.pallas_call(
+        finish_kernel,
+        in_specs=[SMEM] + [VMEM] * 4 + [ANY, VMEM],
+        out_specs=VMEM,
+        out_shape=jax.ShapeDtypeStruct((64, MODEL_WIDTH), BF16),
+        scratch_shapes=[
+            pltpu.VMEM((64, MODEL_WIDTH), F32),
+            pltpu.VMEM((64, MODEL_WIDTH), BF16),
+            pltpu.SemaphoreType.DMA(()),
+        ],
+        compiler_params=pltpu.CompilerParams(vmem_limit_bytes=32 << 20),
+        cost_estimate=pl.CostEstimate(flops=1 << 21, bytes_accessed=3 << 20, transcendentals=0),
+        name="finish",
+    )(pos, own, nxt, last, far, tokens, gain.reshape(1, -1))
+
+
+def shift_by(array, axis, steps):
+    return lax.ppermute(array, axis, [(i, (i + steps) % 4) for i in range(4)])
+
+
+def from_line(pieces):
+    return [shift_by(piece, "z", by) for piece, by in zip(pieces, (1, 3, 2), strict=True)]
+
+
 def per_device(
     tokens, pre_gain, w_query, key_weight, value_weight, query_gain, key_gain,
     prior_key, prior_value, w_out, post_gain, table,
 ):
-    seq = lax.axis_index("y") * 2 + lax.axis_index("c")
-    tp = lax.axis_index("x") * 4 + lax.axis_index("z")
+    device = lax.axis_index(("y", "c", "x", "z"))
+    pos = lax.dynamic_slice_in_dim(jnp.asarray(places()), device, 1, 0).reshape(-1)
+    own_w, *parts = pick(pos, w_out)
+    pos, own_w, *parts = lax.optimization_barrier((pos, own_w, *parts))
+    lines = from_line(parts)
+    swapped = [lax.ppermute(part, "c", [(0, 1), (1, 0)]) for part in lines]
+    weights = [own_w, *lines, *swapped]
     q, kv = project(
-        seq.reshape(1), tokens, pre_gain, w_query, key_weight, value_weight,
+        pos, tokens, pre_gain, w_query, key_weight, value_weight,
         query_gain, key_gain, table,
     )
     got = lax.ppermute(kv, ("y", "c"), [(i, i + 1) for i in range(7)])
-    steps = []
-    for step in range(4):
-        pos = jnp.stack([seq, jnp.int32(step * 256), jnp.int32(step * 256 + 128)])
-        steps.append(attend(pos, q, kv, got, prior_key, prior_value, 2))
-    attended = jnp.concatenate(steps, axis=0)
-    partial = jnp.dot(attended, w_out, preferred_element_type=F32)
-    summed = lax.psum_scatter(
-        partial.astype(BF16), ("x", "z"), scatter_dimension=0, tiled=True
-    ).astype(F32)
-    own = lax.dynamic_slice_in_dim(tokens, tp * 64, 64, 0).astype(F32)
-    mean = jnp.mean(summed * summed, axis=-1, keepdims=True)
-    return (own + summed * lax.rsqrt(mean + EPSILON) * post_gain).astype(BF16)
+
+    def heads(step):
+        mixed = attend(step, pos, q, kv, got, prior_key, prior_value)
+        return [mixed, *from_line([mixed] * 3)]
+
+    def send(step, relays):
+        ahead, behind = send_step(pos, heads(step), weights, relays)
+        return shift_by(ahead, "x", 1), shift_by(behind, "x", 3)
+
+    relays = send(0, ())
+    from_below, from_above = send(1, ())
+    late_below, late_above = send(2, relays)
+    kept = keep_step(pos, heads(3), weights, from_above, from_below)
+    own, *others = total_step(pos, kept, late_below, late_above)
+    return finish(pos, own, *from_line(others), tokens, post_gain)
 
 
 def solution(mesh):

time: 162 us -> 188 us (1.16)
  Pallas kernels: 27.9 us -> 99.7 us
  waiting for transfers between devices: 103 us -> 37.2 us
  starting transfers between devices: 1.32 us -> 45.6 us
  between operations: 13.5 us -> 0.47 us
  matrix products: 7.06 us -> 0 us
  other arithmetic: 3.97 us -> 0.01 us
  local copies, waits for them, and re-layouts: 4.9 us -> 2.72 us
    reduce_scatter x1 -> x0, waiting for transfers between devices: 101 us -> none  [per_device(): lax.psum_scatter(partial.astype(BF16), ('x', 'z'), scatter_dimension=0, t...]
    pallas_call x4 -> x11, Pallas kernels: 7.7 us -> 78.9 us  [the longest x1 56.5 us: pick(): pl.pallas_call(pick_kernel, in_specs=[SMEM, ANY], out_specs=[ANY] * 4, ou...]
    ppermute x0 -> x27, starting transfers between devices: none -> 44.3 us  [the longest x24 35 us: shift_by(): return lax.ppermute(array, axis, [(i, (i + steps) % 4) for i in range(4)])]
    ppermute x0 -> x27, waiting for transfers between devices: none -> 37.2 us  [the longest x24 37.2 us: shift_by(): return lax.ppermute(array, axis, [(i, (i + steps) % 4) for i in range(4)])]
    dot_general x1 -> x0, matrix products: 7.06 us -> none  [per_device(): partial = jnp.dot(attended, w_out, preferred_element_type=F32)]
    unnamed x16 -> x32, local copies, waits for them, and re-layouts: 4 us -> 1.4 us
    convert_element_type x1 -> x0, other arithmetic: 2.48 us -> none  [per_device(): return (own + summed * lax.rsqrt(mean + EPSILON) * post_gain).astype(BF16)]
  transfers between devices with their start and end apart: 2 -> 28, of which waited for: 2 -> 10; matrix products, arithmetic and copies ran while one was open for 0% -> 0% of each run, Pallas kernels for 0% -> 9%
where the time goes in v2:
time: 188 us; the launch traced here: 186 us
  Pallas kernels  99.7 us (53%)
  starting transfers between devices  45.6 us (24%)
  waiting for transfers between devices  37.2 us (20%)
  local copies, waits for them, and re-layouts  2.72 us (1%)
    pallas_call x1, Pallas kernels, pick(): pl.pallas_call(pick_kernel, in_specs=[SMEM, ANY], out_specs=[ANY] * 4, ou...  56.5 us
    ppermute x24, waiting for transfers between devices, shift_by(): return lax.ppermute(array, axis, [(i, (i + steps) % 4) for i in range(4)])  37.2 us
    ppermute x24, starting transfers between devices, shift_by(): return lax.ppermute(array, axis, [(i, (i + steps) % 4) for i in range(4)])  35 us
    pallas_call x1, Pallas kernels, project(): pl.pallas_call(project_kernel, grid_spec=pltpu.PrefetchScalarGridSpec(num...  20.9 us
    ppermute x3, starting transfers between devices, per_device(): swapped = [lax.ppermute(part, 'c', [(0, 1), (1, 0)]) for part in lines]  9.29 us
    pallas_call x3, Pallas kernels, send_step(): pl.pallas_call(functools.partial(send_kernel, bool(relays)), in_specs=[SM...  8.4 us
    pallas_call x4, Pallas kernels, attend(): pl.pallas_call(functools.partial(attend_kernel, step), in_specs=[pl.Block...  7.8 us
  transfers between devices with their start and end apart: 28, of which 10 were waited for; matrix products, arithmetic and copies ran while one was open for 0% of the time, Pallas kernels for 9%

profile of v2, /device:TPU:0, one launch (start us, length us, event | category | flops | bytes accessed | tf_op | source)
XLA Modules:
  0.0 185.8 jit_solution(18268696839284778564)
XLA Ops:
  1.3 56.5 %pick.1 = (bf16[256,1408]{1,0:T(8,128)(2,1)}, bf16[128,1408]{1,0:T(8,128)(2,1)}, bf16[128,1408]{1,0:T(8,128)(2,1)}, bf16[128,1408]{1,0:T(8,128)(2,1)}) custom-call(s32[12]{0:T(128)} %dynamic-slice_bitcast_fusion.pos_ref.seq_ref.refs_0_, bf16[256,5376]{1,0:T(8,128)(2,1)} %w_ref.1), custom_call_target="tpu_custom_call" | custom-call | bytes 4194304 | tf_op jit(solution)/shard_map/pick/pallas_call | solution.py:232
  59.3 20.9 %project.1 = (bf16[1024,256]{1,0:T(8,128)(2,1)S(1)}, bf16[1024,256]{1,0:T(8,128)(2,1)S(1)}) custom-call(s32[12]{0:T(128)S(1)} %copy-done.1, bf16[1024,5376]{1,0:T(8,128)(2,1)} %tok_ref.3, f32[1,5376]{1,0:T(1,128)S(1)} %reshape.16.g_ref, bf16[5376,256]{1,0:T(8,128)(2,1)} %wq_ref.1, bf16[5376,128]{1,0:T(8,128)(2,1)S(1)} %copy-done.2, ...), custom_call_target="tpu_custom_call" | custom-call | flops 5637144576 | bytes 18874368 | tf_op jit(solution)/shard_map/project/pallas_call | solution.py:102
  81.5 2.5 %collective-permute-start.4 = (bf16[128,1408]{1,0:T(8,128)(2,1)S(1)}, bf16[128,1408]{1,0:T(8,128)(2,1)S(1)}, u32[]{:S(2)}, u32[]{:S(2)}) collective-permute-start(bf16[128,1408]{1,0:T(8,128)(2,1)S(1)} %copy-done.12), channel_id=1, source_target_pairs={{0,1},{1,2},{2,3},{3,0},{4,5},{5,6},{6,7},{7,4},{8,9},{9,10},{10,1... | collective-permute-start | bytes 1081352 | tf_op jit(solution)/shard_map/ppermute | solution.py:387
  84.0 2.2 %collective-permute-start.5 = (bf16[128,1408]{1,0:T(8,128)(2,1)S(1)}, bf16[128,1408]{1,0:T(8,128)(2,1)S(1)}, u32[]{:S(2)}, u32[]{:S(2)}) collective-permute-start(bf16[128,1408]{1,0:T(8,128)(2,1)S(1)} %copy-done.11), channel_id=1, source_target_pairs={{0,3},{1,0},{2,1},{3,2},{4,7},{5,4},{6,5},{7,6},{8,11},{9,8},{10,9... | collective-permute-start | bytes 1081352 | tf_op jit(solution)/shard_map/ppermute | solution.py:387
  86.2 1.8 collective-permute-start.6
  88.0 6.2 %collective-permute-done.4.refs_6_ = bf16[128,1408]{1,0:T(8,128)(2,1)S(1)} collective-permute-done((bf16[128,1408]{1,0:T(8,128)(2,1)S(1)}, bf16[128,1408]{1,0:T(8,128)(2,1)S(1)}, u32[]{:S(2)}, u32[]{:S(2)}) %collective-permute-start.4) | collective-permute-done | bytes 360480 | tf_op jit(solution)/shard_map/ppermute | solution.py:387
  95.2 7.6 %collective-permute-start.8 = (bf16[128,1408]{1,0:T(8,128)(2,1)S(1)}, bf16[128,1408]{1,0:T(8,128)(2,1)S(1)}, u32[]{:S(2)}, u32[]{:S(2)}) collective-permute-start(bf16[128,1408]{1,0:T(8,128)(2,1)S(1)} %collective-permute-done.5.refs_7_), channel_id=1, source_target_pairs={{0,16},{16,0},{1,17},{17,1},{2,18},{18,2},{3,19},{19,3},{4,20},{20... | collective-permute-start | bytes 1081352 | tf_op jit(solution)/shard_map/ppermute | solution.py:403
  104.4 1.9 %attend.7.refs_1_ = bf16[256,256]{1,0:T(8,128)(2,1)S(1)} custom-call(s32[12]{0:T(128)S(1)} %copy-done.1, bf16[1024,256]{1,0:T(8,128)(2,1)S(1)} %get-tuple-element.31.q_ref, bf16[1024,256]{1,0:T(8,128)(2,1)S(1)} %get-tuple-element.32.kv_ref, bf16[1024,256]{1,0:T(8,128)(2,1)S(1)} %collective-permute-done.got_ref, bf16[1024,128]{1,0:T(8,128)(2,1)S(1)} %copy-done.4, ...), custom_call_target="tpu_custom_call" | custom-call | flops 603979776 | bytes 2097152 | tf_op jit(solution)/shard_map/attend/pallas_call | solution.py:186
  107.9 1.8 collective-permute-start.19
  109.7 3.4 %collective-permute-done.18.refs_2_ = bf16[256,256]{1,0:T(8,128)(2,1)S(1)} collective-permute-done((bf16[256,256]{1,0:T(8,128)(2,1)S(1)}, bf16[256,256]{1,0:T(8,128)(2,1)S(1)}, u32[]{:S(2)}, u32[]{:S(2)}) %collective-permute-start.18) | collective-permute-done | bytes 131104 | tf_op jit(solution)/shard_map/ppermute | solution.py:387
  113.8 5.8 %collective-permute-done.20.refs_4_ = bf16[256,256]{1,0:T(8,128)(2,1)S(1)} collective-permute-done((bf16[256,256]{1,0:T(8,128)(2,1)S(1)}, bf16[256,256]{1,0:T(8,128)(2,1)S(1)}, u32[]{:S(2)}, u32[]{:S(2)}) %collective-permute-start.20) | collective-permute-done | bytes 131104 | tf_op jit(solution)/shard_map/ppermute | solution.py:387
  119.6 2.8 %send_step.4 = (bf16[128,1408]{1,0:T(8,128)(2,1)S(1)}, bf16[128,1408]{1,0:T(8,128)(2,1)S(1)}) custom-call(s32[12]{0:T(128)S(1)} %copy-done.1, bf16[256,256]{1,0:T(8,128)(2,1)S(1)} %attend.7.refs_1_, bf16[256,256]{1,0:T(8,128)(2,1)S(1)} %collective-permute-done.18.refs_2_, bf16[256,256]{1,0:T(8,128)(2,1)S(1)} %collective-permute-done.19.refs_3_, ...), custom_call_target="tpu_custom_call" | custom-call | flops 738197504 | bytes 5242880 | tf_op jit(solution)/shard_map/send_step/pallas_call | solution.py:296
  122.4 1.6 collective-permute-start.21
  124.0 1.7 collective-permute-start.22
  125.7 1.9 %attend.6.refs_1_ = bf16[256,256]{1,0:T(8,128)(2,1)S(1)} custom-call(s32[12]{0:T(128)S(1)} %copy-done.1, bf16[1024,256]{1,0:T(8,128)(2,1)S(1)} %get-tuple-element.31.q_ref, bf16[1024,256]{1,0:T(8,128)(2,1)S(1)} %get-tuple-element.32.kv_ref, bf16[1024,256]{1,0:T(8,128)(2,1)S(1)} %collective-permute-done.got_ref, bf16[1024,128]{1,0:T(8,128)(2,1)S(1)} %copy-done.4, ...), custom_call_target="tpu_custom_call" | custom-call | flops 603979776 | bytes 2097152 | tf_op jit(solution)/shard_map/attend/pallas_call | solution.py:186
  128.1 2.0 %attend.5.refs_1_ = bf16[256,256]{1,0:T(8,128)(2,1)S(1)} custom-call(s32[12]{0:T(128)S(1)} %copy-done.1, bf16[1024,256]{1,0:T(8,128)(2,1)S(1)} %get-tuple-element.31.q_ref, bf16[1024,256]{1,0:T(8,128)(2,1)S(1)} %get-tuple-element.32.kv_ref, bf16[1024,256]{1,0:T(8,128)(2,1)S(1)} %collective-permute-done.got_ref, bf16[1024,128]{1,0:T(8,128)(2,1)S(1)} %copy-done.4, ...), custom_call_target="tpu_custom_call" | custom-call | flops 603979776 | bytes 2097152 | tf_op jit(solution)/shard_map/attend/pallas_call | solution.py:186
  130.7 2.8 %collective-permute-start.11 = (bf16[256,256]{1,0:T(8,128)(2,1)S(1)}, bf16[256,256]{1,0:T(8,128)(2,1)S(1)}, u32[]{:S(2)}, u32[]{:S(2)}) collective-permute-start(bf16[256,256]{1,0:T(8,128)(2,1)S(1)} %attend.5.refs_1_), channel_id=1, source_target_pairs={{0,3},{1,0},{2,1},{3,2},{4,7},{5,4},{6,5},{7,6},{8,11},{9,8},{10,9... | collective-permute-start | bytes 393224 | tf_op jit(solution)/shard_map/ppermute | solution.py:387
  134.8 2.9 %collective-permute-done.10.refs_2_ = bf16[256,256]{1,0:T(8,128)(2,1)S(1)} collective-permute-done((bf16[256,256]{1,0:T(8,128)(2,1)S(1)}, bf16[256,256]{1,0:T(8,128)(2,1)S(1)}, u32[]{:S(2)}, u32[]{:S(2)}) %collective-permute-start.10) | collective-permute-done | bytes 131104 | tf_op jit(solution)/shard_map/ppermute | solution.py:387
  138.3 2.5 %collective-permute-start.17 = (bf16[256,256]{1,0:T(8,128)(2,1)S(1)}, bf16[256,256]{1,0:T(8,128)(2,1)S(1)}, u32[]{:S(2)}, u32[]{:S(2)}) collective-permute-start(bf16[256,256]{1,0:T(8,128)(2,1)S(1)} %attend.6.refs_1_), channel_id=1, source_target_pairs={{0,2},{1,3},{2,0},{3,1},{4,6},{5,7},{6,4},{7,5},{8,10},{9,11},{10,... | collective-permute-start | bytes 393224 | tf_op jit(solution)/shard_map/ppermute | solution.py:387
  140.7 2.0 %attend.4.refs_1_ = bf16[256,256]{1,0:T(8,128)(2,1)S(1)} custom-call(s32[12]{0:T(128)S(1)} %copy-done.1, bf16[1024,256]{1,0:T(8,128)(2,1)S(1)} %get-tuple-element.31.q_ref, bf16[1024,256]{1,0:T(8,128)(2,1)S(1)} %get-tuple-element.32.kv_ref, bf16[1024,256]{1,0:T(8,128)(2,1)S(1)} %collective-permute-done.got_ref, bf16[1024,128]{1,0:T(8,128)(2,1)S(1)} %copy-done.4, ...), custom_call_target="tpu_custom_call" | custom-call | flops 603979776 | bytes 2097152 | tf_op jit(solution)/shard_map/attend/pallas_call | solution.py:186
  142.7 3.4 %collective-permute-start.1 = (bf16[256,256]{1,0:T(8,128)(2,1)S(1)}, bf16[256,256]{1,0:T(8,128)(2,1)S(1)}, u32[]{:S(2)}, u32[]{:S(2)}) collective-permute-start(bf16[256,256]{1,0:T(8,128)(2,1)S(1)} %attend.4.refs_1_), channel_id=1, source_target_pairs={{0,1},{1,2},{2,3},{3,0},{4,5},{5,6},{6,7},{7,4},{8,9},{9,10},{10,1... | collective-permute-start | bytes 393224 | tf_op jit(solution)/shard_map/ppermute | solution.py:387
  146.1 2.8 %send_step.3 = (bf16[128,1408]{1,0:T(8,128)(2,1)S(1)}, bf16[128,1408]{1,0:T(8,128)(2,1)S(1)}) custom-call(s32[12]{0:T(128)S(1)} %copy-done.1, bf16[256,256]{1,0:T(8,128)(2,1)S(1)} %attend.5.refs_1_, bf16[256,256]{1,0:T(8,128)(2,1)S(1)} %collective-permute-done.10.refs_2_, bf16[256,256]{1,0:T(8,128)(2,1)S(1)} %collective-permute-done.11.refs_3_, ...), custom_call_target="tpu_custom_call" | custom-call | flops 738197504 | bytes 5242880 | tf_op jit(solution)/shard_map/send_step/pallas_call | solution.py:296
  149.1 2.0 %collective-permute-start.14 = (bf16[128,1408]{1,0:T(8,128)(2,1)S(1)}, bf16[128,1408]{1,0:T(8,128)(2,1)S(1)}, u32[]{:S(2)}, u32[]{:S(2)}) collective-permute-start(bf16[128,1408]{1,0:T(8,128)(2,1)S(1)} %get-tuple-element.38), channel_id=1, source_target_pairs={{0,4},{4,8},{8,12},{12,0},{1,5},{5,9},{9,13},{13,1},{2,6},{6,10},{... | collective-permute-start | bytes 1081352 | tf_op jit(solution)/shard_map/ppermute | solution.py:387
  151.1 2.8 %send_step.5 = (bf16[128,1408]{1,0:T(8,128)(2,1)S(1)}, bf16[128,1408]{1,0:T(8,128)(2,1)S(1)}) custom-call(s32[12]{0:T(128)S(1)} %copy-done.1, bf16[256,256]{1,0:T(8,128)(2,1)S(1)} %attend.6.refs_1_, bf16[256,256]{1,0:T(8,128)(2,1)S(1)} %collective-permute-done.15.refs_2_, bf16[256,256]{1,0:T(8,128)(2,1)S(1)} %collective-permute-done.16.refs_3_, ...), custom_call_target="tpu_custom_call" | custom-call | flops 738197504 | bytes 5242880 | tf_op jit(solution)/shard_map/send_step/pallas_call | solution.py:296
  154.0 3.2 %collective-permute-start.24 = (bf16[128,1408]{1,0:T(8,128)(2,1)S(1)}, bf16[128,1408]{1,0:T(8,128)(2,1)S(1)}, u32[]{:S(2)}, u32[]{:S(2)}) collective-permute-start(bf16[128,1408]{1,0:T(8,128)(2,1)S(1)} %get-tuple-element.42), channel_id=1, source_target_pairs={{0,12},{4,0},{8,4},{12,8},{1,13},{5,1},{9,5},{13,9},{2,14},{6,2},{... | collective-permute-start | bytes 1081352 | tf_op jit(solution)/shard_map/ppermute | solution.py:387
  157.2 5.0 %collective-permute-done.2.refs_3_ = bf16[256,256]{1,0:T(8,128)(2,1)S(1)} collective-permute-done((bf16[256,256]{1,0:T(8,128)(2,1)S(1)}, bf16[256,256]{1,0:T(8,128)(2,1)S(1)}, u32[]{:S(2)}, u32[]{:S(2)}) %collective-permute-start.2) | collective-permute-done | bytes 131104 | tf_op jit(solution)/shard_map/ppermute | solution.py:387
  162.8 6.3 %collective-permute-done.3.refs_4_ = bf16[256,256]{1,0:T(8,128)(2,1)S(1)} collective-permute-done((bf16[256,256]{1,0:T(8,128)(2,1)S(1)}, bf16[256,256]{1,0:T(8,128)(2,1)S(1)}, u32[]{:S(2)}, u32[]{:S(2)}) %collective-permute-start.3) | collective-permute-done | bytes 131104 | tf_op jit(solution)/shard_map/ppermute | solution.py:387
  169.1 2.8 %keep_step.1.kept_ref = f32[256,1408]{1,0:T(8,128)S(1)} custom-call(s32[12]{0:T(128)S(1)} %copy-done.1, bf16[256,256]{1,0:T(8,128)(2,1)S(1)} %attend.4.refs_1_, bf16[256,256]{1,0:T(8,128)(2,1)S(1)} %collective-permute-done.1.refs_2_, bf16[256,256]{1,0:T(8,128)(2,1)S(1)} %collective-permute-done.2.refs_3_, ...), custom_call_target="tpu_custom_call" | custom-call | flops 738197504 | bytes 5242880 | tf_op jit(solution)/shard_map/keep_step/pallas_call | solution.py:309
  172.8 3.2 %collective-permute-start.26 = (bf16[64,1408]{1,0:T(8,128)(2,1)S(1)}, bf16[64,1408]{1,0:T(8,128)(2,1)S(1)}, u32[]{:S(2)}, u32[]{:S(2)}) collective-permute-start(bf16[64,1408]{1,0:T(8,128)(2,1)S(1)} %get-tuple-element.45), channel_id=1, source_target_pairs={{0,3},{1,0},{2,1},{3,2},{4,7},{5,4},{6,5},{7,6},{8,11},{9,8},{10,9... | collective-permute-start | bytes 540680 | tf_op jit(solution)/shard_map/ppermute | solution.py:387
  177.1 2.4 %collective-permute-done.25.next_ref = bf16[64,1408]{1,0:T(8,128)(2,1)S(1)} collective-permute-done((bf16[64,1408]{1,0:T(8,128)(2,1)S(1)}, bf16[64,1408]{1,0:T(8,128)(2,1)S(1)}, u32[]{:S(2)}, u32[]{:S(2)}) %collective-permute-start.25) | collective-permute-done | bytes 180256 | tf_op jit(solution)/shard_map/ppermute | solution.py:387
  179.5 3.5 %collective-permute-done.27.far_ref = bf16[64,1408]{1,0:T(8,128)(2,1)S(1)} collective-permute-done((bf16[64,1408]{1,0:T(8,128)(2,1)S(1)}, bf16[64,1408]{1,0:T(8,128)(2,1)S(1)}, u32[]{:S(2)}, u32[]{:S(2)}) %collective-permute-start.27) | collective-permute-done | bytes 180256 | tf_op jit(solution)/shard_map/ppermute | solution.py:387
  183.0 2.6 %finish.1 = bf16[64,5376]{1,0:T(8,128)(2,1)} custom-call(s32[12]{0:T(128)S(1)} %copy-done.1, f32[64,1408]{1,0:T(8,128)S(1)} %get-tuple-element.43.own_ref, bf16[64,1408]{1,0:T(8,128)(2,1)S(1)} %collective-permute-done.25.next_ref, bf16[64,1408]{1,0:T(8,128)(2,1)S(1)} %collective-permute-done.26.last_ref, ...), custom_call_target="tpu_custom_call" | custom-call | flops 2097152 | bytes 3145728 | tf_op jit(solution)/shard_map/finish/pallas_call | solution.py:370
  (72 shorter events, 14.4 us)
Async XLA Ops:
  0.0 57.9 %copy-start.6 = (f32[128]{0:T(128)S(1)}, f32[128]{0:T(128)}, u32[]{:S(2)}) copy-start(f32[128]{0:T(128)} %param.18) | copy-start | bytes 1540
  0.0 57.9 %copy-start.7 = (f32[128]{0:T(128)S(1)}, f32[128]{0:T(128)}, u32[]{:S(2)}) copy-start(f32[128]{0:T(128)} %param.19) | copy-start | bytes 1540
  0.0 57.9 %copy-start.2 = (bf16[5376,128]{1,0:T(8,128)(2,1)S(1)}, bf16[5376,128]{1,0:T(8,128)(2,1)}, u32[]{:S(2)}) copy-start(bf16[5376,128]{1,0:T(8,128)(2,1)} %wk_ref.1) | copy-start | bytes 4128772
  59.3 60.3 %copy-start = (bf16[256,1408]{1,0:T(8,128)(2,1)S(1)}, bf16[256,1408]{1,0:T(8,128)(2,1)}, u32[]{:S(2)}) copy-start(bf16[256,1408]{1,0:T(8,128)(2,1)} %get-tuple-element.33.refs_5_) | copy-start | bytes 2162692
  80.1 24.3 %collective-permute-start = (bf16[1024,256]{1,0:T(8,128)(2,1)S(1)}, bf16[1024,256]{1,0:T(8,128)(2,1)S(1)}, u32[]{:S(2)}, u32[]{:S(2)}) collective-permute-start(bf16[1024,256]{1,0:T(8,128)(2,1)S(1)} %get-tuple-element.32.kv_ref), channel_id=1, source_target_pairs={{0,16},{16,32},{32,48},{48,64},{64,80},{80,96},{96,112},{1,17},{17... | collective-permute-start | bytes 1572872 | tf_op jit(solution)/shard_map/ppermute | solution.py:409
  81.5 12.8 %collective-permute-start.4 = (bf16[128,1408]{1,0:T(8,128)(2,1)S(1)}, bf16[128,1408]{1,0:T(8,128)(2,1)S(1)}, u32[]{:S(2)}, u32[]{:S(2)}) collective-permute-start(bf16[128,1408]{1,0:T(8,128)(2,1)S(1)} %copy-done.12), channel_id=1, source_target_pairs={{0,1},{1,2},{2,3},{3,0},{4,5},{5,6},{6,7},{7,4},{8,9},{9,10},{10,1... | collective-permute-start | bytes 1081352 | tf_op jit(solution)/shard_map/ppermute | solution.py:387
  84.0 11.2 %collective-permute-start.5 = (bf16[128,1408]{1,0:T(8,128)(2,1)S(1)}, bf16[128,1408]{1,0:T(8,128)(2,1)S(1)}, u32[]{:S(2)}, u32[]{:S(2)}) collective-permute-start(bf16[128,1408]{1,0:T(8,128)(2,1)S(1)} %copy-done.11), channel_id=1, source_target_pairs={{0,3},{1,0},{2,1},{3,2},{4,7},{5,4},{6,5},{7,6},{8,11},{9,8},{10,9... | collective-permute-start | bytes 1081352 | tf_op jit(solution)/shard_map/ppermute | solution.py:387
  86.2 17.5 %collective-permute-start.6 = (bf16[128,1408]{1,0:T(8,128)(2,1)S(1)}, bf16[128,1408]{1,0:T(8,128)(2,1)S(1)}, u32[]{:S(2)}, u32[]{:S(2)}) collective-permute-start(bf16[128,1408]{1,0:T(8,128)(2,1)S(1)} %copy-done.10), channel_id=1, source_target_pairs={{0,2},{1,3},{2,0},{3,1},{4,6},{5,7},{6,4},{7,5},{8,10},{9,11},{10,... | collective-permute-start | bytes 1081352 | tf_op jit(solution)/shard_map/ppermute | solution.py:387
  94.3 25.3 %collective-permute-start.7 = (bf16[128,1408]{1,0:T(8,128)(2,1)S(1)}, bf16[128,1408]{1,0:T(8,128)(2,1)S(1)}, u32[]{:S(2)}, u32[]{:S(2)}) collective-permute-start(bf16[128,1408]{1,0:T(8,128)(2,1)S(1)} %collective-permute-done.4.refs_6_), channel_id=1, source_target_pairs={{0,16},{16,0},{1,17},{17,1},{2,18},{18,2},{3,19},{19,3},{4,20},{20... | collective-permute-start | bytes 1081352 | tf_op jit(solution)/shard_map/ppermute | solution.py:403
  95.2 24.3 %collective-permute-start.8 = (bf16[128,1408]{1,0:T(8,128)(2,1)S(1)}, bf16[128,1408]{1,0:T(8,128)(2,1)S(1)}, u32[]{:S(2)}, u32[]{:S(2)}) collective-permute-start(bf16[128,1408]{1,0:T(8,128)(2,1)S(1)} %collective-permute-done.5.refs_7_), channel_id=1, source_target_pairs={{0,16},{16,0},{1,17},{17,1},{2,18},{18,2},{3,19},{19,3},{4,20},{20... | collective-permute-start | bytes 1081352 | tf_op jit(solution)/shard_map/ppermute | solution.py:403
  103.8 15.8 %collective-permute-start.9 = (bf16[128,1408]{1,0:T(8,128)(2,1)S(1)}, bf16[128,1408]{1,0:T(8,128)(2,1)S(1)}, u32[]{:S(2)}, u32[]{:S(2)}) collective-permute-start(bf16[128,1408]{1,0:T(8,128)(2,1)S(1)} %collective-permute-done.6.refs_8_), channel_id=1, source_target_pairs={{0,16},{16,0},{1,17},{17,1},{2,18},{18,2},{3,19},{19,3},{4,20},{20... | collective-permute-start | bytes 1081352 | tf_op jit(solution)/shard_map/ppermute | solution.py:403
  106.4 6.7 %collective-permute-start.18 = (bf16[256,256]{1,0:T(8,128)(2,1)S(1)}, bf16[256,256]{1,0:T(8,128)(2,1)S(1)}, u32[]{:S(2)}, u32[]{:S(2)}) collective-permute-start(bf16[256,256]{1,0:T(8,128)(2,1)S(1)} %attend.7.refs_1_), channel_id=1, source_target_pairs={{0,1},{1,2},{2,3},{3,0},{4,5},{5,6},{6,7},{7,4},{8,9},{9,10},{10,1... | collective-permute-start | bytes 393224 | tf_op jit(solution)/shard_map/ppermute | solution.py:387
  107.9 5.9 %collective-permute-start.19 = (bf16[256,256]{1,0:T(8,128)(2,1)S(1)}, bf16[256,256]{1,0:T(8,128)(2,1)S(1)}, u32[]{:S(2)}, u32[]{:S(2)}) collective-permute-start(bf16[256,256]{1,0:T(8,128)(2,1)S(1)} %attend.7.refs_1_), channel_id=1, source_target_pairs={{0,3},{1,0},{2,1},{3,2},{4,7},{5,4},{6,5},{7,6},{8,11},{9,8},{10,9... | collective-permute-start | bytes 393224 | tf_op jit(solution)/shard_map/ppermute | solution.py:387
  113.1 6.5 %collective-permute-start.20 = (bf16[256,256]{1,0:T(8,128)(2,1)S(1)}, bf16[256,256]{1,0:T(8,128)(2,1)S(1)}, u32[]{:S(2)}, u32[]{:S(2)}) collective-permute-start(bf16[256,256]{1,0:T(8,128)(2,1)S(1)} %attend.7.refs_1_), channel_id=1, source_target_pairs={{0,2},{1,3},{2,0},{3,1},{4,6},{5,7},{6,4},{7,5},{8,10},{9,11},{10,... | collective-permute-start | bytes 393224 | tf_op jit(solution)/shard_map/ppermute | solution.py:387
  122.4 28.6 %collective-permute-start.21 = (bf16[128,1408]{1,0:T(8,128)(2,1)S(1)}, bf16[128,1408]{1,0:T(8,128)(2,1)S(1)}, u32[]{:S(2)}, u32[]{:S(2)}) collective-permute-start(bf16[128,1408]{1,0:T(8,128)(2,1)S(1)} %get-tuple-element.39), channel_id=1, source_target_pairs={{0,4},{4,8},{8,12},{12,0},{1,5},{5,9},{9,13},{13,1},{2,6},{6,10},{... | collective-permute-start | bytes 1081352 | tf_op jit(solution)/shard_map/ppermute | solution.py:387
  124.0 27.1 %collective-permute-start.22 = (bf16[128,1408]{1,0:T(8,128)(2,1)S(1)}, bf16[128,1408]{1,0:T(8,128)(2,1)S(1)}, u32[]{:S(2)}, u32[]{:S(2)}) collective-permute-start(bf16[128,1408]{1,0:T(8,128)(2,1)S(1)} %get-tuple-element.40), channel_id=1, source_target_pairs={{0,12},{4,0},{8,4},{12,8},{1,13},{5,1},{9,5},{13,9},{2,14},{6,2},{... | collective-permute-start | bytes 1081352 | tf_op jit(solution)/shard_map/ppermute | solution.py:387
  127.7 6.7 %collective-permute-start.15 = (bf16[256,256]{1,0:T(8,128)(2,1)S(1)}, bf16[256,256]{1,0:T(8,128)(2,1)S(1)}, u32[]{:S(2)}, u32[]{:S(2)}) collective-permute-start(bf16[256,256]{1,0:T(8,128)(2,1)S(1)} %attend.6.refs_1_), channel_id=1, source_target_pairs={{0,1},{1,2},{2,3},{3,0},{4,5},{5,6},{6,7},{7,4},{8,9},{9,10},{10,1... | collective-permute-start | bytes 393224 | tf_op jit(solution)/shard_map/ppermute | solution.py:387
  130.1 7.6 %collective-permute-start.10 = (bf16[256,256]{1,0:T(8,128)(2,1)S(1)}, bf16[256,256]{1,0:T(8,128)(2,1)S(1)}, u32[]{:S(2)}, u32[]{:S(2)}) collective-permute-start(bf16[256,256]{1,0:T(8,128)(2,1)S(1)} %attend.5.refs_1_), channel_id=1, source_target_pairs={{0,1},{1,2},{2,3},{3,0},{4,5},{5,6},{6,7},{7,4},{8,9},{9,10},{10,1... | collective-permute-start | bytes 393224 | tf_op jit(solution)/shard_map/ppermute | solution.py:387
  130.7 7.5 %collective-permute-start.11 = (bf16[256,256]{1,0:T(8,128)(2,1)S(1)}, bf16[256,256]{1,0:T(8,128)(2,1)S(1)}, u32[]{:S(2)}, u32[]{:S(2)}) collective-permute-start(bf16[256,256]{1,0:T(8,128)(2,1)S(1)} %attend.5.refs_1_), channel_id=1, source_target_pairs={{0,3},{1,0},{2,1},{3,2},{4,7},{5,4},{6,5},{7,6},{8,11},{9,8},{10,9... | collective-permute-start | bytes 393224 | tf_op jit(solution)/shard_map/ppermute | solution.py:387
  134.4 8.3 %collective-permute-start.12 = (bf16[256,256]{1,0:T(8,128)(2,1)S(1)}, bf16[256,256]{1,0:T(8,128)(2,1)S(1)}, u32[]{:S(2)}, u32[]{:S(2)}) collective-permute-start(bf16[256,256]{1,0:T(8,128)(2,1)S(1)} %attend.5.refs_1_), channel_id=1, source_target_pairs={{0,2},{1,3},{2,0},{3,1},{4,6},{5,7},{6,4},{7,5},{8,10},{9,11},{10,... | collective-permute-start | bytes 393224 | tf_op jit(solution)/shard_map/ppermute | solution.py:387
  137.7 11.2 %collective-permute-start.16 = (bf16[256,256]{1,0:T(8,128)(2,1)S(1)}, bf16[256,256]{1,0:T(8,128)(2,1)S(1)}, u32[]{:S(2)}, u32[]{:S(2)}) collective-permute-start(bf16[256,256]{1,0:T(8,128)(2,1)S(1)} %attend.6.refs_1_), channel_id=1, source_target_pairs={{0,3},{1,0},{2,1},{3,2},{4,7},{5,4},{6,5},{7,6},{8,11},{9,8},{10,9... | collective-permute-start | bytes 393224 | tf_op jit(solution)/shard_map/ppermute | solution.py:387
  138.3 10.8 %collective-permute-start.17 = (bf16[256,256]{1,0:T(8,128)(2,1)S(1)}, bf16[256,256]{1,0:T(8,128)(2,1)S(1)}, u32[]{:S(2)}, u32[]{:S(2)}) collective-permute-start(bf16[256,256]{1,0:T(8,128)(2,1)S(1)} %attend.6.refs_1_), channel_id=1, source_target_pairs={{0,2},{1,3},{2,0},{3,1},{4,6},{5,7},{6,4},{7,5},{8,10},{9,11},{10,... | collective-permute-start | bytes 393224 | tf_op jit(solution)/shard_map/ppermute | solution.py:387
  142.7 14.5 %collective-permute-start.1 = (bf16[256,256]{1,0:T(8,128)(2,1)S(1)}, bf16[256,256]{1,0:T(8,128)(2,1)S(1)}, u32[]{:S(2)}, u32[]{:S(2)}) collective-permute-start(bf16[256,256]{1,0:T(8,128)(2,1)S(1)} %attend.4.refs_1_), channel_id=1, source_target_pairs={{0,1},{1,2},{2,3},{3,0},{4,5},{5,6},{6,7},{7,4},{8,9},{9,10},{10,1... | collective-permute-start | bytes 393224 | tf_op jit(solution)/shard_map/ppermute | solution.py:387
  149.0 20.1 %collective-permute-start.13 = (bf16[128,1408]{1,0:T(8,128)(2,1)S(1)}, bf16[128,1408]{1,0:T(8,128)(2,1)S(1)}, u32[]{:S(2)}, u32[]{:S(2)}) collective-permute-start(bf16[128,1408]{1,0:T(8,128)(2,1)S(1)} %get-tuple-element.37), channel_id=1, source_target_pairs={{0,12},{4,0},{8,4},{12,8},{1,13},{5,1},{9,5},{13,9},{2,14},{6,2},{... | collective-permute-start | bytes 1081352 | tf_op jit(solution)/shard_map/ppermute | solution.py:387
  149.1 20.0 %collective-permute-start.14 = (bf16[128,1408]{1,0:T(8,128)(2,1)S(1)}, bf16[128,1408]{1,0:T(8,128)(2,1)S(1)}, u32[]{:S(2)}, u32[]{:S(2)}) collective-permute-start(bf16[128,1408]{1,0:T(8,128)(2,1)S(1)} %get-tuple-element.38), channel_id=1, source_target_pairs={{0,4},{4,8},{8,12},{12,0},{1,5},{5,9},{9,13},{13,1},{2,6},{6,10},{... | collective-permute-start | bytes 1081352 | tf_op jit(solution)/shard_map/ppermute | solution.py:387
  153.9 18.0 %collective-permute-start.23 = (bf16[128,1408]{1,0:T(8,128)(2,1)S(1)}, bf16[128,1408]{1,0:T(8,128)(2,1)S(1)}, u32[]{:S(2)}, u32[]{:S(2)}) collective-permute-start(bf16[128,1408]{1,0:T(8,128)(2,1)S(1)} %get-tuple-element.41), channel_id=1, source_target_pairs={{0,4},{4,8},{8,12},{12,0},{1,5},{5,9},{9,13},{13,1},{2,6},{6,10},{... | collective-permute-start | bytes 1081352 | tf_op jit(solution)/shard_map/ppermute | solution.py:387
  154.0 17.9 %collective-permute-start.24 = (bf16[128,1408]{1,0:T(8,128)(2,1)S(1)}, bf16[128,1408]{1,0:T(8,128)(2,1)S(1)}, u32[]{:S(2)}, u32[]{:S(2)}) collective-permute-start(bf16[128,1408]{1,0:T(8,128)(2,1)S(1)} %get-tuple-element.42), channel_id=1, source_target_pairs={{0,12},{4,0},{8,4},{12,8},{1,13},{5,1},{9,5},{13,9},{2,14},{6,2},{... | collective-permute-start | bytes 1081352 | tf_op jit(solution)/shard_map/ppermute | solution.py:387
  157.2 5.0 %collective-permute-start.2 = (bf16[256,256]{1,0:T(8,128)(2,1)S(1)}, bf16[256,256]{1,0:T(8,128)(2,1)S(1)}, u32[]{:S(2)}, u32[]{:S(2)}) collective-permute-start(bf16[256,256]{1,0:T(8,128)(2,1)S(1)} %attend.4.refs_1_), channel_id=1, source_target_pairs={{0,3},{1,0},{2,1},{3,2},{4,7},{5,4},{6,5},{7,6},{8,11},{9,8},{10,9... | collective-permute-start | bytes 393224 | tf_op jit(solution)/shard_map/ppermute | solution.py:387
  162.2 6.9 %collective-permute-start.3 = (bf16[256,256]{1,0:T(8,128)(2,1)S(1)}, bf16[256,256]{1,0:T(8,128)(2,1)S(1)}, u32[]{:S(2)}, u32[]{:S(2)}) collective-permute-start(bf16[256,256]{1,0:T(8,128)(2,1)S(1)} %attend.4.refs_1_), channel_id=1, source_target_pairs={{0,2},{1,3},{2,0},{3,1},{4,6},{5,7},{6,4},{7,5},{8,10},{9,11},{10,... | collective-permute-start | bytes 393224 | tf_op jit(solution)/shard_map/ppermute | solution.py:387
  172.7 6.8 %collective-permute-start.25 = (bf16[64,1408]{1,0:T(8,128)(2,1)S(1)}, bf16[64,1408]{1,0:T(8,128)(2,1)S(1)}, u32[]{:S(2)}, u32[]{:S(2)}) collective-permute-start(bf16[64,1408]{1,0:T(8,128)(2,1)S(1)} %get-tuple-element.44), channel_id=1, source_target_pairs={{0,1},{1,2},{2,3},{3,0},{4,5},{5,6},{6,7},{7,4},{8,9},{9,10},{10,1... | collective-permute-start | bytes 540680 | tf_op jit(solution)/shard_map/ppermute | solution.py:387
  172.8 6.7 %collective-permute-start.26 = (bf16[64,1408]{1,0:T(8,128)(2,1)S(1)}, bf16[64,1408]{1,0:T(8,128)(2,1)S(1)}, u32[]{:S(2)}, u32[]{:S(2)}) collective-permute-start(bf16[64,1408]{1,0:T(8,128)(2,1)S(1)} %get-tuple-element.45), channel_id=1, source_target_pairs={{0,3},{1,0},{2,1},{3,2},{4,7},{5,4},{6,5},{7,6},{8,11},{9,8},{10,9... | collective-permute-start | bytes 540680 | tf_op jit(solution)/shard_map/ppermute | solution.py:387
  176.0 7.0 %collective-permute-start.27 = (bf16[64,1408]{1,0:T(8,128)(2,1)S(1)}, bf16[64,1408]{1,0:T(8,128)(2,1)S(1)}, u32[]{:S(2)}, u32[]{:S(2)}) collective-permute-start(bf16[64,1408]{1,0:T(8,128)(2,1)S(1)} %get-tuple-element.46), channel_id=1, source_target_pairs={{0,2},{1,3},{2,0},{3,1},{4,6},{5,7},{6,4},{7,5},{8,10},{9,11},{10,... | collective-permute-start | bytes 540680 | tf_op jit(solution)/shard_map/ppermute | solution.py:387
  (12 other events, 429.9 us)

commit v3 on v1

v3 whole, which is shorter than its diff:
```python
import functools

import jax
import jax.numpy as jnp
import numpy as np
from jax import lax
from jax.experimental import pallas as pl
from jax.experimental.pallas import tpu as pltpu
from jax.sharding import Mesh
from jax.sharding import PartitionSpec as P

MODEL_WIDTH = 5376
HQ = 32
HEAD = 128
WINDOW_SPAN = 1024
BLOCK_TOKENS = 8192
SHARD = 1024
EPSILON = 1e-06
LOG2E = 1.4426950408889634
SCORE_SCALE = float(MODEL_WIDTH // HQ) ** (-0.5)

F32 = jnp.float32
BF16 = jnp.bfloat16

ROWS = 256
GROUP = 16
HALF = 128
QUARTER = 1408
ROW_AT = 3


ANY = pl.BlockSpec(memory_space=pl.ANY)
VMEM = pl.BlockSpec(memory_space=pltpu.VMEM)
SMEM = pl.BlockSpec(memory_space=pltpu.SMEM)
SMALL = pl.CostEstimate(flops=0, bytes_accessed=0, transcendentals=0)


def rotary_table():
    half = HEAD // 2
    exponent = np.arange(half, dtype=np.float32) * np.float32(-2.0 / HEAD)
    frequency = np.power(np.float64(10000.0), exponent.astype(np.float64)).astype(np.float32)
    position = (WINDOW_SPAN + np.arange(BLOCK_TOKENS)).astype(np.float32)
    angle = (position[:, None] * frequency[None, :]).astype(np.float64)
    return np.concatenate([np.cos(angle), np.sin(angle)], axis=1).astype(np.float32)


def places():
    rows = []
    for device in range(128):
        seq, x, z = device // 16, device // 4 % 4, device % 4
        far, up, down = ((x + by) % 4 * 256 for by in (2, 1, 3))
        rows.append(
            [seq, z, seq % 2, far, far + 128, up, up + 128, down, down + 128, x * 256,
             x * 256 + 128, x]
        )
    return np.array(rows, np.int32)


def rotate(u, gain, table):
    swapped = pltpu.roll(table, 64, 1)
    low = lax.broadcasted_iota(jnp.int32, table.shape, 1) < 64
    cosine = jnp.where(low, table, swapped)
    sine = jnp.where(low, -swapped, table)
    mean = jnp.sum(u * u, axis=-1, keepdims=True) * (1.0 / HEAD)
    u = u * lax.rsqrt(mean + EPSILON) * gain
    return (u * cosine + pltpu.roll(u, 64, 1) * sine).astype(BF16)


def project_kernel(
    pos_ref, tok_ref, g_ref, wq_ref, wk_ref, wv_ref, qg_ref, kg_ref, tab_ref,
    q_ref, kv_ref, own_ref, w_all, g_all, normed, sems,
):
    step = pl.program_id(0)
    copies = [
        pltpu.make_async_copy(wq_ref, w_all.at[:, 0:256], sems.at[0]),
        pltpu.make_async_copy(wk_ref, w_all.at[:, 256:384], sems.at[1]),
        pltpu.make_async_copy(wv_ref, w_all.at[:, 384:512], sems.at[2]),
    ]
    blocks = MODEL_WIDTH // 128

    def norm_group(i, carry):
        at = i * GROUP if isinstance(i, int) else pl.multiple_of(i * GROUP, GROUP)
        rows = pl.ds(at, GROUP)
        parts = [jnp.zeros((GROUP, 128), F32) for _ in range(2)]
        for b in range(blocks):
            v = tok_ref[rows, b * 128 : (b + 1) * 128].astype(F32)
            parts[b % 2] = parts[b % 2] + v * v
        mean = jnp.sum(parts[0] + parts[1], axis=-1, keepdims=True) * (1.0 / MODEL_WIDTH)
        r = jnp.broadcast_to(lax.rsqrt(mean + EPSILON), (GROUP, 128))
        for b in range(blocks):
            cols = slice(b * 128, (b + 1) * 128)
            v = tok_ref[rows, cols].astype(F32)
            normed[rows, cols] = (v * r * g_all[:, cols]).astype(BF16)
        return carry

    def multiply_and_rotate():
        raw = jnp.dot(normed[...], w_all[...], preferred_element_type=F32)
        table = tab_ref[...]
        q_ref[:, 0:128] = rotate(raw[:, 0:128], qg_ref[...], table)
        q_ref[:, 128:256] = rotate(raw[:, 128:256], qg_ref[...], table)
        kv_ref[:, 0:128] = rotate(raw[:, 256:384], kg_ref[...], table)
        kv_ref[:, 128:256] = raw[:, 384:512].astype(BF16)

    @pl.when(step == 0)
    def _():
        for copy in copies:
            copy.start()
        g_all[...] = jnp.broadcast_to(g_ref[...], g_all.shape)
        lax.fori_loop(0, ROWS // GROUP, norm_group, 0, unroll=4)
        for copy in copies:
            copy.wait()
        multiply_and_rotate()

    @pl.when(step != 0)
    def _():
        for i in range(ROWS // GROUP):
            norm_group(i, 0)
        multiply_and_rotate()

    @pl.when(step == pos_ref[ROW_AT + 8])
    def _():
        own_ref[...] = tok_ref[pl.ds(pl.multiple_of(pos_ref[1] * 64, 64), 64), :]


def project(pos, tokens, pre_gain, wq, wk, wv, q_gain, k_gain, table):
    whole = lambda shape: pl.BlockSpec(shape, lambda i, s: (0, 0))
    tile = lambda width: pl.BlockSpec((ROWS, width), lambda i, s: (i, 0))
    return pl.pallas_call(
        project_kernel,
        grid_spec=pltpu.PrefetchScalarGridSpec(
            num_scalar_prefetch=1,
            grid=(SHARD // ROWS,),
            in_specs=[
                tile(MODEL_WIDTH), whole((1, MODEL_WIDTH)), ANY, ANY, ANY,
                whole((1, 128)), whole((1, 128)),
                pl.BlockSpec((ROWS, 128), lambda i, s: (s[0] * (SHARD // ROWS) + i, 0)),
            ],
            out_specs=[tile(256), tile(256), whole((64, MODEL_WIDTH))],
            scratch_shapes=[
                pltpu.VMEM((MODEL_WIDTH, 512), BF16),
                pltpu.VMEM((GROUP, MODEL_WIDTH), F32),
                pltpu.VMEM((ROWS, MODEL_WIDTH), BF16),
                pltpu.SemaphoreType.DMA((3,)),
            ],
        ),
        out_shape=[
            jax.ShapeDtypeStruct((SHARD, 256), BF16),
            jax.ShapeDtypeStruct((SHARD, 256), BF16),
            jax.ShapeDtypeStruct((64, MODEL_WIDTH), BF16),
        ],
        compiler_params=pltpu.CompilerParams(vmem_limit_bytes=58 << 20),
        cost_estimate=pl.CostEstimate(
            flops=4 * SHARD * MODEL_WIDTH * 512, bytes_accessed=18 << 20, transcendentals=0
        ),
        name="project",
    )(
        pos, tokens, pre_gain.reshape(1, -1), wq, wk, wv,
        q_gain.reshape(1, -1), k_gain.reshape(1, -1), table,
    )


def attend_kernel(first_part, pos_ref, q_ref, kv_ref, got_ref, pk_ref, pv_ref, out_ref, keys, values):
    @pl.when(pos_ref[0] == 0)
    def _():
        keys[0:SHARD] = pk_ref[...]
        values[0:SHARD, 0:128] = pv_ref[...]

    @pl.when(pos_ref[0] != 0)
    def _():
        keys[0:SHARD] = got_ref[:, 0:128]
        values[0:SHARD, 0:128] = got_ref[:, 128:256]

    keys[SHARD:] = kv_ref[:, 0:128]
    values[SHARD:, 0:128] = kv_ref[:, 128:256]
    values[:, 128:256] = jnp.ones((2 * SHARD, 128), BF16)

    span = HALF + WINDOW_SPAN
    row = lax.broadcasted_iota(jnp.int32, (2 * HALF, HALF), 0) % HALF
    col = lax.broadcasted_iota(jnp.int32, (2 * HALF, HALF), 1)
    lowest = jnp.float32(-jnp.inf)
    for part in range(out_ref.shape[0] // HALF):
        first = pl.multiple_of(pos_ref[ROW_AT + first_part + part], HALF)
        q = q_ref[pl.ds(first, HALF), :]
        q = jnp.concatenate([q[:, 0:128], q[:, 128:256]], axis=0)
        k = keys[pl.ds(first, span), :]
        scores = lax.dot_general(q, k, (((1,), (1,)), ((), ())), preferred_element_type=F32)
        scores = jnp.concatenate(
            [
                jnp.where(col > row, scores[:, 0:HALF], lowest),
                scores[:, HALF:WINDOW_SPAN],
                jnp.where(col <= row, scores[:, WINDOW_SPAN:], lowest),
            ],
            axis=1,
        )
        top = jnp.max(scores, axis=-1, keepdims=True)
        weights = jnp.exp2((scores - top) * (SCORE_SCALE * LOG2E)).astype(BF16)
        mixed = jnp.dot(weights, values[pl.ds(first, span), :], preferred_element_type=F32)
        mixed = (mixed[:, 0:128] / mixed[:, 128:256]).astype(BF16)
        out_ref[part * HALF : (part + 1) * HALF, 0:128] = mixed[0:HALF]
        out_ref[part * HALF : (part + 1) * HALF, 128:256] = mixed[HALF:]


def attend(first_part, parts, pos, q, kv, got, prior_k, prior_v):
    vmem = pl.BlockSpec(memory_space=pltpu.VMEM)
    return pl.pallas_call(
        functools.partial(attend_kernel, first_part),
        in_specs=[pl.BlockSpec(memory_space=pltpu.SMEM)] + [vmem] * 5,
        out_specs=vmem,
        out_shape=jax.ShapeDtypeStruct((parts * HALF, 256), BF16),
        scratch_shapes=[
            pltpu.VMEM((2 * SHARD, 128), BF16),
            pltpu.VMEM((2 * SHARD, 256), BF16),
        ],
        compiler_params=pltpu.CompilerParams(vmem_limit_bytes=32 << 20),
        cost_estimate=SMALL,
        name="attend",
    )(pos, q, kv, got, prior_k, prior_v)


def quarter_start(number):
    return pl.multiple_of((number * 21 // 2) * 128, 128)


def pick_kernel(pos_ref, w_ref, own_ref, next_ref, last_ref, far_ref):
    z = pos_ref[1]
    for shift, ref in ((1, next_ref), (3, last_ref), (2, far_ref), (0, own_ref)):
        ref[...] = w_ref[:, pl.ds(quarter_start((z + shift) % 4), QUARTER)]


def pick(pos, w_out):
    return pl.pallas_call(
        pick_kernel,
        in_specs=[SMEM, VMEM],
        out_specs=[VMEM] * 4,
        out_shape=[jax.ShapeDtypeStruct((256, QUARTER), BF16)] * 4,
        compiler_params=pltpu.CompilerParams(vmem_limit_bytes=16 << 20),
        cost_estimate=SMALL,
        name="pick",
    )(pos, w_out)


def product(a_refs, w_refs, rows=slice(None)):
    out = None
    for a_ref, w_ref in zip(a_refs, w_refs, strict=True):
        term = jnp.dot(a_ref[rows, :], w_ref[...], preferred_element_type=F32)
        out = term if out is None else out + term
    return out


def far_kernel(*refs):
    out = product(refs[0:4], refs[4:8])
    refs[8][...] = out[0:HALF].astype(BF16)
    refs[9][...] = out[HALF:].astype(BF16)


def near_kernel(*refs):
    relay_up, relay_down, up_ref, down_ref = refs[8:]
    up = product(refs[0:4], refs[4:8], slice(0, 256))
    up_ref[0:HALF] = (up[0:HALF] + relay_up[...].astype(F32)).astype(BF16)
    up_ref[HALF:] = up[HALF:].astype(BF16)
    down = product(refs[0:4], refs[4:8], slice(256, 512))
    down_ref[0:HALF] = down[0:HALF].astype(BF16)
    down_ref[HALF:] = (down[HALF:] + relay_down[...].astype(F32)).astype(BF16)


def keep_kernel(*refs):
    refs[8][...] = product(refs[0:4], refs[4:8])


def multiply(kernel, pieces, weights, relays, out_shape, name):
    return pl.pallas_call(
        kernel,
        in_specs=[VMEM] * (8 + len(relays)),
        out_specs=jax.tree.map(lambda _: VMEM, out_shape),
        out_shape=out_shape,
        compiler_params=pltpu.CompilerParams(vmem_limit_bytes=24 << 20),
        cost_estimate=SMALL,
        name=name,
    )(*pieces, *weights, *relays)


def total_kernel(pos_ref, kept_ref, up_ref, down_ref, own_ref, next_ref, last_ref, far_ref, total):
    z = pos_ref[1]
    total[...] = kept_ref[...] + up_ref[...].astype(F32) + down_ref[...].astype(F32)

    def rows(shift):
        return total[pl.ds(pl.multiple_of(((z + shift) % 4) * 64, 64), 64), :]

    next_ref[...] = rows(1).astype(BF16)
    last_ref[...] = rows(3).astype(BF16)
    far_ref[...] = rows(2).astype(BF16)
    own_ref[...] = rows(0)


def total_step(pos, kept, up, down):
    part = jax.ShapeDtypeStruct((64, QUARTER), BF16)
    return pl.pallas_call(
        total_kernel,
        in_specs=[SMEM] + [VMEM] * 3,
        out_specs=[VMEM] * 4,
        out_shape=[jax.ShapeDtypeStruct((64, QUARTER), F32), part, part, part],
        scratch_shapes=[pltpu.VMEM((256, QUARTER), F32)],
        compiler_params=pltpu.CompilerParams(vmem_limit_bytes=32 << 20),
        cost_estimate=SMALL,
        name="total_step",
    )(pos, kept, up, down)


def finish_kernel(pos_ref, own_ref, next_ref, last_ref, far_ref, tok_ref, g_ref, out_ref, line):
    z = pos_ref[1]
    for shift, ref in ((0, own_ref), (3, next_ref), (1, last_ref), (2, far_ref)):
        line[:, pl.ds(quarter_start((z + shift) % 4), QUARTER)] = ref[...].astype(F32)
    for i in range(4):
        rows = slice(i * 16, (i + 1) * 16)
        total = jnp.zeros((16, 128), F32)
        for b in range(MODEL_WIDTH // 128):
            part = line[rows, b * 128 : (b + 1) * 128]
            total = total + part * part
        mean = jnp.sum(total, axis=-1, keepdims=True) * (1.0 / MODEL_WIDTH)
        r = jnp.broadcast_to(lax.rsqrt(mean + EPSILON), (16, 128))
        for b in range(MODEL_WIDTH // 128):
            cols = slice(b * 128, (b + 1) * 128)
            normed = line[rows, cols] * r * g_ref[:, cols]
            out_ref[rows, cols] = (tok_ref[rows, cols].astype(F32) + normed).astype(BF16)


def finish(pos, own, nxt, last, far, own_tokens, gain):
    return pl.pallas_call(
        finish_kernel,
        in_specs=[SMEM] + [VMEM] * 6,
        out_specs=VMEM,
        out_shape=jax.ShapeDtypeStruct((64, MODEL_WIDTH), BF16),
        scratch_shapes=[pltpu.VMEM((64, MODEL_WIDTH), F32)],
        compiler_params=pltpu.CompilerParams(vmem_limit_bytes=16 << 20),
        cost_estimate=SMALL,
        name="finish",
    )(pos, own, nxt, last, far, own_tokens, gain.reshape(1, -1))


def shift_by(array, axis, steps):
    return lax.ppermute(array, axis, [(i, (i + steps) % 4) for i in range(4)])


def from_line(pieces):
    return [shift_by(piece, "z", by) for piece, by in zip(pieces, (1, 3, 2), strict=True)]


def per_device(
    tokens, pre_gain, w_query, key_weight, value_weight, query_gain, key_gain,
    prior_key, prior_value, w_out, post_gain, table,
):
    device = lax.axis_index(("y", "c", "x", "z"))
    pos = lax.dynamic_slice_in_dim(jnp.asarray(places()), device, 1, 0).reshape(-1)
    own_w, *parts = pick(pos, w_out)
    pos, *parts = lax.optimization_barrier((pos, *parts))
    weights = [own_w, *from_line(parts)]
    q, kv, own_tokens = project(
        pos, tokens, pre_gain, w_query, key_weight, value_weight, query_gain, key_gain, table
    )
    got = lax.ppermute(kv, ("y", "c"), [(i, i + 1) for i in range(7)])

    pos, *weights[1:3] = lax.optimization_barrier((pos, *weights[1:3]))
    far = attend(0, 2, pos, q, kv, got, prior_key, prior_value)
    far_heads = [far, *from_line([far] * 3)]
    pos, _ = lax.optimization_barrier((pos, far))
    near = attend(2, 4, pos, q, kv, got, prior_key, prior_value)
    near_heads = [near, *from_line([near] * 3)]
    *far_heads, _ = lax.optimization_barrier((*far_heads, near))

    half = jax.ShapeDtypeStruct((HALF, QUARTER), BF16)
    full = jax.ShapeDtypeStruct((256, QUARTER), BF16)
    kept_shape = jax.ShapeDtypeStruct((256, QUARTER), F32)
    up, down = multiply(far_kernel, far_heads, weights, (), [half, half], "far")
    relays = (shift_by(up, "x", 1), shift_by(down, "x", 3))
    pos, _ = lax.optimization_barrier((pos, near))
    kept = attend(6, 2, pos, q, kv, got, prior_key, prior_value)
    kept_heads = [kept, *from_line([kept] * 3)]
    kept, *relays = lax.optimization_barrier((kept, *relays))
    up, down = multiply(near_kernel, near_heads, weights, relays, [full, full], "near")
    up, down = shift_by(up, "x", 1), shift_by(down, "x", 3)
    kept = multiply(keep_kernel, kept_heads, weights, (), kept_shape, "keep")
    own, *others = total_step(pos, kept, up, down)
    return finish(pos, own, *from_line(others), own_tokens, post_gain)


def solution(mesh):
    fine = Mesh(mesh.devices.reshape(4, 2, 4, 4), ("y", "c", "x", "z"))
    seq, tp = ("y", "c"), ("x", "z")
    inner = jax.shard_map(
        per_device,
        mesh=fine,
        in_specs=(
            P(seq, None), P(), P(None, tp), P(None, tp), P(None, tp), P(), P(),
            P(None, tp), P(None, tp), P(tp, None), P(), P(),
        ),
        out_specs=P(seq + tp, None),
        check_vma=False,
    )

    def run(*args):
        return inner(*args, jnp.asarray(rotary_table()))

    return run
```

time: 162 us -> 104 us (0.64)
  the two profiles are of different devices: /device:TPU:0 before, /device:TPU:24 now
where the time goes in v3:
time: 104 us; the launch traced here: 103 us
  waiting for transfers between devices  36.2 us (35%)
  starting transfers between devices  31.2 us (30%)
  Pallas kernels  29.9 us (29%)
  local copies, waits for them, and re-layouts  5.89 us (6%)
    ppermute x19, waiting for transfers between devices, shift_by(): return lax.ppermute(array, axis, [(i, (i + steps) % 4) for i in range(4)])  36.2 us
    ppermute x19, starting transfers between devices, shift_by(): return lax.ppermute(array, axis, [(i, (i + steps) % 4) for i in range(4)])  29.3 us
    pallas_call x1, Pallas kernels, project(): pl.pallas_call(project_kernel, grid_spec=pltpu.PrefetchScalarGridSpec(num...  15.6 us
    pallas_call x3, Pallas kernels, attend(): pl.pallas_call(functools.partial(attend_kernel, first_part), in_specs=[pl...  6.93 us
    unnamed x20, local copies, waits for them, and re-layouts  4.56 us
    pallas_call x3, Pallas kernels, multiply(): pl.pallas_call(kernel, in_specs=[VMEM] * (8 + len(relays)), out_specs=jax...  3.77 us
  transfers between devices with their start and end apart: 20, of which 11 were waited for; matrix products, arithmetic and copies ran while one was open for 1% of the time, Pallas kernels for 23%

profile of v3, /device:TPU:24, one launch (start us, length us, event | category | flops | bytes accessed | tf_op | source)
XLA Modules:
  0.0 103.4 jit_solution(9773553657977139907)
XLA Ops:
  0.7 1.8 %copy-done.2 = bf16[256,5376]{1,0:T(8,128)(2,1)S(1)} copy-done((bf16[256,5376]{1,0:T(8,128)(2,1)S(1)}, bf16[256,5376]{1,0:T(8,128)(2,1)}, u32[]{:S(2)}) %copy-start.2) | copy-done | bytes 2752536
  3.2 2.0 %collective-permute-start = (bf16[256,1408]{1,0:T(8,128)(2,1)S(1)}, bf16[256,1408]{1,0:T(8,128)(2,1)S(1)}, u32[]{:S(2)}, u32[]{:S(2)}) collective-permute-start(bf16[256,1408]{1,0:T(8,128)(2,1)S(1)} %get-tuple-element.39), channel_id=1, source_target_pairs={{0,1},{1,2},{2,3},{3,0},{4,5},{5,6},{6,7},{7,4},{8,9},{9,10},{10,1... | collective-permute-start | bytes 2162696 | tf_op jit(solution)/shard_map/ppermute | solution.py:341
  5.2 2.2 %collective-permute-start.1 = (bf16[256,1408]{1,0:T(8,128)(2,1)S(1)}, bf16[256,1408]{1,0:T(8,128)(2,1)S(1)}, u32[]{:S(2)}, u32[]{:S(2)}) collective-permute-start(bf16[256,1408]{1,0:T(8,128)(2,1)S(1)} %get-tuple-element.40), channel_id=1, source_target_pairs={{0,3},{1,0},{2,1},{3,2},{4,7},{5,4},{6,5},{7,6},{8,11},{9,8},{10,9... | collective-permute-start | bytes 2162696 | tf_op jit(solution)/shard_map/ppermute | solution.py:341
  7.4 1.8 %collective-permute-start.6 = (bf16[256,1408]{1,0:T(8,128)(2,1)S(1)}, bf16[256,1408]{1,0:T(8,128)(2,1)S(1)}, u32[]{:S(2)}, u32[]{:S(2)}) collective-permute-start(bf16[256,1408]{1,0:T(8,128)(2,1)S(1)} %get-tuple-element.49), channel_id=1, source_target_pairs={{0,2},{1,3},{2,0},{3,1},{4,6},{5,7},{6,4},{7,5},{8,10},{9,11},{10,... | collective-permute-start | bytes 2162696 | tf_op jit(solution)/shard_map/ppermute | solution.py:341
  9.8 15.6 %project.1 = (bf16[1024,256]{1,0:T(8,128)(2,1)}, bf16[1024,256]{1,0:T(8,128)(2,1)}, bf16[64,5376]{1,0:T(8,128)(2,1)}) custom-call(s32[12]{0:T(128)} %copy-done.6, bf16[1024,5376]{1,0:T(8,128)(2,1)} %tok_ref.1, f32[1,5376]{1,0:T(1,128)} %reshape.16.g_ref, bf16[5376,256]{1,0:T(8,128)(2,1)} %wq_ref.1, bf16[5376,128]{1,0:T(8,128)(2,1)} %wk_ref.1, ...), custom_call_target="tpu_custom_call" | custom-call | flops 11274289152 | bytes 18874368 | tf_op jit(solution)/shard_map/project/pallas_call | solution.py:128
  25.4 1.9 %collective-permute-start.2 = (bf16[1024,256]{1,0:T(8,128)(2,1)}, bf16[1024,256]{1,0:T(8,128)(2,1)S(1)}, u32[]{:S(2)}, u32[]{:S(2)}) collective-permute-start(bf16[1024,256]{1,0:T(8,128)(2,1)} %get-tuple-element.43.kv_ref), channel_id=1, source_target_pairs={{0,16},{16,32},{32,48},{48,64},{64,80},{80,96},{96,112},{1,17},{17... | collective-permute-start | bytes 1572872 | tf_op jit(solution)/shard_map/ppermute | solution.py:360
  27.4 11.1 %collective-permute-done.1.refs_6_ = bf16[256,1408]{1,0:T(8,128)(2,1)S(1)} collective-permute-done((bf16[256,1408]{1,0:T(8,128)(2,1)S(1)}, bf16[256,1408]{1,0:T(8,128)(2,1)S(1)}, u32[]{:S(2)}, u32[]{:S(2)}) %collective-permute-start.1) | collective-permute-done | bytes 720928 | tf_op jit(solution)/shard_map/ppermute | solution.py:341
  39.5 1.0 %copy-done.1 = bf16[1024,256]{1,0:T(8,128)(2,1)S(1)} copy-done((bf16[1024,256]{1,0:T(8,128)(2,1)S(1)}, bf16[1024,256]{1,0:T(8,128)(2,1)}, u32[]{:S(2)}) %copy-start.1) | copy-done | bytes 524312
  41.3 2.0 %attend.3.refs_0_ = bf16[256,256]{1,0:T(8,128)(2,1)S(1)} custom-call(s32[12]{0:T(128)S(1)} %copy-done.7, bf16[1024,256]{1,0:T(8,128)(2,1)S(1)} %copy-done, bf16[1024,256]{1,0:T(8,128)(2,1)S(1)} %copy-done.1, bf16[1024,256]{1,0:T(8,128)(2,1)S(1)} %collective-permute-done.2.got_ref, bf16[1024,128]{1,0:T(8,128)(2,1)S(1)} %copy-done.3, ...), custom_call_target="tpu_custom_call" | custom-call | tf_op jit(solution)/shard_map/attend/pallas_call | solution.py:205
  43.3 3.9 %collective-permute-start.11 = (bf16[256,256]{1,0:T(8,128)(2,1)S(1)}, bf16[256,256]{1,0:T(8,128)(2,1)S(1)}, u32[]{:S(2)}, u32[]{:S(2)}) collective-permute-start(bf16[256,256]{1,0:T(8,128)(2,1)S(1)} %attend.3.refs_0_), channel_id=1, source_target_pairs={{0,3},{1,0},{2,1},{3,2},{4,7},{5,4},{6,5},{7,6},{8,11},{9,8},{10,9... | collective-permute-start | bytes 393224 | tf_op jit(solution)/shard_map/ppermute | solution.py:341
  47.3 1.4 %collective-permute-start.12 = (bf16[256,256]{1,0:T(8,128)(2,1)S(1)}, bf16[256,256]{1,0:T(8,128)(2,1)S(1)}, u32[]{:S(2)}, u32[]{:S(2)}) collective-permute-start(bf16[256,256]{1,0:T(8,128)(2,1)S(1)} %attend.3.refs_0_), channel_id=1, source_target_pairs={{0,2},{1,3},{2,0},{3,1},{4,6},{5,7},{6,4},{7,5},{8,10},{9,11},{10,... | collective-permute-start | bytes 393224 | tf_op jit(solution)/shard_map/ppermute | solution.py:341
  48.6 3.0 %attend.4.refs_0_ = bf16[512,256]{1,0:T(8,128)(2,1)S(1)} custom-call(s32[12]{0:T(128)S(1)} %copy-done.7, bf16[1024,256]{1,0:T(8,128)(2,1)S(1)} %copy-done, bf16[1024,256]{1,0:T(8,128)(2,1)S(1)} %copy-done.1, bf16[1024,256]{1,0:T(8,128)(2,1)S(1)} %collective-permute-done.2.got_ref, bf16[1024,128]{1,0:T(8,128)(2,1)S(1)} %copy-done.3, ...), custom_call_target="tpu_custom_call" | custom-call | tf_op jit(solution)/shard_map/attend/pallas_call | solution.py:205
  51.7 3.9 %collective-permute-done.12.refs_3_ = bf16[256,256]{1,0:T(8,128)(2,1)S(1)} collective-permute-done((bf16[256,256]{1,0:T(8,128)(2,1)S(1)}, bf16[256,256]{1,0:T(8,128)(2,1)S(1)}, u32[]{:S(2)}, u32[]{:S(2)}) %collective-permute-start.12) | collective-permute-done | bytes 131104 | tf_op jit(solution)/shard_map/ppermute | solution.py:341
  56.6 1.8 %collective-permute-start.13 = (bf16[128,1408]{1,0:T(8,128)(2,1)S(1)}, bf16[128,1408]{1,0:T(8,128)(2,1)S(1)}, u32[]{:S(2)}, u32[]{:S(2)}) collective-permute-start(bf16[128,1408]{1,0:T(8,128)(2,1)S(1)} %get-tuple-element.54), channel_id=1, source_target_pairs={{0,4},{4,8},{8,12},{12,0},{1,5},{5,9},{9,13},{13,1},{2,6},{6,10},{... | collective-permute-start | bytes 1081352 | tf_op jit(solution)/shard_map/ppermute | solution.py:341
  58.4 1.5 %collective-permute-start.14 = (bf16[128,1408]{1,0:T(8,128)(2,1)S(1)}, bf16[128,1408]{1,0:T(8,128)(2,1)S(1)}, u32[]{:S(2)}, u32[]{:S(2)}) collective-permute-start(bf16[128,1408]{1,0:T(8,128)(2,1)S(1)} %get-tuple-element.55), channel_id=1, source_target_pairs={{0,12},{4,0},{8,4},{12,8},{1,13},{5,1},{9,5},{13,9},{2,14},{6,2},{... | collective-permute-start | bytes 1081352 | tf_op jit(solution)/shard_map/ppermute | solution.py:341
  59.9 1.6 %collective-permute-start.7 = (bf16[512,256]{1,0:T(8,128)(2,1)S(1)}, bf16[512,256]{1,0:T(8,128)(2,1)S(1)}, u32[]{:S(2)}, u32[]{:S(2)}) collective-permute-start(bf16[512,256]{1,0:T(8,128)(2,1)S(1)} %attend.4.refs_0_), channel_id=1, source_target_pairs={{0,1},{1,2},{2,3},{3,0},{4,5},{5,6},{6,7},{7,4},{8,9},{9,10},{10,1... | collective-permute-start | bytes 786440 | tf_op jit(solution)/shard_map/ppermute | solution.py:341
  61.5 1.6 %collective-permute-start.8 = (bf16[512,256]{1,0:T(8,128)(2,1)S(1)}, bf16[512,256]{1,0:T(8,128)(2,1)S(1)}, u32[]{:S(2)}, u32[]{:S(2)}) collective-permute-start(bf16[512,256]{1,0:T(8,128)(2,1)S(1)} %attend.4.refs_0_), channel_id=1, source_target_pairs={{0,3},{1,0},{2,1},{3,2},{4,7},{5,4},{6,5},{7,6},{8,11},{9,8},{10,9... | collective-permute-start | bytes 786440 | tf_op jit(solution)/shard_map/ppermute | solution.py:341
  63.1 1.3 %collective-permute-start.9 = (bf16[512,256]{1,0:T(8,128)(2,1)S(1)}, bf16[512,256]{1,0:T(8,128)(2,1)S(1)}, u32[]{:S(2)}, u32[]{:S(2)}) collective-permute-start(bf16[512,256]{1,0:T(8,128)(2,1)S(1)} %attend.4.refs_0_), channel_id=1, source_target_pairs={{0,2},{1,3},{2,0},{3,1},{4,6},{5,7},{6,4},{7,5},{8,10},{9,11},{10,... | collective-permute-start | bytes 786440 | tf_op jit(solution)/shard_map/ppermute | solution.py:341
  64.4 2.0 %attend.5.refs_0_ = bf16[256,256]{1,0:T(8,128)(2,1)S(1)} custom-call(s32[12]{0:T(128)S(1)} %copy-done.7, bf16[1024,256]{1,0:T(8,128)(2,1)S(1)} %copy-done, bf16[1024,256]{1,0:T(8,128)(2,1)S(1)} %copy-done.1, bf16[1024,256]{1,0:T(8,128)(2,1)S(1)} %collective-permute-done.2.got_ref, bf16[1024,128]{1,0:T(8,128)(2,1)S(1)} %copy-done.3, ...), custom_call_target="tpu_custom_call" | custom-call | tf_op jit(solution)/shard_map/attend/pallas_call | solution.py:205
  66.4 2.0 %collective-permute-done.14.refs_9_ = bf16[128,1408]{1,0:T(8,128)(2,1)S(1)} collective-permute-done((bf16[128,1408]{1,0:T(8,128)(2,1)S(1)}, bf16[128,1408]{1,0:T(8,128)(2,1)S(1)}, u32[]{:S(2)}, u32[]{:S(2)}) %collective-permute-start.14) | collective-permute-done | bytes 360480 | tf_op jit(solution)/shard_map/ppermute | solution.py:341
  69.1 5.3 %collective-permute-done.9.refs_3_ = bf16[512,256]{1,0:T(8,128)(2,1)S(1)} collective-permute-done((bf16[512,256]{1,0:T(8,128)(2,1)S(1)}, bf16[512,256]{1,0:T(8,128)(2,1)S(1)}, u32[]{:S(2)}, u32[]{:S(2)}) %collective-permute-start.9) | collective-permute-done | bytes 262176 | tf_op jit(solution)/shard_map/ppermute | solution.py:341
  74.4 1.8 %near.1 = (bf16[256,1408]{1,0:T(8,128)(2,1)S(1)}, bf16[256,1408]{1,0:T(8,128)(2,1)S(1)}) custom-call(bf16[512,256]{1,0:T(8,128)(2,1)S(1)} %attend.4.refs_0_, bf16[512,256]{1,0:T(8,128)(2,1)S(1)} %collective-permute-done.7.refs_1_, bf16[512,256]{1,0:T(8,128)(2,1)S(1)} %collective-permute-done.8.refs_2_, bf16[512,256]{1,0:T(8,128)(2,1)S(1)} %collective-permute-done.9.refs_3_, ...), custom_call_target="tpu_custom_call" | custom-call | tf_op jit(solution)/shard_map/near/pallas_call | solution.py:271
  77.0 2.6 %collective-permute-start.16 = (bf16[256,1408]{1,0:T(8,128)(2,1)S(1)}, bf16[256,1408]{1,0:T(8,128)(2,1)S(1)}, u32[]{:S(2)}, u32[]{:S(2)}) collective-permute-start(bf16[256,1408]{1,0:T(8,128)(2,1)S(1)} %get-tuple-element.59), channel_id=1, source_target_pairs={{0,12},{4,0},{8,4},{12,8},{1,13},{5,1},{9,5},{13,9},{2,14},{6,2},{... | collective-permute-start | bytes 2162696 | tf_op jit(solution)/shard_map/ppermute | solution.py:341
  79.5 1.4 %collective-permute-start.3 = (bf16[256,256]{1,0:T(8,128)(2,1)S(1)}, bf16[256,256]{1,0:T(8,128)(2,1)S(1)}, u32[]{:S(2)}, u32[]{:S(2)}) collective-permute-start(bf16[256,256]{1,0:T(8,128)(2,1)S(1)} %attend.5.refs_0_), channel_id=1, source_target_pairs={{0,1},{1,2},{2,3},{3,0},{4,5},{5,6},{6,7},{7,4},{8,9},{9,10},{10,1... | collective-permute-start | bytes 393224 | tf_op jit(solution)/shard_map/ppermute | solution.py:341
  80.9 1.8 %collective-permute-start.4 = (bf16[256,256]{1,0:T(8,128)(2,1)S(1)}, bf16[256,256]{1,0:T(8,128)(2,1)S(1)}, u32[]{:S(2)}, u32[]{:S(2)}) collective-permute-start(bf16[256,256]{1,0:T(8,128)(2,1)S(1)} %attend.5.refs_0_), channel_id=1, source_target_pairs={{0,3},{1,0},{2,1},{3,2},{4,7},{5,4},{6,5},{7,6},{8,11},{9,8},{10,9... | collective-permute-start | bytes 393224 | tf_op jit(solution)/shard_map/ppermute | solution.py:341
  83.0 2.7 %collective-permute-done.3.refs_1_ = bf16[256,256]{1,0:T(8,128)(2,1)S(1)} collective-permute-done((bf16[256,256]{1,0:T(8,128)(2,1)S(1)}, bf16[256,256]{1,0:T(8,128)(2,1)S(1)}, u32[]{:S(2)}, u32[]{:S(2)}) %collective-permute-start.3) | collective-permute-done | bytes 131104 | tf_op jit(solution)/shard_map/ppermute | solution.py:341
  86.7 2.5 %collective-permute-done.5.refs_3_ = bf16[256,256]{1,0:T(8,128)(2,1)S(1)} collective-permute-done((bf16[256,256]{1,0:T(8,128)(2,1)S(1)}, bf16[256,256]{1,0:T(8,128)(2,1)S(1)}, u32[]{:S(2)}, u32[]{:S(2)}) %collective-permute-start.5) | collective-permute-done | bytes 131104 | tf_op jit(solution)/shard_map/ppermute | solution.py:341
  91.5 3.0 %collective-permute-start.18 = (bf16[64,1408]{1,0:T(8,128)(2,1)S(1)}, bf16[64,1408]{1,0:T(8,128)(2,1)S(1)}, u32[]{:S(2)}, u32[]{:S(2)}) collective-permute-start(bf16[64,1408]{1,0:T(8,128)(2,1)S(1)} %get-tuple-element.62), channel_id=1, source_target_pairs={{0,3},{1,0},{2,1},{3,2},{4,7},{5,4},{6,5},{7,6},{8,11},{9,8},{10,9... | collective-permute-start | bytes 540680 | tf_op jit(solution)/shard_map/ppermute | solution.py:341
  94.6 3.4 %collective-permute-done.17.next_ref = bf16[64,1408]{1,0:T(8,128)(2,1)S(1)} collective-permute-done((bf16[64,1408]{1,0:T(8,128)(2,1)S(1)}, bf16[64,1408]{1,0:T(8,128)(2,1)S(1)}, u32[]{:S(2)}, u32[]{:S(2)}) %collective-permute-start.17) | collective-permute-done | bytes 180256 | tf_op jit(solution)/shard_map/ppermute | solution.py:341
  98.0 1.5 %collective-permute-done.18.last_ref = bf16[64,1408]{1,0:T(8,128)(2,1)S(1)} collective-permute-done((bf16[64,1408]{1,0:T(8,128)(2,1)S(1)}, bf16[64,1408]{1,0:T(8,128)(2,1)S(1)}, u32[]{:S(2)}, u32[]{:S(2)}) %collective-permute-start.18) | collective-permute-done | bytes 180256 | tf_op jit(solution)/shard_map/ppermute | solution.py:341
  99.5 2.1 %collective-permute-done.19.far_ref = bf16[64,1408]{1,0:T(8,128)(2,1)S(1)} collective-permute-done((bf16[64,1408]{1,0:T(8,128)(2,1)S(1)}, bf16[64,1408]{1,0:T(8,128)(2,1)S(1)}, u32[]{:S(2)}, u32[]{:S(2)}) %collective-permute-start.19) | collective-permute-done | bytes 180256 | tf_op jit(solution)/shard_map/ppermute | solution.py:341
  101.5 1.9 %finish.1 = bf16[64,5376]{1,0:T(8,128)(2,1)} custom-call(s32[12]{0:T(128)S(1)} %copy-done.7, f32[64,1408]{1,0:T(8,128)S(1)} %get-tuple-element.60.own_ref, bf16[64,1408]{1,0:T(8,128)(2,1)S(1)} %collective-permute-done.17.next_ref, bf16[64,1408]{1,0:T(8,128)(2,1)S(1)} %collective-permute-done.18.last_ref, ...), custom_call_target="tpu_custom_call" | custom-call | tf_op jit(solution)/shard_map/finish/pallas_call | solution.py:328
  (41 shorter events, 9.8 us)
Async XLA Ops:
  0.0 9.2 %copy-start.8 = (f32[5376]{0:T(1024)S(1)}, f32[5376]{0:T(1024)}, u32[]{:S(2)}) copy-start(f32[5376]{0:T(1024)} %param.14) | copy-start | bytes 64516
  0.7 1.8 %copy-start.2 = (bf16[256,5376]{1,0:T(8,128)(2,1)S(1)}, bf16[256,5376]{1,0:T(8,128)(2,1)}, u32[]{:S(2)}) copy-start(bf16[256,5376]{1,0:T(8,128)(2,1)} %w_ref.1) | copy-start | bytes 8257540
  2.5 7.4 %copy-start.6 = (s32[12]{0:T(128)}, s32[12]{0:T(128)S(1)}, u32[]{:S(2)}) copy-start(s32[12]{0:T(128)S(1)} %dynamic-slice_bitcast_fusion.pos_ref) | copy-start | bytes 148
  3.2 24.1 %collective-permute-start = (bf16[256,1408]{1,0:T(8,128)(2,1)S(1)}, bf16[256,1408]{1,0:T(8,128)(2,1)S(1)}, u32[]{:S(2)}, u32[]{:S(2)}) collective-permute-start(bf16[256,1408]{1,0:T(8,128)(2,1)S(1)} %get-tuple-element.39), channel_id=1, source_target_pairs={{0,1},{1,2},{2,3},{3,0},{4,5},{5,6},{6,7},{7,4},{8,9},{9,10},{10,1... | collective-permute-start | bytes 2162696 | tf_op jit(solution)/shard_map/ppermute | solution.py:341
  5.2 33.2 %collective-permute-start.1 = (bf16[256,1408]{1,0:T(8,128)(2,1)S(1)}, bf16[256,1408]{1,0:T(8,128)(2,1)S(1)}, u32[]{:S(2)}, u32[]{:S(2)}) collective-permute-start(bf16[256,1408]{1,0:T(8,128)(2,1)S(1)} %get-tuple-element.40), channel_id=1, source_target_pairs={{0,3},{1,0},{2,1},{3,2},{4,7},{5,4},{6,5},{7,6},{8,11},{9,8},{10,9... | collective-permute-start | bytes 2162696 | tf_op jit(solution)/shard_map/ppermute | solution.py:341
  7.4 48.2 %collective-permute-start.6 = (bf16[256,1408]{1,0:T(8,128)(2,1)S(1)}, bf16[256,1408]{1,0:T(8,128)(2,1)S(1)}, u32[]{:S(2)}, u32[]{:S(2)}) collective-permute-start(bf16[256,1408]{1,0:T(8,128)(2,1)S(1)} %get-tuple-element.49), channel_id=1, source_target_pairs={{0,2},{1,3},{2,0},{3,1},{4,6},{5,7},{6,4},{7,5},{8,10},{9,11},{10,... | collective-permute-start | bytes 2162696 | tf_op jit(solution)/shard_map/ppermute | solution.py:341
  9.8 28.6 %copy-start.3 = (bf16[1024,128]{1,0:T(8,128)(2,1)S(1)}, bf16[1024,128]{1,0:T(8,128)(2,1)}, u32[]{:S(2)}) copy-start(bf16[1024,128]{1,0:T(8,128)(2,1)} %pk_ref.5) | copy-start | bytes 786436
  9.8 28.6 %copy-start.4 = (bf16[1024,128]{1,0:T(8,128)(2,1)S(1)}, bf16[1024,128]{1,0:T(8,128)(2,1)}, u32[]{:S(2)}) copy-start(bf16[1024,128]{1,0:T(8,128)(2,1)} %pv_ref.5) | copy-start | bytes 786436
  25.4 13.1 %collective-permute-start.2 = (bf16[1024,256]{1,0:T(8,128)(2,1)}, bf16[1024,256]{1,0:T(8,128)(2,1)S(1)}, u32[]{:S(2)}, u32[]{:S(2)}) collective-permute-start(bf16[1024,256]{1,0:T(8,128)(2,1)} %get-tuple-element.43.kv_ref), channel_id=1, source_target_pairs={{0,16},{16,32},{32,48},{48,64},{64,80},{80,96},{96,112},{1,17},{17... | collective-permute-start | bytes 1572872 | tf_op jit(solution)/shard_map/ppermute | solution.py:360
  38.5 1.0 %copy-start = (bf16[1024,256]{1,0:T(8,128)(2,1)S(1)}, bf16[1024,256]{1,0:T(8,128)(2,1)}, u32[]{:S(2)}) copy-start(bf16[1024,256]{1,0:T(8,128)(2,1)} %get-tuple-element.42.q_ref) | copy-start | bytes 1572868
  39.5 1.0 %copy-start.1 = (bf16[1024,256]{1,0:T(8,128)(2,1)S(1)}, bf16[1024,256]{1,0:T(8,128)(2,1)}, u32[]{:S(2)}) copy-start(bf16[1024,256]{1,0:T(8,128)(2,1)} %get-tuple-element.43.kv_ref) | copy-start | bytes 1572868
  40.6 0.7 copy-start.7
  43.2 8.4 %collective-permute-start.10 = (bf16[256,256]{1,0:T(8,128)(2,1)S(1)}, bf16[256,256]{1,0:T(8,128)(2,1)S(1)}, u32[]{:S(2)}, u32[]{:S(2)}) collective-permute-start(bf16[256,256]{1,0:T(8,128)(2,1)S(1)} %attend.3.refs_0_), channel_id=1, source_target_pairs={{0,1},{1,2},{2,3},{3,0},{4,5},{5,6},{6,7},{7,4},{8,9},{9,10},{10,1... | collective-permute-start | bytes 393224 | tf_op jit(solution)/shard_map/ppermute | solution.py:341
  43.3 8.3 %collective-permute-start.11 = (bf16[256,256]{1,0:T(8,128)(2,1)S(1)}, bf16[256,256]{1,0:T(8,128)(2,1)S(1)}, u32[]{:S(2)}, u32[]{:S(2)}) collective-permute-start(bf16[256,256]{1,0:T(8,128)(2,1)S(1)} %attend.3.refs_0_), channel_id=1, source_target_pairs={{0,3},{1,0},{2,1},{3,2},{4,7},{5,4},{6,5},{7,6},{8,11},{9,8},{10,9... | collective-permute-start | bytes 393224 | tf_op jit(solution)/shard_map/ppermute | solution.py:341
  47.3 8.3 %collective-permute-start.12 = (bf16[256,256]{1,0:T(8,128)(2,1)S(1)}, bf16[256,256]{1,0:T(8,128)(2,1)S(1)}, u32[]{:S(2)}, u32[]{:S(2)}) collective-permute-start(bf16[256,256]{1,0:T(8,128)(2,1)S(1)} %attend.3.refs_0_), channel_id=1, source_target_pairs={{0,2},{1,3},{2,0},{3,1},{4,6},{5,7},{6,4},{7,5},{8,10},{9,11},{10,... | collective-permute-start | bytes 393224 | tf_op jit(solution)/shard_map/ppermute | solution.py:341
  56.6 9.8 %collective-permute-start.13 = (bf16[128,1408]{1,0:T(8,128)(2,1)S(1)}, bf16[128,1408]{1,0:T(8,128)(2,1)S(1)}, u32[]{:S(2)}, u32[]{:S(2)}) collective-permute-start(bf16[128,1408]{1,0:T(8,128)(2,1)S(1)} %get-tuple-element.54), channel_id=1, source_target_pairs={{0,4},{4,8},{8,12},{12,0},{1,5},{5,9},{9,13},{13,1},{2,6},{6,10},{... | collective-permute-start | bytes 1081352 | tf_op jit(solution)/shard_map/ppermute | solution.py:341
  58.4 10.1 %collective-permute-start.14 = (bf16[128,1408]{1,0:T(8,128)(2,1)S(1)}, bf16[128,1408]{1,0:T(8,128)(2,1)S(1)}, u32[]{:S(2)}, u32[]{:S(2)}) collective-permute-start(bf16[128,1408]{1,0:T(8,128)(2,1)S(1)} %get-tuple-element.55), channel_id=1, source_target_pairs={{0,12},{4,0},{8,4},{12,8},{1,13},{5,1},{9,5},{13,9},{2,14},{6,2},{... | collective-permute-start | bytes 1081352 | tf_op jit(solution)/shard_map/ppermute | solution.py:341
  59.9 8.5 %collective-permute-start.7 = (bf16[512,256]{1,0:T(8,128)(2,1)S(1)}, bf16[512,256]{1,0:T(8,128)(2,1)S(1)}, u32[]{:S(2)}, u32[]{:S(2)}) collective-permute-start(bf16[512,256]{1,0:T(8,128)(2,1)S(1)} %attend.4.refs_0_), channel_id=1, source_target_pairs={{0,1},{1,2},{2,3},{3,0},{4,5},{5,6},{6,7},{7,4},{8,9},{9,10},{10,1... | collective-permute-start | bytes 786440 | tf_op jit(solution)/shard_map/ppermute | solution.py:341
  61.5 7.5 %collective-permute-start.8 = (bf16[512,256]{1,0:T(8,128)(2,1)S(1)}, bf16[512,256]{1,0:T(8,128)(2,1)S(1)}, u32[]{:S(2)}, u32[]{:S(2)}) collective-permute-start(bf16[512,256]{1,0:T(8,128)(2,1)S(1)} %attend.4.refs_0_), channel_id=1, source_target_pairs={{0,3},{1,0},{2,1},{3,2},{4,7},{5,4},{6,5},{7,6},{8,11},{9,8},{10,9... | collective-permute-start | bytes 786440 | tf_op jit(solution)/shard_map/ppermute | solution.py:341
  63.1 11.3 %collective-permute-start.9 = (bf16[512,256]{1,0:T(8,128)(2,1)S(1)}, bf16[512,256]{1,0:T(8,128)(2,1)S(1)}, u32[]{:S(2)}, u32[]{:S(2)}) collective-permute-start(bf16[512,256]{1,0:T(8,128)(2,1)S(1)} %attend.4.refs_0_), channel_id=1, source_target_pairs={{0,2},{1,3},{2,0},{3,1},{4,6},{5,7},{6,4},{7,5},{8,10},{9,11},{10,... | collective-permute-start | bytes 786440 | tf_op jit(solution)/shard_map/ppermute | solution.py:341
  76.2 14.0 %collective-permute-start.15 = (bf16[256,1408]{1,0:T(8,128)(2,1)S(1)}, bf16[256,1408]{1,0:T(8,128)(2,1)S(1)}, u32[]{:S(2)}, u32[]{:S(2)}) collective-permute-start(bf16[256,1408]{1,0:T(8,128)(2,1)S(1)} %get-tuple-element.58), channel_id=1, source_target_pairs={{0,4},{4,8},{8,12},{12,0},{1,5},{5,9},{9,13},{13,1},{2,6},{6,10},{... | collective-permute-start | bytes 2162696 | tf_op jit(solution)/shard_map/ppermute | solution.py:341
  77.0 17.6 %copy-start.9 = (f32[5376]{0:T(1024)S(1)}, f32[5376]{0:T(1024)}, u32[]{:S(2)}) copy-start(f32[5376]{0:T(1024)} %param.23) | copy-start | bytes 64516
  77.0 24.6 %copy-start.5 = (bf16[64,5376]{1,0:T(8,128)(2,1)S(1)}, bf16[64,5376]{1,0:T(8,128)(2,1)}, u32[]{:S(2)}) copy-start(bf16[64,5376]{1,0:T(8,128)(2,1)} %get-tuple-element.64.tok_ref) | copy-start | bytes 2064388
  77.0 13.3 %collective-permute-start.16 = (bf16[256,1408]{1,0:T(8,128)(2,1)S(1)}, bf16[256,1408]{1,0:T(8,128)(2,1)S(1)}, u32[]{:S(2)}, u32[]{:S(2)}) collective-permute-start(bf16[256,1408]{1,0:T(8,128)(2,1)S(1)} %get-tuple-element.59), channel_id=1, source_target_pairs={{0,12},{4,0},{8,4},{12,8},{1,13},{5,1},{9,5},{13,9},{2,14},{6,2},{... | collective-permute-start | bytes 2162696 | tf_op jit(solution)/shard_map/ppermute | solution.py:341
  79.5 6.2 %collective-permute-start.3 = (bf16[256,256]{1,0:T(8,128)(2,1)S(1)}, bf16[256,256]{1,0:T(8,128)(2,1)S(1)}, u32[]{:S(2)}, u32[]{:S(2)}) collective-permute-start(bf16[256,256]{1,0:T(8,128)(2,1)S(1)} %attend.5.refs_0_), channel_id=1, source_target_pairs={{0,1},{1,2},{2,3},{3,0},{4,5},{5,6},{6,7},{7,4},{8,9},{9,10},{10,1... | collective-permute-start | bytes 393224 | tf_op jit(solution)/shard_map/ppermute | solution.py:341
  80.9 5.7 %collective-permute-start.4 = (bf16[256,256]{1,0:T(8,128)(2,1)S(1)}, bf16[256,256]{1,0:T(8,128)(2,1)S(1)}, u32[]{:S(2)}, u32[]{:S(2)}) collective-permute-start(bf16[256,256]{1,0:T(8,128)(2,1)S(1)} %attend.5.refs_0_), channel_id=1, source_target_pairs={{0,3},{1,0},{2,1},{3,2},{4,7},{5,4},{6,5},{7,6},{8,11},{9,8},{10,9... | collective-permute-start | bytes 393224 | tf_op jit(solution)/shard_map/ppermute | solution.py:341
  82.8 6.5 %collective-permute-start.5 = (bf16[256,256]{1,0:T(8,128)(2,1)S(1)}, bf16[256,256]{1,0:T(8,128)(2,1)S(1)}, u32[]{:S(2)}, u32[]{:S(2)}) collective-permute-start(bf16[256,256]{1,0:T(8,128)(2,1)S(1)} %attend.5.refs_0_), channel_id=1, source_target_pairs={{0,2},{1,3},{2,0},{3,1},{4,6},{5,7},{6,4},{7,5},{8,10},{9,11},{10,... | collective-permute-start | bytes 393224 | tf_op jit(solution)/shard_map/ppermute | solution.py:341
  91.2 6.8 %collective-permute-start.17 = (bf16[64,1408]{1,0:T(8,128)(2,1)S(1)}, bf16[64,1408]{1,0:T(8,128)(2,1)S(1)}, u32[]{:S(2)}, u32[]{:S(2)}) collective-permute-start(bf16[64,1408]{1,0:T(8,128)(2,1)S(1)} %get-tuple-element.61), channel_id=1, source_target_pairs={{0,1},{1,2},{2,3},{3,0},{4,5},{5,6},{6,7},{7,4},{8,9},{9,10},{10,1... | collective-permute-start | bytes 540680 | tf_op jit(solution)/shard_map/ppermute | solution.py:341
  91.5 8.0 %collective-permute-start.18 = (bf16[64,1408]{1,0:T(8,128)(2,1)S(1)}, bf16[64,1408]{1,0:T(8,128)(2,1)S(1)}, u32[]{:S(2)}, u32[]{:S(2)}) collective-permute-start(bf16[64,1408]{1,0:T(8,128)(2,1)S(1)} %get-tuple-element.62), channel_id=1, source_target_pairs={{0,3},{1,0},{2,1},{3,2},{4,7},{5,4},{6,5},{7,6},{8,11},{9,8},{10,9... | collective-permute-start | bytes 540680 | tf_op jit(solution)/shard_map/ppermute | solution.py:341
  94.5 7.0 %collective-permute-start.19 = (bf16[64,1408]{1,0:T(8,128)(2,1)S(1)}, bf16[64,1408]{1,0:T(8,128)(2,1)S(1)}, u32[]{:S(2)}, u32[]{:S(2)}) collective-permute-start(bf16[64,1408]{1,0:T(8,128)(2,1)S(1)} %get-tuple-element.63), channel_id=1, source_target_pairs={{0,2},{1,3},{2,0},{3,1},{4,6},{5,7},{6,4},{7,5},{8,10},{9,11},{10,... | collective-permute-start | bytes 540680 | tf_op jit(solution)/shard_map/ppermute | solution.py:341

commit v4 on v3

--- a/solution.py
+++ b/solution.py
@@ -66,15 +66,14 @@
     return (u * cosine + pltpu.roll(u, 64, 1) * sine).astype(BF16)
 
 
-def project_kernel(
-    pos_ref, tok_ref, g_ref, wq_ref, wk_ref, wv_ref, qg_ref, kg_ref, tab_ref,
-    q_ref, kv_ref, own_ref, w_all, g_all, normed, sems,
+def key_value_kernel(
+    pos_ref, tok_ref, g_ref, wk_ref, wv_ref, gain_ref, tab_ref,
+    normed, kv_ref, own_ref, w_all, g_all, sems,
 ):
     step = pl.program_id(0)
     copies = [
-        pltpu.make_async_copy(wq_ref, w_all.at[:, 0:256], sems.at[0]),
-        pltpu.make_async_copy(wk_ref, w_all.at[:, 256:384], sems.at[1]),
-        pltpu.make_async_copy(wv_ref, w_all.at[:, 384:512], sems.at[2]),
+        pltpu.make_async_copy(wk_ref, w_all.at[:, 0:128], sems.at[0]),
+        pltpu.make_async_copy(wv_ref, w_all.at[:, 128:256], sems.at[1]),
     ]
     blocks = MODEL_WIDTH // 128
 
@@ -95,11 +94,8 @@
 
     def multiply_and_rotate():
         raw = jnp.dot(normed[...], w_all[...], preferred_element_type=F32)
-        table = tab_ref[...]
-        q_ref[:, 0:128] = rotate(raw[:, 0:128], qg_ref[...], table)
-        q_ref[:, 128:256] = rotate(raw[:, 128:256], qg_ref[...], table)
-        kv_ref[:, 0:128] = rotate(raw[:, 256:384], kg_ref[...], table)
-        kv_ref[:, 128:256] = raw[:, 384:512].astype(BF16)
+        kv_ref[:, 0:128] = rotate(raw[:, 0:128], gain_ref[...], tab_ref[...])
+        kv_ref[:, 128:256] = raw[:, 128:256].astype(BF16)
 
     @pl.when(step == 0)
     def _():
@@ -122,41 +118,75 @@
         own_ref[...] = tok_ref[pl.ds(pl.multiple_of(pos_ref[1] * 64, 64), 64), :]
 
 
-def project(pos, tokens, pre_gain, wq, wk, wv, q_gain, k_gain, table):
-    whole = lambda shape: pl.BlockSpec(shape, lambda i, s: (0, 0))
-    tile = lambda width: pl.BlockSpec((ROWS, width), lambda i, s: (i, 0))
-    return pl.pallas_call(
-        project_kernel,
+def in_hbm(*arrays):
+    return [pltpu.with_memory_space_constraint(array, pltpu.HBM) for array in arrays]
+
+
+def whole(shape):
+    return pl.BlockSpec(shape, lambda i, s: (0, 0))
+
+
+def row_tile(width):
+    return pl.BlockSpec((ROWS, width), lambda i, s: (i, 0))
+
+
+TABLE_TILE = pl.BlockSpec((ROWS, 128), lambda i, s: (s[0] * (SHARD // ROWS) + i, 0))
+
+
+def key_value(pos, tokens, pre_gain, wk, wv, gain, table):
+    tokens, wk, wv, table = in_hbm(tokens, wk, wv, table)
+    return pl.pallas_call(
+        key_value_kernel,
         grid_spec=pltpu.PrefetchScalarGridSpec(
             num_scalar_prefetch=1,
             grid=(SHARD // ROWS,),
             in_specs=[
-                tile(MODEL_WIDTH), whole((1, MODEL_WIDTH)), ANY, ANY, ANY,
-                whole((1, 128)), whole((1, 128)),
-                pl.BlockSpec((ROWS, 128), lambda i, s: (s[0] * (SHARD // ROWS) + i, 0)),
+                row_tile(MODEL_WIDTH), whole((1, MODEL_WIDTH)), ANY, ANY,
+                whole((1, 128)), TABLE_TILE,
             ],
-            out_specs=[tile(256), tile(256), whole((64, MODEL_WIDTH))],
+            out_specs=[row_tile(MODEL_WIDTH), row_tile(256), whole((64, MODEL_WIDTH))],
             scratch_shapes=[
-                pltpu.VMEM((MODEL_WIDTH, 512), BF16),
+                pltpu.VMEM((MODEL_WIDTH, 256), BF16),
                 pltpu.VMEM((GROUP, MODEL_WIDTH), F32),
-                pltpu.VMEM((ROWS, MODEL_WIDTH), BF16),
-                pltpu.SemaphoreType.DMA((3,)),
+                pltpu.SemaphoreType.DMA((2,)),
             ],
         ),
         out_shape=[
-            jax.ShapeDtypeStruct((SHARD, 256), BF16),
+            jax.ShapeDtypeStruct((SHARD, MODEL_WIDTH), BF16),
             jax.ShapeDtypeStruct((SHARD, 256), BF16),
             jax.ShapeDtypeStruct((64, MODEL_WIDTH), BF16),
         ],
-        compiler_params=pltpu.CompilerParams(vmem_limit_bytes=58 << 20),
+        compiler_params=pltpu.CompilerParams(vmem_limit_bytes=28 << 20),
         cost_estimate=pl.CostEstimate(
-            flops=4 * SHARD * MODEL_WIDTH * 512, bytes_accessed=18 << 20, transcendentals=0
+            flops=8 * SHARD * MODEL_WIDTH * 256, bytes_accessed=26 << 20, transcendentals=0
         ),
-        name="project",
-    )(
-        pos, tokens, pre_gain.reshape(1, -1), wq, wk, wv,
-        q_gain.reshape(1, -1), k_gain.reshape(1, -1), table,
-    )
+        name="key_value",
+    )(pos, tokens, pre_gain.reshape(1, -1), wk, wv, gain.reshape(1, -1), table)
+
+
+def query_kernel(pos_ref, normed_ref, w_ref, gain_ref, tab_ref, q_ref):
+    raw = jnp.dot(normed_ref[...], w_ref[...], preferred_element_type=F32)
+    q_ref[:, 0:128] = rotate(raw[:, 0:128], gain_ref[...], tab_ref[...])
+    q_ref[:, 128:256] = rotate(raw[:, 128:256], gain_ref[...], tab_ref[...])
+
+
+def query(pos, normed, wq, gain, table):
+    wq, table = in_hbm(wq, table)
+    return pl.pallas_call(
+        query_kernel,
+        grid_spec=pltpu.PrefetchScalarGridSpec(
+            num_scalar_prefetch=1,
+            grid=(SHARD // ROWS,),
+            in_specs=[
+                row_tile(MODEL_WIDTH), whole((MODEL_WIDTH, 256)), whole((1, 128)), TABLE_TILE
+            ],
+            out_specs=row_tile(256),
+        ),
+        out_shape=jax.ShapeDtypeStruct((SHARD, 256), BF16),
+        compiler_params=pltpu.CompilerParams(vmem_limit_bytes=24 << 20),
+        cost_estimate=SMALL,
+        name="query",
+    )(pos, normed, wq, gain.reshape(1, -1), table)
 
 
 def attend_kernel(first_part, pos_ref, q_ref, kv_ref, got_ref, pk_ref, pv_ref, out_ref, keys, values):
@@ -223,54 +253,75 @@
 
 def pick_kernel(pos_ref, w_ref, own_ref, next_ref, last_ref, far_ref):
     z = pos_ref[1]
-    for shift, ref in ((1, next_ref), (3, last_ref), (2, far_ref), (0, own_ref)):
-        ref[...] = w_ref[:, pl.ds(quarter_start((z + shift) % 4), QUARTER)]
+    rows = pl.ds(pl.multiple_of(pos_ref[2] * 128, 128), 128)
+    for shift, ref in ((1, next_ref), (3, last_ref), (2, far_ref)):
+        ref[...] = w_ref[rows, pl.ds(quarter_start((z + shift) % 4), QUARTER)]
+    own_ref[...] = w_ref[:, pl.ds(quarter_start(z), QUARTER)]
 
 
 def pick(pos, w_out):
+    part = jax.ShapeDtypeStruct((128, QUARTER), BF16)
     return pl.pallas_call(
         pick_kernel,
         in_specs=[SMEM, VMEM],
         out_specs=[VMEM] * 4,
-        out_shape=[jax.ShapeDtypeStruct((256, QUARTER), BF16)] * 4,
+        out_shape=[jax.ShapeDtypeStruct((256, QUARTER), BF16), part, part, part],
         compiler_params=pltpu.CompilerParams(vmem_limit_bytes=16 << 20),
         cost_estimate=SMALL,
         name="pick",
     )(pos, w_out)
 
 
+def join_kernel(pos_ref, *refs):
+    c, out_ref = pos_ref[2], refs[6]
+    for i in range(3):
+        out_ref[i, pl.ds(pl.multiple_of(c * 128, 128), 128)] = refs[i][...]
+        out_ref[i, pl.ds(pl.multiple_of((1 - c) * 128, 128), 128)] = refs[3 + i][...]
+
+
+def join(pos, lines, swapped):
+    return pl.pallas_call(
+        join_kernel,
+        in_specs=[SMEM] + [VMEM] * 6,
+        out_specs=VMEM,
+        out_shape=jax.ShapeDtypeStruct((3, 256, QUARTER), BF16),
+        compiler_params=pltpu.CompilerParams(vmem_limit_bytes=16 << 20),
+        cost_estimate=SMALL,
+        name="join",
+    )(pos, *lines, *swapped)
+
+
 def product(a_refs, w_refs, rows=slice(None)):
-    out = None
-    for a_ref, w_ref in zip(a_refs, w_refs, strict=True):
-        term = jnp.dot(a_ref[rows, :], w_ref[...], preferred_element_type=F32)
-        out = term if out is None else out + term
+    out = jnp.dot(a_refs[0][rows, :], w_refs[0][...], preferred_element_type=F32)
+    for i in range(3):
+        out = out + jnp.dot(a_refs[1 + i][rows, :], w_refs[1][i], preferred_element_type=F32)
     return out
 
 
 def far_kernel(*refs):
-    out = product(refs[0:4], refs[4:8])
-    refs[8][...] = out[0:HALF].astype(BF16)
-    refs[9][...] = out[HALF:].astype(BF16)
+    out = product(refs[0:4], refs[4:6])
+    refs[6][...] = out[0:HALF].astype(BF16)
+    refs[7][...] = out[HALF:].astype(BF16)
 
 
 def near_kernel(*refs):
-    relay_up, relay_down, up_ref, down_ref = refs[8:]
-    up = product(refs[0:4], refs[4:8], slice(0, 256))
+    relay_up, relay_down, up_ref, down_ref = refs[6:]
+    up = product(refs[0:4], refs[4:6], slice(0, 256))
     up_ref[0:HALF] = (up[0:HALF] + relay_up[...].astype(F32)).astype(BF16)
     up_ref[HALF:] = up[HALF:].astype(BF16)
-    down = product(refs[0:4], refs[4:8], slice(256, 512))
+    down = product(refs[0:4], refs[4:6], slice(256, 512))
     down_ref[0:HALF] = down[0:HALF].astype(BF16)
     down_ref[HALF:] = (down[HALF:] + relay_down[...].astype(F32)).astype(BF16)
 
 
 def keep_kernel(*refs):
-    refs[8][...] = product(refs[0:4], refs[4:8])
+    refs[6][...] = product(refs[0:4], refs[4:6])
 
 
 def multiply(kernel, pieces, weights, relays, out_shape, name):
     return pl.pallas_call(
         kernel,
-        in_specs=[VMEM] * (8 + len(relays)),
+        in_specs=[VMEM] * (6 + len(relays)),
         out_specs=jax.tree.map(lambda _: VMEM, out_shape),
         out_shape=out_shape,
         compiler_params=pltpu.CompilerParams(vmem_limit_bytes=24 << 20),
@@ -353,13 +404,17 @@
     pos = lax.dynamic_slice_in_dim(jnp.asarray(places()), device, 1, 0).reshape(-1)
     own_w, *parts = pick(pos, w_out)
     pos, *parts = lax.optimization_barrier((pos, *parts))
-    weights = [own_w, *from_line(parts)]
-    q, kv, own_tokens = project(
-        pos, tokens, pre_gain, w_query, key_weight, value_weight, query_gain, key_gain, table
+    lines = from_line(parts)
+    normed, kv, own_tokens = key_value(
+        pos, tokens, pre_gain, key_weight, value_weight, key_gain, table
     )
     got = lax.ppermute(kv, ("y", "c"), [(i, i + 1) for i in range(7)])
-
-    pos, *weights[1:3] = lax.optimization_barrier((pos, *weights[1:3]))
+    q = query(pos, normed, w_query, query_gain, table)
+    *lines, q = lax.optimization_barrier((*lines, q))
+    swapped = [lax.ppermute(part, "c", [(0, 1), (1, 0)]) for part in lines]
+    weights = [own_w, join(pos, lines, swapped)]
+
+    pos, weights[1] = lax.optimization_barrier((pos, weights[1]))
     far = attend(0, 2, pos, q, kv, got, prior_key, prior_value)
     far_heads = [far, *from_line([far] * 3)]
     pos, _ = lax.optimization_barrier((pos, far))

time: 104 us -> 95.9 us (0.922)
  the two profiles are of different devices: /device:TPU:24 before, /device:TPU:0 now
where the time goes in v4:
time: 95.9 us; the launch traced here: 95.6 us
  starting transfers between devices  33.5 us (35%)
  Pallas kernels  32.6 us (34%)
  waiting for transfers between devices  26.8 us (28%)
  local copies, waits for them, and re-layouts  2.54 us (3%)
    ppermute x19, starting transfers between devices, shift_by(): return lax.ppermute(array, axis, [(i, (i + steps) % 4) for i in range(4)])  29.3 us
    ppermute x19, waiting for transfers between devices, shift_by(): return lax.ppermute(array, axis, [(i, (i + steps) % 4) for i in range(4)])  25 us
    pallas_call x1, Pallas kernels, key_value(): pl.pallas_call(key_value_kernel, grid_spec=pltpu.PrefetchScalarGridSpec(n...  11 us
    pallas_call x3, Pallas kernels, attend(): pl.pallas_call(functools.partial(attend_kernel, first_part), in_specs=[pl...  6.86 us
    pallas_call x1, Pallas kernels, query(): pl.pallas_call(query_kernel, grid_spec=pltpu.PrefetchScalarGridSpec(num_s...  6.64 us
    pallas_call x3, Pallas kernels, multiply(): pl.pallas_call(kernel, in_specs=[VMEM] * (6 + len(relays)), out_specs=jax...  3.76 us
    ppermute x3, starting transfers between devices, per_device(): swapped = [lax.ppermute(part, 'c', [(0, 1), (1, 0)]) for part in lines]  2.87 us
  transfers between devices with their start and end apart: 23, of which 15 were waited for; matrix products, arithmetic and copies ran while one was open for 0% of the time, Pallas kernels for 25%

profile of v4, /device:TPU:0, one launch (start us, length us, event | category | flops | bytes accessed | tf_op | source)
XLA Modules:
  0.0 95.6 jit_solution(10405041822518992016)
XLA Ops:
  0.7 1.8 %copy-done = bf16[256,5376]{1,0:T(8,128)(2,1)S(1)} copy-done((bf16[256,5376]{1,0:T(8,128)(2,1)S(1)}, bf16[256,5376]{1,0:T(8,128)(2,1)}, u32[]{:S(2)}) %copy-start) | copy-done | bytes 2752536
  3.2 2.1 %collective-permute-start = (bf16[128,1408]{1,0:T(8,128)(2,1)S(1)}, bf16[128,1408]{1,0:T(8,128)(2,1)S(1)}, u32[]{:S(2)}, u32[]{:S(2)}) collective-permute-start(bf16[128,1408]{1,0:T(8,128)(2,1)S(1)} %get-tuple-element.42), channel_id=1, source_target_pairs={{0,1},{1,2},{2,3},{3,0},{4,5},{5,6},{6,7},{7,4},{8,9},{9,10},{10,1... | collective-permute-start | bytes 1081352 | tf_op jit(solution)/shard_map/ppermute | solution.py:392
  5.2 2.2 %collective-permute-start.1 = (bf16[128,1408]{1,0:T(8,128)(2,1)S(1)}, bf16[128,1408]{1,0:T(8,128)(2,1)S(1)}, u32[]{:S(2)}, u32[]{:S(2)}) collective-permute-start(bf16[128,1408]{1,0:T(8,128)(2,1)S(1)} %get-tuple-element.43), channel_id=1, source_target_pairs={{0,3},{1,0},{2,1},{3,2},{4,7},{5,4},{6,5},{7,6},{8,11},{9,8},{10,9... | collective-permute-start | bytes 1081352 | tf_op jit(solution)/shard_map/ppermute | solution.py:392
  7.4 1.8 %collective-permute-start.2 = (bf16[128,1408]{1,0:T(8,128)(2,1)S(1)}, bf16[128,1408]{1,0:T(8,128)(2,1)S(1)}, u32[]{:S(2)}, u32[]{:S(2)}) collective-permute-start(bf16[128,1408]{1,0:T(8,128)(2,1)S(1)} %get-tuple-element.44), channel_id=1, source_target_pairs={{0,2},{1,3},{2,0},{3,1},{4,6},{5,7},{6,4},{7,5},{8,10},{9,11},{10,... | collective-permute-start | bytes 1081352 | tf_op jit(solution)/shard_map/ppermute | solution.py:392
  9.3 11.0 %key_value.1 = (bf16[1024,5376]{1,0:T(8,128)(2,1)S(1)}, bf16[1024,256]{1,0:T(8,128)(2,1)S(1)}, bf16[64,5376]{1,0:T(8,128)(2,1)S(1)}) custom-call(s32[12]{0:T(128)S(1)} %dynamic-slice_bitcast_fusion.pos_ref, bf16[1024,5376]{1,0:T(8,128)(2,1)} %tok_ref.1, f32[1,5376]{1,0:T(1,128)S(1)} %reshape.16.g_ref, bf16[5376,128]{1,0:T(8,128)(2,1)} %wk_ref.1, ...), custom_call_target="tpu_custom_call" | custom-call | flops 11274289152 | bytes 27262976 | tf_op jit(solution)/shard_map/key_value/pallas_call | solution.py:138
  20.3 1.3 %collective-permute-start.6 = (bf16[1024,256]{1,0:T(8,128)(2,1)S(1)}, bf16[1024,256]{1,0:T(8,128)(2,1)S(1)}, u32[]{:S(2)}, u32[]{:S(2)}) collective-permute-start(bf16[1024,256]{1,0:T(8,128)(2,1)S(1)} %get-tuple-element.51.kv_ref), channel_id=1, source_target_pairs={{0,16},{16,32},{32,48},{48,64},{64,80},{80,96},{96,112},{1,17},{17... | collective-permute-start | bytes 1572872 | tf_op jit(solution)/shard_map/ppermute | solution.py:411
  21.7 6.6 %query.1.q_ref = bf16[1024,256]{1,0:T(8,128)(2,1)S(1)} custom-call(s32[12]{0:T(128)S(1)} %dynamic-slice_bitcast_fusion.pos_ref, bf16[1024,5376]{1,0:T(8,128)(2,1)S(1)} %get-tuple-element.45.normed_ref, bf16[5376,256]{1,0:T(8,128)(2,1)} %w_ref.3, f32[1,128]{1,0:T(1,128)S(1)} %bitcast.4, f32[8192,128]{1,0:T(8,128)} %constant.32.clone.tab_ref), custom_call_target="tpu_custom_call" | custom-call | tf_op jit(solution)/shard_map/query/pallas_call | solution.py:175
  28.4 2.4 %collective-permute-start.3 = (bf16[128,1408]{1,0:T(8,128)(2,1)S(1)}, bf16[128,1408]{1,0:T(8,128)(2,1)S(1)}, u32[]{:S(2)}, u32[]{:S(2)}) collective-permute-start(bf16[128,1408]{1,0:T(8,128)(2,1)S(1)} %collective-permute-done.refs_0_), channel_id=1, source_target_pairs={{0,16},{16,0},{1,17},{17,1},{2,18},{18,2},{3,19},{19,3},{4,20},{20... | collective-permute-start | bytes 1081352 | tf_op jit(solution)/shard_map/ppermute | solution.py:414
  33.8 2.0 %attend.3.refs_0_ = bf16[256,256]{1,0:T(8,128)(2,1)S(1)} custom-call(s32[12]{0:T(128)S(1)} %dynamic-slice_bitcast_fusion.pos_ref, bf16[1024,256]{1,0:T(8,128)(2,1)S(1)} %query.1.q_ref, bf16[1024,256]{1,0:T(8,128)(2,1)S(1)} %get-tuple-element.51.kv_ref, bf16[1024,256]{1,0:T(8,128)(2,1)S(1)} %collective-permute-done.6.got_ref, ...), custom_call_target="tpu_custom_call" | custom-call | tf_op jit(solution)/shard_map/attend/pallas_call | solution.py:235
  35.8 1.1 %collective-permute-start.13 = (bf16[256,256]{1,0:T(8,128)(2,1)S(1)}, bf16[256,256]{1,0:T(8,128)(2,1)S(1)}, u32[]{:S(2)}, u32[]{:S(2)}) collective-permute-start(bf16[256,256]{1,0:T(8,128)(2,1)S(1)} %attend.3.refs_0_), channel_id=1, source_target_pairs={{0,1},{1,2},{2,3},{3,0},{4,5},{5,6},{6,7},{7,4},{8,9},{9,10},{10,1... | collective-permute-start | bytes 393224 | tf_op jit(solution)/shard_map/ppermute | solution.py:392
  36.8 2.2 %collective-permute-start.14 = (bf16[256,256]{1,0:T(8,128)(2,1)S(1)}, bf16[256,256]{1,0:T(8,128)(2,1)S(1)}, u32[]{:S(2)}, u32[]{:S(2)}) collective-permute-start(bf16[256,256]{1,0:T(8,128)(2,1)S(1)} %attend.3.refs_0_), channel_id=1, source_target_pairs={{0,3},{1,0},{2,1},{3,2},{4,7},{5,4},{6,5},{7,6},{8,11},{9,8},{10,9... | collective-permute-start | bytes 393224 | tf_op jit(solution)/shard_map/ppermute | solution.py:392
  39.6 3.0 %attend.4.refs_0_ = bf16[512,256]{1,0:T(8,128)(2,1)S(1)} custom-call(s32[12]{0:T(128)S(1)} %dynamic-slice_bitcast_fusion.pos_ref, bf16[1024,256]{1,0:T(8,128)(2,1)S(1)} %query.1.q_ref, bf16[1024,256]{1,0:T(8,128)(2,1)S(1)} %get-tuple-element.51.kv_ref, bf16[1024,256]{1,0:T(8,128)(2,1)S(1)} %collective-permute-done.6.got_ref, ...), custom_call_target="tpu_custom_call" | custom-call | tf_op jit(solution)/shard_map/attend/pallas_call | solution.py:235
  42.9 2.1 %collective-permute-done.14.refs_2_ = bf16[256,256]{1,0:T(8,128)(2,1)S(1)} collective-permute-done((bf16[256,256]{1,0:T(8,128)(2,1)S(1)}, bf16[256,256]{1,0:T(8,128)(2,1)S(1)}, u32[]{:S(2)}, u32[]{:S(2)}) %collective-permute-start.14) | collective-permute-done | bytes 131104 | tf_op jit(solution)/shard_map/ppermute | solution.py:392
  46.8 1.7 %collective-permute-start.16 = (bf16[128,1408]{1,0:T(8,128)(2,1)S(1)}, bf16[128,1408]{1,0:T(8,128)(2,1)S(1)}, u32[]{:S(2)}, u32[]{:S(2)}) collective-permute-start(bf16[128,1408]{1,0:T(8,128)(2,1)S(1)} %get-tuple-element.60), channel_id=1, source_target_pairs={{0,4},{4,8},{8,12},{12,0},{1,5},{5,9},{9,13},{13,1},{2,6},{6,10},{... | collective-permute-start | bytes 1081352 | tf_op jit(solution)/shard_map/ppermute | solution.py:392
  48.6 1.7 %collective-permute-start.17 = (bf16[128,1408]{1,0:T(8,128)(2,1)S(1)}, bf16[128,1408]{1,0:T(8,128)(2,1)S(1)}, u32[]{:S(2)}, u32[]{:S(2)}) collective-permute-start(bf16[128,1408]{1,0:T(8,128)(2,1)S(1)} %get-tuple-element.61), channel_id=1, source_target_pairs={{0,12},{4,0},{8,4},{12,8},{1,13},{5,1},{9,5},{13,9},{2,14},{6,2},{... | collective-permute-start | bytes 1081352 | tf_op jit(solution)/shard_map/ppermute | solution.py:392
  51.0 2.5 %collective-permute-start.11 = (bf16[512,256]{1,0:T(8,128)(2,1)S(1)}, bf16[512,256]{1,0:T(8,128)(2,1)S(1)}, u32[]{:S(2)}, u32[]{:S(2)}) collective-permute-start(bf16[512,256]{1,0:T(8,128)(2,1)S(1)} %attend.4.refs_0_), channel_id=1, source_target_pairs={{0,3},{1,0},{2,1},{3,2},{4,7},{5,4},{6,5},{7,6},{8,11},{9,8},{10,9... | collective-permute-start | bytes 786440 | tf_op jit(solution)/shard_map/ppermute | solution.py:392
  54.6 1.9 %attend.5.refs_0_ = bf16[256,256]{1,0:T(8,128)(2,1)S(1)} custom-call(s32[12]{0:T(128)S(1)} %dynamic-slice_bitcast_fusion.pos_ref, bf16[1024,256]{1,0:T(8,128)(2,1)S(1)} %query.1.q_ref, bf16[1024,256]{1,0:T(8,128)(2,1)S(1)} %get-tuple-element.51.kv_ref, bf16[1024,256]{1,0:T(8,128)(2,1)S(1)} %collective-permute-done.6.got_ref, ...), custom_call_target="tpu_custom_call" | custom-call | tf_op jit(solution)/shard_map/attend/pallas_call | solution.py:235
  57.6 2.9 %collective-permute-done.10.refs_1_ = bf16[512,256]{1,0:T(8,128)(2,1)S(1)} collective-permute-done((bf16[512,256]{1,0:T(8,128)(2,1)S(1)}, bf16[512,256]{1,0:T(8,128)(2,1)S(1)}, u32[]{:S(2)}, u32[]{:S(2)}) %collective-permute-start.10) | collective-permute-done | bytes 262176 | tf_op jit(solution)/shard_map/ppermute | solution.py:392
  60.5 2.5 %collective-permute-done.11.refs_2_ = bf16[512,256]{1,0:T(8,128)(2,1)S(1)} collective-permute-done((bf16[512,256]{1,0:T(8,128)(2,1)S(1)}, bf16[512,256]{1,0:T(8,128)(2,1)S(1)}, u32[]{:S(2)}, u32[]{:S(2)}) %collective-permute-start.11) | collective-permute-done | bytes 262176 | tf_op jit(solution)/shard_map/ppermute | solution.py:392
  63.1 1.3 %collective-permute-done.12.refs_3_ = bf16[512,256]{1,0:T(8,128)(2,1)S(1)} collective-permute-done((bf16[512,256]{1,0:T(8,128)(2,1)S(1)}, bf16[512,256]{1,0:T(8,128)(2,1)S(1)}, u32[]{:S(2)}, u32[]{:S(2)}) %collective-permute-start.12) | collective-permute-done | bytes 262176 | tf_op jit(solution)/shard_map/ppermute | solution.py:392
  64.4 1.8 %near.1 = (bf16[256,1408]{1,0:T(8,128)(2,1)S(1)}, bf16[256,1408]{1,0:T(8,128)(2,1)S(1)}) custom-call(bf16[512,256]{1,0:T(8,128)(2,1)S(1)} %attend.4.refs_0_, bf16[512,256]{1,0:T(8,128)(2,1)S(1)} %collective-permute-done.10.refs_1_, bf16[512,256]{1,0:T(8,128)(2,1)S(1)} %collective-permute-done.11.refs_2_, ...), custom_call_target="tpu_custom_call" | custom-call | tf_op jit(solution)/shard_map/near/pallas_call | solution.py:322
  66.6 3.0 %collective-permute-start.19 = (bf16[256,1408]{1,0:T(8,128)(2,1)S(1)}, bf16[256,1408]{1,0:T(8,128)(2,1)S(1)}, u32[]{:S(2)}, u32[]{:S(2)}) collective-permute-start(bf16[256,1408]{1,0:T(8,128)(2,1)S(1)} %get-tuple-element.65), channel_id=1, source_target_pairs={{0,12},{4,0},{8,4},{12,8},{1,13},{5,1},{9,5},{13,9},{2,14},{6,2},{... | collective-permute-start | bytes 2162696 | tf_op jit(solution)/shard_map/ppermute | solution.py:392
  69.5 1.1 %collective-permute-start.7 = (bf16[256,256]{1,0:T(8,128)(2,1)S(1)}, bf16[256,256]{1,0:T(8,128)(2,1)S(1)}, u32[]{:S(2)}, u32[]{:S(2)}) collective-permute-start(bf16[256,256]{1,0:T(8,128)(2,1)S(1)} %attend.5.refs_0_), channel_id=1, source_target_pairs={{0,1},{1,2},{2,3},{3,0},{4,5},{5,6},{6,7},{7,4},{8,9},{9,10},{10,1... | collective-permute-start | bytes 393224 | tf_op jit(solution)/shard_map/ppermute | solution.py:392
  70.7 2.1 %collective-permute-start.8 = (bf16[256,256]{1,0:T(8,128)(2,1)S(1)}, bf16[256,256]{1,0:T(8,128)(2,1)S(1)}, u32[]{:S(2)}, u32[]{:S(2)}) collective-permute-start(bf16[256,256]{1,0:T(8,128)(2,1)S(1)} %attend.5.refs_0_), channel_id=1, source_target_pairs={{0,3},{1,0},{2,1},{3,2},{4,7},{5,4},{6,5},{7,6},{8,11},{9,8},{10,9... | collective-permute-start | bytes 393224 | tf_op jit(solution)/shard_map/ppermute | solution.py:392
  73.3 2.4 %collective-permute-done.7.refs_1_ = bf16[256,256]{1,0:T(8,128)(2,1)S(1)} collective-permute-done((bf16[256,256]{1,0:T(8,128)(2,1)S(1)}, bf16[256,256]{1,0:T(8,128)(2,1)S(1)}, u32[]{:S(2)}, u32[]{:S(2)}) %collective-permute-start.7) | collective-permute-done | bytes 131104 | tf_op jit(solution)/shard_map/ppermute | solution.py:392
  75.7 3.5 %collective-permute-done.9.refs_3_ = bf16[256,256]{1,0:T(8,128)(2,1)S(1)} collective-permute-done((bf16[256,256]{1,0:T(8,128)(2,1)S(1)}, bf16[256,256]{1,0:T(8,128)(2,1)S(1)}, u32[]{:S(2)}, u32[]{:S(2)}) %collective-permute-start.9) | collective-permute-done | bytes 131104 | tf_op jit(solution)/shard_map/ppermute | solution.py:392
  80.2 2.1 %collective-permute-done.18.up_ref = bf16[256,1408]{1,0:T(8,128)(2,1)S(1)} collective-permute-done((bf16[256,1408]{1,0:T(8,128)(2,1)S(1)}, bf16[256,1408]{1,0:T(8,128)(2,1)S(1)}, u32[]{:S(2)}, u32[]{:S(2)}) %collective-permute-start.18) | collective-permute-done | bytes 720928 | tf_op jit(solution)/shard_map/ppermute | solution.py:392
  84.3 2.4 %collective-permute-start.21 = (bf16[64,1408]{1,0:T(8,128)(2,1)S(1)}, bf16[64,1408]{1,0:T(8,128)(2,1)S(1)}, u32[]{:S(2)}, u32[]{:S(2)}) collective-permute-start(bf16[64,1408]{1,0:T(8,128)(2,1)S(1)} %get-tuple-element.68), channel_id=1, source_target_pairs={{0,3},{1,0},{2,1},{3,2},{4,7},{5,4},{6,5},{7,6},{8,11},{9,8},{10,9... | collective-permute-start | bytes 540680 | tf_op jit(solution)/shard_map/ppermute | solution.py:392
  86.7 1.2 %collective-permute-start.22 = (bf16[64,1408]{1,0:T(8,128)(2,1)S(1)}, bf16[64,1408]{1,0:T(8,128)(2,1)S(1)}, u32[]{:S(2)}, u32[]{:S(2)}) collective-permute-start(bf16[64,1408]{1,0:T(8,128)(2,1)S(1)} %get-tuple-element.69), channel_id=1, source_target_pairs={{0,2},{1,3},{2,0},{3,1},{4,6},{5,7},{6,4},{7,5},{8,10},{9,11},{10,... | collective-permute-start | bytes 540680 | tf_op jit(solution)/shard_map/ppermute | solution.py:392
  87.9 2.9 %collective-permute-done.20.next_ref = bf16[64,1408]{1,0:T(8,128)(2,1)S(1)} collective-permute-done((bf16[64,1408]{1,0:T(8,128)(2,1)S(1)}, bf16[64,1408]{1,0:T(8,128)(2,1)S(1)}, u32[]{:S(2)}, u32[]{:S(2)}) %collective-permute-start.20) | collective-permute-done | bytes 180256 | tf_op jit(solution)/shard_map/ppermute | solution.py:392
  90.8 2.9 %collective-permute-done.22.far_ref = bf16[64,1408]{1,0:T(8,128)(2,1)S(1)} collective-permute-done((bf16[64,1408]{1,0:T(8,128)(2,1)S(1)}, bf16[64,1408]{1,0:T(8,128)(2,1)S(1)}, u32[]{:S(2)}, u32[]{:S(2)}) %collective-permute-start.22) | collective-permute-done | bytes 180256 | tf_op jit(solution)/shard_map/ppermute | solution.py:392
  93.7 1.9 %finish.1 = bf16[64,5376]{1,0:T(8,128)(2,1)} custom-call(s32[12]{0:T(128)S(1)} %dynamic-slice_bitcast_fusion.pos_ref, f32[64,1408]{1,0:T(8,128)S(1)} %get-tuple-element.66.own_ref, bf16[64,1408]{1,0:T(8,128)(2,1)S(1)} %collective-permute-done.20.next_ref, bf16[64,1408]{1,0:T(8,128)(2,1)S(1)} %collective-permute-done.21.last_ref, ...), custom_call_target="tpu_custom_call" | custom-call | tf_op jit(solution)/shard_map/finish/pallas_call | solution.py:379
  (43 shorter events, 13.8 us)
Async XLA Ops:
  0.0 9.2 %copy-start.5 = (f32[5376]{0:T(1024)S(1)}, f32[5376]{0:T(1024)}, u32[]{:S(2)}) copy-start(f32[5376]{0:T(1024)} %param.14) | copy-start | bytes 64516
  0.0 9.3 %copy-start.4 = (f32[128]{0:T(128)S(1)}, f32[128]{0:T(128)}, u32[]{:S(2)}) copy-start(f32[128]{0:T(128)} %param.19) | copy-start | bytes 1540
  0.7 1.8 %copy-start = (bf16[256,5376]{1,0:T(8,128)(2,1)S(1)}, bf16[256,5376]{1,0:T(8,128)(2,1)}, u32[]{:S(2)}) copy-start(bf16[256,5376]{1,0:T(8,128)(2,1)} %w_ref.2) | copy-start | bytes 8257540
  3.2 25.2 %collective-permute-start = (bf16[128,1408]{1,0:T(8,128)(2,1)S(1)}, bf16[128,1408]{1,0:T(8,128)(2,1)S(1)}, u32[]{:S(2)}, u32[]{:S(2)}) collective-permute-start(bf16[128,1408]{1,0:T(8,128)(2,1)S(1)} %get-tuple-element.42), channel_id=1, source_target_pairs={{0,1},{1,2},{2,3},{3,0},{4,5},{5,6},{6,7},{7,4},{8,9},{9,10},{10,1... | collective-permute-start | bytes 1081352 | tf_op jit(solution)/shard_map/ppermute | solution.py:392
  5.2 23.1 %collective-permute-start.1 = (bf16[128,1408]{1,0:T(8,128)(2,1)S(1)}, bf16[128,1408]{1,0:T(8,128)(2,1)S(1)}, u32[]{:S(2)}, u32[]{:S(2)}) collective-permute-start(bf16[128,1408]{1,0:T(8,128)(2,1)S(1)} %get-tuple-element.43), channel_id=1, source_target_pairs={{0,3},{1,0},{2,1},{3,2},{4,7},{5,4},{6,5},{7,6},{8,11},{9,8},{10,9... | collective-permute-start | bytes 1081352 | tf_op jit(solution)/shard_map/ppermute | solution.py:392
  7.4 20.9 %collective-permute-start.2 = (bf16[128,1408]{1,0:T(8,128)(2,1)S(1)}, bf16[128,1408]{1,0:T(8,128)(2,1)S(1)}, u32[]{:S(2)}, u32[]{:S(2)}) collective-permute-start(bf16[128,1408]{1,0:T(8,128)(2,1)S(1)} %get-tuple-element.44), channel_id=1, source_target_pairs={{0,2},{1,3},{2,0},{3,1},{4,6},{5,7},{6,4},{7,5},{8,10},{9,11},{10,... | collective-permute-start | bytes 1081352 | tf_op jit(solution)/shard_map/ppermute | solution.py:392
  9.3 12.4 %copy-start.3 = (f32[128]{0:T(128)S(1)}, f32[128]{0:T(128)}, u32[]{:S(2)}) copy-start(f32[128]{0:T(128)} %param.18) | copy-start | bytes 1540
  20.3 13.4 %collective-permute-start.6 = (bf16[1024,256]{1,0:T(8,128)(2,1)S(1)}, bf16[1024,256]{1,0:T(8,128)(2,1)S(1)}, u32[]{:S(2)}, u32[]{:S(2)}) collective-permute-start(bf16[1024,256]{1,0:T(8,128)(2,1)S(1)} %get-tuple-element.51.kv_ref), channel_id=1, source_target_pairs={{0,16},{16,32},{32,48},{48,64},{64,80},{80,96},{96,112},{1,17},{17... | collective-permute-start | bytes 1572872 | tf_op jit(solution)/shard_map/ppermute | solution.py:411
  28.3 5.5 %copy-start.1 = (bf16[1024,128]{1,0:T(8,128)(2,1)S(1)}, bf16[1024,128]{1,0:T(8,128)(2,1)}, u32[]{:S(2)}) copy-start(bf16[1024,128]{1,0:T(8,128)(2,1)} %pk_ref.5) | copy-start | bytes 786436
  28.3 5.5 %copy-start.2 = (bf16[1024,128]{1,0:T(8,128)(2,1)S(1)}, bf16[1024,128]{1,0:T(8,128)(2,1)}, u32[]{:S(2)}) copy-start(bf16[1024,128]{1,0:T(8,128)(2,1)} %pv_ref.5) | copy-start | bytes 786436
  28.4 3.7 %collective-permute-start.3 = (bf16[128,1408]{1,0:T(8,128)(2,1)S(1)}, bf16[128,1408]{1,0:T(8,128)(2,1)S(1)}, u32[]{:S(2)}, u32[]{:S(2)}) collective-permute-start(bf16[128,1408]{1,0:T(8,128)(2,1)S(1)} %collective-permute-done.refs_0_), channel_id=1, source_target_pairs={{0,16},{16,0},{1,17},{17,1},{2,18},{18,2},{3,19},{19,3},{4,20},{20... | collective-permute-start | bytes 1081352 | tf_op jit(solution)/shard_map/ppermute | solution.py:414
  30.7 1.8 %collective-permute-start.4 = (bf16[128,1408]{1,0:T(8,128)(2,1)S(1)}, bf16[128,1408]{1,0:T(8,128)(2,1)S(1)}, u32[]{:S(2)}, u32[]{:S(2)}) collective-permute-start(bf16[128,1408]{1,0:T(8,128)(2,1)S(1)} %collective-permute-done.1.refs_1_), channel_id=1, source_target_pairs={{0,16},{16,0},{1,17},{17,1},{2,18},{18,2},{3,19},{19,3},{4,20},{20... | collective-permute-start | bytes 1081352 | tf_op jit(solution)/shard_map/ppermute | solution.py:414
  30.8 2.2 %collective-permute-start.5 = (bf16[128,1408]{1,0:T(8,128)(2,1)S(1)}, bf16[128,1408]{1,0:T(8,128)(2,1)S(1)}, u32[]{:S(2)}, u32[]{:S(2)}) collective-permute-start(bf16[128,1408]{1,0:T(8,128)(2,1)S(1)} %collective-permute-done.2.refs_2_), channel_id=1, source_target_pairs={{0,16},{16,0},{1,17},{17,1},{2,18},{18,2},{3,19},{19,3},{4,20},{20... | collective-permute-start | bytes 1081352 | tf_op jit(solution)/shard_map/ppermute | solution.py:414
  35.8 7.1 %collective-permute-start.13 = (bf16[256,256]{1,0:T(8,128)(2,1)S(1)}, bf16[256,256]{1,0:T(8,128)(2,1)S(1)}, u32[]{:S(2)}, u32[]{:S(2)}) collective-permute-start(bf16[256,256]{1,0:T(8,128)(2,1)S(1)} %attend.3.refs_0_), channel_id=1, source_target_pairs={{0,1},{1,2},{2,3},{3,0},{4,5},{5,6},{6,7},{7,4},{8,9},{9,10},{10,1... | collective-permute-start | bytes 393224 | tf_op jit(solution)/shard_map/ppermute | solution.py:392
  36.8 8.1 %collective-permute-start.14 = (bf16[256,256]{1,0:T(8,128)(2,1)S(1)}, bf16[256,256]{1,0:T(8,128)(2,1)S(1)}, u32[]{:S(2)}, u32[]{:S(2)}) collective-permute-start(bf16[256,256]{1,0:T(8,128)(2,1)S(1)} %attend.3.refs_0_), channel_id=1, source_target_pairs={{0,3},{1,0},{2,1},{3,2},{4,7},{5,4},{6,5},{7,6},{8,11},{9,8},{10,9... | collective-permute-start | bytes 393224 | tf_op jit(solution)/shard_map/ppermute | solution.py:392
  39.1 6.8 %collective-permute-start.15 = (bf16[256,256]{1,0:T(8,128)(2,1)S(1)}, bf16[256,256]{1,0:T(8,128)(2,1)S(1)}, u32[]{:S(2)}, u32[]{:S(2)}) collective-permute-start(bf16[256,256]{1,0:T(8,128)(2,1)S(1)} %attend.3.refs_0_), channel_id=1, source_target_pairs={{0,2},{1,3},{2,0},{3,1},{4,6},{5,7},{6,4},{7,5},{8,10},{9,11},{10,... | collective-permute-start | bytes 393224 | tf_op jit(solution)/shard_map/ppermute | solution.py:392
  46.8 10.8 %collective-permute-start.16 = (bf16[128,1408]{1,0:T(8,128)(2,1)S(1)}, bf16[128,1408]{1,0:T(8,128)(2,1)S(1)}, u32[]{:S(2)}, u32[]{:S(2)}) collective-permute-start(bf16[128,1408]{1,0:T(8,128)(2,1)S(1)} %get-tuple-element.60), channel_id=1, source_target_pairs={{0,4},{4,8},{8,12},{12,0},{1,5},{5,9},{9,13},{13,1},{2,6},{6,10},{... | collective-permute-start | bytes 1081352 | tf_op jit(solution)/shard_map/ppermute | solution.py:392
  48.6 9.0 %collective-permute-start.17 = (bf16[128,1408]{1,0:T(8,128)(2,1)S(1)}, bf16[128,1408]{1,0:T(8,128)(2,1)S(1)}, u32[]{:S(2)}, u32[]{:S(2)}) collective-permute-start(bf16[128,1408]{1,0:T(8,128)(2,1)S(1)} %get-tuple-element.61), channel_id=1, source_target_pairs={{0,12},{4,0},{8,4},{12,8},{1,13},{5,1},{9,5},{13,9},{2,14},{6,2},{... | collective-permute-start | bytes 1081352 | tf_op jit(solution)/shard_map/ppermute | solution.py:392
  50.3 10.2 %collective-permute-start.10 = (bf16[512,256]{1,0:T(8,128)(2,1)S(1)}, bf16[512,256]{1,0:T(8,128)(2,1)S(1)}, u32[]{:S(2)}, u32[]{:S(2)}) collective-permute-start(bf16[512,256]{1,0:T(8,128)(2,1)S(1)} %attend.4.refs_0_), channel_id=1, source_target_pairs={{0,1},{1,2},{2,3},{3,0},{4,5},{5,6},{6,7},{7,4},{8,9},{9,10},{10,1... | collective-permute-start | bytes 786440 | tf_op jit(solution)/shard_map/ppermute | solution.py:392
  51.0 12.1 %collective-permute-start.11 = (bf16[512,256]{1,0:T(8,128)(2,1)S(1)}, bf16[512,256]{1,0:T(8,128)(2,1)S(1)}, u32[]{:S(2)}, u32[]{:S(2)}) collective-permute-start(bf16[512,256]{1,0:T(8,128)(2,1)S(1)} %attend.4.refs_0_), channel_id=1, source_target_pairs={{0,3},{1,0},{2,1},{3,2},{4,7},{5,4},{6,5},{7,6},{8,11},{9,8},{10,9... | collective-permute-start | bytes 786440 | tf_op jit(solution)/shard_map/ppermute | solution.py:392
  53.5 10.9 %collective-permute-start.12 = (bf16[512,256]{1,0:T(8,128)(2,1)S(1)}, bf16[512,256]{1,0:T(8,128)(2,1)S(1)}, u32[]{:S(2)}, u32[]{:S(2)}) collective-permute-start(bf16[512,256]{1,0:T(8,128)(2,1)S(1)} %attend.4.refs_0_), channel_id=1, source_target_pairs={{0,2},{1,3},{2,0},{3,1},{4,6},{5,7},{6,4},{7,5},{8,10},{9,11},{10,... | collective-permute-start | bytes 786440 | tf_op jit(solution)/shard_map/ppermute | solution.py:392
  66.2 16.1 %collective-permute-start.18 = (bf16[256,1408]{1,0:T(8,128)(2,1)S(1)}, bf16[256,1408]{1,0:T(8,128)(2,1)S(1)}, u32[]{:S(2)}, u32[]{:S(2)}) collective-permute-start(bf16[256,1408]{1,0:T(8,128)(2,1)S(1)} %get-tuple-element.64), channel_id=1, source_target_pairs={{0,4},{4,8},{8,12},{12,0},{1,5},{5,9},{9,13},{13,1},{2,6},{6,10},{... | collective-permute-start | bytes 2162696 | tf_op jit(solution)/shard_map/ppermute | solution.py:392
  66.6 21.3 %copy-start.6 = (f32[5376]{0:T(1024)S(1)}, f32[5376]{0:T(1024)}, u32[]{:S(2)}) copy-start(f32[5376]{0:T(1024)} %param.23) | copy-start | bytes 64516
  66.6 15.8 %collective-permute-start.19 = (bf16[256,1408]{1,0:T(8,128)(2,1)S(1)}, bf16[256,1408]{1,0:T(8,128)(2,1)S(1)}, u32[]{:S(2)}, u32[]{:S(2)}) collective-permute-start(bf16[256,1408]{1,0:T(8,128)(2,1)S(1)} %get-tuple-element.65), channel_id=1, source_target_pairs={{0,12},{4,0},{8,4},{12,8},{1,13},{5,1},{9,5},{13,9},{2,14},{6,2},{... | collective-permute-start | bytes 2162696 | tf_op jit(solution)/shard_map/ppermute | solution.py:392
  69.5 6.2 %collective-permute-start.7 = (bf16[256,256]{1,0:T(8,128)(2,1)S(1)}, bf16[256,256]{1,0:T(8,128)(2,1)S(1)}, u32[]{:S(2)}, u32[]{:S(2)}) collective-permute-start(bf16[256,256]{1,0:T(8,128)(2,1)S(1)} %attend.5.refs_0_), channel_id=1, source_target_pairs={{0,1},{1,2},{2,3},{3,0},{4,5},{5,6},{6,7},{7,4},{8,9},{9,10},{10,1... | collective-permute-start | bytes 393224 | tf_op jit(solution)/shard_map/ppermute | solution.py:392
  70.7 5.0 %collective-permute-start.8 = (bf16[256,256]{1,0:T(8,128)(2,1)S(1)}, bf16[256,256]{1,0:T(8,128)(2,1)S(1)}, u32[]{:S(2)}, u32[]{:S(2)}) collective-permute-start(bf16[256,256]{1,0:T(8,128)(2,1)S(1)} %attend.5.refs_0_), channel_id=1, source_target_pairs={{0,3},{1,0},{2,1},{3,2},{4,7},{5,4},{6,5},{7,6},{8,11},{9,8},{10,9... | collective-permute-start | bytes 393224 | tf_op jit(solution)/shard_map/ppermute | solution.py:392
  72.8 6.5 %collective-permute-start.9 = (bf16[256,256]{1,0:T(8,128)(2,1)S(1)}, bf16[256,256]{1,0:T(8,128)(2,1)S(1)}, u32[]{:S(2)}, u32[]{:S(2)}) collective-permute-start(bf16[256,256]{1,0:T(8,128)(2,1)S(1)} %attend.5.refs_0_), channel_id=1, source_target_pairs={{0,2},{1,3},{2,0},{3,1},{4,6},{5,7},{6,4},{7,5},{8,10},{9,11},{10,... | collective-permute-start | bytes 393224 | tf_op jit(solution)/shard_map/ppermute | solution.py:392
  83.3 7.4 %collective-permute-start.20 = (bf16[64,1408]{1,0:T(8,128)(2,1)S(1)}, bf16[64,1408]{1,0:T(8,128)(2,1)S(1)}, u32[]{:S(2)}, u32[]{:S(2)}) collective-permute-start(bf16[64,1408]{1,0:T(8,128)(2,1)S(1)} %get-tuple-element.67), channel_id=1, source_target_pairs={{0,1},{1,2},{2,3},{3,0},{4,5},{5,6},{6,7},{7,4},{8,9},{9,10},{10,1... | collective-permute-start | bytes 540680 | tf_op jit(solution)/shard_map/ppermute | solution.py:392
  84.3 6.5 %collective-permute-start.21 = (bf16[64,1408]{1,0:T(8,128)(2,1)S(1)}, bf16[64,1408]{1,0:T(8,128)(2,1)S(1)}, u32[]{:S(2)}, u32[]{:S(2)}) collective-permute-start(bf16[64,1408]{1,0:T(8,128)(2,1)S(1)} %get-tuple-element.68), channel_id=1, source_target_pairs={{0,3},{1,0},{2,1},{3,2},{4,7},{5,4},{6,5},{7,6},{8,11},{9,8},{10,9... | collective-permute-start | bytes 540680 | tf_op jit(solution)/shard_map/ppermute | solution.py:392
  86.7 7.0 %collective-permute-start.22 = (bf16[64,1408]{1,0:T(8,128)(2,1)S(1)}, bf16[64,1408]{1,0:T(8,128)(2,1)S(1)}, u32[]{:S(2)}, u32[]{:S(2)}) collective-permute-start(bf16[64,1408]{1,0:T(8,128)(2,1)S(1)} %get-tuple-element.69), channel_id=1, source_target_pairs={{0,2},{1,3},{2,0},{3,1},{4,6},{5,7},{6,4},{7,5},{8,10},{9,11},{10,... | collective-permute-start | bytes 540680 | tf_op jit(solution)/shard_map/ppermute | solution.py:392

commit v5 on v4

--- a/solution.py
+++ b/solution.py
@@ -171,7 +171,7 @@
 
 
 def query(pos, normed, wq, gain, table):
-    wq, table = in_hbm(wq, table)
+    (table,) = in_hbm(table)
     return pl.pallas_call(
         query_kernel,
         grid_spec=pltpu.PrefetchScalarGridSpec(
@@ -251,25 +251,33 @@
     return pl.multiple_of((number * 21 // 2) * 128, 128)
 
 
-def pick_kernel(pos_ref, w_ref, own_ref, next_ref, last_ref, far_ref):
+def pick_kernel(pos_ref, w_ref, own_ref, next_ref, last_ref, far_ref, sems):
     z = pos_ref[1]
     rows = pl.ds(pl.multiple_of(pos_ref[2] * 128, 128), 128)
-    for shift, ref in ((1, next_ref), (3, last_ref), (2, far_ref)):
-        ref[...] = w_ref[rows, pl.ds(quarter_start((z + shift) % 4), QUARTER)]
-    own_ref[...] = w_ref[:, pl.ds(quarter_start(z), QUARTER)]
+    copies = []
+    for i, (shift, ref) in enumerate(((1, next_ref), (3, last_ref), (2, far_ref))):
+        cols = pl.ds(quarter_start((z + shift) % 4), QUARTER)
+        copies.append(pltpu.make_async_copy(w_ref.at[rows, cols], ref, sems.at[i]))
+    cols = pl.ds(quarter_start(z), QUARTER)
+    copies.append(pltpu.make_async_copy(w_ref.at[:, cols], own_ref, sems.at[3]))
+    for copy in copies:
+        copy.start()
+    for copy in copies:
+        copy.wait()
 
 
 def pick(pos, w_out):
     part = jax.ShapeDtypeStruct((128, QUARTER), BF16)
     return pl.pallas_call(
         pick_kernel,
-        in_specs=[SMEM, VMEM],
+        in_specs=[SMEM, ANY],
         out_specs=[VMEM] * 4,
         out_shape=[jax.ShapeDtypeStruct((256, QUARTER), BF16), part, part, part],
+        scratch_shapes=[pltpu.SemaphoreType.DMA((4,))],
         compiler_params=pltpu.CompilerParams(vmem_limit_bytes=16 << 20),
         cost_estimate=SMALL,
         name="pick",
-    )(pos, w_out)
+    )(pos, *in_hbm(w_out))
 
 
 def join_kernel(pos_ref, *refs):
@@ -410,17 +418,18 @@
     )
     got = lax.ppermute(kv, ("y", "c"), [(i, i + 1) for i in range(7)])
     q = query(pos, normed, w_query, query_gain, table)
-    *lines, q = lax.optimization_barrier((*lines, q))
+    q, *lines = lax.optimization_barrier((q, *lines))
     swapped = [lax.ppermute(part, "c", [(0, 1), (1, 0)]) for part in lines]
-    weights = [own_w, join(pos, lines, swapped)]
-
-    pos, weights[1] = lax.optimization_barrier((pos, weights[1]))
+    pos, *swapped = lax.optimization_barrier((pos, *swapped))
+
     far = attend(0, 2, pos, q, kv, got, prior_key, prior_value)
     far_heads = [far, *from_line([far] * 3)]
     pos, _ = lax.optimization_barrier((pos, far))
     near = attend(2, 4, pos, q, kv, got, prior_key, prior_value)
     near_heads = [near, *from_line([near] * 3)]
     *far_heads, _ = lax.optimization_barrier((*far_heads, near))
+    last_pos, _ = lax.optimization_barrier((pos, near))
+    weights = [own_w, join(last_pos, lines, swapped)]
 
     half = jax.ShapeDtypeStruct((HALF, QUARTER), BF16)
     full = jax.ShapeDtypeStruct((256, QUARTER), BF16)

time: 95.9 us -> 94.1 us (0.981)
  local copies, waits for them, and re-layouts: 2.54 us -> 0.77 us
    unnamed x14, local copies, waits for them, and re-layouts: 1.81 us -> 0.04 us
    pallas_call x1, Pallas kernels: 0.69 us -> 2.04 us  [pick(): pl.pallas_call(pick_kernel, in_specs=[SMEM, ANY], out_specs=[VMEM] * 4, o...]
  transfers between devices with their start and end apart: 23 -> 23, of which waited for: 15 -> 14; matrix products, arithmetic and copies ran while one was open for 0% -> 0% of each run, Pallas kernels for 25% -> 25%
where the time goes in v5:
time: 94.1 us; the launch traced here: 93.8 us
  starting transfers between devices  33.5 us (36%)
  Pallas kernels  33.2 us (35%)
  waiting for transfers between devices  26.1 us (28%)
    ppermute x19, starting transfers between devices, shift_by(): return lax.ppermute(array, axis, [(i, (i + steps) % 4) for i in range(4)])  29.3 us
    ppermute x19, waiting for transfers between devices, shift_by(): return lax.ppermute(array, axis, [(i, (i + steps) % 4) for i in range(4)])  24.3 us
    pallas_call x1, Pallas kernels, key_value(): pl.pallas_call(key_value_kernel, grid_spec=pltpu.PrefetchScalarGridSpec(n...  11.3 us
    pallas_call x3, Pallas kernels, attend(): pl.pallas_call(functools.partial(attend_kernel, first_part), in_specs=[pl...  6.86 us
    pallas_call x1, Pallas kernels, query(): pl.pallas_call(query_kernel, grid_spec=pltpu.PrefetchScalarGridSpec(num_s...  5.69 us
    pallas_call x3, Pallas kernels, multiply(): pl.pallas_call(kernel, in_specs=[VMEM] * (6 + len(relays)), out_specs=jax...  3.77 us
    ppermute x3, starting transfers between devices, per_device(): swapped = [lax.ppermute(part, 'c', [(0, 1), (1, 0)]) for part in lines]  2.87 us
    pallas_call x1, Pallas kernels, pick(): pl.pallas_call(pick_kernel, in_specs=[SMEM, ANY], out_specs=[VMEM] * 4, o...  2.04 us
  transfers between devices with their start and end apart: 23, of which 14 were waited for; matrix products, arithmetic and copies ran while one was open for 0% of the time, Pallas kernels for 25%

profile of v5, /device:TPU:0, one launch (start us, length us, event | category | flops | bytes accessed | tf_op | source)
XLA Modules:
  0.0 93.8 jit_solution(2735183583825649780)
XLA Ops:
  0.7 2.0 %pick.1 = (bf16[256,1408]{1,0:T(8,128)(2,1)S(1)}, bf16[128,1408]{1,0:T(8,128)(2,1)S(1)}, bf16[128,1408]{1,0:T(8,128)(2,1)S(1)}, bf16[128,1408]{1,0:T(8,128)(2,1)S(1)}) custom-call(s32[12]{0:T(128)S(1)} %dynamic-slice_bitcast_fusion.pos_ref, bf16[256,5376]{1,0:T(8,128)(2,1)} %w_ref.2), custom_call_target="tpu_custom_call" | custom-call | tf_op jit(solution)/shard_map/pick/pallas_call | solution.py:271
  2.8 2.1 %collective-permute-start = (bf16[128,1408]{1,0:T(8,128)(2,1)S(1)}, bf16[128,1408]{1,0:T(8,128)(2,1)S(1)}, u32[]{:S(2)}, u32[]{:S(2)}) collective-permute-start(bf16[128,1408]{1,0:T(8,128)(2,1)S(1)} %get-tuple-element.45), channel_id=1, source_target_pairs={{0,1},{1,2},{2,3},{3,0},{4,5},{5,6},{6,7},{7,4},{8,9},{9,10},{10,1... | collective-permute-start | bytes 1081352 | tf_op jit(solution)/shard_map/ppermute | solution.py:400
  4.8 2.2 %collective-permute-start.1 = (bf16[128,1408]{1,0:T(8,128)(2,1)S(1)}, bf16[128,1408]{1,0:T(8,128)(2,1)S(1)}, u32[]{:S(2)}, u32[]{:S(2)}) collective-permute-start(bf16[128,1408]{1,0:T(8,128)(2,1)S(1)} %get-tuple-element.46), channel_id=1, source_target_pairs={{0,3},{1,0},{2,1},{3,2},{4,7},{5,4},{6,5},{7,6},{8,11},{9,8},{10,9... | collective-permute-start | bytes 1081352 | tf_op jit(solution)/shard_map/ppermute | solution.py:400
  7.0 1.8 %collective-permute-start.2 = (bf16[128,1408]{1,0:T(8,128)(2,1)S(1)}, bf16[128,1408]{1,0:T(8,128)(2,1)S(1)}, u32[]{:S(2)}, u32[]{:S(2)}) collective-permute-start(bf16[128,1408]{1,0:T(8,128)(2,1)S(1)} %get-tuple-element.47), channel_id=1, source_target_pairs={{0,2},{1,3},{2,0},{3,1},{4,6},{5,7},{6,4},{7,5},{8,10},{9,11},{10,... | collective-permute-start | bytes 1081352 | tf_op jit(solution)/shard_map/ppermute | solution.py:400
  8.9 11.3 %key_value.1 = (bf16[1024,5376]{1,0:T(8,128)(2,1)S(1)}, bf16[1024,256]{1,0:T(8,128)(2,1)S(1)}, bf16[64,5376]{1,0:T(8,128)(2,1)S(1)}) custom-call(s32[12]{0:T(128)S(1)} %dynamic-slice_bitcast_fusion.pos_ref, bf16[1024,5376]{1,0:T(8,128)(2,1)} %tok_ref.1, f32[1,5376]{1,0:T(1,128)S(1)} %reshape.16.g_ref, bf16[5376,128]{1,0:T(8,128)(2,1)} %wk_ref.1, ...), custom_call_target="tpu_custom_call" | custom-call | flops 11274289152 | bytes 27262976 | tf_op jit(solution)/shard_map/key_value/pallas_call | solution.py:138
  20.2 1.3 %collective-permute-start.6 = (bf16[1024,256]{1,0:T(8,128)(2,1)S(1)}, bf16[1024,256]{1,0:T(8,128)(2,1)S(1)}, u32[]{:S(2)}, u32[]{:S(2)}) collective-permute-start(bf16[1024,256]{1,0:T(8,128)(2,1)S(1)} %get-tuple-element.53.kv_ref), channel_id=1, source_target_pairs={{0,16},{16,32},{32,48},{48,64},{64,80},{80,96},{96,112},{1,17},{17... | collective-permute-start | bytes 1572872 | tf_op jit(solution)/shard_map/ppermute | solution.py:419
  21.5 5.7 %query.1.q_ref = bf16[1024,256]{1,0:T(8,128)(2,1)S(1)} custom-call(s32[12]{0:T(128)S(1)} %dynamic-slice_bitcast_fusion.pos_ref, bf16[1024,5376]{1,0:T(8,128)(2,1)S(1)} %get-tuple-element.44.normed_ref, bf16[5376,256]{1,0:T(8,128)(2,1)S(1)} %copy-done, f32[1,128]{1,0:T(1,128)S(1)} %bitcast.4, f32[8192,128]{1,0:T(8,128)} %constant.32.clone.tab_ref), custom_call_target="tpu_custom_call" | custom-call | tf_op jit(solution)/shard_map/query/pallas_call | solution.py:175
  27.3 2.4 %collective-permute-start.3 = (bf16[128,1408]{1,0:T(8,128)(2,1)S(1)}, bf16[128,1408]{1,0:T(8,128)(2,1)S(1)}, u32[]{:S(2)}, u32[]{:S(2)}) collective-permute-start(bf16[128,1408]{1,0:T(8,128)(2,1)S(1)} %collective-permute-done.refs_0_), channel_id=1, source_target_pairs={{0,16},{16,0},{1,17},{17,1},{2,18},{18,2},{3,19},{19,3},{4,20},{20... | collective-permute-start | bytes 1081352 | tf_op jit(solution)/shard_map/ppermute | solution.py:422
  32.0 1.9 %attend.3.refs_0_ = bf16[256,256]{1,0:T(8,128)(2,1)S(1)} custom-call(s32[12]{0:T(128)S(1)} %dynamic-slice_bitcast_fusion.pos_ref, bf16[1024,256]{1,0:T(8,128)(2,1)S(1)} %query.1.q_ref, bf16[1024,256]{1,0:T(8,128)(2,1)S(1)} %get-tuple-element.53.kv_ref, bf16[1024,256]{1,0:T(8,128)(2,1)S(1)} %collective-permute-done.6.got_ref, ...), custom_call_target="tpu_custom_call" | custom-call | tf_op jit(solution)/shard_map/attend/pallas_call | solution.py:235
  33.9 1.1 %collective-permute-start.13 = (bf16[256,256]{1,0:T(8,128)(2,1)S(1)}, bf16[256,256]{1,0:T(8,128)(2,1)S(1)}, u32[]{:S(2)}, u32[]{:S(2)}) collective-permute-start(bf16[256,256]{1,0:T(8,128)(2,1)S(1)} %attend.3.refs_0_), channel_id=1, source_target_pairs={{0,1},{1,2},{2,3},{3,0},{4,5},{5,6},{6,7},{7,4},{8,9},{9,10},{10,1... | collective-permute-start | bytes 393224 | tf_op jit(solution)/shard_map/ppermute | solution.py:400
  35.0 2.2 %collective-permute-start.14 = (bf16[256,256]{1,0:T(8,128)(2,1)S(1)}, bf16[256,256]{1,0:T(8,128)(2,1)S(1)}, u32[]{:S(2)}, u32[]{:S(2)}) collective-permute-start(bf16[256,256]{1,0:T(8,128)(2,1)S(1)} %attend.3.refs_0_), channel_id=1, source_target_pairs={{0,3},{1,0},{2,1},{3,2},{4,7},{5,4},{6,5},{7,6},{8,11},{9,8},{10,9... | collective-permute-start | bytes 393224 | tf_op jit(solution)/shard_map/ppermute | solution.py:400
  37.8 3.0 %attend.4.refs_0_ = bf16[512,256]{1,0:T(8,128)(2,1)S(1)} custom-call(s32[12]{0:T(128)S(1)} %dynamic-slice_bitcast_fusion.pos_ref, bf16[1024,256]{1,0:T(8,128)(2,1)S(1)} %query.1.q_ref, bf16[1024,256]{1,0:T(8,128)(2,1)S(1)} %get-tuple-element.53.kv_ref, bf16[1024,256]{1,0:T(8,128)(2,1)S(1)} %collective-permute-done.6.got_ref, ...), custom_call_target="tpu_custom_call" | custom-call | tf_op jit(solution)/shard_map/attend/pallas_call | solution.py:235
  41.5 1.7 %collective-permute-done.14.refs_2_ = bf16[256,256]{1,0:T(8,128)(2,1)S(1)} collective-permute-done((bf16[256,256]{1,0:T(8,128)(2,1)S(1)}, bf16[256,256]{1,0:T(8,128)(2,1)S(1)}, u32[]{:S(2)}, u32[]{:S(2)}) %collective-permute-start.14) | collective-permute-done | bytes 131104 | tf_op jit(solution)/shard_map/ppermute | solution.py:400
  45.0 1.7 %collective-permute-start.16 = (bf16[128,1408]{1,0:T(8,128)(2,1)S(1)}, bf16[128,1408]{1,0:T(8,128)(2,1)S(1)}, u32[]{:S(2)}, u32[]{:S(2)}) collective-permute-start(bf16[128,1408]{1,0:T(8,128)(2,1)S(1)} %get-tuple-element.64), channel_id=1, source_target_pairs={{0,4},{4,8},{8,12},{12,0},{1,5},{5,9},{9,13},{13,1},{2,6},{6,10},{... | collective-permute-start | bytes 1081352 | tf_op jit(solution)/shard_map/ppermute | solution.py:400
  46.7 1.7 %collective-permute-start.17 = (bf16[128,1408]{1,0:T(8,128)(2,1)S(1)}, bf16[128,1408]{1,0:T(8,128)(2,1)S(1)}, u32[]{:S(2)}, u32[]{:S(2)}) collective-permute-start(bf16[128,1408]{1,0:T(8,128)(2,1)S(1)} %get-tuple-element.65), channel_id=1, source_target_pairs={{0,12},{4,0},{8,4},{12,8},{1,13},{5,1},{9,5},{13,9},{2,14},{6,2},{... | collective-permute-start | bytes 1081352 | tf_op jit(solution)/shard_map/ppermute | solution.py:400
  49.2 2.5 %collective-permute-start.11 = (bf16[512,256]{1,0:T(8,128)(2,1)S(1)}, bf16[512,256]{1,0:T(8,128)(2,1)S(1)}, u32[]{:S(2)}, u32[]{:S(2)}) collective-permute-start(bf16[512,256]{1,0:T(8,128)(2,1)S(1)} %attend.4.refs_0_), channel_id=1, source_target_pairs={{0,3},{1,0},{2,1},{3,2},{4,7},{5,4},{6,5},{7,6},{8,11},{9,8},{10,9... | collective-permute-start | bytes 786440 | tf_op jit(solution)/shard_map/ppermute | solution.py:400
  52.7 1.9 %attend.5.refs_0_ = bf16[256,256]{1,0:T(8,128)(2,1)S(1)} custom-call(s32[12]{0:T(128)S(1)} %dynamic-slice_bitcast_fusion.pos_ref, bf16[1024,256]{1,0:T(8,128)(2,1)S(1)} %query.1.q_ref, bf16[1024,256]{1,0:T(8,128)(2,1)S(1)} %get-tuple-element.53.kv_ref, bf16[1024,256]{1,0:T(8,128)(2,1)S(1)} %collective-permute-done.6.got_ref, ...), custom_call_target="tpu_custom_call" | custom-call | tf_op jit(solution)/shard_map/attend/pallas_call | solution.py:235
  55.8 2.9 %collective-permute-done.10.refs_1_ = bf16[512,256]{1,0:T(8,128)(2,1)S(1)} collective-permute-done((bf16[512,256]{1,0:T(8,128)(2,1)S(1)}, bf16[512,256]{1,0:T(8,128)(2,1)S(1)}, u32[]{:S(2)}, u32[]{:S(2)}) %collective-permute-start.10) | collective-permute-done | bytes 262176 | tf_op jit(solution)/shard_map/ppermute | solution.py:400
  58.7 2.6 %collective-permute-done.11.refs_2_ = bf16[512,256]{1,0:T(8,128)(2,1)S(1)} collective-permute-done((bf16[512,256]{1,0:T(8,128)(2,1)S(1)}, bf16[512,256]{1,0:T(8,128)(2,1)S(1)}, u32[]{:S(2)}, u32[]{:S(2)}) %collective-permute-start.11) | collective-permute-done | bytes 262176 | tf_op jit(solution)/shard_map/ppermute | solution.py:400
  61.3 1.3 %collective-permute-done.12.refs_3_ = bf16[512,256]{1,0:T(8,128)(2,1)S(1)} collective-permute-done((bf16[512,256]{1,0:T(8,128)(2,1)S(1)}, bf16[512,256]{1,0:T(8,128)(2,1)S(1)}, u32[]{:S(2)}, u32[]{:S(2)}) %collective-permute-start.12) | collective-permute-done | bytes 262176 | tf_op jit(solution)/shard_map/ppermute | solution.py:400
  62.6 1.8 %near.1 = (bf16[256,1408]{1,0:T(8,128)(2,1)S(1)}, bf16[256,1408]{1,0:T(8,128)(2,1)S(1)}) custom-call(bf16[512,256]{1,0:T(8,128)(2,1)S(1)} %attend.4.refs_0_, bf16[512,256]{1,0:T(8,128)(2,1)S(1)} %collective-permute-done.10.refs_1_, bf16[512,256]{1,0:T(8,128)(2,1)S(1)} %collective-permute-done.11.refs_2_, ...), custom_call_target="tpu_custom_call" | custom-call | tf_op jit(solution)/shard_map/near/pallas_call | solution.py:330
  64.8 3.0 %collective-permute-start.19 = (bf16[256,1408]{1,0:T(8,128)(2,1)S(1)}, bf16[256,1408]{1,0:T(8,128)(2,1)S(1)}, u32[]{:S(2)}, u32[]{:S(2)}) collective-permute-start(bf16[256,1408]{1,0:T(8,128)(2,1)S(1)} %get-tuple-element.69), channel_id=1, source_target_pairs={{0,12},{4,0},{8,4},{12,8},{1,13},{5,1},{9,5},{13,9},{2,14},{6,2},{... | collective-permute-start | bytes 2162696 | tf_op jit(solution)/shard_map/ppermute | solution.py:400
  67.7 1.1 %collective-permute-start.7 = (bf16[256,256]{1,0:T(8,128)(2,1)S(1)}, bf16[256,256]{1,0:T(8,128)(2,1)S(1)}, u32[]{:S(2)}, u32[]{:S(2)}) collective-permute-start(bf16[256,256]{1,0:T(8,128)(2,1)S(1)} %attend.5.refs_0_), channel_id=1, source_target_pairs={{0,1},{1,2},{2,3},{3,0},{4,5},{5,6},{6,7},{7,4},{8,9},{9,10},{10,1... | collective-permute-start | bytes 393224 | tf_op jit(solution)/shard_map/ppermute | solution.py:400
  68.9 2.1 %collective-permute-start.8 = (bf16[256,256]{1,0:T(8,128)(2,1)S(1)}, bf16[256,256]{1,0:T(8,128)(2,1)S(1)}, u32[]{:S(2)}, u32[]{:S(2)}) collective-permute-start(bf16[256,256]{1,0:T(8,128)(2,1)S(1)} %attend.5.refs_0_), channel_id=1, source_target_pairs={{0,3},{1,0},{2,1},{3,2},{4,7},{5,4},{6,5},{7,6},{8,11},{9,8},{10,9... | collective-permute-start | bytes 393224 | tf_op jit(solution)/shard_map/ppermute | solution.py:400
  71.5 2.4 %collective-permute-done.7.refs_1_ = bf16[256,256]{1,0:T(8,128)(2,1)S(1)} collective-permute-done((bf16[256,256]{1,0:T(8,128)(2,1)S(1)}, bf16[256,256]{1,0:T(8,128)(2,1)S(1)}, u32[]{:S(2)}, u32[]{:S(2)}) %collective-permute-start.7) | collective-permute-done | bytes 131104 | tf_op jit(solution)/shard_map/ppermute | solution.py:400
  73.9 3.5 %collective-permute-done.9.refs_3_ = bf16[256,256]{1,0:T(8,128)(2,1)S(1)} collective-permute-done((bf16[256,256]{1,0:T(8,128)(2,1)S(1)}, bf16[256,256]{1,0:T(8,128)(2,1)S(1)}, u32[]{:S(2)}, u32[]{:S(2)}) %collective-permute-start.9) | collective-permute-done | bytes 131104 | tf_op jit(solution)/shard_map/ppermute | solution.py:400
  78.4 2.1 %collective-permute-done.18.up_ref = bf16[256,1408]{1,0:T(8,128)(2,1)S(1)} collective-permute-done((bf16[256,1408]{1,0:T(8,128)(2,1)S(1)}, bf16[256,1408]{1,0:T(8,128)(2,1)S(1)}, u32[]{:S(2)}, u32[]{:S(2)}) %collective-permute-start.18) | collective-permute-done | bytes 720928 | tf_op jit(solution)/shard_map/ppermute | solution.py:400
  82.5 2.4 %collective-permute-start.21 = (bf16[64,1408]{1,0:T(8,128)(2,1)S(1)}, bf16[64,1408]{1,0:T(8,128)(2,1)S(1)}, u32[]{:S(2)}, u32[]{:S(2)}) collective-permute-start(bf16[64,1408]{1,0:T(8,128)(2,1)S(1)} %get-tuple-element.72), channel_id=1, source_target_pairs={{0,3},{1,0},{2,1},{3,2},{4,7},{5,4},{6,5},{7,6},{8,11},{9,8},{10,9... | collective-permute-start | bytes 540680 | tf_op jit(solution)/shard_map/ppermute | solution.py:400
  84.9 1.2 %collective-permute-start.22 = (bf16[64,1408]{1,0:T(8,128)(2,1)S(1)}, bf16[64,1408]{1,0:T(8,128)(2,1)S(1)}, u32[]{:S(2)}, u32[]{:S(2)}) collective-permute-start(bf16[64,1408]{1,0:T(8,128)(2,1)S(1)} %get-tuple-element.73), channel_id=1, source_target_pairs={{0,2},{1,3},{2,0},{3,1},{4,6},{5,7},{6,4},{7,5},{8,10},{9,11},{10,... | collective-permute-start | bytes 540680 | tf_op jit(solution)/shard_map/ppermute | solution.py:400
  86.1 2.9 %collective-permute-done.20.next_ref = bf16[64,1408]{1,0:T(8,128)(2,1)S(1)} collective-permute-done((bf16[64,1408]{1,0:T(8,128)(2,1)S(1)}, bf16[64,1408]{1,0:T(8,128)(2,1)S(1)}, u32[]{:S(2)}, u32[]{:S(2)}) %collective-permute-start.20) | collective-permute-done | bytes 180256 | tf_op jit(solution)/shard_map/ppermute | solution.py:400
  89.0 2.9 %collective-permute-done.22.far_ref = bf16[64,1408]{1,0:T(8,128)(2,1)S(1)} collective-permute-done((bf16[64,1408]{1,0:T(8,128)(2,1)S(1)}, bf16[64,1408]{1,0:T(8,128)(2,1)S(1)}, u32[]{:S(2)}, u32[]{:S(2)}) %collective-permute-start.22) | collective-permute-done | bytes 180256 | tf_op jit(solution)/shard_map/ppermute | solution.py:400
  91.9 1.9 %finish.1 = bf16[64,5376]{1,0:T(8,128)(2,1)} custom-call(s32[12]{0:T(128)S(1)} %dynamic-slice_bitcast_fusion.pos_ref, f32[64,1408]{1,0:T(8,128)S(1)} %get-tuple-element.70.own_ref, bf16[64,1408]{1,0:T(8,128)(2,1)S(1)} %collective-permute-done.20.next_ref, bf16[64,1408]{1,0:T(8,128)(2,1)S(1)} %collective-permute-done.21.last_ref, ...), custom_call_target="tpu_custom_call" | custom-call | tf_op jit(solution)/shard_map/finish/pallas_call | solution.py:387
  (43 shorter events, 12.8 us)
Async XLA Ops:
  0.0 8.8 %copy-start.5 = (f32[5376]{0:T(1024)S(1)}, f32[5376]{0:T(1024)}, u32[]{:S(2)}) copy-start(f32[5376]{0:T(1024)} %param.14) | copy-start | bytes 64516
  0.0 8.8 %copy-start.4 = (f32[128]{0:T(128)S(1)}, f32[128]{0:T(128)}, u32[]{:S(2)}) copy-start(f32[128]{0:T(128)} %param.19) | copy-start | bytes 1540
  2.8 24.5 %collective-permute-start = (bf16[128,1408]{1,0:T(8,128)(2,1)S(1)}, bf16[128,1408]{1,0:T(8,128)(2,1)S(1)}, u32[]{:S(2)}, u32[]{:S(2)}) collective-permute-start(bf16[128,1408]{1,0:T(8,128)(2,1)S(1)} %get-tuple-element.45), channel_id=1, source_target_pairs={{0,1},{1,2},{2,3},{3,0},{4,5},{5,6},{6,7},{7,4},{8,9},{9,10},{10,1... | collective-permute-start | bytes 1081352 | tf_op jit(solution)/shard_map/ppermute | solution.py:400
  4.8 22.4 %collective-permute-start.1 = (bf16[128,1408]{1,0:T(8,128)(2,1)S(1)}, bf16[128,1408]{1,0:T(8,128)(2,1)S(1)}, u32[]{:S(2)}, u32[]{:S(2)}) collective-permute-start(bf16[128,1408]{1,0:T(8,128)(2,1)S(1)} %get-tuple-element.46), channel_id=1, source_target_pairs={{0,3},{1,0},{2,1},{3,2},{4,7},{5,4},{6,5},{7,6},{8,11},{9,8},{10,9... | collective-permute-start | bytes 1081352 | tf_op jit(solution)/shard_map/ppermute | solution.py:400
  7.0 20.2 %collective-permute-start.2 = (bf16[128,1408]{1,0:T(8,128)(2,1)S(1)}, bf16[128,1408]{1,0:T(8,128)(2,1)S(1)}, u32[]{:S(2)}, u32[]{:S(2)}) collective-permute-start(bf16[128,1408]{1,0:T(8,128)(2,1)S(1)} %get-tuple-element.47), channel_id=1, source_target_pairs={{0,2},{1,3},{2,0},{3,1},{4,6},{5,7},{6,4},{7,5},{8,10},{9,11},{10,... | collective-permute-start | bytes 1081352 | tf_op jit(solution)/shard_map/ppermute | solution.py:400
  8.8 12.7 %copy-start = (bf16[5376,256]{1,0:T(8,128)(2,1)S(1)}, bf16[5376,256]{1,0:T(8,128)(2,1)}, u32[]{:S(2)}) copy-start(bf16[5376,256]{1,0:T(8,128)(2,1)} %w_ref.3) | copy-start | bytes 8257540
  8.9 12.7 %copy-start.3 = (f32[128]{0:T(128)S(1)}, f32[128]{0:T(128)}, u32[]{:S(2)}) copy-start(f32[128]{0:T(128)} %param.18) | copy-start | bytes 1540
  20.2 11.8 %collective-permute-start.6 = (bf16[1024,256]{1,0:T(8,128)(2,1)S(1)}, bf16[1024,256]{1,0:T(8,128)(2,1)S(1)}, u32[]{:S(2)}, u32[]{:S(2)}) collective-permute-start(bf16[1024,256]{1,0:T(8,128)(2,1)S(1)} %get-tuple-element.53.kv_ref), channel_id=1, source_target_pairs={{0,16},{16,32},{32,48},{48,64},{64,80},{80,96},{96,112},{1,17},{17... | collective-permute-start | bytes 1572872 | tf_op jit(solution)/shard_map/ppermute | solution.py:419
  21.5 10.4 %copy-start.1 = (bf16[1024,128]{1,0:T(8,128)(2,1)S(1)}, bf16[1024,128]{1,0:T(8,128)(2,1)}, u32[]{:S(2)}) copy-start(bf16[1024,128]{1,0:T(8,128)(2,1)} %pk_ref.5) | copy-start | bytes 786436
  21.5 10.4 %copy-start.2 = (bf16[1024,128]{1,0:T(8,128)(2,1)S(1)}, bf16[1024,128]{1,0:T(8,128)(2,1)}, u32[]{:S(2)}) copy-start(bf16[1024,128]{1,0:T(8,128)(2,1)} %pv_ref.5) | copy-start | bytes 786436
  27.3 3.7 %collective-permute-start.3 = (bf16[128,1408]{1,0:T(8,128)(2,1)S(1)}, bf16[128,1408]{1,0:T(8,128)(2,1)S(1)}, u32[]{:S(2)}, u32[]{:S(2)}) collective-permute-start(bf16[128,1408]{1,0:T(8,128)(2,1)S(1)} %collective-permute-done.refs_0_), channel_id=1, source_target_pairs={{0,16},{16,0},{1,17},{17,1},{2,18},{18,2},{3,19},{19,3},{4,20},{20... | collective-permute-start | bytes 1081352 | tf_op jit(solution)/shard_map/ppermute | solution.py:422
  29.6 1.8 %collective-permute-start.4 = (bf16[128,1408]{1,0:T(8,128)(2,1)S(1)}, bf16[128,1408]{1,0:T(8,128)(2,1)S(1)}, u32[]{:S(2)}, u32[]{:S(2)}) collective-permute-start(bf16[128,1408]{1,0:T(8,128)(2,1)S(1)} %collective-permute-done.1.refs_1_), channel_id=1, source_target_pairs={{0,16},{16,0},{1,17},{17,1},{2,18},{18,2},{3,19},{19,3},{4,20},{20... | collective-permute-start | bytes 1081352 | tf_op jit(solution)/shard_map/ppermute | solution.py:422
  29.7 2.2 %collective-permute-start.5 = (bf16[128,1408]{1,0:T(8,128)(2,1)S(1)}, bf16[128,1408]{1,0:T(8,128)(2,1)S(1)}, u32[]{:S(2)}, u32[]{:S(2)}) collective-permute-start(bf16[128,1408]{1,0:T(8,128)(2,1)S(1)} %collective-permute-done.2.refs_2_), channel_id=1, source_target_pairs={{0,16},{16,0},{1,17},{17,1},{2,18},{18,2},{3,19},{19,3},{4,20},{20... | collective-permute-start | bytes 1081352 | tf_op jit(solution)/shard_map/ppermute | solution.py:422
  33.9 7.5 %collective-permute-start.13 = (bf16[256,256]{1,0:T(8,128)(2,1)S(1)}, bf16[256,256]{1,0:T(8,128)(2,1)S(1)}, u32[]{:S(2)}, u32[]{:S(2)}) collective-permute-start(bf16[256,256]{1,0:T(8,128)(2,1)S(1)} %attend.3.refs_0_), channel_id=1, source_target_pairs={{0,1},{1,2},{2,3},{3,0},{4,5},{5,6},{6,7},{7,4},{8,9},{9,10},{10,1... | collective-permute-start | bytes 393224 | tf_op jit(solution)/shard_map/ppermute | solution.py:400
  35.0 8.1 %collective-permute-start.14 = (bf16[256,256]{1,0:T(8,128)(2,1)S(1)}, bf16[256,256]{1,0:T(8,128)(2,1)S(1)}, u32[]{:S(2)}, u32[]{:S(2)}) collective-permute-start(bf16[256,256]{1,0:T(8,128)(2,1)S(1)} %attend.3.refs_0_), channel_id=1, source_target_pairs={{0,3},{1,0},{2,1},{3,2},{4,7},{5,4},{6,5},{7,6},{8,11},{9,8},{10,9... | collective-permute-start | bytes 393224 | tf_op jit(solution)/shard_map/ppermute | solution.py:400
  37.2 6.8 %collective-permute-start.15 = (bf16[256,256]{1,0:T(8,128)(2,1)S(1)}, bf16[256,256]{1,0:T(8,128)(2,1)S(1)}, u32[]{:S(2)}, u32[]{:S(2)}) collective-permute-start(bf16[256,256]{1,0:T(8,128)(2,1)S(1)} %attend.3.refs_0_), channel_id=1, source_target_pairs={{0,2},{1,3},{2,0},{3,1},{4,6},{5,7},{6,4},{7,5},{8,10},{9,11},{10,... | collective-permute-start | bytes 393224 | tf_op jit(solution)/shard_map/ppermute | solution.py:400
  45.0 10.8 %collective-permute-start.16 = (bf16[128,1408]{1,0:T(8,128)(2,1)S(1)}, bf16[128,1408]{1,0:T(8,128)(2,1)S(1)}, u32[]{:S(2)}, u32[]{:S(2)}) collective-permute-start(bf16[128,1408]{1,0:T(8,128)(2,1)S(1)} %get-tuple-element.64), channel_id=1, source_target_pairs={{0,4},{4,8},{8,12},{12,0},{1,5},{5,9},{9,13},{13,1},{2,6},{6,10},{... | collective-permute-start | bytes 1081352 | tf_op jit(solution)/shard_map/ppermute | solution.py:400
  46.7 9.0 %collective-permute-start.17 = (bf16[128,1408]{1,0:T(8,128)(2,1)S(1)}, bf16[128,1408]{1,0:T(8,128)(2,1)S(1)}, u32[]{:S(2)}, u32[]{:S(2)}) collective-permute-start(bf16[128,1408]{1,0:T(8,128)(2,1)S(1)} %get-tuple-element.65), channel_id=1, source_target_pairs={{0,12},{4,0},{8,4},{12,8},{1,13},{5,1},{9,5},{13,9},{2,14},{6,2},{... | collective-permute-start | bytes 1081352 | tf_op jit(solution)/shard_map/ppermute | solution.py:400
  48.5 10.2 %collective-permute-start.10 = (bf16[512,256]{1,0:T(8,128)(2,1)S(1)}, bf16[512,256]{1,0:T(8,128)(2,1)S(1)}, u32[]{:S(2)}, u32[]{:S(2)}) collective-permute-start(bf16[512,256]{1,0:T(8,128)(2,1)S(1)} %attend.4.refs_0_), channel_id=1, source_target_pairs={{0,1},{1,2},{2,3},{3,0},{4,5},{5,6},{6,7},{7,4},{8,9},{9,10},{10,1... | collective-permute-start | bytes 786440 | tf_op jit(solution)/shard_map/ppermute | solution.py:400
  49.2 12.1 %collective-permute-start.11 = (bf16[512,256]{1,0:T(8,128)(2,1)S(1)}, bf16[512,256]{1,0:T(8,128)(2,1)S(1)}, u32[]{:S(2)}, u32[]{:S(2)}) collective-permute-start(bf16[512,256]{1,0:T(8,128)(2,1)S(1)} %attend.4.refs_0_), channel_id=1, source_target_pairs={{0,3},{1,0},{2,1},{3,2},{4,7},{5,4},{6,5},{7,6},{8,11},{9,8},{10,9... | collective-permute-start | bytes 786440 | tf_op jit(solution)/shard_map/ppermute | solution.py:400
  51.7 10.9 %collective-permute-start.12 = (bf16[512,256]{1,0:T(8,128)(2,1)S(1)}, bf16[512,256]{1,0:T(8,128)(2,1)S(1)}, u32[]{:S(2)}, u32[]{:S(2)}) collective-permute-start(bf16[512,256]{1,0:T(8,128)(2,1)S(1)} %attend.4.refs_0_), channel_id=1, source_target_pairs={{0,2},{1,3},{2,0},{3,1},{4,6},{5,7},{6,4},{7,5},{8,10},{9,11},{10,... | collective-permute-start | bytes 786440 | tf_op jit(solution)/shard_map/ppermute | solution.py:400
  64.4 16.2 %collective-permute-start.18 = (bf16[256,1408]{1,0:T(8,128)(2,1)S(1)}, bf16[256,1408]{1,0:T(8,128)(2,1)S(1)}, u32[]{:S(2)}, u32[]{:S(2)}) collective-permute-start(bf16[256,1408]{1,0:T(8,128)(2,1)S(1)} %get-tuple-element.68), channel_id=1, source_target_pairs={{0,4},{4,8},{8,12},{12,0},{1,5},{5,9},{9,13},{13,1},{2,6},{6,10},{... | collective-permute-start | bytes 2162696 | tf_op jit(solution)/shard_map/ppermute | solution.py:400
  64.8 21.3 %copy-start.6 = (f32[5376]{0:T(1024)S(1)}, f32[5376]{0:T(1024)}, u32[]{:S(2)}) copy-start(f32[5376]{0:T(1024)} %param.23) | copy-start | bytes 64516
  64.8 15.8 %collective-permute-start.19 = (bf16[256,1408]{1,0:T(8,128)(2,1)S(1)}, bf16[256,1408]{1,0:T(8,128)(2,1)S(1)}, u32[]{:S(2)}, u32[]{:S(2)}) collective-permute-start(bf16[256,1408]{1,0:T(8,128)(2,1)S(1)} %get-tuple-element.69), channel_id=1, source_target_pairs={{0,12},{4,0},{8,4},{12,8},{1,13},{5,1},{9,5},{13,9},{2,14},{6,2},{... | collective-permute-start | bytes 2162696 | tf_op jit(solution)/shard_map/ppermute | solution.py:400
  67.7 6.2 %collective-permute-start.7 = (bf16[256,256]{1,0:T(8,128)(2,1)S(1)}, bf16[256,256]{1,0:T(8,128)(2,1)S(1)}, u32[]{:S(2)}, u32[]{:S(2)}) collective-permute-start(bf16[256,256]{1,0:T(8,128)(2,1)S(1)} %attend.5.refs_0_), channel_id=1, source_target_pairs={{0,1},{1,2},{2,3},{3,0},{4,5},{5,6},{6,7},{7,4},{8,9},{9,10},{10,1... | collective-permute-start | bytes 393224 | tf_op jit(solution)/shard_map/ppermute | solution.py:400
  68.9 5.0 %collective-permute-start.8 = (bf16[256,256]{1,0:T(8,128)(2,1)S(1)}, bf16[256,256]{1,0:T(8,128)(2,1)S(1)}, u32[]{:S(2)}, u32[]{:S(2)}) collective-permute-start(bf16[256,256]{1,0:T(8,128)(2,1)S(1)} %attend.5.refs_0_), channel_id=1, source_target_pairs={{0,3},{1,0},{2,1},{3,2},{4,7},{5,4},{6,5},{7,6},{8,11},{9,8},{10,9... | collective-permute-start | bytes 393224 | tf_op jit(solution)/shard_map/ppermute | solution.py:400
  71.0 6.5 %collective-permute-start.9 = (bf16[256,256]{1,0:T(8,128)(2,1)S(1)}, bf16[256,256]{1,0:T(8,128)(2,1)S(1)}, u32[]{:S(2)}, u32[]{:S(2)}) collective-permute-start(bf16[256,256]{1,0:T(8,128)(2,1)S(1)} %attend.5.refs_0_), channel_id=1, source_target_pairs={{0,2},{1,3},{2,0},{3,1},{4,6},{5,7},{6,4},{7,5},{8,10},{9,11},{10,... | collective-permute-start | bytes 393224 | tf_op jit(solution)/shard_map/ppermute | solution.py:400
  81.6 7.4 %collective-permute-start.20 = (bf16[64,1408]{1,0:T(8,128)(2,1)S(1)}, bf16[64,1408]{1,0:T(8,128)(2,1)S(1)}, u32[]{:S(2)}, u32[]{:S(2)}) collective-permute-start(bf16[64,1408]{1,0:T(8,128)(2,1)S(1)} %get-tuple-element.71), channel_id=1, source_target_pairs={{0,1},{1,2},{2,3},{3,0},{4,5},{5,6},{6,7},{7,4},{8,9},{9,10},{10,1... | collective-permute-start | bytes 540680 | tf_op jit(solution)/shard_map/ppermute | solution.py:400
  82.5 6.5 %collective-permute-start.21 = (bf16[64,1408]{1,0:T(8,128)(2,1)S(1)}, bf16[64,1408]{1,0:T(8,128)(2,1)S(1)}, u32[]{:S(2)}, u32[]{:S(2)}) collective-permute-start(bf16[64,1408]{1,0:T(8,128)(2,1)S(1)} %get-tuple-element.72), channel_id=1, source_target_pairs={{0,3},{1,0},{2,1},{3,2},{4,7},{5,4},{6,5},{7,6},{8,11},{9,8},{10,9... | collective-permute-start | bytes 540680 | tf_op jit(solution)/shard_map/ppermute | solution.py:400
  84.9 7.0 %collective-permute-start.22 = (bf16[64,1408]{1,0:T(8,128)(2,1)S(1)}, bf16[64,1408]{1,0:T(8,128)(2,1)S(1)}, u32[]{:S(2)}, u32[]{:S(2)}) collective-permute-start(bf16[64,1408]{1,0:T(8,128)(2,1)S(1)} %get-tuple-element.73), channel_id=1, source_target_pairs={{0,2},{1,3},{2,0},{3,1},{4,6},{5,7},{6,4},{7,5},{8,10},{9,11},{10,... | collective-permute-start | bytes 540680 | tf_op jit(solution)/shard_map/ppermute | solution.py:400

commit v6 on v5

--- a/solution.py
+++ b/solution.py
@@ -27,6 +27,7 @@
 HALF = 128
 QUARTER = 1408
 ROW_AT = 3
+LINE_AT = 12
 
 
 ANY = pl.BlockSpec(memory_space=pl.ANY)
@@ -48,10 +49,10 @@
     rows = []
     for device in range(128):
         seq, x, z = device // 16, device // 4 % 4, device % 4
-        far, up, down = ((x + by) % 4 * 256 for by in (2, 1, 3))
+        far, up, down = ((x ^ by) * 256 for by in (2, 1, 3))
         rows.append(
             [seq, z, seq % 2, far, far + 128, up, up + 128, down, down + 128, x * 256,
-             x * 256 + 128, x]
+             x * 256 + 128, x, z ^ 1, z ^ 3, z ^ 2]
         )
     return np.array(rows, np.int32)
 
@@ -255,8 +256,8 @@
     z = pos_ref[1]
     rows = pl.ds(pl.multiple_of(pos_ref[2] * 128, 128), 128)
     copies = []
-    for i, (shift, ref) in enumerate(((1, next_ref), (3, last_ref), (2, far_ref))):
-        cols = pl.ds(quarter_start((z + shift) % 4), QUARTER)
+    for i, ref in enumerate((next_ref, last_ref, far_ref)):
+        cols = pl.ds(quarter_start(pos_ref[LINE_AT + i]), QUARTER)
         copies.append(pltpu.make_async_copy(w_ref.at[rows, cols], ref, sems.at[i]))
     cols = pl.ds(quarter_start(z), QUARTER)
     copies.append(pltpu.make_async_copy(w_ref.at[:, cols], own_ref, sems.at[3]))
@@ -313,13 +314,13 @@
 
 
 def near_kernel(*refs):
-    relay_up, relay_down, up_ref, down_ref = refs[6:]
+    for_down, for_up, up_ref, down_ref = refs[6:]
     up = product(refs[0:4], refs[4:6], slice(0, 256))
-    up_ref[0:HALF] = (up[0:HALF] + relay_up[...].astype(F32)).astype(BF16)
-    up_ref[HALF:] = up[HALF:].astype(BF16)
+    up_ref[0:HALF] = up[0:HALF].astype(BF16)
+    up_ref[HALF:] = (up[HALF:] + for_up[...].astype(F32)).astype(BF16)
     down = product(refs[0:4], refs[4:6], slice(256, 512))
-    down_ref[0:HALF] = down[0:HALF].astype(BF16)
-    down_ref[HALF:] = (down[HALF:] + relay_down[...].astype(F32)).astype(BF16)
+    down_ref[0:HALF] = (down[0:HALF] + for_down[...].astype(F32)).astype(BF16)
+    down_ref[HALF:] = down[HALF:].astype(BF16)
 
 
 def keep_kernel(*refs):
@@ -342,13 +343,12 @@
     z = pos_ref[1]
     total[...] = kept_ref[...] + up_ref[...].astype(F32) + down_ref[...].astype(F32)
 
-    def rows(shift):
-        return total[pl.ds(pl.multiple_of(((z + shift) % 4) * 64, 64), 64), :]
-
-    next_ref[...] = rows(1).astype(BF16)
-    last_ref[...] = rows(3).astype(BF16)
-    far_ref[...] = rows(2).astype(BF16)
-    own_ref[...] = rows(0)
+    def rows(number):
+        return total[pl.ds(pl.multiple_of(number * 64, 64), 64), :]
+
+    for i, ref in enumerate((next_ref, last_ref, far_ref)):
+        ref[...] = rows(pos_ref[LINE_AT + i]).astype(BF16)
+    own_ref[...] = rows(z)
 
 
 def total_step(pos, kept, up, down):
@@ -366,9 +366,8 @@
 
 
 def finish_kernel(pos_ref, own_ref, next_ref, last_ref, far_ref, tok_ref, g_ref, out_ref, line):
-    z = pos_ref[1]
-    for shift, ref in ((0, own_ref), (3, next_ref), (1, last_ref), (2, far_ref)):
-        line[:, pl.ds(quarter_start((z + shift) % 4), QUARTER)] = ref[...].astype(F32)
+    for at, ref in ((1, own_ref), (LINE_AT, next_ref), (LINE_AT + 1, last_ref), (LINE_AT + 2, far_ref)):
+        line[:, pl.ds(quarter_start(pos_ref[at]), QUARTER)] = ref[...].astype(F32)
     for i in range(4):
         rows = slice(i * 16, (i + 1) * 16)
         total = jnp.zeros((16, 128), F32)
@@ -396,12 +395,12 @@
     )(pos, own, nxt, last, far, own_tokens, gain.reshape(1, -1))
 
 
-def shift_by(array, axis, steps):
-    return lax.ppermute(array, axis, [(i, (i + steps) % 4) for i in range(4)])
+def exchange(array, axis, by):
+    return lax.ppermute(array, axis, [(i, i ^ by) for i in range(4)])
 
 
 def from_line(pieces):
-    return [shift_by(piece, "z", by) for piece, by in zip(pieces, (1, 3, 2), strict=True)]
+    return [exchange(piece, "z", by) for piece, by in zip(pieces, (1, 3, 2), strict=True)]
 
 
 def per_device(
@@ -435,13 +434,13 @@
     full = jax.ShapeDtypeStruct((256, QUARTER), BF16)
     kept_shape = jax.ShapeDtypeStruct((256, QUARTER), F32)
     up, down = multiply(far_kernel, far_heads, weights, (), [half, half], "far")
-    relays = (shift_by(up, "x", 1), shift_by(down, "x", 3))
+    relays = (exchange(up, "x", 1), exchange(down, "x", 3))
     pos, _ = lax.optimization_barrier((pos, near))
     kept = attend(6, 2, pos, q, kv, got, prior_key, prior_value)
     kept_heads = [kept, *from_line([kept] * 3)]
     kept, *relays = lax.optimization_barrier((kept, *relays))
     up, down = multiply(near_kernel, near_heads, weights, relays, [full, full], "near")
-    up, down = shift_by(up, "x", 1), shift_by(down, "x", 3)
+    up, down = exchange(up, "x", 1), exchange(down, "x", 3)
     kept = multiply(keep_kernel, kept_heads, weights, (), kept_shape, "keep")
     own, *others = total_step(pos, kept, up, down)
     return finish(pos, own, *from_line(others), own_tokens, post_gain)

time: 94.1 us -> 94.5 us (level)
  waiting for transfers between devices: 26.1 us -> 28.5 us
  starting transfers between devices: 33.5 us -> 31.6 us
    ppermute x19, waiting for transfers between devices: 24.3 us -> 26.6 us  [exchange(): return lax.ppermute(array, axis, [(i, i ^ by) for i in range(4)])]
    ppermute x19, starting transfers between devices: 29.3 us -> 27.4 us  [exchange(): return lax.ppermute(array, axis, [(i, i ^ by) for i in range(4)])]
  transfers between devices with their start and end apart: 23 -> 23, of which waited for: 14 -> 17; matrix products, arithmetic and copies ran while one was open for 0% -> 0% of each run, Pallas kernels for 25% -> 25%
where the time goes in v6:
time: 94.5 us; the launch traced here: 94.3 us
  Pallas kernels  33.2 us (35%)
  starting transfers between devices  31.6 us (33%)
  waiting for transfers between devices  28.5 us (30%)
    ppermute x19, starting transfers between devices, exchange(): return lax.ppermute(array, axis, [(i, i ^ by) for i in range(4)])  27.4 us
    ppermute x19, waiting for transfers between devices, exchange(): return lax.ppermute(array, axis, [(i, i ^ by) for i in range(4)])  26.6 us
    pallas_call x1, Pallas kernels, key_value(): pl.pallas_call(key_value_kernel, grid_spec=pltpu.PrefetchScalarGridSpec(n...  11.3 us
    pallas_call x3, Pallas kernels, attend(): pl.pallas_call(functools.partial(attend_kernel, first_part), in_specs=[pl...  6.86 us
    pallas_call x1, Pallas kernels, query(): pl.pallas_call(query_kernel, grid_spec=pltpu.PrefetchScalarGridSpec(num_s...  5.69 us
    pallas_call x3, Pallas kernels, multiply(): pl.pallas_call(kernel, in_specs=[VMEM] * (6 + len(relays)), out_specs=jax...  3.77 us
    ppermute x3, starting transfers between devices, per_device(): swapped = [lax.ppermute(part, 'c', [(0, 1), (1, 0)]) for part in lines]  2.87 us
    pallas_call x1, Pallas kernels, pick(): pl.pallas_call(pick_kernel, in_specs=[SMEM, ANY], out_specs=[VMEM] * 4, o...  2.03 us
  transfers between devices with their start and end apart: 23, of which 17 were waited for; matrix products, arithmetic and copies ran while one was open for 0% of the time, Pallas kernels for 25%

profile of v6, /device:TPU:0, one launch (start us, length us, event | category | flops | bytes accessed | tf_op | source)
XLA Modules:
  0.0 94.3 jit_solution(10643470872717142025)
XLA Ops:
  0.7 2.0 %pick.1 = (bf16[256,1408]{1,0:T(8,128)(2,1)S(1)}, bf16[128,1408]{1,0:T(8,128)(2,1)S(1)}, bf16[128,1408]{1,0:T(8,128)(2,1)S(1)}, bf16[128,1408]{1,0:T(8,128)(2,1)S(1)}) custom-call(s32[15]{0:T(128)S(1)} %dynamic-slice_bitcast_fusion.pos_ref, bf16[256,5376]{1,0:T(8,128)(2,1)} %w_ref.2), custom_call_target="tpu_custom_call" | custom-call | tf_op jit(solution)/shard_map/pick/pallas_call | solution.py:272
  2.7 2.1 %collective-permute-start = (bf16[128,1408]{1,0:T(8,128)(2,1)S(1)}, bf16[128,1408]{1,0:T(8,128)(2,1)S(1)}, u32[]{:S(2)}, u32[]{:S(2)}) collective-permute-start(bf16[128,1408]{1,0:T(8,128)(2,1)S(1)} %get-tuple-element.45), channel_id=1, source_target_pairs={{0,1},{1,0},{2,3},{3,2},{4,5},{5,4},{6,7},{7,6},{8,9},{9,8},{10,11... | collective-permute-start | bytes 1081352 | tf_op jit(solution)/shard_map/ppermute | solution.py:399
  4.8 2.5 %collective-permute-start.1 = (bf16[128,1408]{1,0:T(8,128)(2,1)S(1)}, bf16[128,1408]{1,0:T(8,128)(2,1)S(1)}, u32[]{:S(2)}, u32[]{:S(2)}) collective-permute-start(bf16[128,1408]{1,0:T(8,128)(2,1)S(1)} %get-tuple-element.46), channel_id=1, source_target_pairs={{0,3},{1,2},{2,1},{3,0},{4,7},{5,6},{6,5},{7,4},{8,11},{9,10},{10,... | collective-permute-start | bytes 1081352 | tf_op jit(solution)/shard_map/ppermute | solution.py:399
  8.5 11.3 %key_value.1 = (bf16[1024,5376]{1,0:T(8,128)(2,1)S(1)}, bf16[1024,256]{1,0:T(8,128)(2,1)S(1)}, bf16[64,5376]{1,0:T(8,128)(2,1)S(1)}) custom-call(s32[15]{0:T(128)S(1)} %dynamic-slice_bitcast_fusion.pos_ref, bf16[1024,5376]{1,0:T(8,128)(2,1)} %tok_ref.1, f32[1,5376]{1,0:T(1,128)S(1)} %reshape.16.g_ref, bf16[5376,128]{1,0:T(8,128)(2,1)} %wk_ref.1, ...), custom_call_target="tpu_custom_call" | custom-call | flops 11274289152 | bytes 27262976 | tf_op jit(solution)/shard_map/key_value/pallas_call | solution.py:139
  19.8 1.3 %collective-permute-start.6 = (bf16[1024,256]{1,0:T(8,128)(2,1)S(1)}, bf16[1024,256]{1,0:T(8,128)(2,1)S(1)}, u32[]{:S(2)}, u32[]{:S(2)}) collective-permute-start(bf16[1024,256]{1,0:T(8,128)(2,1)S(1)} %get-tuple-element.53.kv_ref), channel_id=1, source_target_pairs={{0,16},{16,32},{32,48},{48,64},{64,80},{80,96},{96,112},{1,17},{17... | collective-permute-start | bytes 1572872 | tf_op jit(solution)/shard_map/ppermute | solution.py:418
  21.1 5.7 %query.1.q_ref = bf16[1024,256]{1,0:T(8,128)(2,1)S(1)} custom-call(s32[15]{0:T(128)S(1)} %dynamic-slice_bitcast_fusion.pos_ref, bf16[1024,5376]{1,0:T(8,128)(2,1)S(1)} %get-tuple-element.44.normed_ref, bf16[5376,256]{1,0:T(8,128)(2,1)S(1)} %copy-done, f32[1,128]{1,0:T(1,128)S(1)} %bitcast.4, f32[8192,128]{1,0:T(8,128)} %constant.32.clone.tab_ref), custom_call_target="tpu_custom_call" | custom-call | tf_op jit(solution)/shard_map/query/pallas_call | solution.py:176
  26.9 2.4 %collective-permute-start.3 = (bf16[128,1408]{1,0:T(8,128)(2,1)S(1)}, bf16[128,1408]{1,0:T(8,128)(2,1)S(1)}, u32[]{:S(2)}, u32[]{:S(2)}) collective-permute-start(bf16[128,1408]{1,0:T(8,128)(2,1)S(1)} %collective-permute-done.refs_0_), channel_id=1, source_target_pairs={{0,16},{16,0},{1,17},{17,1},{2,18},{18,2},{3,19},{19,3},{4,20},{20... | collective-permute-start | bytes 1081352 | tf_op jit(solution)/shard_map/ppermute | solution.py:421
  31.6 2.0 %attend.3.refs_0_ = bf16[256,256]{1,0:T(8,128)(2,1)S(1)} custom-call(s32[15]{0:T(128)S(1)} %dynamic-slice_bitcast_fusion.pos_ref, bf16[1024,256]{1,0:T(8,128)(2,1)S(1)} %query.1.q_ref, bf16[1024,256]{1,0:T(8,128)(2,1)S(1)} %get-tuple-element.53.kv_ref, bf16[1024,256]{1,0:T(8,128)(2,1)S(1)} %collective-permute-done.6.got_ref, ...), custom_call_target="tpu_custom_call" | custom-call | tf_op jit(solution)/shard_map/attend/pallas_call | solution.py:236
  34.1 2.5 %collective-permute-start.14 = (bf16[256,256]{1,0:T(8,128)(2,1)S(1)}, bf16[256,256]{1,0:T(8,128)(2,1)S(1)}, u32[]{:S(2)}, u32[]{:S(2)}) collective-permute-start(bf16[256,256]{1,0:T(8,128)(2,1)S(1)} %attend.3.refs_0_), channel_id=1, source_target_pairs={{0,3},{1,2},{2,1},{3,0},{4,7},{5,6},{6,5},{7,4},{8,11},{9,10},{10,... | collective-permute-start | bytes 393224 | tf_op jit(solution)/shard_map/ppermute | solution.py:399
  37.7 3.0 %attend.4.refs_0_ = bf16[512,256]{1,0:T(8,128)(2,1)S(1)} custom-call(s32[15]{0:T(128)S(1)} %dynamic-slice_bitcast_fusion.pos_ref, bf16[1024,256]{1,0:T(8,128)(2,1)S(1)} %query.1.q_ref, bf16[1024,256]{1,0:T(8,128)(2,1)S(1)} %get-tuple-element.53.kv_ref, bf16[1024,256]{1,0:T(8,128)(2,1)S(1)} %collective-permute-done.6.got_ref, ...), custom_call_target="tpu_custom_call" | custom-call | tf_op jit(solution)/shard_map/attend/pallas_call | solution.py:236
  41.4 1.2 %collective-permute-done.14.refs_2_ = bf16[256,256]{1,0:T(8,128)(2,1)S(1)} collective-permute-done((bf16[256,256]{1,0:T(8,128)(2,1)S(1)}, bf16[256,256]{1,0:T(8,128)(2,1)S(1)}, u32[]{:S(2)}, u32[]{:S(2)}) %collective-permute-start.14) | collective-permute-done | bytes 131104 | tf_op jit(solution)/shard_map/ppermute | solution.py:399
  42.6 1.8 %collective-permute-done.15.refs_3_ = bf16[256,256]{1,0:T(8,128)(2,1)S(1)} collective-permute-done((bf16[256,256]{1,0:T(8,128)(2,1)S(1)}, bf16[256,256]{1,0:T(8,128)(2,1)S(1)}, u32[]{:S(2)}, u32[]{:S(2)}) %collective-permute-start.15) | collective-permute-done | bytes 131104 | tf_op jit(solution)/shard_map/ppermute | solution.py:399
  45.3 1.6 %collective-permute-start.16 = (bf16[128,1408]{1,0:T(8,128)(2,1)S(1)}, bf16[128,1408]{1,0:T(8,128)(2,1)S(1)}, u32[]{:S(2)}, u32[]{:S(2)}) collective-permute-start(bf16[128,1408]{1,0:T(8,128)(2,1)S(1)} %get-tuple-element.64), channel_id=1, source_target_pairs={{0,4},{4,0},{8,12},{12,8},{1,5},{5,1},{9,13},{13,9},{2,6},{6,2},{1... | collective-permute-start | bytes 1081352 | tf_op jit(solution)/shard_map/ppermute | solution.py:399
  46.9 2.1 %collective-permute-start.17 = (bf16[128,1408]{1,0:T(8,128)(2,1)S(1)}, bf16[128,1408]{1,0:T(8,128)(2,1)S(1)}, u32[]{:S(2)}, u32[]{:S(2)}) collective-permute-start(bf16[128,1408]{1,0:T(8,128)(2,1)S(1)} %get-tuple-element.65), channel_id=1, source_target_pairs={{0,12},{4,8},{8,4},{12,0},{1,13},{5,9},{9,5},{13,1},{2,14},{6,10},... | collective-permute-start | bytes 1081352 | tf_op jit(solution)/shard_map/ppermute | solution.py:399
  49.1 2.2 %collective-permute-start.11 = (bf16[512,256]{1,0:T(8,128)(2,1)S(1)}, bf16[512,256]{1,0:T(8,128)(2,1)S(1)}, u32[]{:S(2)}, u32[]{:S(2)}) collective-permute-start(bf16[512,256]{1,0:T(8,128)(2,1)S(1)} %attend.4.refs_0_), channel_id=1, source_target_pairs={{0,3},{1,2},{2,1},{3,0},{4,7},{5,6},{6,5},{7,4},{8,11},{9,10},{10,... | collective-permute-start | bytes 786440 | tf_op jit(solution)/shard_map/ppermute | solution.py:399
  51.3 1.8 %collective-permute-start.12 = (bf16[512,256]{1,0:T(8,128)(2,1)S(1)}, bf16[512,256]{1,0:T(8,128)(2,1)S(1)}, u32[]{:S(2)}, u32[]{:S(2)}) collective-permute-start(bf16[512,256]{1,0:T(8,128)(2,1)S(1)} %attend.4.refs_0_), channel_id=1, source_target_pairs={{0,2},{1,3},{2,0},{3,1},{4,6},{5,7},{6,4},{7,5},{8,10},{9,11},{10,... | collective-permute-start | bytes 786440 | tf_op jit(solution)/shard_map/ppermute | solution.py:399
  53.1 1.9 %attend.5.refs_0_ = bf16[256,256]{1,0:T(8,128)(2,1)S(1)} custom-call(s32[15]{0:T(128)S(1)} %dynamic-slice_bitcast_fusion.pos_ref, bf16[1024,256]{1,0:T(8,128)(2,1)S(1)} %query.1.q_ref, bf16[1024,256]{1,0:T(8,128)(2,1)S(1)} %get-tuple-element.53.kv_ref, bf16[1024,256]{1,0:T(8,128)(2,1)S(1)} %collective-permute-done.6.got_ref, ...), custom_call_target="tpu_custom_call" | custom-call | tf_op jit(solution)/shard_map/attend/pallas_call | solution.py:236
  55.3 2.4 %collective-permute-done.17.refs_7_ = bf16[128,1408]{1,0:T(8,128)(2,1)S(1)} collective-permute-done((bf16[128,1408]{1,0:T(8,128)(2,1)S(1)}, bf16[128,1408]{1,0:T(8,128)(2,1)S(1)}, u32[]{:S(2)}, u32[]{:S(2)}) %collective-permute-start.17) | collective-permute-done | bytes 360480 | tf_op jit(solution)/shard_map/ppermute | solution.py:399
  58.2 4.9 %collective-permute-done.11.refs_2_ = bf16[512,256]{1,0:T(8,128)(2,1)S(1)} collective-permute-done((bf16[512,256]{1,0:T(8,128)(2,1)S(1)}, bf16[512,256]{1,0:T(8,128)(2,1)S(1)}, u32[]{:S(2)}, u32[]{:S(2)}) %collective-permute-start.11) | collective-permute-done | bytes 262176 | tf_op jit(solution)/shard_map/ppermute | solution.py:399
  63.1 1.8 %near.1 = (bf16[256,1408]{1,0:T(8,128)(2,1)S(1)}, bf16[256,1408]{1,0:T(8,128)(2,1)S(1)}) custom-call(bf16[512,256]{1,0:T(8,128)(2,1)S(1)} %attend.4.refs_0_, bf16[512,256]{1,0:T(8,128)(2,1)S(1)} %collective-permute-done.10.refs_1_, bf16[512,256]{1,0:T(8,128)(2,1)S(1)} %collective-permute-done.11.refs_2_, ...), custom_call_target="tpu_custom_call" | custom-call | tf_op jit(solution)/shard_map/near/pallas_call | solution.py:331
  67.0 1.6 %collective-permute-start.8 = (bf16[256,256]{1,0:T(8,128)(2,1)S(1)}, bf16[256,256]{1,0:T(8,128)(2,1)S(1)}, u32[]{:S(2)}, u32[]{:S(2)}) collective-permute-start(bf16[256,256]{1,0:T(8,128)(2,1)S(1)} %attend.5.refs_0_), channel_id=1, source_target_pairs={{0,3},{1,2},{2,1},{3,0},{4,7},{5,6},{6,5},{7,4},{8,11},{9,10},{10,... | collective-permute-start | bytes 393224 | tf_op jit(solution)/shard_map/ppermute | solution.py:399
  68.6 2.0 %collective-permute-start.9 = (bf16[256,256]{1,0:T(8,128)(2,1)S(1)}, bf16[256,256]{1,0:T(8,128)(2,1)S(1)}, u32[]{:S(2)}, u32[]{:S(2)}) collective-permute-start(bf16[256,256]{1,0:T(8,128)(2,1)S(1)} %attend.5.refs_0_), channel_id=1, source_target_pairs={{0,2},{1,3},{2,0},{3,1},{4,6},{5,7},{6,4},{7,5},{8,10},{9,11},{10,... | collective-permute-start | bytes 393224 | tf_op jit(solution)/shard_map/ppermute | solution.py:399
  71.4 1.7 %collective-permute-done.8.refs_2_ = bf16[256,256]{1,0:T(8,128)(2,1)S(1)} collective-permute-done((bf16[256,256]{1,0:T(8,128)(2,1)S(1)}, bf16[256,256]{1,0:T(8,128)(2,1)S(1)}, u32[]{:S(2)}, u32[]{:S(2)}) %collective-permute-start.8) | collective-permute-done | bytes 131104 | tf_op jit(solution)/shard_map/ppermute | solution.py:399
  73.2 1.9 %collective-permute-done.9.refs_3_ = bf16[256,256]{1,0:T(8,128)(2,1)S(1)} collective-permute-done((bf16[256,256]{1,0:T(8,128)(2,1)S(1)}, bf16[256,256]{1,0:T(8,128)(2,1)S(1)}, u32[]{:S(2)}, u32[]{:S(2)}) %collective-permute-start.9) | collective-permute-done | bytes 131104 | tf_op jit(solution)/shard_map/ppermute | solution.py:399
  76.0 4.7 %collective-permute-done.18.up_ref = bf16[256,1408]{1,0:T(8,128)(2,1)S(1)} collective-permute-done((bf16[256,1408]{1,0:T(8,128)(2,1)S(1)}, bf16[256,1408]{1,0:T(8,128)(2,1)S(1)}, u32[]{:S(2)}, u32[]{:S(2)}) %collective-permute-start.18) | collective-permute-done | bytes 720928 | tf_op jit(solution)/shard_map/ppermute | solution.py:399
  80.7 1.5 %collective-permute-done.19.down_ref = bf16[256,1408]{1,0:T(8,128)(2,1)S(1)} collective-permute-done((bf16[256,1408]{1,0:T(8,128)(2,1)S(1)}, bf16[256,1408]{1,0:T(8,128)(2,1)S(1)}, u32[]{:S(2)}, u32[]{:S(2)}) %collective-permute-start.19) | collective-permute-done | bytes 720928 | tf_op jit(solution)/shard_map/ppermute | solution.py:399
  83.3 2.1 %collective-permute-start.21 = (bf16[64,1408]{1,0:T(8,128)(2,1)S(1)}, bf16[64,1408]{1,0:T(8,128)(2,1)S(1)}, u32[]{:S(2)}, u32[]{:S(2)}) collective-permute-start(bf16[64,1408]{1,0:T(8,128)(2,1)S(1)} %get-tuple-element.72), channel_id=1, source_target_pairs={{0,3},{1,2},{2,1},{3,0},{4,7},{5,6},{6,5},{7,4},{8,11},{9,10},{10,... | collective-permute-start | bytes 540680 | tf_op jit(solution)/shard_map/ppermute | solution.py:399
  85.4 2.0 %collective-permute-start.22 = (bf16[64,1408]{1,0:T(8,128)(2,1)S(1)}, bf16[64,1408]{1,0:T(8,128)(2,1)S(1)}, u32[]{:S(2)}, u32[]{:S(2)}) collective-permute-start(bf16[64,1408]{1,0:T(8,128)(2,1)S(1)} %get-tuple-element.73), channel_id=1, source_target_pairs={{0,2},{1,3},{2,0},{3,1},{4,6},{5,7},{6,4},{7,5},{8,10},{9,11},{10,... | collective-permute-start | bytes 540680 | tf_op jit(solution)/shard_map/ppermute | solution.py:399
  87.4 1.4 %collective-permute-done.20.next_ref = bf16[64,1408]{1,0:T(8,128)(2,1)S(1)} collective-permute-done((bf16[64,1408]{1,0:T(8,128)(2,1)S(1)}, bf16[64,1408]{1,0:T(8,128)(2,1)S(1)}, u32[]{:S(2)}, u32[]{:S(2)}) %collective-permute-start.20) | collective-permute-done | bytes 180256 | tf_op jit(solution)/shard_map/ppermute | solution.py:399
  88.8 1.6 %collective-permute-done.21.last_ref = bf16[64,1408]{1,0:T(8,128)(2,1)S(1)} collective-permute-done((bf16[64,1408]{1,0:T(8,128)(2,1)S(1)}, bf16[64,1408]{1,0:T(8,128)(2,1)S(1)}, u32[]{:S(2)}, u32[]{:S(2)}) %collective-permute-start.21) | collective-permute-done | bytes 180256 | tf_op jit(solution)/shard_map/ppermute | solution.py:399
  90.4 2.0 %collective-permute-done.22.far_ref = bf16[64,1408]{1,0:T(8,128)(2,1)S(1)} collective-permute-done((bf16[64,1408]{1,0:T(8,128)(2,1)S(1)}, bf16[64,1408]{1,0:T(8,128)(2,1)S(1)}, u32[]{:S(2)}, u32[]{:S(2)}) %collective-permute-start.22) | collective-permute-done | bytes 180256 | tf_op jit(solution)/shard_map/ppermute | solution.py:399
  92.4 1.9 %finish.1 = bf16[64,5376]{1,0:T(8,128)(2,1)} custom-call(s32[15]{0:T(128)S(1)} %dynamic-slice_bitcast_fusion.pos_ref, f32[64,1408]{1,0:T(8,128)S(1)} %get-tuple-element.70.own_ref, bf16[64,1408]{1,0:T(8,128)(2,1)S(1)} %collective-permute-done.20.next_ref, bf16[64,1408]{1,0:T(8,128)(2,1)S(1)} %collective-permute-done.21.last_ref, ...), custom_call_target="tpu_custom_call" | custom-call | tf_op jit(solution)/shard_map/finish/pallas_call | solution.py:386
  (43 shorter events, 13.4 us)
Async XLA Ops:
  0.0 8.4 %copy-start.5 = (f32[5376]{0:T(1024)S(1)}, f32[5376]{0:T(1024)}, u32[]{:S(2)}) copy-start(f32[5376]{0:T(1024)} %param.14) | copy-start | bytes 64516
  0.0 8.4 %copy-start.4 = (f32[128]{0:T(128)S(1)}, f32[128]{0:T(128)}, u32[]{:S(2)}) copy-start(f32[128]{0:T(128)} %param.19) | copy-start | bytes 1540
  2.7 24.1 %collective-permute-start = (bf16[128,1408]{1,0:T(8,128)(2,1)S(1)}, bf16[128,1408]{1,0:T(8,128)(2,1)S(1)}, u32[]{:S(2)}, u32[]{:S(2)}) collective-permute-start(bf16[128,1408]{1,0:T(8,128)(2,1)S(1)} %get-tuple-element.45), channel_id=1, source_target_pairs={{0,1},{1,0},{2,3},{3,2},{4,5},{5,4},{6,7},{7,6},{8,9},{9,8},{10,11... | collective-permute-start | bytes 1081352 | tf_op jit(solution)/shard_map/ppermute | solution.py:399
  4.8 22.0 %collective-permute-start.1 = (bf16[128,1408]{1,0:T(8,128)(2,1)S(1)}, bf16[128,1408]{1,0:T(8,128)(2,1)S(1)}, u32[]{:S(2)}, u32[]{:S(2)}) collective-permute-start(bf16[128,1408]{1,0:T(8,128)(2,1)S(1)} %get-tuple-element.46), channel_id=1, source_target_pairs={{0,3},{1,2},{2,1},{3,0},{4,7},{5,6},{6,5},{7,4},{8,11},{9,10},{10,... | collective-permute-start | bytes 1081352 | tf_op jit(solution)/shard_map/ppermute | solution.py:399
  7.3 19.5 %collective-permute-start.2 = (bf16[128,1408]{1,0:T(8,128)(2,1)S(1)}, bf16[128,1408]{1,0:T(8,128)(2,1)S(1)}, u32[]{:S(2)}, u32[]{:S(2)}) collective-permute-start(bf16[128,1408]{1,0:T(8,128)(2,1)S(1)} %get-tuple-element.47), channel_id=1, source_target_pairs={{0,2},{1,3},{2,0},{3,1},{4,6},{5,7},{6,4},{7,5},{8,10},{9,11},{10,... | collective-permute-start | bytes 1081352 | tf_op jit(solution)/shard_map/ppermute | solution.py:399
  8.4 12.7 %copy-start = (bf16[5376,256]{1,0:T(8,128)(2,1)S(1)}, bf16[5376,256]{1,0:T(8,128)(2,1)}, u32[]{:S(2)}) copy-start(bf16[5376,256]{1,0:T(8,128)(2,1)} %w_ref.3) | copy-start | bytes 8257540
  8.5 12.7 %copy-start.3 = (f32[128]{0:T(128)S(1)}, f32[128]{0:T(128)}, u32[]{:S(2)}) copy-start(f32[128]{0:T(128)} %param.18) | copy-start | bytes 1540
  19.8 11.8 %collective-permute-start.6 = (bf16[1024,256]{1,0:T(8,128)(2,1)S(1)}, bf16[1024,256]{1,0:T(8,128)(2,1)S(1)}, u32[]{:S(2)}, u32[]{:S(2)}) collective-permute-start(bf16[1024,256]{1,0:T(8,128)(2,1)S(1)} %get-tuple-element.53.kv_ref), channel_id=1, source_target_pairs={{0,16},{16,32},{32,48},{48,64},{64,80},{80,96},{96,112},{1,17},{17... | collective-permute-start | bytes 1572872 | tf_op jit(solution)/shard_map/ppermute | solution.py:418
  21.1 10.5 %copy-start.1 = (bf16[1024,128]{1,0:T(8,128)(2,1)S(1)}, bf16[1024,128]{1,0:T(8,128)(2,1)}, u32[]{:S(2)}) copy-start(bf16[1024,128]{1,0:T(8,128)(2,1)} %pk_ref.5) | copy-start | bytes 786436
  21.1 10.4 %copy-start.2 = (bf16[1024,128]{1,0:T(8,128)(2,1)S(1)}, bf16[1024,128]{1,0:T(8,128)(2,1)}, u32[]{:S(2)}) copy-start(bf16[1024,128]{1,0:T(8,128)(2,1)} %pv_ref.5) | copy-start | bytes 786436
  26.9 3.7 %collective-permute-start.3 = (bf16[128,1408]{1,0:T(8,128)(2,1)S(1)}, bf16[128,1408]{1,0:T(8,128)(2,1)S(1)}, u32[]{:S(2)}, u32[]{:S(2)}) collective-permute-start(bf16[128,1408]{1,0:T(8,128)(2,1)S(1)} %collective-permute-done.refs_0_), channel_id=1, source_target_pairs={{0,16},{16,0},{1,17},{17,1},{2,18},{18,2},{3,19},{19,3},{4,20},{20... | collective-permute-start | bytes 1081352 | tf_op jit(solution)/shard_map/ppermute | solution.py:421
  29.2 1.8 %collective-permute-start.4 = (bf16[128,1408]{1,0:T(8,128)(2,1)S(1)}, bf16[128,1408]{1,0:T(8,128)(2,1)S(1)}, u32[]{:S(2)}, u32[]{:S(2)}) collective-permute-start(bf16[128,1408]{1,0:T(8,128)(2,1)S(1)} %collective-permute-done.1.refs_1_), channel_id=1, source_target_pairs={{0,16},{16,0},{1,17},{17,1},{2,18},{18,2},{3,19},{19,3},{4,20},{20... | collective-permute-start | bytes 1081352 | tf_op jit(solution)/shard_map/ppermute | solution.py:421
  29.3 2.2 %collective-permute-start.5 = (bf16[128,1408]{1,0:T(8,128)(2,1)S(1)}, bf16[128,1408]{1,0:T(8,128)(2,1)S(1)}, u32[]{:S(2)}, u32[]{:S(2)}) collective-permute-start(bf16[128,1408]{1,0:T(8,128)(2,1)S(1)} %collective-permute-done.2.refs_2_), channel_id=1, source_target_pairs={{0,16},{16,0},{1,17},{17,1},{2,18},{18,2},{3,19},{19,3},{4,20},{20... | collective-permute-start | bytes 1081352 | tf_op jit(solution)/shard_map/ppermute | solution.py:421
  33.5 7.9 %collective-permute-start.13 = (bf16[256,256]{1,0:T(8,128)(2,1)S(1)}, bf16[256,256]{1,0:T(8,128)(2,1)S(1)}, u32[]{:S(2)}, u32[]{:S(2)}) collective-permute-start(bf16[256,256]{1,0:T(8,128)(2,1)S(1)} %attend.3.refs_0_), channel_id=1, source_target_pairs={{0,1},{1,0},{2,3},{3,2},{4,5},{5,4},{6,7},{7,6},{8,9},{9,8},{10,11... | collective-permute-start | bytes 393224 | tf_op jit(solution)/shard_map/ppermute | solution.py:399
  34.1 8.4 %collective-permute-start.14 = (bf16[256,256]{1,0:T(8,128)(2,1)S(1)}, bf16[256,256]{1,0:T(8,128)(2,1)S(1)}, u32[]{:S(2)}, u32[]{:S(2)}) collective-permute-start(bf16[256,256]{1,0:T(8,128)(2,1)S(1)} %attend.3.refs_0_), channel_id=1, source_target_pairs={{0,3},{1,2},{2,1},{3,0},{4,7},{5,6},{6,5},{7,4},{8,11},{9,10},{10,... | collective-permute-start | bytes 393224 | tf_op jit(solution)/shard_map/ppermute | solution.py:399
  36.6 7.7 %collective-permute-start.15 = (bf16[256,256]{1,0:T(8,128)(2,1)S(1)}, bf16[256,256]{1,0:T(8,128)(2,1)S(1)}, u32[]{:S(2)}, u32[]{:S(2)}) collective-permute-start(bf16[256,256]{1,0:T(8,128)(2,1)S(1)} %attend.3.refs_0_), channel_id=1, source_target_pairs={{0,2},{1,3},{2,0},{3,1},{4,6},{5,7},{6,4},{7,5},{8,10},{9,11},{10,... | collective-permute-start | bytes 393224 | tf_op jit(solution)/shard_map/ppermute | solution.py:399
  45.3 10.0 %collective-permute-start.16 = (bf16[128,1408]{1,0:T(8,128)(2,1)S(1)}, bf16[128,1408]{1,0:T(8,128)(2,1)S(1)}, u32[]{:S(2)}, u32[]{:S(2)}) collective-permute-start(bf16[128,1408]{1,0:T(8,128)(2,1)S(1)} %get-tuple-element.64), channel_id=1, source_target_pairs={{0,4},{4,0},{8,12},{12,8},{1,5},{5,1},{9,13},{13,9},{2,6},{6,2},{1... | collective-permute-start | bytes 1081352 | tf_op jit(solution)/shard_map/ppermute | solution.py:399
  46.9 10.9 %collective-permute-start.17 = (bf16[128,1408]{1,0:T(8,128)(2,1)S(1)}, bf16[128,1408]{1,0:T(8,128)(2,1)S(1)}, u32[]{:S(2)}, u32[]{:S(2)}) collective-permute-start(bf16[128,1408]{1,0:T(8,128)(2,1)S(1)} %get-tuple-element.65), channel_id=1, source_target_pairs={{0,12},{4,8},{8,4},{12,0},{1,13},{5,9},{9,5},{13,1},{2,14},{6,10},... | collective-permute-start | bytes 1081352 | tf_op jit(solution)/shard_map/ppermute | solution.py:399
  49.0 9.2 %collective-permute-start.10 = (bf16[512,256]{1,0:T(8,128)(2,1)S(1)}, bf16[512,256]{1,0:T(8,128)(2,1)S(1)}, u32[]{:S(2)}, u32[]{:S(2)}) collective-permute-start(bf16[512,256]{1,0:T(8,128)(2,1)S(1)} %attend.4.refs_0_), channel_id=1, source_target_pairs={{0,1},{1,0},{2,3},{3,2},{4,5},{5,4},{6,7},{7,6},{8,9},{9,8},{10,11... | collective-permute-start | bytes 786440 | tf_op jit(solution)/shard_map/ppermute | solution.py:399
  49.1 14.0 %collective-permute-start.11 = (bf16[512,256]{1,0:T(8,128)(2,1)S(1)}, bf16[512,256]{1,0:T(8,128)(2,1)S(1)}, u32[]{:S(2)}, u32[]{:S(2)}) collective-permute-start(bf16[512,256]{1,0:T(8,128)(2,1)S(1)} %attend.4.refs_0_), channel_id=1, source_target_pairs={{0,3},{1,2},{2,1},{3,0},{4,7},{5,6},{6,5},{7,4},{8,11},{9,10},{10,... | collective-permute-start | bytes 786440 | tf_op jit(solution)/shard_map/ppermute | solution.py:399
  51.3 11.8 %collective-permute-start.12 = (bf16[512,256]{1,0:T(8,128)(2,1)S(1)}, bf16[512,256]{1,0:T(8,128)(2,1)S(1)}, u32[]{:S(2)}, u32[]{:S(2)}) collective-permute-start(bf16[512,256]{1,0:T(8,128)(2,1)S(1)} %attend.4.refs_0_), channel_id=1, source_target_pairs={{0,2},{1,3},{2,0},{3,1},{4,6},{5,7},{6,4},{7,5},{8,10},{9,11},{10,... | collective-permute-start | bytes 786440 | tf_op jit(solution)/shard_map/ppermute | solution.py:399
  64.9 15.8 %collective-permute-start.18 = (bf16[256,1408]{1,0:T(8,128)(2,1)S(1)}, bf16[256,1408]{1,0:T(8,128)(2,1)S(1)}, u32[]{:S(2)}, u32[]{:S(2)}) collective-permute-start(bf16[256,1408]{1,0:T(8,128)(2,1)S(1)} %get-tuple-element.68), channel_id=1, source_target_pairs={{0,4},{4,0},{8,12},{12,8},{1,5},{5,1},{9,13},{13,9},{2,6},{6,2},{1... | collective-permute-start | bytes 2162696 | tf_op jit(solution)/shard_map/ppermute | solution.py:399
  65.6 21.8 %copy-start.6 = (f32[5376]{0:T(1024)S(1)}, f32[5376]{0:T(1024)}, u32[]{:S(2)}) copy-start(f32[5376]{0:T(1024)} %param.23) | copy-start | bytes 64516
  65.6 16.6 %collective-permute-start.19 = (bf16[256,1408]{1,0:T(8,128)(2,1)S(1)}, bf16[256,1408]{1,0:T(8,128)(2,1)S(1)}, u32[]{:S(2)}, u32[]{:S(2)}) collective-permute-start(bf16[256,1408]{1,0:T(8,128)(2,1)S(1)} %get-tuple-element.69), channel_id=1, source_target_pairs={{0,12},{4,8},{8,4},{12,0},{1,13},{5,9},{9,5},{13,1},{2,14},{6,10},... | collective-permute-start | bytes 2162696 | tf_op jit(solution)/shard_map/ppermute | solution.py:399
  66.5 5.0 %collective-permute-start.7 = (bf16[256,256]{1,0:T(8,128)(2,1)S(1)}, bf16[256,256]{1,0:T(8,128)(2,1)S(1)}, u32[]{:S(2)}, u32[]{:S(2)}) collective-permute-start(bf16[256,256]{1,0:T(8,128)(2,1)S(1)} %attend.5.refs_0_), channel_id=1, source_target_pairs={{0,1},{1,0},{2,3},{3,2},{4,5},{5,4},{6,7},{7,6},{8,9},{9,8},{10,11... | collective-permute-start | bytes 393224 | tf_op jit(solution)/shard_map/ppermute | solution.py:399
  67.0 6.2 %collective-permute-start.8 = (bf16[256,256]{1,0:T(8,128)(2,1)S(1)}, bf16[256,256]{1,0:T(8,128)(2,1)S(1)}, u32[]{:S(2)}, u32[]{:S(2)}) collective-permute-start(bf16[256,256]{1,0:T(8,128)(2,1)S(1)} %attend.5.refs_0_), channel_id=1, source_target_pairs={{0,3},{1,2},{2,1},{3,0},{4,7},{5,6},{6,5},{7,4},{8,11},{9,10},{10,... | collective-permute-start | bytes 393224 | tf_op jit(solution)/shard_map/ppermute | solution.py:399
  68.6 6.5 %collective-permute-start.9 = (bf16[256,256]{1,0:T(8,128)(2,1)S(1)}, bf16[256,256]{1,0:T(8,128)(2,1)S(1)}, u32[]{:S(2)}, u32[]{:S(2)}) collective-permute-start(bf16[256,256]{1,0:T(8,128)(2,1)S(1)} %attend.5.refs_0_), channel_id=1, source_target_pairs={{0,2},{1,3},{2,0},{3,1},{4,6},{5,7},{6,4},{7,5},{8,10},{9,11},{10,... | collective-permute-start | bytes 393224 | tf_op jit(solution)/shard_map/ppermute | solution.py:399
  83.2 5.6 %collective-permute-start.20 = (bf16[64,1408]{1,0:T(8,128)(2,1)S(1)}, bf16[64,1408]{1,0:T(8,128)(2,1)S(1)}, u32[]{:S(2)}, u32[]{:S(2)}) collective-permute-start(bf16[64,1408]{1,0:T(8,128)(2,1)S(1)} %get-tuple-element.71), channel_id=1, source_target_pairs={{0,1},{1,0},{2,3},{3,2},{4,5},{5,4},{6,7},{7,6},{8,9},{9,8},{10,11... | collective-permute-start | bytes 540680 | tf_op jit(solution)/shard_map/ppermute | solution.py:399
  83.3 7.0 %collective-permute-start.21 = (bf16[64,1408]{1,0:T(8,128)(2,1)S(1)}, bf16[64,1408]{1,0:T(8,128)(2,1)S(1)}, u32[]{:S(2)}, u32[]{:S(2)}) collective-permute-start(bf16[64,1408]{1,0:T(8,128)(2,1)S(1)} %get-tuple-element.72), channel_id=1, source_target_pairs={{0,3},{1,2},{2,1},{3,0},{4,7},{5,6},{6,5},{7,4},{8,11},{9,10},{10,... | collective-permute-start | bytes 540680 | tf_op jit(solution)/shard_map/ppermute | solution.py:399
  85.4 7.0 %collective-permute-start.22 = (bf16[64,1408]{1,0:T(8,128)(2,1)S(1)}, bf16[64,1408]{1,0:T(8,128)(2,1)S(1)}, u32[]{:S(2)}, u32[]{:S(2)}) collective-permute-start(bf16[64,1408]{1,0:T(8,128)(2,1)S(1)} %get-tuple-element.73), channel_id=1, source_target_pairs={{0,2},{1,3},{2,0},{3,1},{4,6},{5,7},{6,4},{7,5},{8,10},{9,11},{10,... | collective-permute-start | bytes 540680 | tf_op jit(solution)/shard_map/ppermute | solution.py:399

commit v7 on v5

--- a/solution.py
+++ b/solution.py
@@ -33,6 +33,8 @@
 VMEM = pl.BlockSpec(memory_space=pltpu.VMEM)
 SMEM = pl.BlockSpec(memory_space=pltpu.SMEM)
 SMALL = pl.CostEstimate(flops=0, bytes_accessed=0, transcendentals=0)
+MEDIUM = pl.CostEstimate(flops=4_000_000_000, bytes_accessed=0, transcendentals=0)
+LARGE = pl.CostEstimate(flops=30_000_000_000, bytes_accessed=0, transcendentals=0)
 
 
 def rotary_table():
@@ -230,7 +232,7 @@
         out_ref[part * HALF : (part + 1) * HALF, 128:256] = mixed[HALF:]
 
 
-def attend(first_part, parts, pos, q, kv, got, prior_k, prior_v):
+def attend(first_part, parts, pos, q, kv, got, prior_k, prior_v, cost=SMALL):
     vmem = pl.BlockSpec(memory_space=pltpu.VMEM)
     return pl.pallas_call(
         functools.partial(attend_kernel, first_part),
@@ -242,7 +244,7 @@
             pltpu.VMEM((2 * SHARD, 256), BF16),
         ],
         compiler_params=pltpu.CompilerParams(vmem_limit_bytes=32 << 20),
-        cost_estimate=SMALL,
+        cost_estimate=cost,
         name="attend",
     )(pos, q, kv, got, prior_k, prior_v)
 
@@ -313,29 +315,44 @@
 
 
 def near_kernel(*refs):
-    relay_up, relay_down, up_ref, down_ref = refs[6:]
-    up = product(refs[0:4], refs[4:6], slice(0, 256))
-    up_ref[0:HALF] = (up[0:HALF] + relay_up[...].astype(F32)).astype(BF16)
-    up_ref[HALF:] = up[HALF:].astype(BF16)
-    down = product(refs[0:4], refs[4:6], slice(256, 512))
-    down_ref[0:HALF] = down[0:HALF].astype(BF16)
-    down_ref[HALF:] = (down[HALF:] + relay_down[...].astype(F32)).astype(BF16)
+    refs[6][...] = product(refs[0:4], refs[4:6], slice(0, 256)).astype(BF16)
+    refs[7][...] = product(refs[0:4], refs[4:6], slice(256, 512)).astype(BF16)
+
+
+def relay_kernel(relay_up, relay_down, up_in, down_in, up_ref, down_ref):
+    up_ref[0:HALF] = (up_in[0:HALF].astype(F32) + relay_up[...].astype(F32)).astype(BF16)
+    up_ref[HALF:] = up_in[HALF:]
+    down_ref[0:HALF] = down_in[0:HALF]
+    down_ref[HALF:] = (down_in[HALF:].astype(F32) + relay_down[...].astype(F32)).astype(BF16)
+
+
+def relay(relays, up, down):
+    return pl.pallas_call(
+        relay_kernel,
+        in_specs=[VMEM] * 4,
+        out_specs=[VMEM] * 2,
+        out_shape=[jax.ShapeDtypeStruct((256, QUARTER), BF16)] * 2,
+        input_output_aliases={2: 0, 3: 1},
+        compiler_params=pltpu.CompilerParams(vmem_limit_bytes=16 << 20),
+        cost_estimate=SMALL,
+        name="relay",
+    )(*relays, up, down)
 
 
 def keep_kernel(*refs):
     refs[6][...] = product(refs[0:4], refs[4:6])
 
 
-def multiply(kernel, pieces, weights, relays, out_shape, name):
+def multiply(kernel, pieces, weights, out_shape, name, cost=SMALL):
     return pl.pallas_call(
         kernel,
-        in_specs=[VMEM] * (6 + len(relays)),
+        in_specs=[VMEM] * 6,
         out_specs=jax.tree.map(lambda _: VMEM, out_shape),
         out_shape=out_shape,
         compiler_params=pltpu.CompilerParams(vmem_limit_bytes=24 << 20),
-        cost_estimate=SMALL,
+        cost_estimate=cost,
         name=name,
-    )(*pieces, *weights, *relays)
+    )(*pieces, *weights)
 
 
 def total_kernel(pos_ref, kept_ref, up_ref, down_ref, own_ref, next_ref, last_ref, far_ref, total):
@@ -434,15 +451,16 @@
     half = jax.ShapeDtypeStruct((HALF, QUARTER), BF16)
     full = jax.ShapeDtypeStruct((256, QUARTER), BF16)
     kept_shape = jax.ShapeDtypeStruct((256, QUARTER), F32)
-    up, down = multiply(far_kernel, far_heads, weights, (), [half, half], "far")
+    up, down = multiply(far_kernel, far_heads, weights, [half, half], "far")
     relays = (shift_by(up, "x", 1), shift_by(down, "x", 3))
-    pos, _ = lax.optimization_barrier((pos, near))
-    kept = attend(6, 2, pos, q, kv, got, prior_key, prior_value)
+    pos, *_ = lax.optimization_barrier((pos, near, up))
+    kept = attend(6, 2, pos, q, kv, got, prior_key, prior_value, MEDIUM)
     kept_heads = [kept, *from_line([kept] * 3)]
-    kept, *relays = lax.optimization_barrier((kept, *relays))
-    up, down = multiply(near_kernel, near_heads, weights, relays, [full, full], "near")
+    *near_heads, _ = lax.optimization_barrier((*near_heads, kept))
+    up, down = multiply(near_kernel, near_heads, weights, [full, full], "near", LARGE)
+    up, down = relay(relays, up, down)
     up, down = shift_by(up, "x", 1), shift_by(down, "x", 3)
-    kept = multiply(keep_kernel, kept_heads, weights, (), kept_shape, "keep")
+    kept = multiply(keep_kernel, kept_heads, weights, kept_shape, "keep")
     own, *others = total_step(pos, kept, up, down)
     return finish(pos, own, *from_line(others), own_tokens, post_gain)
 

time: 94.1 us -> 89.5 us (0.951)
  waiting for transfers between devices: 26.1 us -> 20.9 us
    ppermute x19, waiting for transfers between devices: 24.3 us -> 19 us  [shift_by(): return lax.ppermute(array, axis, [(i, (i + steps) % 4) for i in range(4)])]
    pallas_call x3 -> x4, Pallas kernels: 3.77 us -> 4.26 us  [the longest x3 3.77 us: multiply(): pl.pallas_call(kernel, in_specs=[VMEM] * 6, out_specs=jax.tree.map(lambda...]
  transfers between devices with their start and end apart: 23 -> 23, of which waited for: 14 -> 12; matrix products, arithmetic and copies ran while one was open for 0% -> 0% of each run, Pallas kernels for 25% -> 30%
where the time goes in v7:
time: 89.5 us; the launch traced here: 89.2 us
  Pallas kernels  33.7 us (38%)
  starting transfers between devices  33.6 us (38%)
  waiting for transfers between devices  20.9 us (23%)
    ppermute x19, starting transfers between devices, shift_by(): return lax.ppermute(array, axis, [(i, (i + steps) % 4) for i in range(4)])  29.4 us
    ppermute x19, waiting for transfers between devices, shift_by(): return lax.ppermute(array, axis, [(i, (i + steps) % 4) for i in range(4)])  19 us
    pallas_call x1, Pallas kernels, key_value(): pl.pallas_call(key_value_kernel, grid_spec=pltpu.PrefetchScalarGridSpec(n...  11.3 us
    pallas_call x3, Pallas kernels, attend(): pl.pallas_call(functools.partial(attend_kernel, first_part), in_specs=[pl...  6.86 us
    pallas_call x1, Pallas kernels, query(): pl.pallas_call(query_kernel, grid_spec=pltpu.PrefetchScalarGridSpec(num_s...  5.69 us
    pallas_call x3, Pallas kernels, multiply(): pl.pallas_call(kernel, in_specs=[VMEM] * 6, out_specs=jax.tree.map(lambda...  3.77 us
    ppermute x3, starting transfers between devices, per_device(): swapped = [lax.ppermute(part, 'c', [(0, 1), (1, 0)]) for part in lines]  2.87 us
    pallas_call x1, Pallas kernels, pick(): pl.pallas_call(pick_kernel, in_specs=[SMEM, ANY], out_specs=[VMEM] * 4, o...  2.04 us
  transfers between devices with their start and end apart: 23, of which 12 were waited for; matrix products, arithmetic and copies ran while one was open for 0% of the time, Pallas kernels for 30%

profile of v7, /device:TPU:0, one launch (start us, length us, event | category | flops | bytes accessed | tf_op | source)
XLA Modules:
  0.0 89.2 jit_solution(15160706154447673437)
XLA Ops:
  0.7 2.0 %pick.1 = (bf16[256,1408]{1,0:T(8,128)(2,1)S(1)}, bf16[128,1408]{1,0:T(8,128)(2,1)S(1)}, bf16[128,1408]{1,0:T(8,128)(2,1)S(1)}, bf16[128,1408]{1,0:T(8,128)(2,1)S(1)}) custom-call(s32[12]{0:T(128)S(1)} %dynamic-slice_bitcast_fusion.pos_ref, bf16[256,5376]{1,0:T(8,128)(2,1)} %w_ref.2), custom_call_target="tpu_custom_call" | custom-call | tf_op jit(solution)/shard_map/pick/pallas_call | solution.py:273
  2.8 2.1 %collective-permute-start = (bf16[128,1408]{1,0:T(8,128)(2,1)S(1)}, bf16[128,1408]{1,0:T(8,128)(2,1)S(1)}, u32[]{:S(2)}, u32[]{:S(2)}) collective-permute-start(bf16[128,1408]{1,0:T(8,128)(2,1)S(1)} %get-tuple-element.50), channel_id=1, source_target_pairs={{0,1},{1,2},{2,3},{3,0},{4,5},{5,6},{6,7},{7,4},{8,9},{9,10},{10,1... | collective-permute-start | bytes 1081352 | tf_op jit(solution)/shard_map/ppermute | solution.py:417
  4.8 2.2 %collective-permute-start.1 = (bf16[128,1408]{1,0:T(8,128)(2,1)S(1)}, bf16[128,1408]{1,0:T(8,128)(2,1)S(1)}, u32[]{:S(2)}, u32[]{:S(2)}) collective-permute-start(bf16[128,1408]{1,0:T(8,128)(2,1)S(1)} %get-tuple-element.51), channel_id=1, source_target_pairs={{0,3},{1,0},{2,1},{3,2},{4,7},{5,4},{6,5},{7,6},{8,11},{9,8},{10,9... | collective-permute-start | bytes 1081352 | tf_op jit(solution)/shard_map/ppermute | solution.py:417
  7.0 1.8 %collective-permute-start.2 = (bf16[128,1408]{1,0:T(8,128)(2,1)S(1)}, bf16[128,1408]{1,0:T(8,128)(2,1)S(1)}, u32[]{:S(2)}, u32[]{:S(2)}) collective-permute-start(bf16[128,1408]{1,0:T(8,128)(2,1)S(1)} %get-tuple-element.52), channel_id=1, source_target_pairs={{0,2},{1,3},{2,0},{3,1},{4,6},{5,7},{6,4},{7,5},{8,10},{9,11},{10,... | collective-permute-start | bytes 1081352 | tf_op jit(solution)/shard_map/ppermute | solution.py:417
  8.9 11.3 %key_value.1 = (bf16[1024,5376]{1,0:T(8,128)(2,1)S(1)}, bf16[1024,256]{1,0:T(8,128)(2,1)S(1)}, bf16[64,5376]{1,0:T(8,128)(2,1)S(1)}) custom-call(s32[12]{0:T(128)S(1)} %dynamic-slice_bitcast_fusion.pos_ref, bf16[1024,5376]{1,0:T(8,128)(2,1)} %tok_ref.1, f32[1,5376]{1,0:T(1,128)S(1)} %reshape.16.g_ref, bf16[5376,128]{1,0:T(8,128)(2,1)} %wk_ref.1, ...), custom_call_target="tpu_custom_call" | custom-call | flops 11274289152 | bytes 27262976 | tf_op jit(solution)/shard_map/key_value/pallas_call | solution.py:140
  20.2 1.3 %collective-permute-start.6 = (bf16[1024,256]{1,0:T(8,128)(2,1)S(1)}, bf16[1024,256]{1,0:T(8,128)(2,1)S(1)}, u32[]{:S(2)}, u32[]{:S(2)}) collective-permute-start(bf16[1024,256]{1,0:T(8,128)(2,1)S(1)} %get-tuple-element.58.kv_ref), channel_id=1, source_target_pairs={{0,16},{16,32},{32,48},{48,64},{64,80},{80,96},{96,112},{1,17},{17... | collective-permute-start | bytes 1572872 | tf_op jit(solution)/shard_map/ppermute | solution.py:436
  21.5 5.7 %query.1.q_ref = bf16[1024,256]{1,0:T(8,128)(2,1)S(1)} custom-call(s32[12]{0:T(128)S(1)} %dynamic-slice_bitcast_fusion.pos_ref, bf16[1024,5376]{1,0:T(8,128)(2,1)S(1)} %get-tuple-element.49.normed_ref, bf16[5376,256]{1,0:T(8,128)(2,1)S(1)} %copy-done, f32[1,128]{1,0:T(1,128)S(1)} %bitcast.4, f32[8192,128]{1,0:T(8,128)} %constant.32.clone.tab_ref), custom_call_target="tpu_custom_call" | custom-call | tf_op jit(solution)/shard_map/query/pallas_call | solution.py:177
  27.3 2.4 %collective-permute-start.3 = (bf16[128,1408]{1,0:T(8,128)(2,1)S(1)}, bf16[128,1408]{1,0:T(8,128)(2,1)S(1)}, u32[]{:S(2)}, u32[]{:S(2)}) collective-permute-start(bf16[128,1408]{1,0:T(8,128)(2,1)S(1)} %collective-permute-done.refs_0_), channel_id=1, source_target_pairs={{0,16},{16,0},{1,17},{17,1},{2,18},{18,2},{3,19},{19,3},{4,20},{20... | collective-permute-start | bytes 1081352 | tf_op jit(solution)/shard_map/ppermute | solution.py:439
  32.0 1.9 %attend.3.refs_0_ = bf16[256,256]{1,0:T(8,128)(2,1)S(1)} custom-call(s32[12]{0:T(128)S(1)} %dynamic-slice_bitcast_fusion.pos_ref, bf16[1024,256]{1,0:T(8,128)(2,1)S(1)} %query.1.q_ref, bf16[1024,256]{1,0:T(8,128)(2,1)S(1)} %get-tuple-element.58.kv_ref, bf16[1024,256]{1,0:T(8,128)(2,1)S(1)} %collective-permute-done.6.got_ref, ...), custom_call_target="tpu_custom_call" | custom-call | tf_op jit(solution)/shard_map/attend/pallas_call | solution.py:237
  33.9 1.1 %collective-permute-start.7 = (bf16[256,256]{1,0:T(8,128)(2,1)S(1)}, bf16[256,256]{1,0:T(8,128)(2,1)S(1)}, u32[]{:S(2)}, u32[]{:S(2)}) collective-permute-start(bf16[256,256]{1,0:T(8,128)(2,1)S(1)} %attend.3.refs_0_), channel_id=1, source_target_pairs={{0,1},{1,2},{2,3},{3,0},{4,5},{5,6},{6,7},{7,4},{8,9},{9,10},{10,1... | collective-permute-start | bytes 393224 | tf_op jit(solution)/shard_map/ppermute | solution.py:417
  35.0 2.2 %collective-permute-start.8 = (bf16[256,256]{1,0:T(8,128)(2,1)S(1)}, bf16[256,256]{1,0:T(8,128)(2,1)S(1)}, u32[]{:S(2)}, u32[]{:S(2)}) collective-permute-start(bf16[256,256]{1,0:T(8,128)(2,1)S(1)} %attend.3.refs_0_), channel_id=1, source_target_pairs={{0,3},{1,0},{2,1},{3,2},{4,7},{5,4},{6,5},{7,6},{8,11},{9,8},{10,9... | collective-permute-start | bytes 393224 | tf_op jit(solution)/shard_map/ppermute | solution.py:417
  37.8 3.0 %attend.4.refs_0_ = bf16[512,256]{1,0:T(8,128)(2,1)S(1)} custom-call(s32[12]{0:T(128)S(1)} %dynamic-slice_bitcast_fusion.pos_ref, bf16[1024,256]{1,0:T(8,128)(2,1)S(1)} %query.1.q_ref, bf16[1024,256]{1,0:T(8,128)(2,1)S(1)} %get-tuple-element.58.kv_ref, bf16[1024,256]{1,0:T(8,128)(2,1)S(1)} %collective-permute-done.6.got_ref, ...), custom_call_target="tpu_custom_call" | custom-call | tf_op jit(solution)/shard_map/attend/pallas_call | solution.py:237
  41.1 2.9 %collective-permute-start.16 = (bf16[512,256]{1,0:T(8,128)(2,1)S(1)}, bf16[512,256]{1,0:T(8,128)(2,1)S(1)}, u32[]{:S(2)}, u32[]{:S(2)}) collective-permute-start(bf16[512,256]{1,0:T(8,128)(2,1)S(1)} %attend.4.refs_0_), channel_id=1, source_target_pairs={{0,3},{1,0},{2,1},{3,2},{4,7},{5,4},{6,5},{7,6},{8,11},{9,8},{10,9... | collective-permute-start | bytes 786440 | tf_op jit(solution)/shard_map/ppermute | solution.py:417
  44.8 2.0 %collective-permute-start.17 = (bf16[512,256]{1,0:T(8,128)(2,1)S(1)}, bf16[512,256]{1,0:T(8,128)(2,1)S(1)}, u32[]{:S(2)}, u32[]{:S(2)}) collective-permute-start(bf16[512,256]{1,0:T(8,128)(2,1)S(1)} %attend.4.refs_0_), channel_id=1, source_target_pairs={{0,2},{1,3},{2,0},{3,1},{4,6},{5,7},{6,4},{7,5},{8,10},{9,11},{10,... | collective-permute-start | bytes 786440 | tf_op jit(solution)/shard_map/ppermute | solution.py:417
  46.8 1.0 %far.1 = (bf16[128,1408]{1,0:T(8,128)(2,1)S(1)}, bf16[128,1408]{1,0:T(8,128)(2,1)S(1)}) custom-call(bf16[256,256]{1,0:T(8,128)(2,1)S(1)} %attend.3.refs_0_, bf16[256,256]{1,0:T(8,128)(2,1)S(1)} %collective-permute-done.7.refs_1_, bf16[256,256]{1,0:T(8,128)(2,1)S(1)} %collective-permute-done.8.refs_2_, bf16[256,256]{1,0:T(8,128)(2,1)S(1)} %collective-permute-done.9.refs_3_, ...), custom_call_target="tpu_custom_call" | custom-call | tf_op jit(solution)/shard_map/far/pallas_call | solution.py:347
  47.8 1.6 %collective-permute-start.13 = (bf16[128,1408]{1,0:T(8,128)(2,1)S(1)}, bf16[128,1408]{1,0:T(8,128)(2,1)S(1)}, u32[]{:S(2)}, u32[]{:S(2)}) collective-permute-start(bf16[128,1408]{1,0:T(8,128)(2,1)S(1)} %get-tuple-element.69), channel_id=1, source_target_pairs={{0,4},{4,8},{8,12},{12,0},{1,5},{5,9},{9,13},{13,1},{2,6},{6,10},{... | collective-permute-start | bytes 1081352 | tf_op jit(solution)/shard_map/ppermute | solution.py:417
  49.4 1.7 %collective-permute-start.14 = (bf16[128,1408]{1,0:T(8,128)(2,1)S(1)}, bf16[128,1408]{1,0:T(8,128)(2,1)S(1)}, u32[]{:S(2)}, u32[]{:S(2)}) collective-permute-start(bf16[128,1408]{1,0:T(8,128)(2,1)S(1)} %get-tuple-element.71), channel_id=1, source_target_pairs={{0,12},{4,0},{8,4},{12,8},{1,13},{5,1},{9,5},{13,9},{2,14},{6,2},{... | collective-permute-start | bytes 1081352 | tf_op jit(solution)/shard_map/ppermute | solution.py:417
  51.1 1.9 %attend.5.refs_0_ = bf16[256,256]{1,0:T(8,128)(2,1)S(1)} custom-call(s32[12]{0:T(128)S(1)} %dynamic-slice_bitcast_fusion.pos_ref, bf16[1024,256]{1,0:T(8,128)(2,1)S(1)} %query.1.q_ref, bf16[1024,256]{1,0:T(8,128)(2,1)S(1)} %get-tuple-element.58.kv_ref, bf16[1024,256]{1,0:T(8,128)(2,1)S(1)} %collective-permute-done.6.got_ref, ...), custom_call_target="tpu_custom_call" | custom-call | flops 4000000000 | tf_op jit(solution)/shard_map/attend/pallas_call | solution.py:237
  53.1 1.7 %collective-permute-done.16.refs_2_ = bf16[512,256]{1,0:T(8,128)(2,1)S(1)} collective-permute-done((bf16[512,256]{1,0:T(8,128)(2,1)S(1)}, bf16[512,256]{1,0:T(8,128)(2,1)S(1)}, u32[]{:S(2)}, u32[]{:S(2)}) %collective-permute-start.16) | collective-permute-done | bytes 262176 | tf_op jit(solution)/shard_map/ppermute | solution.py:417
  55.6 1.8 %near.1 = (bf16[256,1408]{1,0:T(8,128)(2,1)S(1)}, bf16[256,1408]{1,0:T(8,128)(2,1)S(1)}) custom-call(bf16[512,256]{1,0:T(8,128)(2,1)S(1)} %attend.4.refs_0_, bf16[512,256]{1,0:T(8,128)(2,1)S(1)} %collective-permute-done.15.refs_1_, bf16[512,256]{1,0:T(8,128)(2,1)S(1)} %collective-permute-done.16.refs_2_, ...), custom_call_target="tpu_custom_call" | custom-call | flops 30000001024 | tf_op jit(solution)/shard_map/near/pallas_call | solution.py:347
  58.7 1.6 %collective-permute-start.18 = (bf16[256,1408]{1,0:T(8,128)(2,1)S(1)}, bf16[256,1408]{1,0:T(8,128)(2,1)S(1)}, u32[]{:S(2)}, u32[]{:S(2)}) collective-permute-start(bf16[256,1408]{1,0:T(8,128)(2,1)S(1)} %get-tuple-element.78), channel_id=1, source_target_pairs={{0,4},{4,8},{8,12},{12,0},{1,5},{5,9},{9,13},{13,1},{2,6},{6,10},{... | collective-permute-start | bytes 2162696 | tf_op jit(solution)/shard_map/ppermute | solution.py:417
  60.2 1.7 %collective-permute-start.19 = (bf16[256,1408]{1,0:T(8,128)(2,1)S(1)}, bf16[256,1408]{1,0:T(8,128)(2,1)S(1)}, u32[]{:S(2)}, u32[]{:S(2)}) collective-permute-start(bf16[256,1408]{1,0:T(8,128)(2,1)S(1)} %get-tuple-element.79), channel_id=1, source_target_pairs={{0,12},{4,0},{8,4},{12,8},{1,13},{5,1},{9,5},{13,9},{2,14},{6,2},{... | collective-permute-start | bytes 2162696 | tf_op jit(solution)/shard_map/ppermute | solution.py:417
  62.6 2.7 %collective-permute-start.11 = (bf16[256,256]{1,0:T(8,128)(2,1)S(1)}, bf16[256,256]{1,0:T(8,128)(2,1)S(1)}, u32[]{:S(2)}, u32[]{:S(2)}) collective-permute-start(bf16[256,256]{1,0:T(8,128)(2,1)S(1)} %attend.5.refs_0_), channel_id=1, source_target_pairs={{0,3},{1,0},{2,1},{3,2},{4,7},{5,4},{6,5},{7,6},{8,11},{9,8},{10,9... | collective-permute-start | bytes 393224 | tf_op jit(solution)/shard_map/ppermute | solution.py:417
  65.8 3.2 %collective-permute-done.10.refs_1_ = bf16[256,256]{1,0:T(8,128)(2,1)S(1)} collective-permute-done((bf16[256,256]{1,0:T(8,128)(2,1)S(1)}, bf16[256,256]{1,0:T(8,128)(2,1)S(1)}, u32[]{:S(2)}, u32[]{:S(2)}) %collective-permute-start.10) | collective-permute-done | bytes 131104 | tf_op jit(solution)/shard_map/ppermute | solution.py:417
  69.0 2.7 %collective-permute-done.12.refs_3_ = bf16[256,256]{1,0:T(8,128)(2,1)S(1)} collective-permute-done((bf16[256,256]{1,0:T(8,128)(2,1)S(1)}, bf16[256,256]{1,0:T(8,128)(2,1)S(1)}, u32[]{:S(2)}, u32[]{:S(2)}) %collective-permute-start.12) | collective-permute-done | bytes 131104 | tf_op jit(solution)/shard_map/ppermute | solution.py:417
  71.7 1.0 %keep.1.kept_ref = f32[256,1408]{1,0:T(8,128)S(1)} custom-call(bf16[256,256]{1,0:T(8,128)(2,1)S(1)} %attend.5.refs_0_, bf16[256,256]{1,0:T(8,128)(2,1)S(1)} %collective-permute-done.10.refs_1_, bf16[256,256]{1,0:T(8,128)(2,1)S(1)} %collective-permute-done.11.refs_2_, bf16[256,256]{1,0:T(8,128)(2,1)S(1)} %collective-permute-done.12.refs_3_, ...), custom_call_target="tpu_custom_call" | custom-call | tf_op jit(solution)/shard_map/keep/pallas_call | solution.py:347
  72.7 3.3 %collective-permute-done.18.up_ref = bf16[256,1408]{1,0:T(8,128)(2,1)S(1)} collective-permute-done((bf16[256,1408]{1,0:T(8,128)(2,1)S(1)}, bf16[256,1408]{1,0:T(8,128)(2,1)S(1)}, u32[]{:S(2)}, u32[]{:S(2)}) %collective-permute-start.18) | collective-permute-done | bytes 720928 | tf_op jit(solution)/shard_map/ppermute | solution.py:417
  76.0 1.0 %total_step.1 = (f32[64,1408]{1,0:T(8,128)S(1)}, bf16[64,1408]{1,0:T(8,128)(2,1)S(1)}, bf16[64,1408]{1,0:T(8,128)(2,1)S(1)}, bf16[64,1408]{1,0:T(8,128)(2,1)S(1)}) custom-call(s32[12]{0:T(128)S(1)} %dynamic-slice_bitcast_fusion.pos_ref, f32[256,1408]{1,0:T(8,128)S(1)} %keep.1.kept_ref, bf16[256,1408]{1,0:T(8,128)(2,1)S(1)} %collective-permute-done.18.up_ref, ...), custom_call_target="tpu_custom_call" | custom-call | tf_op jit(solution)/shard_map/total_step/pallas_call | solution.py:373
  77.9 2.3 %collective-permute-start.21 = (bf16[64,1408]{1,0:T(8,128)(2,1)S(1)}, bf16[64,1408]{1,0:T(8,128)(2,1)S(1)}, u32[]{:S(2)}, u32[]{:S(2)}) collective-permute-start(bf16[64,1408]{1,0:T(8,128)(2,1)S(1)} %get-tuple-element.82), channel_id=1, source_target_pairs={{0,3},{1,0},{2,1},{3,2},{4,7},{5,4},{6,5},{7,6},{8,11},{9,8},{10,9... | collective-permute-start | bytes 540680 | tf_op jit(solution)/shard_map/ppermute | solution.py:417
  80.8 4.0 %collective-permute-done.20.next_ref = bf16[64,1408]{1,0:T(8,128)(2,1)S(1)} collective-permute-done((bf16[64,1408]{1,0:T(8,128)(2,1)S(1)}, bf16[64,1408]{1,0:T(8,128)(2,1)S(1)}, u32[]{:S(2)}, u32[]{:S(2)}) %collective-permute-start.20) | collective-permute-done | bytes 180256 | tf_op jit(solution)/shard_map/ppermute | solution.py:417
  85.3 2.0 %collective-permute-done.22.far_ref = bf16[64,1408]{1,0:T(8,128)(2,1)S(1)} collective-permute-done((bf16[64,1408]{1,0:T(8,128)(2,1)S(1)}, bf16[64,1408]{1,0:T(8,128)(2,1)S(1)}, u32[]{:S(2)}, u32[]{:S(2)}) %collective-permute-start.22) | collective-permute-done | bytes 180256 | tf_op jit(solution)/shard_map/ppermute | solution.py:417
  87.3 1.9 %finish.1 = bf16[64,5376]{1,0:T(8,128)(2,1)} custom-call(s32[12]{0:T(128)S(1)} %dynamic-slice_bitcast_fusion.pos_ref, f32[64,1408]{1,0:T(8,128)S(1)} %get-tuple-element.80.own_ref, bf16[64,1408]{1,0:T(8,128)(2,1)S(1)} %collective-permute-done.20.next_ref, bf16[64,1408]{1,0:T(8,128)(2,1)S(1)} %collective-permute-done.21.last_ref, ...), custom_call_target="tpu_custom_call" | custom-call | tf_op jit(solution)/shard_map/finish/pallas_call | solution.py:404
  (44 shorter events, 9.9 us)
Async XLA Ops:
  0.0 8.8 %copy-start.5 = (f32[5376]{0:T(1024)S(1)}, f32[5376]{0:T(1024)}, u32[]{:S(2)}) copy-start(f32[5376]{0:T(1024)} %param.14) | copy-start | bytes 64516
  0.0 8.8 %copy-start.4 = (f32[128]{0:T(128)S(1)}, f32[128]{0:T(128)}, u32[]{:S(2)}) copy-start(f32[128]{0:T(128)} %param.19) | copy-start | bytes 1540
  2.8 24.5 %collective-permute-start = (bf16[128,1408]{1,0:T(8,128)(2,1)S(1)}, bf16[128,1408]{1,0:T(8,128)(2,1)S(1)}, u32[]{:S(2)}, u32[]{:S(2)}) collective-permute-start(bf16[128,1408]{1,0:T(8,128)(2,1)S(1)} %get-tuple-element.50), channel_id=1, source_target_pairs={{0,1},{1,2},{2,3},{3,0},{4,5},{5,6},{6,7},{7,4},{8,9},{9,10},{10,1... | collective-permute-start | bytes 1081352 | tf_op jit(solution)/shard_map/ppermute | solution.py:417
  4.8 22.4 %collective-permute-start.1 = (bf16[128,1408]{1,0:T(8,128)(2,1)S(1)}, bf16[128,1408]{1,0:T(8,128)(2,1)S(1)}, u32[]{:S(2)}, u32[]{:S(2)}) collective-permute-start(bf16[128,1408]{1,0:T(8,128)(2,1)S(1)} %get-tuple-element.51), channel_id=1, source_target_pairs={{0,3},{1,0},{2,1},{3,2},{4,7},{5,4},{6,5},{7,6},{8,11},{9,8},{10,9... | collective-permute-start | bytes 1081352 | tf_op jit(solution)/shard_map/ppermute | solution.py:417
  7.0 20.2 %collective-permute-start.2 = (bf16[128,1408]{1,0:T(8,128)(2,1)S(1)}, bf16[128,1408]{1,0:T(8,128)(2,1)S(1)}, u32[]{:S(2)}, u32[]{:S(2)}) collective-permute-start(bf16[128,1408]{1,0:T(8,128)(2,1)S(1)} %get-tuple-element.52), channel_id=1, source_target_pairs={{0,2},{1,3},{2,0},{3,1},{4,6},{5,7},{6,4},{7,5},{8,10},{9,11},{10,... | collective-permute-start | bytes 1081352 | tf_op jit(solution)/shard_map/ppermute | solution.py:417
  8.8 12.7 %copy-start = (bf16[5376,256]{1,0:T(8,128)(2,1)S(1)}, bf16[5376,256]{1,0:T(8,128)(2,1)}, u32[]{:S(2)}) copy-start(bf16[5376,256]{1,0:T(8,128)(2,1)} %w_ref.3) | copy-start | bytes 8257540
  8.9 12.7 %copy-start.3 = (f32[128]{0:T(128)S(1)}, f32[128]{0:T(128)}, u32[]{:S(2)}) copy-start(f32[128]{0:T(128)} %param.18) | copy-start | bytes 1540
  20.2 11.8 %collective-permute-start.6 = (bf16[1024,256]{1,0:T(8,128)(2,1)S(1)}, bf16[1024,256]{1,0:T(8,128)(2,1)S(1)}, u32[]{:S(2)}, u32[]{:S(2)}) collective-permute-start(bf16[1024,256]{1,0:T(8,128)(2,1)S(1)} %get-tuple-element.58.kv_ref), channel_id=1, source_target_pairs={{0,16},{16,32},{32,48},{48,64},{64,80},{80,96},{96,112},{1,17},{17... | collective-permute-start | bytes 1572872 | tf_op jit(solution)/shard_map/ppermute | solution.py:436
  21.5 10.4 %copy-start.1 = (bf16[1024,128]{1,0:T(8,128)(2,1)S(1)}, bf16[1024,128]{1,0:T(8,128)(2,1)}, u32[]{:S(2)}) copy-start(bf16[1024,128]{1,0:T(8,128)(2,1)} %pk_ref.5) | copy-start | bytes 786436
  21.5 10.4 %copy-start.2 = (bf16[1024,128]{1,0:T(8,128)(2,1)S(1)}, bf16[1024,128]{1,0:T(8,128)(2,1)}, u32[]{:S(2)}) copy-start(bf16[1024,128]{1,0:T(8,128)(2,1)} %pv_ref.5) | copy-start | bytes 786436
  27.3 3.7 %collective-permute-start.3 = (bf16[128,1408]{1,0:T(8,128)(2,1)S(1)}, bf16[128,1408]{1,0:T(8,128)(2,1)S(1)}, u32[]{:S(2)}, u32[]{:S(2)}) collective-permute-start(bf16[128,1408]{1,0:T(8,128)(2,1)S(1)} %collective-permute-done.refs_0_), channel_id=1, source_target_pairs={{0,16},{16,0},{1,17},{17,1},{2,18},{18,2},{3,19},{19,3},{4,20},{20... | collective-permute-start | bytes 1081352 | tf_op jit(solution)/shard_map/ppermute | solution.py:439
  29.6 1.8 %collective-permute-start.4 = (bf16[128,1408]{1,0:T(8,128)(2,1)S(1)}, bf16[128,1408]{1,0:T(8,128)(2,1)S(1)}, u32[]{:S(2)}, u32[]{:S(2)}) collective-permute-start(bf16[128,1408]{1,0:T(8,128)(2,1)S(1)} %collective-permute-done.1.refs_1_), channel_id=1, source_target_pairs={{0,16},{16,0},{1,17},{17,1},{2,18},{18,2},{3,19},{19,3},{4,20},{20... | collective-permute-start | bytes 1081352 | tf_op jit(solution)/shard_map/ppermute | solution.py:439
  29.7 2.2 %collective-permute-start.5 = (bf16[128,1408]{1,0:T(8,128)(2,1)S(1)}, bf16[128,1408]{1,0:T(8,128)(2,1)S(1)}, u32[]{:S(2)}, u32[]{:S(2)}) collective-permute-start(bf16[128,1408]{1,0:T(8,128)(2,1)S(1)} %collective-permute-done.2.refs_2_), channel_id=1, source_target_pairs={{0,16},{16,0},{1,17},{17,1},{2,18},{18,2},{3,19},{19,3},{4,20},{20... | collective-permute-start | bytes 1081352 | tf_op jit(solution)/shard_map/ppermute | solution.py:439
  33.9 10.8 %collective-permute-start.7 = (bf16[256,256]{1,0:T(8,128)(2,1)S(1)}, bf16[256,256]{1,0:T(8,128)(2,1)S(1)}, u32[]{:S(2)}, u32[]{:S(2)}) collective-permute-start(bf16[256,256]{1,0:T(8,128)(2,1)S(1)} %attend.3.refs_0_), channel_id=1, source_target_pairs={{0,1},{1,2},{2,3},{3,0},{4,5},{5,6},{6,7},{7,4},{8,9},{9,10},{10,1... | collective-permute-start | bytes 393224 | tf_op jit(solution)/shard_map/ppermute | solution.py:417
  35.0 11.8 %collective-permute-start.8 = (bf16[256,256]{1,0:T(8,128)(2,1)S(1)}, bf16[256,256]{1,0:T(8,128)(2,1)S(1)}, u32[]{:S(2)}, u32[]{:S(2)}) collective-permute-start(bf16[256,256]{1,0:T(8,128)(2,1)S(1)} %attend.3.refs_0_), channel_id=1, source_target_pairs={{0,3},{1,0},{2,1},{3,2},{4,7},{5,4},{6,5},{7,6},{8,11},{9,8},{10,9... | collective-permute-start | bytes 393224 | tf_op jit(solution)/shard_map/ppermute | solution.py:417
  37.2 9.6 %collective-permute-start.9 = (bf16[256,256]{1,0:T(8,128)(2,1)S(1)}, bf16[256,256]{1,0:T(8,128)(2,1)S(1)}, u32[]{:S(2)}, u32[]{:S(2)}) collective-permute-start(bf16[256,256]{1,0:T(8,128)(2,1)S(1)} %attend.3.refs_0_), channel_id=1, source_target_pairs={{0,2},{1,3},{2,0},{3,1},{4,6},{5,7},{6,4},{7,5},{8,10},{9,11},{10,... | collective-permute-start | bytes 393224 | tf_op jit(solution)/shard_map/ppermute | solution.py:417
  40.7 12.3 %collective-permute-start.15 = (bf16[512,256]{1,0:T(8,128)(2,1)S(1)}, bf16[512,256]{1,0:T(8,128)(2,1)S(1)}, u32[]{:S(2)}, u32[]{:S(2)}) collective-permute-start(bf16[512,256]{1,0:T(8,128)(2,1)S(1)} %attend.4.refs_0_), channel_id=1, source_target_pairs={{0,1},{1,2},{2,3},{3,0},{4,5},{5,6},{6,7},{7,4},{8,9},{9,10},{10,1... | collective-permute-start | bytes 786440 | tf_op jit(solution)/shard_map/ppermute | solution.py:417
  41.1 13.6 %collective-permute-start.16 = (bf16[512,256]{1,0:T(8,128)(2,1)S(1)}, bf16[512,256]{1,0:T(8,128)(2,1)S(1)}, u32[]{:S(2)}, u32[]{:S(2)}) collective-permute-start(bf16[512,256]{1,0:T(8,128)(2,1)S(1)} %attend.4.refs_0_), channel_id=1, source_target_pairs={{0,3},{1,0},{2,1},{3,2},{4,7},{5,4},{6,5},{7,6},{8,11},{9,8},{10,9... | collective-permute-start | bytes 786440 | tf_op jit(solution)/shard_map/ppermute | solution.py:417
  44.8 10.9 %collective-permute-start.17 = (bf16[512,256]{1,0:T(8,128)(2,1)S(1)}, bf16[512,256]{1,0:T(8,128)(2,1)S(1)}, u32[]{:S(2)}, u32[]{:S(2)}) collective-permute-start(bf16[512,256]{1,0:T(8,128)(2,1)S(1)} %attend.4.refs_0_), channel_id=1, source_target_pairs={{0,2},{1,3},{2,0},{3,1},{4,6},{5,7},{6,4},{7,5},{8,10},{9,11},{10,... | collective-permute-start | bytes 786440 | tf_op jit(solution)/shard_map/ppermute | solution.py:417
  47.8 10.4 %collective-permute-start.13 = (bf16[128,1408]{1,0:T(8,128)(2,1)S(1)}, bf16[128,1408]{1,0:T(8,128)(2,1)S(1)}, u32[]{:S(2)}, u32[]{:S(2)}) collective-permute-start(bf16[128,1408]{1,0:T(8,128)(2,1)S(1)} %get-tuple-element.69), channel_id=1, source_target_pairs={{0,4},{4,8},{8,12},{12,0},{1,5},{5,9},{9,13},{13,1},{2,6},{6,10},{... | collective-permute-start | bytes 1081352 | tf_op jit(solution)/shard_map/ppermute | solution.py:417
  49.4 8.8 %collective-permute-start.14 = (bf16[128,1408]{1,0:T(8,128)(2,1)S(1)}, bf16[128,1408]{1,0:T(8,128)(2,1)S(1)}, u32[]{:S(2)}, u32[]{:S(2)}) collective-permute-start(bf16[128,1408]{1,0:T(8,128)(2,1)S(1)} %get-tuple-element.71), channel_id=1, source_target_pairs={{0,12},{4,0},{8,4},{12,8},{1,13},{5,1},{9,5},{13,9},{2,14},{6,2},{... | collective-permute-start | bytes 1081352 | tf_op jit(solution)/shard_map/ppermute | solution.py:417
  58.7 17.3 %collective-permute-start.18 = (bf16[256,1408]{1,0:T(8,128)(2,1)S(1)}, bf16[256,1408]{1,0:T(8,128)(2,1)S(1)}, u32[]{:S(2)}, u32[]{:S(2)}) collective-permute-start(bf16[256,1408]{1,0:T(8,128)(2,1)S(1)} %get-tuple-element.78), channel_id=1, source_target_pairs={{0,4},{4,8},{8,12},{12,0},{1,5},{5,9},{9,13},{13,1},{2,6},{6,10},{... | collective-permute-start | bytes 2162696 | tf_op jit(solution)/shard_map/ppermute | solution.py:417
  60.2 20.6 %copy-start.6 = (f32[5376]{0:T(1024)S(1)}, f32[5376]{0:T(1024)}, u32[]{:S(2)}) copy-start(f32[5376]{0:T(1024)} %param.23) | copy-start | bytes 64516
  60.2 15.8 %collective-permute-start.19 = (bf16[256,1408]{1,0:T(8,128)(2,1)S(1)}, bf16[256,1408]{1,0:T(8,128)(2,1)S(1)}, u32[]{:S(2)}, u32[]{:S(2)}) collective-permute-start(bf16[256,1408]{1,0:T(8,128)(2,1)S(1)} %get-tuple-element.79), channel_id=1, source_target_pairs={{0,12},{4,0},{8,4},{12,8},{1,13},{5,1},{9,5},{13,9},{2,14},{6,2},{... | collective-permute-start | bytes 2162696 | tf_op jit(solution)/shard_map/ppermute | solution.py:417
  62.0 7.0 %collective-permute-start.10 = (bf16[256,256]{1,0:T(8,128)(2,1)S(1)}, bf16[256,256]{1,0:T(8,128)(2,1)S(1)}, u32[]{:S(2)}, u32[]{:S(2)}) collective-permute-start(bf16[256,256]{1,0:T(8,128)(2,1)S(1)} %attend.5.refs_0_), channel_id=1, source_target_pairs={{0,1},{1,2},{2,3},{3,0},{4,5},{5,6},{6,7},{7,4},{8,9},{9,10},{10,1... | collective-permute-start | bytes 393224 | tf_op jit(solution)/shard_map/ppermute | solution.py:417
  62.6 6.4 %collective-permute-start.11 = (bf16[256,256]{1,0:T(8,128)(2,1)S(1)}, bf16[256,256]{1,0:T(8,128)(2,1)S(1)}, u32[]{:S(2)}, u32[]{:S(2)}) collective-permute-start(bf16[256,256]{1,0:T(8,128)(2,1)S(1)} %attend.5.refs_0_), channel_id=1, source_target_pairs={{0,3},{1,0},{2,1},{3,2},{4,7},{5,4},{6,5},{7,6},{8,11},{9,8},{10,9... | collective-permute-start | bytes 393224 | tf_op jit(solution)/shard_map/ppermute | solution.py:417
  65.2 6.5 %collective-permute-start.12 = (bf16[256,256]{1,0:T(8,128)(2,1)S(1)}, bf16[256,256]{1,0:T(8,128)(2,1)S(1)}, u32[]{:S(2)}, u32[]{:S(2)}) collective-permute-start(bf16[256,256]{1,0:T(8,128)(2,1)S(1)} %attend.5.refs_0_), channel_id=1, source_target_pairs={{0,2},{1,3},{2,0},{3,1},{4,6},{5,7},{6,4},{7,5},{8,10},{9,11},{10,... | collective-permute-start | bytes 393224 | tf_op jit(solution)/shard_map/ppermute | solution.py:417
  77.0 7.8 %collective-permute-start.20 = (bf16[64,1408]{1,0:T(8,128)(2,1)S(1)}, bf16[64,1408]{1,0:T(8,128)(2,1)S(1)}, u32[]{:S(2)}, u32[]{:S(2)}) collective-permute-start(bf16[64,1408]{1,0:T(8,128)(2,1)S(1)} %get-tuple-element.81), channel_id=1, source_target_pairs={{0,1},{1,2},{2,3},{3,0},{4,5},{5,6},{6,7},{7,4},{8,9},{9,10},{10,1... | collective-permute-start | bytes 540680 | tf_op jit(solution)/shard_map/ppermute | solution.py:417
  77.9 7.3 %collective-permute-start.21 = (bf16[64,1408]{1,0:T(8,128)(2,1)S(1)}, bf16[64,1408]{1,0:T(8,128)(2,1)S(1)}, u32[]{:S(2)}, u32[]{:S(2)}) collective-permute-start(bf16[64,1408]{1,0:T(8,128)(2,1)S(1)} %get-tuple-element.82), channel_id=1, source_target_pairs={{0,3},{1,0},{2,1},{3,2},{4,7},{5,4},{6,5},{7,6},{8,11},{9,8},{10,9... | collective-permute-start | bytes 540680 | tf_op jit(solution)/shard_map/ppermute | solution.py:417
  80.3 7.0 %collective-permute-start.22 = (bf16[64,1408]{1,0:T(8,128)(2,1)S(1)}, bf16[64,1408]{1,0:T(8,128)(2,1)S(1)}, u32[]{:S(2)}, u32[]{:S(2)}) collective-permute-start(bf16[64,1408]{1,0:T(8,128)(2,1)S(1)} %get-tuple-element.83), channel_id=1, source_target_pairs={{0,2},{1,3},{2,0},{3,1},{4,6},{5,7},{6,4},{7,5},{8,10},{9,11},{10,... | collective-permute-start | bytes 540680 | tf_op jit(solution)/shard_map/ppermute | solution.py:417

commit v8 on v7

--- a/solution.py
+++ b/solution.py
@@ -68,97 +68,91 @@
     return (u * cosine + pltpu.roll(u, 64, 1) * sine).astype(BF16)
 
 
+def table_copy(pos_ref, tab_ref, table, sem):
+    rows = pl.ds(pl.multiple_of(pos_ref[0] * SHARD, SHARD), SHARD)
+    return pltpu.make_async_copy(tab_ref.at[rows], table, sem)
+
+
 def key_value_kernel(
     pos_ref, tok_ref, g_ref, wk_ref, wv_ref, gain_ref, tab_ref,
-    normed, kv_ref, own_ref, w_all, g_all, sems,
+    normed, kv_ref, own_ref, tok, w_all, g_all, table, sems, tok_sems,
 ):
-    step = pl.program_id(0)
     copies = [
         pltpu.make_async_copy(wk_ref, w_all.at[:, 0:128], sems.at[0]),
         pltpu.make_async_copy(wv_ref, w_all.at[:, 128:256], sems.at[1]),
+        table_copy(pos_ref, tab_ref, table, sems.at[2]),
     ]
+
+    def tile_copy(i):
+        rows = pl.ds(pl.multiple_of(i * ROWS, ROWS), ROWS)
+        return pltpu.make_async_copy(tok_ref.at[rows], tok.at[rows], tok_sems.at[i])
+
+    tile_copy(0).start()
+    for copy in copies:
+        copy.start()
+    for i in range(1, SHARD // ROWS):
+        tile_copy(i).start()
+    g_all[...] = jnp.broadcast_to(g_ref[...], g_all.shape)
     blocks = MODEL_WIDTH // 128
 
-    def norm_group(i, carry):
-        at = i * GROUP if isinstance(i, int) else pl.multiple_of(i * GROUP, GROUP)
-        rows = pl.ds(at, GROUP)
+    def norm_group(first):
+        rows = pl.ds(pl.multiple_of(first, GROUP), GROUP)
         parts = [jnp.zeros((GROUP, 128), F32) for _ in range(2)]
         for b in range(blocks):
-            v = tok_ref[rows, b * 128 : (b + 1) * 128].astype(F32)
+            v = tok[rows, b * 128 : (b + 1) * 128].astype(F32)
             parts[b % 2] = parts[b % 2] + v * v
         mean = jnp.sum(parts[0] + parts[1], axis=-1, keepdims=True) * (1.0 / MODEL_WIDTH)
         r = jnp.broadcast_to(lax.rsqrt(mean + EPSILON), (GROUP, 128))
         for b in range(blocks):
             cols = slice(b * 128, (b + 1) * 128)
-            v = tok_ref[rows, cols].astype(F32)
+            v = tok[rows, cols].astype(F32)
             normed[rows, cols] = (v * r * g_all[:, cols]).astype(BF16)
+
+    def tile(i, carry):
+        tile_copy(i).wait()
+        for j in range(ROWS // GROUP):
+            norm_group(i * ROWS + j * GROUP)
+
+        @pl.when(i == 0)
+        def _():
+            for copy in copies:
+                copy.wait()
+
+        rows = pl.ds(pl.multiple_of(i * ROWS, ROWS), ROWS)
+        raw = jnp.dot(normed[rows, :], w_all[...], preferred_element_type=F32)
+        kv_ref[rows, 0:128] = rotate(raw[:, 0:128], gain_ref[...], table[rows, :])
+        kv_ref[rows, 128:256] = raw[:, 128:256].astype(BF16)
         return carry
 
-    def multiply_and_rotate():
-        raw = jnp.dot(normed[...], w_all[...], preferred_element_type=F32)
-        kv_ref[:, 0:128] = rotate(raw[:, 0:128], gain_ref[...], tab_ref[...])
-        kv_ref[:, 128:256] = raw[:, 128:256].astype(BF16)
-
-    @pl.when(step == 0)
-    def _():
-        for copy in copies:
-            copy.start()
-        g_all[...] = jnp.broadcast_to(g_ref[...], g_all.shape)
-        lax.fori_loop(0, ROWS // GROUP, norm_group, 0, unroll=4)
-        for copy in copies:
-            copy.wait()
-        multiply_and_rotate()
-
-    @pl.when(step != 0)
-    def _():
-        for i in range(ROWS // GROUP):
-            norm_group(i, 0)
-        multiply_and_rotate()
-
-    @pl.when(step == pos_ref[ROW_AT + 8])
-    def _():
-        own_ref[...] = tok_ref[pl.ds(pl.multiple_of(pos_ref[1] * 64, 64), 64), :]
+    lax.fori_loop(0, SHARD // ROWS, tile, 0)
+    first = pos_ref[ROW_AT + 8] * ROWS + pos_ref[1] * 64
+    own_ref[...] = tok[pl.ds(pl.multiple_of(first, 64), 64), :]
 
 
 def in_hbm(*arrays):
     return [pltpu.with_memory_space_constraint(array, pltpu.HBM) for array in arrays]
 
 
-def whole(shape):
-    return pl.BlockSpec(shape, lambda i, s: (0, 0))
-
-
-def row_tile(width):
-    return pl.BlockSpec((ROWS, width), lambda i, s: (i, 0))
-
-
-TABLE_TILE = pl.BlockSpec((ROWS, 128), lambda i, s: (s[0] * (SHARD // ROWS) + i, 0))
-
-
 def key_value(pos, tokens, pre_gain, wk, wv, gain, table):
     tokens, wk, wv, table = in_hbm(tokens, wk, wv, table)
     return pl.pallas_call(
         key_value_kernel,
-        grid_spec=pltpu.PrefetchScalarGridSpec(
-            num_scalar_prefetch=1,
-            grid=(SHARD // ROWS,),
-            in_specs=[
-                row_tile(MODEL_WIDTH), whole((1, MODEL_WIDTH)), ANY, ANY,
-                whole((1, 128)), TABLE_TILE,
-            ],
-            out_specs=[row_tile(MODEL_WIDTH), row_tile(256), whole((64, MODEL_WIDTH))],
-            scratch_shapes=[
-                pltpu.VMEM((MODEL_WIDTH, 256), BF16),
-                pltpu.VMEM((GROUP, MODEL_WIDTH), F32),
-                pltpu.SemaphoreType.DMA((2,)),
-            ],
-        ),
+        in_specs=[SMEM, ANY, VMEM, ANY, ANY, VMEM, ANY],
+        out_specs=[VMEM] * 3,
         out_shape=[
             jax.ShapeDtypeStruct((SHARD, MODEL_WIDTH), BF16),
             jax.ShapeDtypeStruct((SHARD, 256), BF16),
             jax.ShapeDtypeStruct((64, MODEL_WIDTH), BF16),
         ],
-        compiler_params=pltpu.CompilerParams(vmem_limit_bytes=28 << 20),
+        scratch_shapes=[
+            pltpu.VMEM((SHARD, MODEL_WIDTH), BF16),
+            pltpu.VMEM((MODEL_WIDTH, 256), BF16),
+            pltpu.VMEM((GROUP, MODEL_WIDTH), F32),
+            pltpu.VMEM((SHARD, 128), F32),
+            pltpu.SemaphoreType.DMA((3,)),
+            pltpu.SemaphoreType.DMA((SHARD // ROWS,)),
+        ],
+        compiler_params=pltpu.CompilerParams(vmem_limit_bytes=34 << 20),
         cost_estimate=pl.CostEstimate(
             flops=8 * SHARD * MODEL_WIDTH * 256, bytes_accessed=26 << 20, transcendentals=0
         ),
@@ -166,25 +160,25 @@
     )(pos, tokens, pre_gain.reshape(1, -1), wk, wv, gain.reshape(1, -1), table)
 
 
-def query_kernel(pos_ref, normed_ref, w_ref, gain_ref, tab_ref, q_ref):
-    raw = jnp.dot(normed_ref[...], w_ref[...], preferred_element_type=F32)
-    q_ref[:, 0:128] = rotate(raw[:, 0:128], gain_ref[...], tab_ref[...])
-    q_ref[:, 128:256] = rotate(raw[:, 128:256], gain_ref[...], tab_ref[...])
+def query_kernel(pos_ref, normed_ref, w_ref, gain_ref, tab_ref, q_ref, table, sem):
+    copy = table_copy(pos_ref, tab_ref, table, sem)
+    copy.start()
+    copy.wait()
+    for i in range(SHARD // ROWS):
+        rows = slice(i * ROWS, (i + 1) * ROWS)
+        raw = jnp.dot(normed_ref[rows, :], w_ref[...], preferred_element_type=F32)
+        q_ref[rows, 0:128] = rotate(raw[:, 0:128], gain_ref[...], table[rows, :])
+        q_ref[rows, 128:256] = rotate(raw[:, 128:256], gain_ref[...], table[rows, :])
 
 
 def query(pos, normed, wq, gain, table):
     (table,) = in_hbm(table)
     return pl.pallas_call(
         query_kernel,
-        grid_spec=pltpu.PrefetchScalarGridSpec(
-            num_scalar_prefetch=1,
-            grid=(SHARD // ROWS,),
-            in_specs=[
-                row_tile(MODEL_WIDTH), whole((MODEL_WIDTH, 256)), whole((1, 128)), TABLE_TILE
-            ],
-            out_specs=row_tile(256),
-        ),
+        in_specs=[SMEM, VMEM, VMEM, VMEM, ANY],
+        out_specs=VMEM,
         out_shape=jax.ShapeDtypeStruct((SHARD, 256), BF16),
+        scratch_shapes=[pltpu.VMEM((SHARD, 128), F32), pltpu.SemaphoreType.DMA(())],
         compiler_params=pltpu.CompilerParams(vmem_limit_bytes=24 << 20),
         cost_estimate=SMALL,
         name="query",
@@ -382,9 +376,9 @@
     )(pos, kept, up, down)
 
 
-def finish_kernel(pos_ref, own_ref, next_ref, last_ref, far_ref, tok_ref, g_ref, out_ref, line):
+def finish_kernel(pos_ref, own_ref, far_ref, last_ref, next_ref, tok_ref, g_ref, out_ref, line):
     z = pos_ref[1]
-    for shift, ref in ((0, own_ref), (3, next_ref), (1, last_ref), (2, far_ref)):
+    for shift, ref in ((0, own_ref), (2, far_ref), (3, last_ref), (1, next_ref)):
         line[:, pl.ds(quarter_start((z + shift) % 4), QUARTER)] = ref[...].astype(F32)
     for i in range(4):
         rows = slice(i * 16, (i + 1) * 16)
@@ -400,7 +394,7 @@
             out_ref[rows, cols] = (tok_ref[rows, cols].astype(F32) + normed).astype(BF16)
 
 
-def finish(pos, own, nxt, last, far, own_tokens, gain):
+def finish(pos, own, far, last, nxt, own_tokens, gain):
     return pl.pallas_call(
         finish_kernel,
         in_specs=[SMEM] + [VMEM] * 6,
@@ -410,7 +404,7 @@
         compiler_params=pltpu.CompilerParams(vmem_limit_bytes=16 << 20),
         cost_estimate=SMALL,
         name="finish",
-    )(pos, own, nxt, last, far, own_tokens, gain.reshape(1, -1))
+    )(pos, own, far, last, nxt, own_tokens, gain.reshape(1, -1))
 
 
 def shift_by(array, axis, steps):
@@ -418,7 +412,8 @@
 
 
 def from_line(pieces):
-    return [shift_by(piece, "z", by) for piece, by in zip(pieces, (1, 3, 2), strict=True)]
+    after, before, across = pieces
+    return [shift_by(across, "z", 2), shift_by(after, "z", 1), shift_by(before, "z", 3)]
 
 
 def per_device(

time: 89.5 us -> 93.2 us (1.041)
  starting transfers between devices: 33.6 us -> 36.4 us
  Pallas kernels: 33.7 us -> 34.9 us
    ppermute x19, starting transfers between devices: 29.4 us -> 32.2 us  [shift_by(): return lax.ppermute(array, axis, [(i, (i + steps) % 4) for i in range(4)])]
    pallas_call x2, Pallas kernels: 17 us -> 18.2 us  [the longest x1 13.2 us: key_value(): pl.pallas_call(key_value_kernel, in_specs=[SMEM, ANY, VMEM, ANY, ANY, VME...]
  transfers between devices with their start and end apart: 23 -> 23, of which waited for: 12 -> 10; matrix products, arithmetic and copies ran while one was open for 0% -> 0% of each run, Pallas kernels for 30% -> 30%
where the time goes in v8:
time: 93.2 us; the launch traced here: 93 us
  starting transfers between devices  36.4 us (39%)
  Pallas kernels  34.9 us (37%)
  waiting for transfers between devices  20.8 us (22%)
    ppermute x19, starting transfers between devices, shift_by(): return lax.ppermute(array, axis, [(i, (i + steps) % 4) for i in range(4)])  32.2 us
    ppermute x19, waiting for transfers between devices, shift_by(): return lax.ppermute(array, axis, [(i, (i + steps) % 4) for i in range(4)])  18.9 us
    pallas_call x1, Pallas kernels, key_value(): pl.pallas_call(key_value_kernel, in_specs=[SMEM, ANY, VMEM, ANY, ANY, VME...  13.2 us
    pallas_call x3, Pallas kernels, attend(): pl.pallas_call(functools.partial(attend_kernel, first_part), in_specs=[pl...  6.87 us
    pallas_call x1, Pallas kernels, query(): pl.pallas_call(query_kernel, in_specs=[SMEM, VMEM, VMEM, VMEM, ANY], out_...  4.93 us
    pallas_call x3, Pallas kernels, multiply(): pl.pallas_call(kernel, in_specs=[VMEM] * 6, out_specs=jax.tree.map(lambda...  3.77 us
    ppermute x3, starting transfers between devices, per_device(): swapped = [lax.ppermute(part, 'c', [(0, 1), (1, 0)]) for part in lines]  2.87 us
    pallas_call x1, Pallas kernels, pick(): pl.pallas_call(pick_kernel, in_specs=[SMEM, ANY], out_specs=[VMEM] * 4, o...  2.04 us
  transfers between devices with their start and end apart: 23, of which 10 were waited for; matrix products, arithmetic and copies ran while one was open for 0% of the time, Pallas kernels for 30%

profile of v8, /device:TPU:0, one launch (start us, length us, event | category | flops | bytes accessed | tf_op | source)
XLA Modules:
  0.0 93.0 jit_solution(17544498811889121988)
XLA Ops:
  0.7 2.0 %pick.1 = (bf16[256,1408]{1,0:T(8,128)(2,1)S(1)}, bf16[128,1408]{1,0:T(8,128)(2,1)S(1)}, bf16[128,1408]{1,0:T(8,128)(2,1)S(1)}, bf16[128,1408]{1,0:T(8,128)(2,1)S(1)}) custom-call(s32[12]{0:T(128)S(1)} %dynamic-slice_bitcast_fusion.pos_ref, bf16[256,5376]{1,0:T(8,128)(2,1)} %w_ref.2), custom_call_target="tpu_custom_call" | custom-call | tf_op jit(solution)/shard_map/pick/pallas_call | solution.py:267
  2.8 4.0 %collective-permute-start = (bf16[128,1408]{1,0:T(8,128)(2,1)S(1)}, bf16[128,1408]{1,0:T(8,128)(2,1)S(1)}, u32[]{:S(2)}, u32[]{:S(2)}) collective-permute-start(bf16[128,1408]{1,0:T(8,128)(2,1)S(1)} %get-tuple-element.50), channel_id=1, source_target_pairs={{0,2},{1,3},{2,0},{3,1},{4,6},{5,7},{6,4},{7,5},{8,10},{9,11},{10,... | collective-permute-start | bytes 1081352 | tf_op jit(solution)/shard_map/ppermute | solution.py:411
  6.8 1.0 %collective-permute-start.1 = (bf16[128,1408]{1,0:T(8,128)(2,1)S(1)}, bf16[128,1408]{1,0:T(8,128)(2,1)S(1)}, u32[]{:S(2)}, u32[]{:S(2)}) collective-permute-start(bf16[128,1408]{1,0:T(8,128)(2,1)S(1)} %get-tuple-element.51), channel_id=1, source_target_pairs={{0,1},{1,2},{2,3},{3,0},{4,5},{5,6},{6,7},{7,4},{8,9},{9,10},{10,1... | collective-permute-start | bytes 1081352 | tf_op jit(solution)/shard_map/ppermute | solution.py:411
  7.8 2.2 %collective-permute-start.2 = (bf16[128,1408]{1,0:T(8,128)(2,1)S(1)}, bf16[128,1408]{1,0:T(8,128)(2,1)S(1)}, u32[]{:S(2)}, u32[]{:S(2)}) collective-permute-start(bf16[128,1408]{1,0:T(8,128)(2,1)S(1)} %get-tuple-element.52), channel_id=1, source_target_pairs={{0,3},{1,0},{2,1},{3,2},{4,7},{5,4},{6,5},{7,6},{8,11},{9,8},{10,9... | collective-permute-start | bytes 1081352 | tf_op jit(solution)/shard_map/ppermute | solution.py:411
  10.1 13.2 %key_value.1 = (bf16[1024,5376]{1,0:T(8,128)(2,1)S(1)}, bf16[1024,256]{1,0:T(8,128)(2,1)S(1)}, bf16[64,5376]{1,0:T(8,128)(2,1)S(1)}) custom-call(s32[12]{0:T(128)S(1)} %dynamic-slice_bitcast_fusion.pos_ref, bf16[1024,5376]{1,0:T(8,128)(2,1)} %tok_ref.1, f32[1,5376]{1,0:T(1,128)S(1)} %reshape.16.g_ref, bf16[5376,128]{1,0:T(8,128)(2,1)} %wk_ref.1, ...), custom_call_target="tpu_custom_call" | custom-call | flops 11274289152 | bytes 27262976 | tf_op jit(solution)/shard_map/key_value/pallas_call | solution.py:138
  23.3 1.3 %collective-permute-start.6 = (bf16[1024,256]{1,0:T(8,128)(2,1)S(1)}, bf16[1024,256]{1,0:T(8,128)(2,1)S(1)}, u32[]{:S(2)}, u32[]{:S(2)}) collective-permute-start(bf16[1024,256]{1,0:T(8,128)(2,1)S(1)} %get-tuple-element.58.kv_ref), channel_id=1, source_target_pairs={{0,16},{16,32},{32,48},{48,64},{64,80},{80,96},{96,112},{1,17},{17... | collective-permute-start | bytes 1572872 | tf_op jit(solution)/shard_map/ppermute | solution.py:431
  24.7 4.9 %query.1.q_ref = bf16[1024,256]{1,0:T(8,128)(2,1)S(1)} custom-call(s32[12]{0:T(128)S(1)} %dynamic-slice_bitcast_fusion.pos_ref, bf16[1024,5376]{1,0:T(8,128)(2,1)S(1)} %get-tuple-element.49.normed_ref, bf16[5376,256]{1,0:T(8,128)(2,1)S(1)} %copy-done, f32[1,128]{1,0:T(1,128)S(1)} %bitcast.4, f32[8192,128]{1,0:T(8,128)} %constant.32.clone.tab_ref), custom_call_target="tpu_custom_call" | custom-call | tf_op jit(solution)/shard_map/query/pallas_call | solution.py:176
  29.7 2.4 %collective-permute-start.3 = (bf16[128,1408]{1,0:T(8,128)(2,1)S(1)}, bf16[128,1408]{1,0:T(8,128)(2,1)S(1)}, u32[]{:S(2)}, u32[]{:S(2)}) collective-permute-start(bf16[128,1408]{1,0:T(8,128)(2,1)S(1)} %collective-permute-done.refs_0_), channel_id=1, source_target_pairs={{0,16},{16,0},{1,17},{17,1},{2,18},{18,2},{3,19},{19,3},{4,20},{20... | collective-permute-start | bytes 1081352 | tf_op jit(solution)/shard_map/ppermute | solution.py:434
  34.4 2.0 %attend.3.refs_0_ = bf16[256,256]{1,0:T(8,128)(2,1)S(1)} custom-call(s32[12]{0:T(128)S(1)} %dynamic-slice_bitcast_fusion.pos_ref, bf16[1024,256]{1,0:T(8,128)(2,1)S(1)} %query.1.q_ref, bf16[1024,256]{1,0:T(8,128)(2,1)S(1)} %get-tuple-element.58.kv_ref, bf16[1024,256]{1,0:T(8,128)(2,1)S(1)} %collective-permute-done.6.got_ref, ...), custom_call_target="tpu_custom_call" | custom-call | tf_op jit(solution)/shard_map/attend/pallas_call | solution.py:231
  37.3 2.5 %collective-permute-start.9 = (bf16[256,256]{1,0:T(8,128)(2,1)S(1)}, bf16[256,256]{1,0:T(8,128)(2,1)S(1)}, u32[]{:S(2)}, u32[]{:S(2)}) collective-permute-start(bf16[256,256]{1,0:T(8,128)(2,1)S(1)} %attend.3.refs_0_), channel_id=1, source_target_pairs={{0,3},{1,0},{2,1},{3,2},{4,7},{5,4},{6,5},{7,6},{8,11},{9,8},{10,9... | collective-permute-start | bytes 393224 | tf_op jit(solution)/shard_map/ppermute | solution.py:411
  39.8 3.0 %attend.4.refs_0_ = bf16[512,256]{1,0:T(8,128)(2,1)S(1)} custom-call(s32[12]{0:T(128)S(1)} %dynamic-slice_bitcast_fusion.pos_ref, bf16[1024,256]{1,0:T(8,128)(2,1)S(1)} %query.1.q_ref, bf16[1024,256]{1,0:T(8,128)(2,1)S(1)} %get-tuple-element.58.kv_ref, bf16[1024,256]{1,0:T(8,128)(2,1)S(1)} %collective-permute-done.6.got_ref, ...), custom_call_target="tpu_custom_call" | custom-call | tf_op jit(solution)/shard_map/attend/pallas_call | solution.py:231
  42.7 2.3 %collective-permute-start.15 = (bf16[512,256]{1,0:T(8,128)(2,1)S(1)}, bf16[512,256]{1,0:T(8,128)(2,1)S(1)}, u32[]{:S(2)}, u32[]{:S(2)}) collective-permute-start(bf16[512,256]{1,0:T(8,128)(2,1)S(1)} %attend.4.refs_0_), channel_id=1, source_target_pairs={{0,2},{1,3},{2,0},{3,1},{4,6},{5,7},{6,4},{7,5},{8,10},{9,11},{10,... | collective-permute-start | bytes 786440 | tf_op jit(solution)/shard_map/ppermute | solution.py:411
  45.8 3.3 %collective-permute-start.17 = (bf16[512,256]{1,0:T(8,128)(2,1)S(1)}, bf16[512,256]{1,0:T(8,128)(2,1)S(1)}, u32[]{:S(2)}, u32[]{:S(2)}) collective-permute-start(bf16[512,256]{1,0:T(8,128)(2,1)S(1)} %attend.4.refs_0_), channel_id=1, source_target_pairs={{0,3},{1,0},{2,1},{3,2},{4,7},{5,4},{6,5},{7,6},{8,11},{9,8},{10,9... | collective-permute-start | bytes 786440 | tf_op jit(solution)/shard_map/ppermute | solution.py:411
  50.1 1.5 %collective-permute-start.13 = (bf16[128,1408]{1,0:T(8,128)(2,1)S(1)}, bf16[128,1408]{1,0:T(8,128)(2,1)S(1)}, u32[]{:S(2)}, u32[]{:S(2)}) collective-permute-start(bf16[128,1408]{1,0:T(8,128)(2,1)S(1)} %get-tuple-element.69), channel_id=1, source_target_pairs={{0,4},{4,8},{8,12},{12,0},{1,5},{5,9},{9,13},{13,1},{2,6},{6,10},{... | collective-permute-start | bytes 1081352 | tf_op jit(solution)/shard_map/ppermute | solution.py:411
  51.6 1.8 %collective-permute-start.14 = (bf16[128,1408]{1,0:T(8,128)(2,1)S(1)}, bf16[128,1408]{1,0:T(8,128)(2,1)S(1)}, u32[]{:S(2)}, u32[]{:S(2)}) collective-permute-start(bf16[128,1408]{1,0:T(8,128)(2,1)S(1)} %get-tuple-element.71), channel_id=1, source_target_pairs={{0,12},{4,0},{8,4},{12,8},{1,13},{5,1},{9,5},{13,9},{2,14},{6,2},{... | collective-permute-start | bytes 1081352 | tf_op jit(solution)/shard_map/ppermute | solution.py:411
  53.4 2.0 %attend.5.refs_0_ = bf16[256,256]{1,0:T(8,128)(2,1)S(1)} custom-call(s32[12]{0:T(128)S(1)} %dynamic-slice_bitcast_fusion.pos_ref, bf16[1024,256]{1,0:T(8,128)(2,1)S(1)} %query.1.q_ref, bf16[1024,256]{1,0:T(8,128)(2,1)S(1)} %get-tuple-element.58.kv_ref, bf16[1024,256]{1,0:T(8,128)(2,1)S(1)} %collective-permute-done.6.got_ref, ...), custom_call_target="tpu_custom_call" | custom-call | flops 4000000000 | tf_op jit(solution)/shard_map/attend/pallas_call | solution.py:231
  55.3 2.7 %collective-permute-done.16.refs_2_ = bf16[512,256]{1,0:T(8,128)(2,1)S(1)} collective-permute-done((bf16[512,256]{1,0:T(8,128)(2,1)S(1)}, bf16[512,256]{1,0:T(8,128)(2,1)S(1)}, u32[]{:S(2)}, u32[]{:S(2)}) %collective-permute-start.16) | collective-permute-done | bytes 262176 | tf_op jit(solution)/shard_map/ppermute | solution.py:411
  58.0 1.8 %near.1 = (bf16[256,1408]{1,0:T(8,128)(2,1)S(1)}, bf16[256,1408]{1,0:T(8,128)(2,1)S(1)}) custom-call(bf16[512,256]{1,0:T(8,128)(2,1)S(1)} %attend.4.refs_0_, bf16[512,256]{1,0:T(8,128)(2,1)S(1)} %collective-permute-done.15.refs_1_, bf16[512,256]{1,0:T(8,128)(2,1)S(1)} %collective-permute-done.16.refs_2_, ...), custom_call_target="tpu_custom_call" | custom-call | flops 30000001024 | tf_op jit(solution)/shard_map/near/pallas_call | solution.py:341
  60.9 1.6 %collective-permute-start.18 = (bf16[256,1408]{1,0:T(8,128)(2,1)S(1)}, bf16[256,1408]{1,0:T(8,128)(2,1)S(1)}, u32[]{:S(2)}, u32[]{:S(2)}) collective-permute-start(bf16[256,1408]{1,0:T(8,128)(2,1)S(1)} %get-tuple-element.78), channel_id=1, source_target_pairs={{0,4},{4,8},{8,12},{12,0},{1,5},{5,9},{9,13},{13,1},{2,6},{6,10},{... | collective-permute-start | bytes 2162696 | tf_op jit(solution)/shard_map/ppermute | solution.py:411
  62.5 1.8 %collective-permute-start.19 = (bf16[256,1408]{1,0:T(8,128)(2,1)S(1)}, bf16[256,1408]{1,0:T(8,128)(2,1)S(1)}, u32[]{:S(2)}, u32[]{:S(2)}) collective-permute-start(bf16[256,1408]{1,0:T(8,128)(2,1)S(1)} %get-tuple-element.79), channel_id=1, source_target_pairs={{0,12},{4,0},{8,4},{12,8},{1,13},{5,1},{9,5},{13,9},{2,14},{6,2},{... | collective-permute-start | bytes 2162696 | tf_op jit(solution)/shard_map/ppermute | solution.py:411
  64.2 1.2 %collective-permute-start.10 = (bf16[256,256]{1,0:T(8,128)(2,1)S(1)}, bf16[256,256]{1,0:T(8,128)(2,1)S(1)}, u32[]{:S(2)}, u32[]{:S(2)}) collective-permute-start(bf16[256,256]{1,0:T(8,128)(2,1)S(1)} %attend.5.refs_0_), channel_id=1, source_target_pairs={{0,2},{1,3},{2,0},{3,1},{4,6},{5,7},{6,4},{7,5},{8,10},{9,11},{10,... | collective-permute-start | bytes 393224 | tf_op jit(solution)/shard_map/ppermute | solution.py:411
  65.4 3.2 %collective-permute-start.12 = (bf16[256,256]{1,0:T(8,128)(2,1)S(1)}, bf16[256,256]{1,0:T(8,128)(2,1)S(1)}, u32[]{:S(2)}, u32[]{:S(2)}) collective-permute-start(bf16[256,256]{1,0:T(8,128)(2,1)S(1)} %attend.5.refs_0_), channel_id=1, source_target_pairs={{0,3},{1,0},{2,1},{3,2},{4,7},{5,4},{6,5},{7,6},{8,11},{9,8},{10,9... | collective-permute-start | bytes 393224 | tf_op jit(solution)/shard_map/ppermute | solution.py:411
  68.7 2.8 %collective-permute-done.10.refs_1_ = bf16[256,256]{1,0:T(8,128)(2,1)S(1)} collective-permute-done((bf16[256,256]{1,0:T(8,128)(2,1)S(1)}, bf16[256,256]{1,0:T(8,128)(2,1)S(1)}, u32[]{:S(2)}, u32[]{:S(2)}) %collective-permute-start.10) | collective-permute-done | bytes 131104 | tf_op jit(solution)/shard_map/ppermute | solution.py:411
  71.5 1.3 %collective-permute-done.11.refs_2_ = bf16[256,256]{1,0:T(8,128)(2,1)S(1)} collective-permute-done((bf16[256,256]{1,0:T(8,128)(2,1)S(1)}, bf16[256,256]{1,0:T(8,128)(2,1)S(1)}, u32[]{:S(2)}, u32[]{:S(2)}) %collective-permute-start.11) | collective-permute-done | bytes 131104 | tf_op jit(solution)/shard_map/ppermute | solution.py:411
  72.8 1.0 %keep.1.kept_ref = f32[256,1408]{1,0:T(8,128)S(1)} custom-call(bf16[256,256]{1,0:T(8,128)(2,1)S(1)} %attend.5.refs_0_, bf16[256,256]{1,0:T(8,128)(2,1)S(1)} %collective-permute-done.10.refs_1_, bf16[256,256]{1,0:T(8,128)(2,1)S(1)} %collective-permute-done.11.refs_2_, bf16[256,256]{1,0:T(8,128)(2,1)S(1)} %collective-permute-done.12.refs_3_, ...), custom_call_target="tpu_custom_call" | custom-call | tf_op jit(solution)/shard_map/keep/pallas_call | solution.py:341
  73.8 5.9 %collective-permute-done.18.up_ref = bf16[256,1408]{1,0:T(8,128)(2,1)S(1)} collective-permute-done((bf16[256,1408]{1,0:T(8,128)(2,1)S(1)}, bf16[256,1408]{1,0:T(8,128)(2,1)S(1)}, u32[]{:S(2)}, u32[]{:S(2)}) %collective-permute-start.18) | collective-permute-done | bytes 720928 | tf_op jit(solution)/shard_map/ppermute | solution.py:411
  79.7 1.0 %total_step.1 = (f32[64,1408]{1,0:T(8,128)S(1)}, bf16[64,1408]{1,0:T(8,128)(2,1)S(1)}, bf16[64,1408]{1,0:T(8,128)(2,1)S(1)}, bf16[64,1408]{1,0:T(8,128)(2,1)S(1)}) custom-call(s32[12]{0:T(128)S(1)} %dynamic-slice_bitcast_fusion.pos_ref, f32[256,1408]{1,0:T(8,128)S(1)} %keep.1.kept_ref, bf16[256,1408]{1,0:T(8,128)(2,1)S(1)} %collective-permute-done.18.up_ref, ...), custom_call_target="tpu_custom_call" | custom-call | tf_op jit(solution)/shard_map/total_step/pallas_call | solution.py:367
  80.7 1.6 %collective-permute-start.20 = (bf16[64,1408]{1,0:T(8,128)(2,1)S(1)}, bf16[64,1408]{1,0:T(8,128)(2,1)S(1)}, u32[]{:S(2)}, u32[]{:S(2)}) collective-permute-start(bf16[64,1408]{1,0:T(8,128)(2,1)S(1)} %get-tuple-element.81), channel_id=1, source_target_pairs={{0,2},{1,3},{2,0},{3,1},{4,6},{5,7},{6,4},{7,5},{8,10},{9,11},{10,... | collective-permute-start | bytes 540680 | tf_op jit(solution)/shard_map/ppermute | solution.py:411
  82.3 3.2 %collective-permute-start.22 = (bf16[64,1408]{1,0:T(8,128)(2,1)S(1)}, bf16[64,1408]{1,0:T(8,128)(2,1)S(1)}, u32[]{:S(2)}, u32[]{:S(2)}) collective-permute-start(bf16[64,1408]{1,0:T(8,128)(2,1)S(1)} %get-tuple-element.83), channel_id=1, source_target_pairs={{0,3},{1,0},{2,1},{3,2},{4,7},{5,4},{6,5},{7,6},{8,11},{9,8},{10,9... | collective-permute-start | bytes 540680 | tf_op jit(solution)/shard_map/ppermute | solution.py:411
  85.6 3.7 %collective-permute-done.20.far_ref = bf16[64,1408]{1,0:T(8,128)(2,1)S(1)} collective-permute-done((bf16[64,1408]{1,0:T(8,128)(2,1)S(1)}, bf16[64,1408]{1,0:T(8,128)(2,1)S(1)}, u32[]{:S(2)}, u32[]{:S(2)}) %collective-permute-start.20) | collective-permute-done | bytes 180256 | tf_op jit(solution)/shard_map/ppermute | solution.py:411
  89.2 1.9 %collective-permute-done.21.last_ref = bf16[64,1408]{1,0:T(8,128)(2,1)S(1)} collective-permute-done((bf16[64,1408]{1,0:T(8,128)(2,1)S(1)}, bf16[64,1408]{1,0:T(8,128)(2,1)S(1)}, u32[]{:S(2)}, u32[]{:S(2)}) %collective-permute-start.21) | collective-permute-done | bytes 180256 | tf_op jit(solution)/shard_map/ppermute | solution.py:411
  91.1 1.9 %finish.1 = bf16[64,5376]{1,0:T(8,128)(2,1)} custom-call(s32[12]{0:T(128)S(1)} %dynamic-slice_bitcast_fusion.pos_ref, f32[64,1408]{1,0:T(8,128)S(1)} %get-tuple-element.80.own_ref, bf16[64,1408]{1,0:T(8,128)(2,1)S(1)} %collective-permute-done.20.far_ref, bf16[64,1408]{1,0:T(8,128)(2,1)S(1)} %collective-permute-done.21.last_ref, ...), custom_call_target="tpu_custom_call" | custom-call | tf_op jit(solution)/shard_map/finish/pallas_call | solution.py:398
  (44 shorter events, 6.8 us)
Async XLA Ops:
  0.0 10.0 %copy-start.5 = (f32[5376]{0:T(1024)S(1)}, f32[5376]{0:T(1024)}, u32[]{:S(2)}) copy-start(f32[5376]{0:T(1024)} %param.14) | copy-start | bytes 64516
  0.0 10.1 %copy-start.4 = (f32[128]{0:T(128)S(1)}, f32[128]{0:T(128)}, u32[]{:S(2)}) copy-start(f32[128]{0:T(128)} %param.19) | copy-start | bytes 1540
  2.8 26.9 %collective-permute-start = (bf16[128,1408]{1,0:T(8,128)(2,1)S(1)}, bf16[128,1408]{1,0:T(8,128)(2,1)S(1)}, u32[]{:S(2)}, u32[]{:S(2)}) collective-permute-start(bf16[128,1408]{1,0:T(8,128)(2,1)S(1)} %get-tuple-element.50), channel_id=1, source_target_pairs={{0,2},{1,3},{2,0},{3,1},{4,6},{5,7},{6,4},{7,5},{8,10},{9,11},{10,... | collective-permute-start | bytes 1081352 | tf_op jit(solution)/shard_map/ppermute | solution.py:411
  6.8 22.9 %collective-permute-start.1 = (bf16[128,1408]{1,0:T(8,128)(2,1)S(1)}, bf16[128,1408]{1,0:T(8,128)(2,1)S(1)}, u32[]{:S(2)}, u32[]{:S(2)}) collective-permute-start(bf16[128,1408]{1,0:T(8,128)(2,1)S(1)} %get-tuple-element.51), channel_id=1, source_target_pairs={{0,1},{1,2},{2,3},{3,0},{4,5},{5,6},{6,7},{7,4},{8,9},{9,10},{10,1... | collective-permute-start | bytes 1081352 | tf_op jit(solution)/shard_map/ppermute | solution.py:411
  7.8 21.9 %collective-permute-start.2 = (bf16[128,1408]{1,0:T(8,128)(2,1)S(1)}, bf16[128,1408]{1,0:T(8,128)(2,1)S(1)}, u32[]{:S(2)}, u32[]{:S(2)}) collective-permute-start(bf16[128,1408]{1,0:T(8,128)(2,1)S(1)} %get-tuple-element.52), channel_id=1, source_target_pairs={{0,3},{1,0},{2,1},{3,2},{4,7},{5,4},{6,5},{7,6},{8,11},{9,8},{10,9... | collective-permute-start | bytes 1081352 | tf_op jit(solution)/shard_map/ppermute | solution.py:411
  10.1 14.6 %copy-start = (bf16[5376,256]{1,0:T(8,128)(2,1)S(1)}, bf16[5376,256]{1,0:T(8,128)(2,1)}, u32[]{:S(2)}) copy-start(bf16[5376,256]{1,0:T(8,128)(2,1)} %w_ref.3) | copy-start | bytes 8257540
  10.1 14.6 %copy-start.3 = (f32[128]{0:T(128)S(1)}, f32[128]{0:T(128)}, u32[]{:S(2)}) copy-start(f32[128]{0:T(128)} %param.18) | copy-start | bytes 1540
  23.3 11.0 %collective-permute-start.6 = (bf16[1024,256]{1,0:T(8,128)(2,1)S(1)}, bf16[1024,256]{1,0:T(8,128)(2,1)S(1)}, u32[]{:S(2)}, u32[]{:S(2)}) collective-permute-start(bf16[1024,256]{1,0:T(8,128)(2,1)S(1)} %get-tuple-element.58.kv_ref), channel_id=1, source_target_pairs={{0,16},{16,32},{32,48},{48,64},{64,80},{80,96},{96,112},{1,17},{17... | collective-permute-start | bytes 1572872 | tf_op jit(solution)/shard_map/ppermute | solution.py:431
  24.7 9.7 %copy-start.1 = (bf16[1024,128]{1,0:T(8,128)(2,1)S(1)}, bf16[1024,128]{1,0:T(8,128)(2,1)}, u32[]{:S(2)}) copy-start(bf16[1024,128]{1,0:T(8,128)(2,1)} %pk_ref.5) | copy-start | bytes 786436
  24.7 9.7 %copy-start.2 = (bf16[1024,128]{1,0:T(8,128)(2,1)S(1)}, bf16[1024,128]{1,0:T(8,128)(2,1)}, u32[]{:S(2)}) copy-start(bf16[1024,128]{1,0:T(8,128)(2,1)} %pv_ref.5) | copy-start | bytes 786436
  29.7 3.7 %collective-permute-start.3 = (bf16[128,1408]{1,0:T(8,128)(2,1)S(1)}, bf16[128,1408]{1,0:T(8,128)(2,1)S(1)}, u32[]{:S(2)}, u32[]{:S(2)}) collective-permute-start(bf16[128,1408]{1,0:T(8,128)(2,1)S(1)} %collective-permute-done.refs_0_), channel_id=1, source_target_pairs={{0,16},{16,0},{1,17},{17,1},{2,18},{18,2},{3,19},{19,3},{4,20},{20... | collective-permute-start | bytes 1081352 | tf_op jit(solution)/shard_map/ppermute | solution.py:434
  32.0 1.8 %collective-permute-start.4 = (bf16[128,1408]{1,0:T(8,128)(2,1)S(1)}, bf16[128,1408]{1,0:T(8,128)(2,1)S(1)}, u32[]{:S(2)}, u32[]{:S(2)}) collective-permute-start(bf16[128,1408]{1,0:T(8,128)(2,1)S(1)} %collective-permute-done.1.refs_1_), channel_id=1, source_target_pairs={{0,16},{16,0},{1,17},{17,1},{2,18},{18,2},{3,19},{19,3},{4,20},{20... | collective-permute-start | bytes 1081352 | tf_op jit(solution)/shard_map/ppermute | solution.py:434
  32.1 2.2 %collective-permute-start.5 = (bf16[128,1408]{1,0:T(8,128)(2,1)S(1)}, bf16[128,1408]{1,0:T(8,128)(2,1)S(1)}, u32[]{:S(2)}, u32[]{:S(2)}) collective-permute-start(bf16[128,1408]{1,0:T(8,128)(2,1)S(1)} %collective-permute-done.2.refs_2_), channel_id=1, source_target_pairs={{0,16},{16,0},{1,17},{17,1},{2,18},{18,2},{3,19},{19,3},{4,20},{20... | collective-permute-start | bytes 1081352 | tf_op jit(solution)/shard_map/ppermute | solution.py:434
  36.4 9.4 %collective-permute-start.7 = (bf16[256,256]{1,0:T(8,128)(2,1)S(1)}, bf16[256,256]{1,0:T(8,128)(2,1)S(1)}, u32[]{:S(2)}, u32[]{:S(2)}) collective-permute-start(bf16[256,256]{1,0:T(8,128)(2,1)S(1)} %attend.3.refs_0_), channel_id=1, source_target_pairs={{0,2},{1,3},{2,0},{3,1},{4,6},{5,7},{6,4},{7,5},{8,10},{9,11},{10,... | collective-permute-start | bytes 393224 | tf_op jit(solution)/shard_map/ppermute | solution.py:411
  36.4 12.6 %collective-permute-start.8 = (bf16[256,256]{1,0:T(8,128)(2,1)S(1)}, bf16[256,256]{1,0:T(8,128)(2,1)S(1)}, u32[]{:S(2)}, u32[]{:S(2)}) collective-permute-start(bf16[256,256]{1,0:T(8,128)(2,1)S(1)} %attend.3.refs_0_), channel_id=1, source_target_pairs={{0,1},{1,2},{2,3},{3,0},{4,5},{5,6},{6,7},{7,4},{8,9},{9,10},{10,1... | collective-permute-start | bytes 393224 | tf_op jit(solution)/shard_map/ppermute | solution.py:411
  37.3 11.8 %collective-permute-start.9 = (bf16[256,256]{1,0:T(8,128)(2,1)S(1)}, bf16[256,256]{1,0:T(8,128)(2,1)S(1)}, u32[]{:S(2)}, u32[]{:S(2)}) collective-permute-start(bf16[256,256]{1,0:T(8,128)(2,1)S(1)} %attend.3.refs_0_), channel_id=1, source_target_pairs={{0,3},{1,0},{2,1},{3,2},{4,7},{5,4},{6,5},{7,6},{8,11},{9,8},{10,9... | collective-permute-start | bytes 393224 | tf_op jit(solution)/shard_map/ppermute | solution.py:411
  42.7 12.6 %collective-permute-start.15 = (bf16[512,256]{1,0:T(8,128)(2,1)S(1)}, bf16[512,256]{1,0:T(8,128)(2,1)S(1)}, u32[]{:S(2)}, u32[]{:S(2)}) collective-permute-start(bf16[512,256]{1,0:T(8,128)(2,1)S(1)} %attend.4.refs_0_), channel_id=1, source_target_pairs={{0,2},{1,3},{2,0},{3,1},{4,6},{5,7},{6,4},{7,5},{8,10},{9,11},{10,... | collective-permute-start | bytes 786440 | tf_op jit(solution)/shard_map/ppermute | solution.py:411
  45.0 13.0 %collective-permute-start.16 = (bf16[512,256]{1,0:T(8,128)(2,1)S(1)}, bf16[512,256]{1,0:T(8,128)(2,1)S(1)}, u32[]{:S(2)}, u32[]{:S(2)}) collective-permute-start(bf16[512,256]{1,0:T(8,128)(2,1)S(1)} %attend.4.refs_0_), channel_id=1, source_target_pairs={{0,1},{1,2},{2,3},{3,0},{4,5},{5,6},{6,7},{7,4},{8,9},{9,10},{10,1... | collective-permute-start | bytes 786440 | tf_op jit(solution)/shard_map/ppermute | solution.py:411
  45.8 12.3 %collective-permute-start.17 = (bf16[512,256]{1,0:T(8,128)(2,1)S(1)}, bf16[512,256]{1,0:T(8,128)(2,1)S(1)}, u32[]{:S(2)}, u32[]{:S(2)}) collective-permute-start(bf16[512,256]{1,0:T(8,128)(2,1)S(1)} %attend.4.refs_0_), channel_id=1, source_target_pairs={{0,3},{1,0},{2,1},{3,2},{4,7},{5,4},{6,5},{7,6},{8,11},{9,8},{10,9... | collective-permute-start | bytes 786440 | tf_op jit(solution)/shard_map/ppermute | solution.py:411
  50.1 10.4 %collective-permute-start.13 = (bf16[128,1408]{1,0:T(8,128)(2,1)S(1)}, bf16[128,1408]{1,0:T(8,128)(2,1)S(1)}, u32[]{:S(2)}, u32[]{:S(2)}) collective-permute-start(bf16[128,1408]{1,0:T(8,128)(2,1)S(1)} %get-tuple-element.69), channel_id=1, source_target_pairs={{0,4},{4,8},{8,12},{12,0},{1,5},{5,9},{9,13},{13,1},{2,6},{6,10},{... | collective-permute-start | bytes 1081352 | tf_op jit(solution)/shard_map/ppermute | solution.py:411
  51.6 8.8 %collective-permute-start.14 = (bf16[128,1408]{1,0:T(8,128)(2,1)S(1)}, bf16[128,1408]{1,0:T(8,128)(2,1)S(1)}, u32[]{:S(2)}, u32[]{:S(2)}) collective-permute-start(bf16[128,1408]{1,0:T(8,128)(2,1)S(1)} %get-tuple-element.71), channel_id=1, source_target_pairs={{0,12},{4,0},{8,4},{12,8},{1,13},{5,1},{9,5},{13,9},{2,14},{6,2},{... | collective-permute-start | bytes 1081352 | tf_op jit(solution)/shard_map/ppermute | solution.py:411
  60.9 18.8 %collective-permute-start.18 = (bf16[256,1408]{1,0:T(8,128)(2,1)S(1)}, bf16[256,1408]{1,0:T(8,128)(2,1)S(1)}, u32[]{:S(2)}, u32[]{:S(2)}) collective-permute-start(bf16[256,1408]{1,0:T(8,128)(2,1)S(1)} %get-tuple-element.78), channel_id=1, source_target_pairs={{0,4},{4,8},{8,12},{12,0},{1,5},{5,9},{9,13},{13,1},{2,6},{6,10},{... | collective-permute-start | bytes 2162696 | tf_op jit(solution)/shard_map/ppermute | solution.py:411
  62.5 23.1 %copy-start.6 = (f32[5376]{0:T(1024)S(1)}, f32[5376]{0:T(1024)}, u32[]{:S(2)}) copy-start(f32[5376]{0:T(1024)} %param.23) | copy-start | bytes 64516
  62.5 17.2 %collective-permute-start.19 = (bf16[256,1408]{1,0:T(8,128)(2,1)S(1)}, bf16[256,1408]{1,0:T(8,128)(2,1)S(1)}, u32[]{:S(2)}, u32[]{:S(2)}) collective-permute-start(bf16[256,1408]{1,0:T(8,128)(2,1)S(1)} %get-tuple-element.79), channel_id=1, source_target_pairs={{0,12},{4,0},{8,4},{12,8},{1,13},{5,1},{9,5},{13,9},{2,14},{6,2},{... | collective-permute-start | bytes 2162696 | tf_op jit(solution)/shard_map/ppermute | solution.py:411
  64.2 7.3 %collective-permute-start.10 = (bf16[256,256]{1,0:T(8,128)(2,1)S(1)}, bf16[256,256]{1,0:T(8,128)(2,1)S(1)}, u32[]{:S(2)}, u32[]{:S(2)}) collective-permute-start(bf16[256,256]{1,0:T(8,128)(2,1)S(1)} %attend.5.refs_0_), channel_id=1, source_target_pairs={{0,2},{1,3},{2,0},{3,1},{4,6},{5,7},{6,4},{7,5},{8,10},{9,11},{10,... | collective-permute-start | bytes 393224 | tf_op jit(solution)/shard_map/ppermute | solution.py:411
  65.4 7.4 %collective-permute-start.11 = (bf16[256,256]{1,0:T(8,128)(2,1)S(1)}, bf16[256,256]{1,0:T(8,128)(2,1)S(1)}, u32[]{:S(2)}, u32[]{:S(2)}) collective-permute-start(bf16[256,256]{1,0:T(8,128)(2,1)S(1)} %attend.5.refs_0_), channel_id=1, source_target_pairs={{0,1},{1,2},{2,3},{3,0},{4,5},{5,6},{6,7},{7,4},{8,9},{9,10},{10,1... | collective-permute-start | bytes 393224 | tf_op jit(solution)/shard_map/ppermute | solution.py:411
  65.4 7.4 %collective-permute-start.12 = (bf16[256,256]{1,0:T(8,128)(2,1)S(1)}, bf16[256,256]{1,0:T(8,128)(2,1)S(1)}, u32[]{:S(2)}, u32[]{:S(2)}) collective-permute-start(bf16[256,256]{1,0:T(8,128)(2,1)S(1)} %attend.5.refs_0_), channel_id=1, source_target_pairs={{0,3},{1,0},{2,1},{3,2},{4,7},{5,4},{6,5},{7,6},{8,11},{9,8},{10,9... | collective-permute-start | bytes 393224 | tf_op jit(solution)/shard_map/ppermute | solution.py:411
  80.7 8.6 %collective-permute-start.20 = (bf16[64,1408]{1,0:T(8,128)(2,1)S(1)}, bf16[64,1408]{1,0:T(8,128)(2,1)S(1)}, u32[]{:S(2)}, u32[]{:S(2)}) collective-permute-start(bf16[64,1408]{1,0:T(8,128)(2,1)S(1)} %get-tuple-element.81), channel_id=1, source_target_pairs={{0,2},{1,3},{2,0},{3,1},{4,6},{5,7},{6,4},{7,5},{8,10},{9,11},{10,... | collective-permute-start | bytes 540680 | tf_op jit(solution)/shard_map/ppermute | solution.py:411
  82.3 8.8 %collective-permute-start.21 = (bf16[64,1408]{1,0:T(8,128)(2,1)S(1)}, bf16[64,1408]{1,0:T(8,128)(2,1)S(1)}, u32[]{:S(2)}, u32[]{:S(2)}) collective-permute-start(bf16[64,1408]{1,0:T(8,128)(2,1)S(1)} %get-tuple-element.82), channel_id=1, source_target_pairs={{0,1},{1,2},{2,3},{3,0},{4,5},{5,6},{6,7},{7,4},{8,9},{9,10},{10,1... | collective-permute-start | bytes 540680 | tf_op jit(solution)/shard_map/ppermute | solution.py:411
  82.3 8.8 %collective-permute-start.22 = (bf16[64,1408]{1,0:T(8,128)(2,1)S(1)}, bf16[64,1408]{1,0:T(8,128)(2,1)S(1)}, u32[]{:S(2)}, u32[]{:S(2)}) collective-permute-start(bf16[64,1408]{1,0:T(8,128)(2,1)S(1)} %get-tuple-element.83), channel_id=1, source_target_pairs={{0,3},{1,0},{2,1},{3,2},{4,7},{5,4},{6,5},{7,6},{8,11},{9,8},{10,9... | collective-permute-start | bytes 540680 | tf_op jit(solution)/shard_map/ppermute | solution.py:411

commit v9 on v7

--- a/solution.py
+++ b/solution.py
@@ -166,25 +166,30 @@
     )(pos, tokens, pre_gain.reshape(1, -1), wk, wv, gain.reshape(1, -1), table)
 
 
-def query_kernel(pos_ref, normed_ref, w_ref, gain_ref, tab_ref, q_ref):
-    raw = jnp.dot(normed_ref[...], w_ref[...], preferred_element_type=F32)
-    q_ref[:, 0:128] = rotate(raw[:, 0:128], gain_ref[...], tab_ref[...])
-    q_ref[:, 128:256] = rotate(raw[:, 128:256], gain_ref[...], tab_ref[...])
+def table_copy(pos_ref, tab_ref, table, sem):
+    rows = pl.ds(pl.multiple_of(pos_ref[0] * SHARD, SHARD), SHARD)
+    return pltpu.make_async_copy(tab_ref.at[rows], table, sem)
+
+
+def query_kernel(pos_ref, normed_ref, w_ref, gain_ref, tab_ref, q_ref, table, sem):
+    copy = table_copy(pos_ref, tab_ref, table, sem)
+    copy.start()
+    copy.wait()
+    for i in range(SHARD // ROWS):
+        rows = slice(i * ROWS, (i + 1) * ROWS)
+        raw = jnp.dot(normed_ref[rows, :], w_ref[...], preferred_element_type=F32)
+        q_ref[rows, 0:128] = rotate(raw[:, 0:128], gain_ref[...], table[rows, :])
+        q_ref[rows, 128:256] = rotate(raw[:, 128:256], gain_ref[...], table[rows, :])
 
 
 def query(pos, normed, wq, gain, table):
     (table,) = in_hbm(table)
     return pl.pallas_call(
         query_kernel,
-        grid_spec=pltpu.PrefetchScalarGridSpec(
-            num_scalar_prefetch=1,
-            grid=(SHARD // ROWS,),
-            in_specs=[
-                row_tile(MODEL_WIDTH), whole((MODEL_WIDTH, 256)), whole((1, 128)), TABLE_TILE
-            ],
-            out_specs=row_tile(256),
-        ),
+        in_specs=[SMEM, VMEM, VMEM, VMEM, ANY],
+        out_specs=VMEM,
         out_shape=jax.ShapeDtypeStruct((SHARD, 256), BF16),
+        scratch_shapes=[pltpu.VMEM((SHARD, 128), F32), pltpu.SemaphoreType.DMA(())],
         compiler_params=pltpu.CompilerParams(vmem_limit_bytes=24 << 20),
         cost_estimate=SMALL,
         name="query",
@@ -253,15 +258,13 @@
     return pl.multiple_of((number * 21 // 2) * 128, 128)
 
 
-def pick_kernel(pos_ref, w_ref, own_ref, next_ref, last_ref, far_ref, sems):
+def pick_kernel(pos_ref, w_ref, next_ref, last_ref, far_ref, sems):
     z = pos_ref[1]
     rows = pl.ds(pl.multiple_of(pos_ref[2] * 128, 128), 128)
     copies = []
     for i, (shift, ref) in enumerate(((1, next_ref), (3, last_ref), (2, far_ref))):
         cols = pl.ds(quarter_start((z + shift) % 4), QUARTER)
         copies.append(pltpu.make_async_copy(w_ref.at[rows, cols], ref, sems.at[i]))
-    cols = pl.ds(quarter_start(z), QUARTER)
-    copies.append(pltpu.make_async_copy(w_ref.at[:, cols], own_ref, sems.at[3]))
     for copy in copies:
         copy.start()
     for copy in copies:
@@ -273,50 +276,55 @@
     return pl.pallas_call(
         pick_kernel,
         in_specs=[SMEM, ANY],
-        out_specs=[VMEM] * 4,
-        out_shape=[jax.ShapeDtypeStruct((256, QUARTER), BF16), part, part, part],
-        scratch_shapes=[pltpu.SemaphoreType.DMA((4,))],
+        out_specs=[VMEM] * 3,
+        out_shape=[part, part, part],
+        scratch_shapes=[pltpu.SemaphoreType.DMA((3,))],
         compiler_params=pltpu.CompilerParams(vmem_limit_bytes=16 << 20),
         cost_estimate=SMALL,
         name="pick",
     )(pos, *in_hbm(w_out))
 
 
-def join_kernel(pos_ref, *refs):
-    c, out_ref = pos_ref[2], refs[6]
+def join_kernel(pos_ref, w_ref, *refs):
+    c, out_ref, sem = pos_ref[2], refs[6], refs[7]
+    cols = pl.ds(quarter_start(pos_ref[1]), QUARTER)
+    copy = pltpu.make_async_copy(w_ref.at[:, cols], out_ref.at[0], sem)
+    copy.start()
     for i in range(3):
-        out_ref[i, pl.ds(pl.multiple_of(c * 128, 128), 128)] = refs[i][...]
-        out_ref[i, pl.ds(pl.multiple_of((1 - c) * 128, 128), 128)] = refs[3 + i][...]
-
-
-def join(pos, lines, swapped):
+        out_ref[1 + i, pl.ds(pl.multiple_of(c * 128, 128), 128)] = refs[i][...]
+        out_ref[1 + i, pl.ds(pl.multiple_of((1 - c) * 128, 128), 128)] = refs[3 + i][...]
+    copy.wait()
+
+
+def join(pos, w_out, lines, swapped):
     return pl.pallas_call(
         join_kernel,
-        in_specs=[SMEM] + [VMEM] * 6,
+        in_specs=[SMEM, ANY] + [VMEM] * 6,
         out_specs=VMEM,
-        out_shape=jax.ShapeDtypeStruct((3, 256, QUARTER), BF16),
+        out_shape=jax.ShapeDtypeStruct((4, 256, QUARTER), BF16),
+        scratch_shapes=[pltpu.SemaphoreType.DMA(())],
         compiler_params=pltpu.CompilerParams(vmem_limit_bytes=16 << 20),
         cost_estimate=SMALL,
         name="join",
-    )(pos, *lines, *swapped)
-
-
-def product(a_refs, w_refs, rows=slice(None)):
-    out = jnp.dot(a_refs[0][rows, :], w_refs[0][...], preferred_element_type=F32)
-    for i in range(3):
-        out = out + jnp.dot(a_refs[1 + i][rows, :], w_refs[1][i], preferred_element_type=F32)
+    )(pos, *in_hbm(w_out), *lines, *swapped)
+
+
+def product(a_refs, w_ref, rows=slice(None)):
+    out = jnp.dot(a_refs[0][rows, :], w_ref[0], preferred_element_type=F32)
+    for i in range(1, 4):
+        out = out + jnp.dot(a_refs[i][rows, :], w_ref[i], preferred_element_type=F32)
     return out
 
 
 def far_kernel(*refs):
-    out = product(refs[0:4], refs[4:6])
-    refs[6][...] = out[0:HALF].astype(BF16)
-    refs[7][...] = out[HALF:].astype(BF16)
+    out = product(refs[0:4], refs[4])
+    refs[5][...] = out[0:HALF].astype(BF16)
+    refs[6][...] = out[HALF:].astype(BF16)
 
 
 def near_kernel(*refs):
-    refs[6][...] = product(refs[0:4], refs[4:6], slice(0, 256)).astype(BF16)
-    refs[7][...] = product(refs[0:4], refs[4:6], slice(256, 512)).astype(BF16)
+    refs[5][...] = product(refs[0:4], refs[4], slice(0, 256)).astype(BF16)
+    refs[6][...] = product(refs[0:4], refs[4], slice(256, 512)).astype(BF16)
 
 
 def relay_kernel(relay_up, relay_down, up_in, down_in, up_ref, down_ref):
@@ -340,19 +348,19 @@
 
 
 def keep_kernel(*refs):
-    refs[6][...] = product(refs[0:4], refs[4:6])
-
-
-def multiply(kernel, pieces, weights, out_shape, name, cost=SMALL):
+    refs[5][...] = product(refs[0:4], refs[4])
+
+
+def multiply(kernel, pieces, weight, out_shape, name, cost=SMALL):
     return pl.pallas_call(
         kernel,
-        in_specs=[VMEM] * 6,
+        in_specs=[VMEM] * 5,
         out_specs=jax.tree.map(lambda _: VMEM, out_shape),
         out_shape=out_shape,
         compiler_params=pltpu.CompilerParams(vmem_limit_bytes=24 << 20),
         cost_estimate=cost,
         name=name,
-    )(*pieces, *weights)
+    )(*pieces, weight)
 
 
 def total_kernel(pos_ref, kept_ref, up_ref, down_ref, own_ref, next_ref, last_ref, far_ref, total):
@@ -427,7 +435,7 @@
 ):
     device = lax.axis_index(("y", "c", "x", "z"))
     pos = lax.dynamic_slice_in_dim(jnp.asarray(places()), device, 1, 0).reshape(-1)
-    own_w, *parts = pick(pos, w_out)
+    parts = pick(pos, w_out)
     pos, *parts = lax.optimization_barrier((pos, *parts))
     lines = from_line(parts)
     normed, kv, own_tokens = key_value(
@@ -446,21 +454,21 @@
     near_heads = [near, *from_line([near] * 3)]
     *far_heads, _ = lax.optimization_barrier((*far_heads, near))
     last_pos, _ = lax.optimization_barrier((pos, near))
-    weights = [own_w, join(last_pos, lines, swapped)]
+    weight = join(last_pos, w_out, lines, swapped)
 
     half = jax.ShapeDtypeStruct((HALF, QUARTER), BF16)
     full = jax.ShapeDtypeStruct((256, QUARTER), BF16)
     kept_shape = jax.ShapeDtypeStruct((256, QUARTER), F32)
-    up, down = multiply(far_kernel, far_heads, weights, [half, half], "far")
+    up, down = multiply(far_kernel, far_heads, weight, [half, half], "far")
     relays = (shift_by(up, "x", 1), shift_by(down, "x", 3))
     pos, *_ = lax.optimization_barrier((pos, near, up))
     kept = attend(6, 2, pos, q, kv, got, prior_key, prior_value, MEDIUM)
     kept_heads = [kept, *from_line([kept] * 3)]
     *near_heads, _ = lax.optimization_barrier((*near_heads, kept))
-    up, down = multiply(near_kernel, near_heads, weights, [full, full], "near", LARGE)
+    up, down = multiply(near_kernel, near_heads, weight, [full, full], "near", LARGE)
     up, down = relay(relays, up, down)
     up, down = shift_by(up, "x", 1), shift_by(down, "x", 3)
-    kept = multiply(keep_kernel, kept_heads, weights, kept_shape, "keep")
+    kept = multiply(keep_kernel, kept_heads, weight, kept_shape, "keep")
     own, *others = total_step(pos, kept, up, down)
     return finish(pos, own, *from_line(others), own_tokens, post_gain)
 

time: 89.5 us -> 89.4 us (level)
  no operation moved by 1% of the time
where the time goes in v9:
time: 89.4 us; the launch traced here: 89 us
  Pallas kernels  33.9 us (38%)
  starting transfers between devices  33.5 us (37%)
  waiting for transfers between devices  20.7 us (23%)
    ppermute x19, starting transfers between devices, shift_by(): return lax.ppermute(array, axis, [(i, (i + steps) % 4) for i in range(4)])  29.3 us
    ppermute x19, waiting for transfers between devices, shift_by(): return lax.ppermute(array, axis, [(i, (i + steps) % 4) for i in range(4)])  18.9 us
    pallas_call x1, Pallas kernels, key_value(): pl.pallas_call(key_value_kernel, grid_spec=pltpu.PrefetchScalarGridSpec(n...  11.3 us
    pallas_call x3, Pallas kernels, attend(): pl.pallas_call(functools.partial(attend_kernel, first_part), in_specs=[pl...  7.04 us
    pallas_call x1, Pallas kernels, query(): pl.pallas_call(query_kernel, in_specs=[SMEM, VMEM, VMEM, VMEM, ANY], out_...  4.93 us
    pallas_call x3, Pallas kernels, multiply(): pl.pallas_call(kernel, in_specs=[VMEM] * 5, out_specs=jax.tree.map(lambda...  3.76 us
    ppermute x3, starting transfers between devices, per_device(): swapped = [lax.ppermute(part, 'c', [(0, 1), (1, 0)]) for part in lines]  2.87 us
    pallas_call x1, Pallas kernels, finish(): pl.pallas_call(finish_kernel, in_specs=[SMEM] + [VMEM] * 6, out_specs=VME...  1.9 us
  transfers between devices with their start and end apart: 23, of which 12 were waited for; matrix products, arithmetic and copies ran while one was open for 0% of the time, Pallas kernels for 30%

profile of v9, /device:TPU:0, one launch (start us, length us, event | category | flops | bytes accessed | tf_op | source)
XLA Modules:
  0.0 89.0 jit_solution(6466387831222701185)
XLA Ops:
  0.7 1.8 %pick.1 = (bf16[128,1408]{1,0:T(8,128)(2,1)S(1)}, bf16[128,1408]{1,0:T(8,128)(2,1)S(1)}, bf16[128,1408]{1,0:T(8,128)(2,1)S(1)}) custom-call(s32[12]{0:T(128)S(1)} %dynamic-slice_bitcast_fusion.pos_ref, bf16[256,5376]{1,0:T(8,128)(2,1)} %w_ref.5), custom_call_target="tpu_custom_call" | custom-call | tf_op jit(solution)/shard_map/pick/pallas_call | solution.py:276
  2.5 2.1 %collective-permute-start = (bf16[128,1408]{1,0:T(8,128)(2,1)S(1)}, bf16[128,1408]{1,0:T(8,128)(2,1)S(1)}, u32[]{:S(2)}, u32[]{:S(2)}) collective-permute-start(bf16[128,1408]{1,0:T(8,128)(2,1)S(1)} %get-tuple-element.49), channel_id=1, source_target_pairs={{0,1},{1,2},{2,3},{3,0},{4,5},{5,6},{6,7},{7,4},{8,9},{9,10},{10,1... | collective-permute-start | bytes 1081352 | tf_op jit(solution)/shard_map/ppermute | solution.py:425
  4.6 2.2 %collective-permute-start.1 = (bf16[128,1408]{1,0:T(8,128)(2,1)S(1)}, bf16[128,1408]{1,0:T(8,128)(2,1)S(1)}, u32[]{:S(2)}, u32[]{:S(2)}) collective-permute-start(bf16[128,1408]{1,0:T(8,128)(2,1)S(1)} %get-tuple-element.50), channel_id=1, source_target_pairs={{0,3},{1,0},{2,1},{3,2},{4,7},{5,4},{6,5},{7,6},{8,11},{9,8},{10,9... | collective-permute-start | bytes 1081352 | tf_op jit(solution)/shard_map/ppermute | solution.py:425
  6.8 1.8 %collective-permute-start.2 = (bf16[128,1408]{1,0:T(8,128)(2,1)S(1)}, bf16[128,1408]{1,0:T(8,128)(2,1)S(1)}, u32[]{:S(2)}, u32[]{:S(2)}) collective-permute-start(bf16[128,1408]{1,0:T(8,128)(2,1)S(1)} %get-tuple-element.51), channel_id=1, source_target_pairs={{0,2},{1,3},{2,0},{3,1},{4,6},{5,7},{6,4},{7,5},{8,10},{9,11},{10,... | collective-permute-start | bytes 1081352 | tf_op jit(solution)/shard_map/ppermute | solution.py:425
  8.6 11.3 %key_value.1 = (bf16[1024,5376]{1,0:T(8,128)(2,1)S(1)}, bf16[1024,256]{1,0:T(8,128)(2,1)S(1)}, bf16[64,5376]{1,0:T(8,128)(2,1)S(1)}) custom-call(s32[12]{0:T(128)S(1)} %dynamic-slice_bitcast_fusion.pos_ref, bf16[1024,5376]{1,0:T(8,128)(2,1)} %tok_ref.1, f32[1,5376]{1,0:T(1,128)S(1)} %reshape.16.g_ref, bf16[5376,128]{1,0:T(8,128)(2,1)} %wk_ref.1, ...), custom_call_target="tpu_custom_call" | custom-call | flops 11274289152 | bytes 27262976 | tf_op jit(solution)/shard_map/key_value/pallas_call | solution.py:140
  19.9 1.3 %collective-permute-start.6 = (bf16[1024,256]{1,0:T(8,128)(2,1)S(1)}, bf16[1024,256]{1,0:T(8,128)(2,1)S(1)}, u32[]{:S(2)}, u32[]{:S(2)}) collective-permute-start(bf16[1024,256]{1,0:T(8,128)(2,1)S(1)} %get-tuple-element.57.kv_ref), channel_id=1, source_target_pairs={{0,16},{16,32},{32,48},{48,64},{64,80},{80,96},{96,112},{1,17},{17... | collective-permute-start | bytes 1572872 | tf_op jit(solution)/shard_map/ppermute | solution.py:444
  21.3 4.9 %query.1.q_ref = bf16[1024,256]{1,0:T(8,128)(2,1)S(1)} custom-call(s32[12]{0:T(128)S(1)} %dynamic-slice_bitcast_fusion.pos_ref, bf16[1024,5376]{1,0:T(8,128)(2,1)S(1)} %get-tuple-element.48.normed_ref, bf16[5376,256]{1,0:T(8,128)(2,1)S(1)} %copy-done, f32[1,128]{1,0:T(1,128)S(1)} %bitcast.4, f32[8192,128]{1,0:T(8,128)} %constant.32.clone.tab_ref), custom_call_target="tpu_custom_call" | custom-call | tf_op jit(solution)/shard_map/query/pallas_call | solution.py:187
  26.3 2.4 %collective-permute-start.3 = (bf16[128,1408]{1,0:T(8,128)(2,1)S(1)}, bf16[128,1408]{1,0:T(8,128)(2,1)S(1)}, u32[]{:S(2)}, u32[]{:S(2)}) collective-permute-start(bf16[128,1408]{1,0:T(8,128)(2,1)S(1)} %collective-permute-done.refs_0_), channel_id=1, source_target_pairs={{0,16},{16,0},{1,17},{17,1},{2,18},{18,2},{3,19},{19,3},{4,20},{20... | collective-permute-start | bytes 1081352 | tf_op jit(solution)/shard_map/ppermute | solution.py:447
  31.0 2.0 %attend.3.refs_0_ = bf16[256,256]{1,0:T(8,128)(2,1)S(1)} custom-call(s32[12]{0:T(128)S(1)} %dynamic-slice_bitcast_fusion.pos_ref, bf16[1024,256]{1,0:T(8,128)(2,1)S(1)} %query.1.q_ref, bf16[1024,256]{1,0:T(8,128)(2,1)S(1)} %get-tuple-element.57.kv_ref, bf16[1024,256]{1,0:T(8,128)(2,1)S(1)} %collective-permute-done.6.got_ref, ...), custom_call_target="tpu_custom_call" | custom-call | tf_op jit(solution)/shard_map/attend/pallas_call | solution.py:242
  32.9 1.1 %collective-permute-start.7 = (bf16[256,256]{1,0:T(8,128)(2,1)S(1)}, bf16[256,256]{1,0:T(8,128)(2,1)S(1)}, u32[]{:S(2)}, u32[]{:S(2)}) collective-permute-start(bf16[256,256]{1,0:T(8,128)(2,1)S(1)} %attend.3.refs_0_), channel_id=1, source_target_pairs={{0,1},{1,2},{2,3},{3,0},{4,5},{5,6},{6,7},{7,4},{8,9},{9,10},{10,1... | collective-permute-start | bytes 393224 | tf_op jit(solution)/shard_map/ppermute | solution.py:425
  34.0 2.2 %collective-permute-start.8 = (bf16[256,256]{1,0:T(8,128)(2,1)S(1)}, bf16[256,256]{1,0:T(8,128)(2,1)S(1)}, u32[]{:S(2)}, u32[]{:S(2)}) collective-permute-start(bf16[256,256]{1,0:T(8,128)(2,1)S(1)} %attend.3.refs_0_), channel_id=1, source_target_pairs={{0,3},{1,0},{2,1},{3,2},{4,7},{5,4},{6,5},{7,6},{8,11},{9,8},{10,9... | collective-permute-start | bytes 393224 | tf_op jit(solution)/shard_map/ppermute | solution.py:425
  36.8 3.1 %attend.4.refs_0_ = bf16[512,256]{1,0:T(8,128)(2,1)S(1)} custom-call(s32[12]{0:T(128)S(1)} %dynamic-slice_bitcast_fusion.pos_ref, bf16[1024,256]{1,0:T(8,128)(2,1)S(1)} %query.1.q_ref, bf16[1024,256]{1,0:T(8,128)(2,1)S(1)} %get-tuple-element.57.kv_ref, bf16[1024,256]{1,0:T(8,128)(2,1)S(1)} %collective-permute-done.6.got_ref, ...), custom_call_target="tpu_custom_call" | custom-call | tf_op jit(solution)/shard_map/attend/pallas_call | solution.py:242
  40.3 2.9 %collective-permute-start.16 = (bf16[512,256]{1,0:T(8,128)(2,1)S(1)}, bf16[512,256]{1,0:T(8,128)(2,1)S(1)}, u32[]{:S(2)}, u32[]{:S(2)}) collective-permute-start(bf16[512,256]{1,0:T(8,128)(2,1)S(1)} %attend.4.refs_0_), channel_id=1, source_target_pairs={{0,3},{1,0},{2,1},{3,2},{4,7},{5,4},{6,5},{7,6},{8,11},{9,8},{10,9... | collective-permute-start | bytes 786440 | tf_op jit(solution)/shard_map/ppermute | solution.py:425
  43.2 1.7 %join.1.refs_4_ = bf16[4,256,1408]{2,1,0:T(8,128)(2,1)S(1)} custom-call(s32[12]{0:T(128)S(1)} %dynamic-slice_bitcast_fusion.pos_ref, bf16[256,5376]{1,0:T(8,128)(2,1)} %w_ref.5, bf16[128,1408]{1,0:T(8,128)(2,1)S(1)} %collective-permute-done.refs_0_, bf16[128,1408]{1,0:T(8,128)(2,1)S(1)} %collective-permute-done.1.refs_1_, ...), custom_call_target="tpu_custom_call" | custom-call | tf_op jit(solution)/shard_map/join/pallas_call | solution.py:300
  44.9 1.9 %collective-permute-start.17 = (bf16[512,256]{1,0:T(8,128)(2,1)S(1)}, bf16[512,256]{1,0:T(8,128)(2,1)S(1)}, u32[]{:S(2)}, u32[]{:S(2)}) collective-permute-start(bf16[512,256]{1,0:T(8,128)(2,1)S(1)} %attend.4.refs_0_), channel_id=1, source_target_pairs={{0,2},{1,3},{2,0},{3,1},{4,6},{5,7},{6,4},{7,5},{8,10},{9,11},{10,... | collective-permute-start | bytes 786440 | tf_op jit(solution)/shard_map/ppermute | solution.py:425
  46.8 1.0 %far.1 = (bf16[128,1408]{1,0:T(8,128)(2,1)S(1)}, bf16[128,1408]{1,0:T(8,128)(2,1)S(1)}) custom-call(bf16[256,256]{1,0:T(8,128)(2,1)S(1)} %attend.3.refs_0_, bf16[256,256]{1,0:T(8,128)(2,1)S(1)} %collective-permute-done.7.refs_1_, bf16[256,256]{1,0:T(8,128)(2,1)S(1)} %collective-permute-done.8.refs_2_, bf16[256,256]{1,0:T(8,128)(2,1)S(1)} %collective-permute-done.9.refs_3_, ...), custom_call_target="tpu_custom_call" | custom-call | tf_op jit(solution)/shard_map/far/pallas_call | solution.py:355
  47.8 1.6 %collective-permute-start.13 = (bf16[128,1408]{1,0:T(8,128)(2,1)S(1)}, bf16[128,1408]{1,0:T(8,128)(2,1)S(1)}, u32[]{:S(2)}, u32[]{:S(2)}) collective-permute-start(bf16[128,1408]{1,0:T(8,128)(2,1)S(1)} %get-tuple-element.67), channel_id=1, source_target_pairs={{0,4},{4,8},{8,12},{12,0},{1,5},{5,9},{9,13},{13,1},{2,6},{6,10},{... | collective-permute-start | bytes 1081352 | tf_op jit(solution)/shard_map/ppermute | solution.py:425
  49.3 1.7 %collective-permute-start.14 = (bf16[128,1408]{1,0:T(8,128)(2,1)S(1)}, bf16[128,1408]{1,0:T(8,128)(2,1)S(1)}, u32[]{:S(2)}, u32[]{:S(2)}) collective-permute-start(bf16[128,1408]{1,0:T(8,128)(2,1)S(1)} %get-tuple-element.69), channel_id=1, source_target_pairs={{0,12},{4,0},{8,4},{12,8},{1,13},{5,1},{9,5},{13,9},{2,14},{6,2},{... | collective-permute-start | bytes 1081352 | tf_op jit(solution)/shard_map/ppermute | solution.py:425
  51.1 1.9 %attend.5.refs_0_ = bf16[256,256]{1,0:T(8,128)(2,1)S(1)} custom-call(s32[12]{0:T(128)S(1)} %dynamic-slice_bitcast_fusion.pos_ref, bf16[1024,256]{1,0:T(8,128)(2,1)S(1)} %query.1.q_ref, bf16[1024,256]{1,0:T(8,128)(2,1)S(1)} %get-tuple-element.57.kv_ref, bf16[1024,256]{1,0:T(8,128)(2,1)S(1)} %collective-permute-done.6.got_ref, ...), custom_call_target="tpu_custom_call" | custom-call | flops 4000000000 | tf_op jit(solution)/shard_map/attend/pallas_call | solution.py:242
  54.8 1.8 %near.1 = (bf16[256,1408]{1,0:T(8,128)(2,1)S(1)}, bf16[256,1408]{1,0:T(8,128)(2,1)S(1)}) custom-call(bf16[512,256]{1,0:T(8,128)(2,1)S(1)} %attend.4.refs_0_, bf16[512,256]{1,0:T(8,128)(2,1)S(1)} %collective-permute-done.15.refs_1_, bf16[512,256]{1,0:T(8,128)(2,1)S(1)} %collective-permute-done.16.refs_2_, ...), custom_call_target="tpu_custom_call" | custom-call | flops 30000001024 | tf_op jit(solution)/shard_map/near/pallas_call | solution.py:355
  56.6 1.5 %collective-permute-done.13.relay_up = bf16[128,1408]{1,0:T(8,128)(2,1)S(1)} collective-permute-done((bf16[128,1408]{1,0:T(8,128)(2,1)S(1)}, bf16[128,1408]{1,0:T(8,128)(2,1)S(1)}, u32[]{:S(2)}, u32[]{:S(2)}) %collective-permute-start.13) | collective-permute-done | bytes 360480 | tf_op jit(solution)/shard_map/ppermute | solution.py:425
  58.6 1.6 %collective-permute-start.18 = (bf16[256,1408]{1,0:T(8,128)(2,1)S(1)}, bf16[256,1408]{1,0:T(8,128)(2,1)S(1)}, u32[]{:S(2)}, u32[]{:S(2)}) collective-permute-start(bf16[256,1408]{1,0:T(8,128)(2,1)S(1)} %get-tuple-element.76), channel_id=1, source_target_pairs={{0,4},{4,8},{8,12},{12,0},{1,5},{5,9},{9,13},{13,1},{2,6},{6,10},{... | collective-permute-start | bytes 2162696 | tf_op jit(solution)/shard_map/ppermute | solution.py:425
  60.2 1.8 %collective-permute-start.19 = (bf16[256,1408]{1,0:T(8,128)(2,1)S(1)}, bf16[256,1408]{1,0:T(8,128)(2,1)S(1)}, u32[]{:S(2)}, u32[]{:S(2)}) collective-permute-start(bf16[256,1408]{1,0:T(8,128)(2,1)S(1)} %get-tuple-element.77), channel_id=1, source_target_pairs={{0,12},{4,0},{8,4},{12,8},{1,13},{5,1},{9,5},{13,9},{2,14},{6,2},{... | collective-permute-start | bytes 2162696 | tf_op jit(solution)/shard_map/ppermute | solution.py:425
  62.0 3.2 %collective-permute-start.11 = (bf16[256,256]{1,0:T(8,128)(2,1)S(1)}, bf16[256,256]{1,0:T(8,128)(2,1)S(1)}, u32[]{:S(2)}, u32[]{:S(2)}) collective-permute-start(bf16[256,256]{1,0:T(8,128)(2,1)S(1)} %attend.5.refs_0_), channel_id=1, source_target_pairs={{0,3},{1,0},{2,1},{3,2},{4,7},{5,4},{6,5},{7,6},{8,11},{9,8},{10,9... | collective-permute-start | bytes 393224 | tf_op jit(solution)/shard_map/ppermute | solution.py:425
  65.7 3.4 %collective-permute-done.10.refs_1_ = bf16[256,256]{1,0:T(8,128)(2,1)S(1)} collective-permute-done((bf16[256,256]{1,0:T(8,128)(2,1)S(1)}, bf16[256,256]{1,0:T(8,128)(2,1)S(1)}, u32[]{:S(2)}, u32[]{:S(2)}) %collective-permute-start.10) | collective-permute-done | bytes 131104 | tf_op jit(solution)/shard_map/ppermute | solution.py:425
  69.1 2.5 %collective-permute-done.12.refs_3_ = bf16[256,256]{1,0:T(8,128)(2,1)S(1)} collective-permute-done((bf16[256,256]{1,0:T(8,128)(2,1)S(1)}, bf16[256,256]{1,0:T(8,128)(2,1)S(1)}, u32[]{:S(2)}, u32[]{:S(2)}) %collective-permute-start.12) | collective-permute-done | bytes 131104 | tf_op jit(solution)/shard_map/ppermute | solution.py:425
  72.7 3.2 %collective-permute-done.18.up_ref = bf16[256,1408]{1,0:T(8,128)(2,1)S(1)} collective-permute-done((bf16[256,1408]{1,0:T(8,128)(2,1)S(1)}, bf16[256,1408]{1,0:T(8,128)(2,1)S(1)}, u32[]{:S(2)}, u32[]{:S(2)}) %collective-permute-start.18) | collective-permute-done | bytes 720928 | tf_op jit(solution)/shard_map/ppermute | solution.py:425
  75.8 1.0 %total_step.1 = (f32[64,1408]{1,0:T(8,128)S(1)}, bf16[64,1408]{1,0:T(8,128)(2,1)S(1)}, bf16[64,1408]{1,0:T(8,128)(2,1)S(1)}, bf16[64,1408]{1,0:T(8,128)(2,1)S(1)}) custom-call(s32[12]{0:T(128)S(1)} %dynamic-slice_bitcast_fusion.pos_ref, f32[256,1408]{1,0:T(8,128)S(1)} %keep.1.kept_ref, bf16[256,1408]{1,0:T(8,128)(2,1)S(1)} %collective-permute-done.18.up_ref, ...), custom_call_target="tpu_custom_call" | custom-call | tf_op jit(solution)/shard_map/total_step/pallas_call | solution.py:381
  77.1 3.0 %collective-permute-start.21 = (bf16[64,1408]{1,0:T(8,128)(2,1)S(1)}, bf16[64,1408]{1,0:T(8,128)(2,1)S(1)}, u32[]{:S(2)}, u32[]{:S(2)}) collective-permute-start(bf16[64,1408]{1,0:T(8,128)(2,1)S(1)} %get-tuple-element.80), channel_id=1, source_target_pairs={{0,3},{1,0},{2,1},{3,2},{4,7},{5,4},{6,5},{7,6},{8,11},{9,8},{10,9... | collective-permute-start | bytes 540680 | tf_op jit(solution)/shard_map/ppermute | solution.py:425
  80.7 3.9 %collective-permute-done.20.next_ref = bf16[64,1408]{1,0:T(8,128)(2,1)S(1)} collective-permute-done((bf16[64,1408]{1,0:T(8,128)(2,1)S(1)}, bf16[64,1408]{1,0:T(8,128)(2,1)S(1)}, u32[]{:S(2)}, u32[]{:S(2)}) %collective-permute-start.20) | collective-permute-done | bytes 180256 | tf_op jit(solution)/shard_map/ppermute | solution.py:425
  85.1 2.0 %collective-permute-done.22.far_ref = bf16[64,1408]{1,0:T(8,128)(2,1)S(1)} collective-permute-done((bf16[64,1408]{1,0:T(8,128)(2,1)S(1)}, bf16[64,1408]{1,0:T(8,128)(2,1)S(1)}, u32[]{:S(2)}, u32[]{:S(2)}) %collective-permute-start.22) | collective-permute-done | bytes 180256 | tf_op jit(solution)/shard_map/ppermute | solution.py:425
  87.1 1.9 %finish.1 = bf16[64,5376]{1,0:T(8,128)(2,1)} custom-call(s32[12]{0:T(128)S(1)} %dynamic-slice_bitcast_fusion.pos_ref, f32[64,1408]{1,0:T(8,128)S(1)} %get-tuple-element.78.own_ref, bf16[64,1408]{1,0:T(8,128)(2,1)S(1)} %collective-permute-done.20.next_ref, bf16[64,1408]{1,0:T(8,128)(2,1)S(1)} %collective-permute-done.21.last_ref, ...), custom_call_target="tpu_custom_call" | custom-call | tf_op jit(solution)/shard_map/finish/pallas_call | solution.py:412
  (44 shorter events, 9.2 us)
Async XLA Ops:
  0.0 8.6 %copy-start.5 = (f32[5376]{0:T(1024)S(1)}, f32[5376]{0:T(1024)}, u32[]{:S(2)}) copy-start(f32[5376]{0:T(1024)} %param.14) | copy-start | bytes 64516
  0.0 8.6 %copy-start.4 = (f32[128]{0:T(128)S(1)}, f32[128]{0:T(128)}, u32[]{:S(2)}) copy-start(f32[128]{0:T(128)} %param.19) | copy-start | bytes 1540
  2.5 23.7 %collective-permute-start = (bf16[128,1408]{1,0:T(8,128)(2,1)S(1)}, bf16[128,1408]{1,0:T(8,128)(2,1)S(1)}, u32[]{:S(2)}, u32[]{:S(2)}) collective-permute-start(bf16[128,1408]{1,0:T(8,128)(2,1)S(1)} %get-tuple-element.49), channel_id=1, source_target_pairs={{0,1},{1,2},{2,3},{3,0},{4,5},{5,6},{6,7},{7,4},{8,9},{9,10},{10,1... | collective-permute-start | bytes 1081352 | tf_op jit(solution)/shard_map/ppermute | solution.py:425
  4.6 21.7 %collective-permute-start.1 = (bf16[128,1408]{1,0:T(8,128)(2,1)S(1)}, bf16[128,1408]{1,0:T(8,128)(2,1)S(1)}, u32[]{:S(2)}, u32[]{:S(2)}) collective-permute-start(bf16[128,1408]{1,0:T(8,128)(2,1)S(1)} %get-tuple-element.50), channel_id=1, source_target_pairs={{0,3},{1,0},{2,1},{3,2},{4,7},{5,4},{6,5},{7,6},{8,11},{9,8},{10,9... | collective-permute-start | bytes 1081352 | tf_op jit(solution)/shard_map/ppermute | solution.py:425
  6.8 19.5 %collective-permute-start.2 = (bf16[128,1408]{1,0:T(8,128)(2,1)S(1)}, bf16[128,1408]{1,0:T(8,128)(2,1)S(1)}, u32[]{:S(2)}, u32[]{:S(2)}) collective-permute-start(bf16[128,1408]{1,0:T(8,128)(2,1)S(1)} %get-tuple-element.51), channel_id=1, source_target_pairs={{0,2},{1,3},{2,0},{3,1},{4,6},{5,7},{6,4},{7,5},{8,10},{9,11},{10,... | collective-permute-start | bytes 1081352 | tf_op jit(solution)/shard_map/ppermute | solution.py:425
  8.6 12.7 %copy-start = (bf16[5376,256]{1,0:T(8,128)(2,1)S(1)}, bf16[5376,256]{1,0:T(8,128)(2,1)}, u32[]{:S(2)}) copy-start(bf16[5376,256]{1,0:T(8,128)(2,1)} %w_ref.4) | copy-start | bytes 8257540
  8.6 12.7 %copy-start.3 = (f32[128]{0:T(128)S(1)}, f32[128]{0:T(128)}, u32[]{:S(2)}) copy-start(f32[128]{0:T(128)} %param.18) | copy-start | bytes 1540
  19.9 11.0 %collective-permute-start.6 = (bf16[1024,256]{1,0:T(8,128)(2,1)S(1)}, bf16[1024,256]{1,0:T(8,128)(2,1)S(1)}, u32[]{:S(2)}, u32[]{:S(2)}) collective-permute-start(bf16[1024,256]{1,0:T(8,128)(2,1)S(1)} %get-tuple-element.57.kv_ref), channel_id=1, source_target_pairs={{0,16},{16,32},{32,48},{48,64},{64,80},{80,96},{96,112},{1,17},{17... | collective-permute-start | bytes 1572872 | tf_op jit(solution)/shard_map/ppermute | solution.py:444
  21.3 9.7 %copy-start.1 = (bf16[1024,128]{1,0:T(8,128)(2,1)S(1)}, bf16[1024,128]{1,0:T(8,128)(2,1)}, u32[]{:S(2)}) copy-start(bf16[1024,128]{1,0:T(8,128)(2,1)} %pk_ref.5) | copy-start | bytes 786436
  21.3 9.7 %copy-start.2 = (bf16[1024,128]{1,0:T(8,128)(2,1)S(1)}, bf16[1024,128]{1,0:T(8,128)(2,1)}, u32[]{:S(2)}) copy-start(bf16[1024,128]{1,0:T(8,128)(2,1)} %pv_ref.5) | copy-start | bytes 786436
  26.3 3.7 %collective-permute-start.3 = (bf16[128,1408]{1,0:T(8,128)(2,1)S(1)}, bf16[128,1408]{1,0:T(8,128)(2,1)S(1)}, u32[]{:S(2)}, u32[]{:S(2)}) collective-permute-start(bf16[128,1408]{1,0:T(8,128)(2,1)S(1)} %collective-permute-done.refs_0_), channel_id=1, source_target_pairs={{0,16},{16,0},{1,17},{17,1},{2,18},{18,2},{3,19},{19,3},{4,20},{20... | collective-permute-start | bytes 1081352 | tf_op jit(solution)/shard_map/ppermute | solution.py:447
  28.6 1.8 %collective-permute-start.4 = (bf16[128,1408]{1,0:T(8,128)(2,1)S(1)}, bf16[128,1408]{1,0:T(8,128)(2,1)S(1)}, u32[]{:S(2)}, u32[]{:S(2)}) collective-permute-start(bf16[128,1408]{1,0:T(8,128)(2,1)S(1)} %collective-permute-done.1.refs_1_), channel_id=1, source_target_pairs={{0,16},{16,0},{1,17},{17,1},{2,18},{18,2},{3,19},{19,3},{4,20},{20... | collective-permute-start | bytes 1081352 | tf_op jit(solution)/shard_map/ppermute | solution.py:447
  28.7 2.2 %collective-permute-start.5 = (bf16[128,1408]{1,0:T(8,128)(2,1)S(1)}, bf16[128,1408]{1,0:T(8,128)(2,1)S(1)}, u32[]{:S(2)}, u32[]{:S(2)}) collective-permute-start(bf16[128,1408]{1,0:T(8,128)(2,1)S(1)} %collective-permute-done.2.refs_2_), channel_id=1, source_target_pairs={{0,16},{16,0},{1,17},{17,1},{2,18},{18,2},{3,19},{19,3},{4,20},{20... | collective-permute-start | bytes 1081352 | tf_op jit(solution)/shard_map/ppermute | solution.py:447
  32.9 12.0 %collective-permute-start.7 = (bf16[256,256]{1,0:T(8,128)(2,1)S(1)}, bf16[256,256]{1,0:T(8,128)(2,1)S(1)}, u32[]{:S(2)}, u32[]{:S(2)}) collective-permute-start(bf16[256,256]{1,0:T(8,128)(2,1)S(1)} %attend.3.refs_0_), channel_id=1, source_target_pairs={{0,1},{1,2},{2,3},{3,0},{4,5},{5,6},{6,7},{7,4},{8,9},{9,10},{10,1... | collective-permute-start | bytes 393224 | tf_op jit(solution)/shard_map/ppermute | solution.py:425
  34.0 12.8 %collective-permute-start.8 = (bf16[256,256]{1,0:T(8,128)(2,1)S(1)}, bf16[256,256]{1,0:T(8,128)(2,1)S(1)}, u32[]{:S(2)}, u32[]{:S(2)}) collective-permute-start(bf16[256,256]{1,0:T(8,128)(2,1)S(1)} %attend.3.refs_0_), channel_id=1, source_target_pairs={{0,3},{1,0},{2,1},{3,2},{4,7},{5,4},{6,5},{7,6},{8,11},{9,8},{10,9... | collective-permute-start | bytes 393224 | tf_op jit(solution)/shard_map/ppermute | solution.py:425
  36.2 10.6 %collective-permute-start.9 = (bf16[256,256]{1,0:T(8,128)(2,1)S(1)}, bf16[256,256]{1,0:T(8,128)(2,1)S(1)}, u32[]{:S(2)}, u32[]{:S(2)}) collective-permute-start(bf16[256,256]{1,0:T(8,128)(2,1)S(1)} %attend.3.refs_0_), channel_id=1, source_target_pairs={{0,2},{1,3},{2,0},{3,1},{4,6},{5,7},{6,4},{7,5},{8,10},{9,11},{10,... | collective-permute-start | bytes 393224 | tf_op jit(solution)/shard_map/ppermute | solution.py:425
  39.9 13.1 %collective-permute-start.15 = (bf16[512,256]{1,0:T(8,128)(2,1)S(1)}, bf16[512,256]{1,0:T(8,128)(2,1)S(1)}, u32[]{:S(2)}, u32[]{:S(2)}) collective-permute-start(bf16[512,256]{1,0:T(8,128)(2,1)S(1)} %attend.4.refs_0_), channel_id=1, source_target_pairs={{0,1},{1,2},{2,3},{3,0},{4,5},{5,6},{6,7},{7,4},{8,9},{9,10},{10,1... | collective-permute-start | bytes 786440 | tf_op jit(solution)/shard_map/ppermute | solution.py:425
  40.3 13.6 %collective-permute-start.16 = (bf16[512,256]{1,0:T(8,128)(2,1)S(1)}, bf16[512,256]{1,0:T(8,128)(2,1)S(1)}, u32[]{:S(2)}, u32[]{:S(2)}) collective-permute-start(bf16[512,256]{1,0:T(8,128)(2,1)S(1)} %attend.4.refs_0_), channel_id=1, source_target_pairs={{0,3},{1,0},{2,1},{3,2},{4,7},{5,4},{6,5},{7,6},{8,11},{9,8},{10,9... | collective-permute-start | bytes 786440 | tf_op jit(solution)/shard_map/ppermute | solution.py:425
  44.9 9.9 %collective-permute-start.17 = (bf16[512,256]{1,0:T(8,128)(2,1)S(1)}, bf16[512,256]{1,0:T(8,128)(2,1)S(1)}, u32[]{:S(2)}, u32[]{:S(2)}) collective-permute-start(bf16[512,256]{1,0:T(8,128)(2,1)S(1)} %attend.4.refs_0_), channel_id=1, source_target_pairs={{0,2},{1,3},{2,0},{3,1},{4,6},{5,7},{6,4},{7,5},{8,10},{9,11},{10,... | collective-permute-start | bytes 786440 | tf_op jit(solution)/shard_map/ppermute | solution.py:425
  47.8 10.4 %collective-permute-start.13 = (bf16[128,1408]{1,0:T(8,128)(2,1)S(1)}, bf16[128,1408]{1,0:T(8,128)(2,1)S(1)}, u32[]{:S(2)}, u32[]{:S(2)}) collective-permute-start(bf16[128,1408]{1,0:T(8,128)(2,1)S(1)} %get-tuple-element.67), channel_id=1, source_target_pairs={{0,4},{4,8},{8,12},{12,0},{1,5},{5,9},{9,13},{13,1},{2,6},{6,10},{... | collective-permute-start | bytes 1081352 | tf_op jit(solution)/shard_map/ppermute | solution.py:425
  49.3 8.8 %collective-permute-start.14 = (bf16[128,1408]{1,0:T(8,128)(2,1)S(1)}, bf16[128,1408]{1,0:T(8,128)(2,1)S(1)}, u32[]{:S(2)}, u32[]{:S(2)}) collective-permute-start(bf16[128,1408]{1,0:T(8,128)(2,1)S(1)} %get-tuple-element.69), channel_id=1, source_target_pairs={{0,12},{4,0},{8,4},{12,8},{1,13},{5,1},{9,5},{13,9},{2,14},{6,2},{... | collective-permute-start | bytes 1081352 | tf_op jit(solution)/shard_map/ppermute | solution.py:425
  58.6 17.2 %collective-permute-start.18 = (bf16[256,1408]{1,0:T(8,128)(2,1)S(1)}, bf16[256,1408]{1,0:T(8,128)(2,1)S(1)}, u32[]{:S(2)}, u32[]{:S(2)}) collective-permute-start(bf16[256,1408]{1,0:T(8,128)(2,1)S(1)} %get-tuple-element.76), channel_id=1, source_target_pairs={{0,4},{4,8},{8,12},{12,0},{1,5},{5,9},{9,13},{13,1},{2,6},{6,10},{... | collective-permute-start | bytes 2162696 | tf_op jit(solution)/shard_map/ppermute | solution.py:425
  60.2 20.5 %copy-start.6 = (f32[5376]{0:T(1024)S(1)}, f32[5376]{0:T(1024)}, u32[]{:S(2)}) copy-start(f32[5376]{0:T(1024)} %param.23) | copy-start | bytes 64516
  60.2 15.6 %collective-permute-start.19 = (bf16[256,1408]{1,0:T(8,128)(2,1)S(1)}, bf16[256,1408]{1,0:T(8,128)(2,1)S(1)}, u32[]{:S(2)}, u32[]{:S(2)}) collective-permute-start(bf16[256,1408]{1,0:T(8,128)(2,1)S(1)} %get-tuple-element.77), channel_id=1, source_target_pairs={{0,12},{4,0},{8,4},{12,8},{1,13},{5,1},{9,5},{13,9},{2,14},{6,2},{... | collective-permute-start | bytes 2162696 | tf_op jit(solution)/shard_map/ppermute | solution.py:425
  62.0 7.1 %collective-permute-start.10 = (bf16[256,256]{1,0:T(8,128)(2,1)S(1)}, bf16[256,256]{1,0:T(8,128)(2,1)S(1)}, u32[]{:S(2)}, u32[]{:S(2)}) collective-permute-start(bf16[256,256]{1,0:T(8,128)(2,1)S(1)} %attend.5.refs_0_), channel_id=1, source_target_pairs={{0,1},{1,2},{2,3},{3,0},{4,5},{5,6},{6,7},{7,4},{8,9},{9,10},{10,1... | collective-permute-start | bytes 393224 | tf_op jit(solution)/shard_map/ppermute | solution.py:425
  62.0 7.2 %collective-permute-start.11 = (bf16[256,256]{1,0:T(8,128)(2,1)S(1)}, bf16[256,256]{1,0:T(8,128)(2,1)S(1)}, u32[]{:S(2)}, u32[]{:S(2)}) collective-permute-start(bf16[256,256]{1,0:T(8,128)(2,1)S(1)} %attend.5.refs_0_), channel_id=1, source_target_pairs={{0,3},{1,0},{2,1},{3,2},{4,7},{5,4},{6,5},{7,6},{8,11},{9,8},{10,9... | collective-permute-start | bytes 393224 | tf_op jit(solution)/shard_map/ppermute | solution.py:425
  65.2 6.5 %collective-permute-start.12 = (bf16[256,256]{1,0:T(8,128)(2,1)S(1)}, bf16[256,256]{1,0:T(8,128)(2,1)S(1)}, u32[]{:S(2)}, u32[]{:S(2)}) collective-permute-start(bf16[256,256]{1,0:T(8,128)(2,1)S(1)} %attend.5.refs_0_), channel_id=1, source_target_pairs={{0,2},{1,3},{2,0},{3,1},{4,6},{5,7},{6,4},{7,5},{8,10},{9,11},{10,... | collective-permute-start | bytes 393224 | tf_op jit(solution)/shard_map/ppermute | solution.py:425
  76.8 7.7 %collective-permute-start.20 = (bf16[64,1408]{1,0:T(8,128)(2,1)S(1)}, bf16[64,1408]{1,0:T(8,128)(2,1)S(1)}, u32[]{:S(2)}, u32[]{:S(2)}) collective-permute-start(bf16[64,1408]{1,0:T(8,128)(2,1)S(1)} %get-tuple-element.79), channel_id=1, source_target_pairs={{0,1},{1,2},{2,3},{3,0},{4,5},{5,6},{6,7},{7,4},{8,9},{9,10},{10,1... | collective-permute-start | bytes 540680 | tf_op jit(solution)/shard_map/ppermute | solution.py:425
  77.1 8.0 %collective-permute-start.21 = (bf16[64,1408]{1,0:T(8,128)(2,1)S(1)}, bf16[64,1408]{1,0:T(8,128)(2,1)S(1)}, u32[]{:S(2)}, u32[]{:S(2)}) collective-permute-start(bf16[64,1408]{1,0:T(8,128)(2,1)S(1)} %get-tuple-element.80), channel_id=1, source_target_pairs={{0,3},{1,0},{2,1},{3,2},{4,7},{5,4},{6,5},{7,6},{8,11},{9,8},{10,9... | collective-permute-start | bytes 540680 | tf_op jit(solution)/shard_map/ppermute | solution.py:425
  80.1 7.0 %collective-permute-start.22 = (bf16[64,1408]{1,0:T(8,128)(2,1)S(1)}, bf16[64,1408]{1,0:T(8,128)(2,1)S(1)}, u32[]{:S(2)}, u32[]{:S(2)}) collective-permute-start(bf16[64,1408]{1,0:T(8,128)(2,1)S(1)} %get-tuple-element.81), channel_id=1, source_target_pairs={{0,2},{1,3},{2,0},{3,1},{4,6},{5,7},{6,4},{7,5},{8,10},{9,11},{10,... | collective-permute-start | bytes 540680 | tf_op jit(solution)/shard_map/ppermute | solution.py:425

commit v10 on v7

--- a/solution.py
+++ b/solution.py
@@ -166,32 +166,48 @@
     )(pos, tokens, pre_gain.reshape(1, -1), wk, wv, gain.reshape(1, -1), table)
 
 
-def query_kernel(pos_ref, normed_ref, w_ref, gain_ref, tab_ref, q_ref):
-    raw = jnp.dot(normed_ref[...], w_ref[...], preferred_element_type=F32)
-    q_ref[:, 0:128] = rotate(raw[:, 0:128], gain_ref[...], tab_ref[...])
-    q_ref[:, 128:256] = rotate(raw[:, 128:256], gain_ref[...], tab_ref[...])
-
-
-def query(pos, normed, wq, gain, table):
-    (table,) = in_hbm(table)
+def table_copy(pos_ref, tab_ref, table, sem):
+    rows = pl.ds(pl.multiple_of(pos_ref[0] * SHARD, SHARD), SHARD)
+    return pltpu.make_async_copy(tab_ref.at[rows], table, sem)
+
+
+def query_kernel(
+    pos_ref, normed_ref, w_ref, gain_ref, tab_ref, w_out_ref, q_ref, own_w_ref, table, sems
+):
+    copy = table_copy(pos_ref, tab_ref, table, sems.at[0])
+    copy.start()
+    cols = pl.ds(quarter_start(pos_ref[1]), QUARTER)
+    fetch = pltpu.make_async_copy(w_out_ref.at[:, cols], own_w_ref, sems.at[1])
+    fetch.start()
+    copy.wait()
+    for i in range(SHARD // ROWS):
+        rows = slice(i * ROWS, (i + 1) * ROWS)
+        raw = jnp.dot(normed_ref[rows, :], w_ref[...], preferred_element_type=F32)
+        q_ref[rows, 0:128] = rotate(raw[:, 0:128], gain_ref[...], table[rows, :])
+        q_ref[rows, 128:256] = rotate(raw[:, 128:256], gain_ref[...], table[rows, :])
+    fetch.wait()
+
+
+def query(pos, normed, wq, gain, table, w_out):
+    table, w_out = in_hbm(table, w_out)
     return pl.pallas_call(
         query_kernel,
-        grid_spec=pltpu.PrefetchScalarGridSpec(
-            num_scalar_prefetch=1,
-            grid=(SHARD // ROWS,),
-            in_specs=[
-                row_tile(MODEL_WIDTH), whole((MODEL_WIDTH, 256)), whole((1, 128)), TABLE_TILE
-            ],
-            out_specs=row_tile(256),
-        ),
-        out_shape=jax.ShapeDtypeStruct((SHARD, 256), BF16),
+        in_specs=[SMEM, VMEM, VMEM, VMEM, ANY, ANY],
+        out_specs=[VMEM] * 2,
+        out_shape=[
+            jax.ShapeDtypeStruct((SHARD, 256), BF16),
+            jax.ShapeDtypeStruct((256, QUARTER), BF16),
+        ],
+        scratch_shapes=[pltpu.VMEM((SHARD, 128), F32), pltpu.SemaphoreType.DMA((2,))],
         compiler_params=pltpu.CompilerParams(vmem_limit_bytes=24 << 20),
         cost_estimate=SMALL,
         name="query",
-    )(pos, normed, wq, gain.reshape(1, -1), table)
-
-
-def attend_kernel(first_part, pos_ref, q_ref, kv_ref, got_ref, pk_ref, pv_ref, out_ref, keys, values):
+    )(pos, normed, wq, gain.reshape(1, -1), table, w_out)
+
+
+def first_attend_kernel(
+    first_part, pos_ref, q_ref, kv_ref, got_ref, pk_ref, pv_ref, out_ref, keys, values
+):
     @pl.when(pos_ref[0] == 0)
     def _():
         keys[0:SHARD] = pk_ref[...]
@@ -205,7 +221,10 @@
     keys[SHARD:] = kv_ref[:, 0:128]
     values[SHARD:, 0:128] = kv_ref[:, 128:256]
     values[:, 128:256] = jnp.ones((2 * SHARD, 128), BF16)
-
+    attend_kernel(first_part, pos_ref, q_ref, keys, values, out_ref)
+
+
+def attend_kernel(first_part, pos_ref, q_ref, keys, values, out_ref):
     span = HALF + WINDOW_SPAN
     row = lax.broadcasted_iota(jnp.int32, (2 * HALF, HALF), 0) % HALF
     col = lax.broadcasted_iota(jnp.int32, (2 * HALF, HALF), 1)
@@ -232,36 +251,37 @@
         out_ref[part * HALF : (part + 1) * HALF, 128:256] = mixed[HALF:]
 
 
-def attend(first_part, parts, pos, q, kv, got, prior_k, prior_v, cost=SMALL):
-    vmem = pl.BlockSpec(memory_space=pltpu.VMEM)
-    return pl.pallas_call(
-        functools.partial(attend_kernel, first_part),
-        in_specs=[pl.BlockSpec(memory_space=pltpu.SMEM)] + [vmem] * 5,
-        out_specs=vmem,
-        out_shape=jax.ShapeDtypeStruct((parts * HALF, 256), BF16),
-        scratch_shapes=[
-            pltpu.VMEM((2 * SHARD, 128), BF16),
-            pltpu.VMEM((2 * SHARD, 256), BF16),
-        ],
+def attend(first_part, parts, pos, q, sources, cost=SMALL):
+    out_shape = [jax.ShapeDtypeStruct((parts * HALF, 256), BF16)]
+    kernel = attend_kernel
+    if len(sources) > 2:
+        kernel = first_attend_kernel
+        out_shape += [
+            jax.ShapeDtypeStruct((2 * SHARD, 128), BF16),
+            jax.ShapeDtypeStruct((2 * SHARD, 256), BF16),
+        ]
+    return pl.pallas_call(
+        functools.partial(kernel, first_part),
+        in_specs=[SMEM] + [VMEM] * (1 + len(sources)),
+        out_specs=[VMEM] * len(out_shape),
+        out_shape=out_shape,
         compiler_params=pltpu.CompilerParams(vmem_limit_bytes=32 << 20),
         cost_estimate=cost,
         name="attend",
-    )(pos, q, kv, got, prior_k, prior_v)
+    )(pos, q, *sources)
 
 
 def quarter_start(number):
     return pl.multiple_of((number * 21 // 2) * 128, 128)
 
 
-def pick_kernel(pos_ref, w_ref, own_ref, next_ref, last_ref, far_ref, sems):
+def pick_kernel(pos_ref, w_ref, next_ref, last_ref, far_ref, sems):
     z = pos_ref[1]
     rows = pl.ds(pl.multiple_of(pos_ref[2] * 128, 128), 128)
     copies = []
     for i, (shift, ref) in enumerate(((1, next_ref), (3, last_ref), (2, far_ref))):
         cols = pl.ds(quarter_start((z + shift) % 4), QUARTER)
         copies.append(pltpu.make_async_copy(w_ref.at[rows, cols], ref, sems.at[i]))
-    cols = pl.ds(quarter_start(z), QUARTER)
-    copies.append(pltpu.make_async_copy(w_ref.at[:, cols], own_ref, sems.at[3]))
     for copy in copies:
         copy.start()
     for copy in copies:
@@ -273,9 +293,9 @@
     return pl.pallas_call(
         pick_kernel,
         in_specs=[SMEM, ANY],
-        out_specs=[VMEM] * 4,
-        out_shape=[jax.ShapeDtypeStruct((256, QUARTER), BF16), part, part, part],
-        scratch_shapes=[pltpu.SemaphoreType.DMA((4,))],
+        out_specs=[VMEM] * 3,
+        out_shape=[part, part, part],
+        scratch_shapes=[pltpu.SemaphoreType.DMA((3,))],
         compiler_params=pltpu.CompilerParams(vmem_limit_bytes=16 << 20),
         cost_estimate=SMALL,
         name="pick",
@@ -301,22 +321,22 @@
     )(pos, *lines, *swapped)
 
 
-def product(a_refs, w_refs, rows=slice(None)):
-    out = jnp.dot(a_refs[0][rows, :], w_refs[0][...], preferred_element_type=F32)
+def product(a_refs, own_ref, line_ref, rows=slice(None)):
+    out = jnp.dot(a_refs[0][rows, :], own_ref[...], preferred_element_type=F32)
     for i in range(3):
-        out = out + jnp.dot(a_refs[1 + i][rows, :], w_refs[1][i], preferred_element_type=F32)
+        out = out + jnp.dot(a_refs[1 + i][rows, :], line_ref[i], preferred_element_type=F32)
     return out
 
 
 def far_kernel(*refs):
-    out = product(refs[0:4], refs[4:6])
+    out = product(refs[0:4], refs[4], refs[5])
     refs[6][...] = out[0:HALF].astype(BF16)
     refs[7][...] = out[HALF:].astype(BF16)
 
 
 def near_kernel(*refs):
-    refs[6][...] = product(refs[0:4], refs[4:6], slice(0, 256)).astype(BF16)
-    refs[7][...] = product(refs[0:4], refs[4:6], slice(256, 512)).astype(BF16)
+    refs[6][...] = product(refs[0:4], refs[4], refs[5], slice(0, 256)).astype(BF16)
+    refs[7][...] = product(refs[0:4], refs[4], refs[5], slice(256, 512)).astype(BF16)
 
 
 def relay_kernel(relay_up, relay_down, up_in, down_in, up_ref, down_ref):
@@ -340,7 +360,7 @@
 
 
 def keep_kernel(*refs):
-    refs[6][...] = product(refs[0:4], refs[4:6])
+    refs[6][...] = product(refs[0:4], refs[4], refs[5])
 
 
 def multiply(kernel, pieces, weights, out_shape, name, cost=SMALL):
@@ -427,22 +447,22 @@
 ):
     device = lax.axis_index(("y", "c", "x", "z"))
     pos = lax.dynamic_slice_in_dim(jnp.asarray(places()), device, 1, 0).reshape(-1)
-    own_w, *parts = pick(pos, w_out)
+    parts = pick(pos, w_out)
     pos, *parts = lax.optimization_barrier((pos, *parts))
     lines = from_line(parts)
     normed, kv, own_tokens = key_value(
         pos, tokens, pre_gain, key_weight, value_weight, key_gain, table
     )
     got = lax.ppermute(kv, ("y", "c"), [(i, i + 1) for i in range(7)])
-    q = query(pos, normed, w_query, query_gain, table)
+    q, own_w = query(pos, normed, w_query, query_gain, table, w_out)
     q, *lines = lax.optimization_barrier((q, *lines))
     swapped = [lax.ppermute(part, "c", [(0, 1), (1, 0)]) for part in lines]
     pos, *swapped = lax.optimization_barrier((pos, *swapped))
 
-    far = attend(0, 2, pos, q, kv, got, prior_key, prior_value)
+    far, *extended = attend(0, 2, pos, q, (kv, got, prior_key, prior_value))
     far_heads = [far, *from_line([far] * 3)]
     pos, _ = lax.optimization_barrier((pos, far))
-    near = attend(2, 4, pos, q, kv, got, prior_key, prior_value)
+    (near,) = attend(2, 4, pos, q, extended)
     near_heads = [near, *from_line([near] * 3)]
     *far_heads, _ = lax.optimization_barrier((*far_heads, near))
     last_pos, _ = lax.optimization_barrier((pos, near))
@@ -454,7 +474,7 @@
     up, down = multiply(far_kernel, far_heads, weights, [half, half], "far")
     relays = (shift_by(up, "x", 1), shift_by(down, "x", 3))
     pos, *_ = lax.optimization_barrier((pos, near, up))
-    kept = attend(6, 2, pos, q, kv, got, prior_key, prior_value, MEDIUM)
+    (kept,) = attend(6, 2, pos, q, extended, MEDIUM)
     kept_heads = [kept, *from_line([kept] * 3)]
     *near_heads, _ = lax.optimization_barrier((*near_heads, kept))
     up, down = multiply(near_kernel, near_heads, weights, [full, full], "near", LARGE)

time: 89.5 us -> 88.6 us (0.990)
  Pallas kernels: 33.7 us -> 32.5 us
    pallas_call x5, Pallas kernels: 14.6 us -> 13.4 us  [the longest x3 6.68 us: attend(): pl.pallas_call(functools.partial(kernel, first_part), in_specs=[SMEM] + [...]
  transfers between devices with their start and end apart: 23 -> 23, of which waited for: 12 -> 12; matrix products, arithmetic and copies ran while one was open for 0% -> 0% of each run, Pallas kernels for 30% -> 29%
where the time goes in v10:
time: 88.6 us; the launch traced here: 88.3 us
  starting transfers between devices  33.6 us (38%)
  Pallas kernels  32.5 us (37%)
  waiting for transfers between devices  21.1 us (24%)
    ppermute x19, starting transfers between devices, shift_by(): return lax.ppermute(array, axis, [(i, (i + steps) % 4) for i in range(4)])  29.4 us
    ppermute x19, waiting for transfers between devices, shift_by(): return lax.ppermute(array, axis, [(i, (i + steps) % 4) for i in range(4)])  19.3 us
    pallas_call x1, Pallas kernels, key_value(): pl.pallas_call(key_value_kernel, grid_spec=pltpu.PrefetchScalarGridSpec(n...  11.3 us
    pallas_call x3, Pallas kernels, attend(): pl.pallas_call(functools.partial(kernel, first_part), in_specs=[SMEM] + [...  6.68 us
    pallas_call x1, Pallas kernels, query(): pl.pallas_call(query_kernel, in_specs=[SMEM, VMEM, VMEM, VMEM, ANY, ANY],...  4.94 us
    pallas_call x3, Pallas kernels, multiply(): pl.pallas_call(kernel, in_specs=[VMEM] * 6, out_specs=jax.tree.map(lambda...  3.77 us
    ppermute x3, starting transfers between devices, per_device(): swapped = [lax.ppermute(part, 'c', [(0, 1), (1, 0)]) for part in lines]  2.87 us
    pallas_call x1, Pallas kernels, finish(): pl.pallas_call(finish_kernel, in_specs=[SMEM] + [VMEM] * 6, out_specs=VME...  1.89 us
  transfers between devices with their start and end apart: 23, of which 12 were waited for; matrix products, arithmetic and copies ran while one was open for 0% of the time, Pallas kernels for 29%

profile of v10, /device:TPU:0, one launch (start us, length us, event | category | flops | bytes accessed | tf_op | source)
XLA Modules:
  0.0 88.3 jit_solution(8970971910380629874)
XLA Ops:
  0.7 1.8 %pick.1 = (bf16[128,1408]{1,0:T(8,128)(2,1)S(1)}, bf16[128,1408]{1,0:T(8,128)(2,1)S(1)}, bf16[128,1408]{1,0:T(8,128)(2,1)S(1)}) custom-call(s32[12]{0:T(128)S(1)} %dynamic-slice_bitcast_fusion.pos_ref, bf16[256,5376]{1,0:T(8,128)(2,1)} %w_out_ref.1), custom_call_target="tpu_custom_call" | custom-call | tf_op jit(solution)/shard_map/pick/pallas_call | solution.py:293
  2.5 2.1 %collective-permute-start = (bf16[128,1408]{1,0:T(8,128)(2,1)S(1)}, bf16[128,1408]{1,0:T(8,128)(2,1)S(1)}, u32[]{:S(2)}, u32[]{:S(2)}) collective-permute-start(bf16[128,1408]{1,0:T(8,128)(2,1)S(1)} %get-tuple-element.55), channel_id=1, source_target_pairs={{0,1},{1,2},{2,3},{3,0},{4,5},{5,6},{6,7},{7,4},{8,9},{9,10},{10,1... | collective-permute-start | bytes 1081352 | tf_op jit(solution)/shard_map/ppermute | solution.py:437
  4.6 2.2 %collective-permute-start.1 = (bf16[128,1408]{1,0:T(8,128)(2,1)S(1)}, bf16[128,1408]{1,0:T(8,128)(2,1)S(1)}, u32[]{:S(2)}, u32[]{:S(2)}) collective-permute-start(bf16[128,1408]{1,0:T(8,128)(2,1)S(1)} %get-tuple-element.56), channel_id=1, source_target_pairs={{0,3},{1,0},{2,1},{3,2},{4,7},{5,4},{6,5},{7,6},{8,11},{9,8},{10,9... | collective-permute-start | bytes 1081352 | tf_op jit(solution)/shard_map/ppermute | solution.py:437
  6.8 1.8 %collective-permute-start.2 = (bf16[128,1408]{1,0:T(8,128)(2,1)S(1)}, bf16[128,1408]{1,0:T(8,128)(2,1)S(1)}, u32[]{:S(2)}, u32[]{:S(2)}) collective-permute-start(bf16[128,1408]{1,0:T(8,128)(2,1)S(1)} %get-tuple-element.57), channel_id=1, source_target_pairs={{0,2},{1,3},{2,0},{3,1},{4,6},{5,7},{6,4},{7,5},{8,10},{9,11},{10,... | collective-permute-start | bytes 1081352 | tf_op jit(solution)/shard_map/ppermute | solution.py:437
  8.6 11.3 %key_value.1 = (bf16[1024,5376]{1,0:T(8,128)(2,1)S(1)}, bf16[1024,256]{1,0:T(8,128)(2,1)S(1)}, bf16[64,5376]{1,0:T(8,128)(2,1)S(1)}) custom-call(s32[12]{0:T(128)S(1)} %dynamic-slice_bitcast_fusion.pos_ref, bf16[1024,5376]{1,0:T(8,128)(2,1)} %tok_ref.1, f32[1,5376]{1,0:T(1,128)S(1)} %reshape.16.g_ref, bf16[5376,128]{1,0:T(8,128)(2,1)} %wk_ref.1, ...), custom_call_target="tpu_custom_call" | custom-call | flops 11274289152 | bytes 27262976 | tf_op jit(solution)/shard_map/key_value/pallas_call | solution.py:140
  19.9 1.3 %collective-permute-start.6 = (bf16[1024,256]{1,0:T(8,128)(2,1)S(1)}, bf16[1024,256]{1,0:T(8,128)(2,1)S(1)}, u32[]{:S(2)}, u32[]{:S(2)}) collective-permute-start(bf16[1024,256]{1,0:T(8,128)(2,1)S(1)} %get-tuple-element.63.kv_ref), channel_id=1, source_target_pairs={{0,16},{16,32},{32,48},{48,64},{64,80},{80,96},{96,112},{1,17},{17... | collective-permute-start | bytes 1572872 | tf_op jit(solution)/shard_map/ppermute | solution.py:456
  21.3 4.9 %query.1 = (bf16[1024,256]{1,0:T(8,128)(2,1)S(1)}, bf16[256,1408]{1,0:T(8,128)(2,1)S(1)}) custom-call(s32[12]{0:T(128)S(1)} %dynamic-slice_bitcast_fusion.pos_ref, bf16[1024,5376]{1,0:T(8,128)(2,1)S(1)} %get-tuple-element.53.normed_ref, bf16[5376,256]{1,0:T(8,128)(2,1)S(1)} %copy-done, f32[1,128]{1,0:T(1,128)S(1)} %bitcast.4, ...), custom_call_target="tpu_custom_call" | custom-call | tf_op jit(solution)/shard_map/query/pallas_call | solution.py:193
  26.3 2.4 %collective-permute-start.3 = (bf16[128,1408]{1,0:T(8,128)(2,1)S(1)}, bf16[128,1408]{1,0:T(8,128)(2,1)S(1)}, u32[]{:S(2)}, u32[]{:S(2)}) collective-permute-start(bf16[128,1408]{1,0:T(8,128)(2,1)S(1)} %collective-permute-done.refs_0_), channel_id=1, source_target_pairs={{0,16},{16,0},{1,17},{17,1},{2,18},{18,2},{3,19},{19,3},{4,20},{20... | collective-permute-start | bytes 1081352 | tf_op jit(solution)/shard_map/ppermute | solution.py:459
  31.0 2.0 %attend.3 = (bf16[256,256]{1,0:T(8,128)(2,1)S(1)}, bf16[2048,128]{1,0:T(8,128)(2,1)S(1)}, bf16[2048,256]{1,0:T(8,128)(2,1)S(1)}) custom-call(s32[12]{0:T(128)S(1)} %dynamic-slice_bitcast_fusion.pos_ref, bf16[1024,256]{1,0:T(8,128)(2,1)S(1)} %get-tuple-element.62.q_ref, bf16[1024,256]{1,0:T(8,128)(2,1)S(1)} %get-tuple-element.63.kv_ref, ...), custom_call_target="tpu_custom_call" | custom-call | tf_op jit(solution)/shard_map/attend/pallas_call | solution.py:263
  33.0 1.1 %collective-permute-start.7 = (bf16[256,256]{1,0:T(8,128)(2,1)S(1)}, bf16[256,256]{1,0:T(8,128)(2,1)S(1)}, u32[]{:S(2)}, u32[]{:S(2)}) collective-permute-start(bf16[256,256]{1,0:T(8,128)(2,1)S(1)} %get-tuple-element.68.refs_0_), channel_id=1, source_target_pairs={{0,1},{1,2},{2,3},{3,0},{4,5},{5,6},{6,7},{7,4},{8,9},{9,10},{10,1... | collective-permute-start | bytes 393224 | tf_op jit(solution)/shard_map/ppermute | solution.py:437
  34.1 2.2 %collective-permute-start.8 = (bf16[256,256]{1,0:T(8,128)(2,1)S(1)}, bf16[256,256]{1,0:T(8,128)(2,1)S(1)}, u32[]{:S(2)}, u32[]{:S(2)}) collective-permute-start(bf16[256,256]{1,0:T(8,128)(2,1)S(1)} %get-tuple-element.68.refs_0_), channel_id=1, source_target_pairs={{0,3},{1,0},{2,1},{3,2},{4,7},{5,4},{6,5},{7,6},{8,11},{9,8},{10,9... | collective-permute-start | bytes 393224 | tf_op jit(solution)/shard_map/ppermute | solution.py:437
  36.8 2.9 %attend.4.refs_0_ = bf16[512,256]{1,0:T(8,128)(2,1)S(1)} custom-call(s32[12]{0:T(128)S(1)} %dynamic-slice_bitcast_fusion.pos_ref, bf16[1024,256]{1,0:T(8,128)(2,1)S(1)} %get-tuple-element.62.q_ref, bf16[2048,128]{1,0:T(8,128)(2,1)S(1)} %get-tuple-element.66.keys, bf16[2048,256]{1,0:T(8,128)(2,1)S(1)} %get-tuple-element.67.values), custom_call_target="tpu_custom_call" | custom-call | tf_op jit(solution)/shard_map/attend/pallas_call | solution.py:263
  40.3 2.9 %collective-permute-start.16 = (bf16[512,256]{1,0:T(8,128)(2,1)S(1)}, bf16[512,256]{1,0:T(8,128)(2,1)S(1)}, u32[]{:S(2)}, u32[]{:S(2)}) collective-permute-start(bf16[512,256]{1,0:T(8,128)(2,1)S(1)} %attend.4.refs_0_), channel_id=1, source_target_pairs={{0,3},{1,0},{2,1},{3,2},{4,7},{5,4},{6,5},{7,6},{8,11},{9,8},{10,9... | collective-permute-start | bytes 786440 | tf_op jit(solution)/shard_map/ppermute | solution.py:437
  43.9 1.9 %collective-permute-start.17 = (bf16[512,256]{1,0:T(8,128)(2,1)S(1)}, bf16[512,256]{1,0:T(8,128)(2,1)S(1)}, u32[]{:S(2)}, u32[]{:S(2)}) collective-permute-start(bf16[512,256]{1,0:T(8,128)(2,1)S(1)} %attend.4.refs_0_), channel_id=1, source_target_pairs={{0,2},{1,3},{2,0},{3,1},{4,6},{5,7},{6,4},{7,5},{8,10},{9,11},{10,... | collective-permute-start | bytes 786440 | tf_op jit(solution)/shard_map/ppermute | solution.py:437
  45.8 1.0 %far.1 = (bf16[128,1408]{1,0:T(8,128)(2,1)S(1)}, bf16[128,1408]{1,0:T(8,128)(2,1)S(1)}) custom-call(bf16[256,256]{1,0:T(8,128)(2,1)S(1)} %get-tuple-element.68.refs_0_, bf16[256,256]{1,0:T(8,128)(2,1)S(1)} %collective-permute-done.7.refs_1_, bf16[256,256]{1,0:T(8,128)(2,1)S(1)} %collective-permute-done.8.refs_2_, ...), custom_call_target="tpu_custom_call" | custom-call | tf_op jit(solution)/shard_map/far/pallas_call | solution.py:367
  46.8 1.6 %collective-permute-start.13 = (bf16[128,1408]{1,0:T(8,128)(2,1)S(1)}, bf16[128,1408]{1,0:T(8,128)(2,1)S(1)}, u32[]{:S(2)}, u32[]{:S(2)}) collective-permute-start(bf16[128,1408]{1,0:T(8,128)(2,1)S(1)} %get-tuple-element.77), channel_id=1, source_target_pairs={{0,4},{4,8},{8,12},{12,0},{1,5},{5,9},{9,13},{13,1},{2,6},{6,10},{... | collective-permute-start | bytes 1081352 | tf_op jit(solution)/shard_map/ppermute | solution.py:437
  48.3 1.7 %collective-permute-start.14 = (bf16[128,1408]{1,0:T(8,128)(2,1)S(1)}, bf16[128,1408]{1,0:T(8,128)(2,1)S(1)}, u32[]{:S(2)}, u32[]{:S(2)}) collective-permute-start(bf16[128,1408]{1,0:T(8,128)(2,1)S(1)} %get-tuple-element.79), channel_id=1, source_target_pairs={{0,12},{4,0},{8,4},{12,8},{1,13},{5,1},{9,5},{13,9},{2,14},{6,2},{... | collective-permute-start | bytes 1081352 | tf_op jit(solution)/shard_map/ppermute | solution.py:437
  50.1 1.8 %attend.5.refs_0_ = bf16[256,256]{1,0:T(8,128)(2,1)S(1)} custom-call(s32[12]{0:T(128)S(1)} %dynamic-slice_bitcast_fusion.pos_ref, bf16[1024,256]{1,0:T(8,128)(2,1)S(1)} %get-tuple-element.62.q_ref, bf16[2048,128]{1,0:T(8,128)(2,1)S(1)} %get-tuple-element.66.keys, bf16[2048,256]{1,0:T(8,128)(2,1)S(1)} %get-tuple-element.67.values), custom_call_target="tpu_custom_call" | custom-call | flops 4000000000 | tf_op jit(solution)/shard_map/attend/pallas_call | solution.py:263
  51.9 2.0 %collective-permute-done.16.refs_2_ = bf16[512,256]{1,0:T(8,128)(2,1)S(1)} collective-permute-done((bf16[512,256]{1,0:T(8,128)(2,1)S(1)}, bf16[512,256]{1,0:T(8,128)(2,1)S(1)}, u32[]{:S(2)}, u32[]{:S(2)}) %collective-permute-start.16) | collective-permute-done | bytes 262176 | tf_op jit(solution)/shard_map/ppermute | solution.py:437
  54.8 1.8 %near.1 = (bf16[256,1408]{1,0:T(8,128)(2,1)S(1)}, bf16[256,1408]{1,0:T(8,128)(2,1)S(1)}) custom-call(bf16[512,256]{1,0:T(8,128)(2,1)S(1)} %attend.4.refs_0_, bf16[512,256]{1,0:T(8,128)(2,1)S(1)} %collective-permute-done.15.refs_1_, bf16[512,256]{1,0:T(8,128)(2,1)S(1)} %collective-permute-done.16.refs_2_, ...), custom_call_target="tpu_custom_call" | custom-call | flops 30000001024 | tf_op jit(solution)/shard_map/near/pallas_call | solution.py:367
  57.6 1.6 %collective-permute-start.18 = (bf16[256,1408]{1,0:T(8,128)(2,1)S(1)}, bf16[256,1408]{1,0:T(8,128)(2,1)S(1)}, u32[]{:S(2)}, u32[]{:S(2)}) collective-permute-start(bf16[256,1408]{1,0:T(8,128)(2,1)S(1)} %get-tuple-element.86), channel_id=1, source_target_pairs={{0,4},{4,8},{8,12},{12,0},{1,5},{5,9},{9,13},{13,1},{2,6},{6,10},{... | collective-permute-start | bytes 2162696 | tf_op jit(solution)/shard_map/ppermute | solution.py:437
  59.2 1.7 %collective-permute-start.19 = (bf16[256,1408]{1,0:T(8,128)(2,1)S(1)}, bf16[256,1408]{1,0:T(8,128)(2,1)S(1)}, u32[]{:S(2)}, u32[]{:S(2)}) collective-permute-start(bf16[256,1408]{1,0:T(8,128)(2,1)S(1)} %get-tuple-element.87), channel_id=1, source_target_pairs={{0,12},{4,0},{8,4},{12,8},{1,13},{5,1},{9,5},{13,9},{2,14},{6,2},{... | collective-permute-start | bytes 2162696 | tf_op jit(solution)/shard_map/ppermute | solution.py:437
  61.7 2.5 %collective-permute-start.11 = (bf16[256,256]{1,0:T(8,128)(2,1)S(1)}, bf16[256,256]{1,0:T(8,128)(2,1)S(1)}, u32[]{:S(2)}, u32[]{:S(2)}) collective-permute-start(bf16[256,256]{1,0:T(8,128)(2,1)S(1)} %attend.5.refs_0_), channel_id=1, source_target_pairs={{0,3},{1,0},{2,1},{3,2},{4,7},{5,4},{6,5},{7,6},{8,11},{9,8},{10,9... | collective-permute-start | bytes 393224 | tf_op jit(solution)/shard_map/ppermute | solution.py:437
  64.7 3.4 %collective-permute-done.10.refs_1_ = bf16[256,256]{1,0:T(8,128)(2,1)S(1)} collective-permute-done((bf16[256,256]{1,0:T(8,128)(2,1)S(1)}, bf16[256,256]{1,0:T(8,128)(2,1)S(1)}, u32[]{:S(2)}, u32[]{:S(2)}) %collective-permute-start.10) | collective-permute-done | bytes 131104 | tf_op jit(solution)/shard_map/ppermute | solution.py:437
  68.1 2.5 %collective-permute-done.12.refs_3_ = bf16[256,256]{1,0:T(8,128)(2,1)S(1)} collective-permute-done((bf16[256,256]{1,0:T(8,128)(2,1)S(1)}, bf16[256,256]{1,0:T(8,128)(2,1)S(1)}, u32[]{:S(2)}, u32[]{:S(2)}) %collective-permute-start.12) | collective-permute-done | bytes 131104 | tf_op jit(solution)/shard_map/ppermute | solution.py:437
  70.6 1.0 %keep.1.kept_ref = f32[256,1408]{1,0:T(8,128)S(1)} custom-call(bf16[256,256]{1,0:T(8,128)(2,1)S(1)} %attend.5.refs_0_, bf16[256,256]{1,0:T(8,128)(2,1)S(1)} %collective-permute-done.10.refs_1_, bf16[256,256]{1,0:T(8,128)(2,1)S(1)} %collective-permute-done.11.refs_2_, bf16[256,256]{1,0:T(8,128)(2,1)S(1)} %collective-permute-done.12.refs_3_, ...), custom_call_target="tpu_custom_call" | custom-call | tf_op jit(solution)/shard_map/keep/pallas_call | solution.py:367
  71.6 3.5 %collective-permute-done.18.up_ref = bf16[256,1408]{1,0:T(8,128)(2,1)S(1)} collective-permute-done((bf16[256,1408]{1,0:T(8,128)(2,1)S(1)}, bf16[256,1408]{1,0:T(8,128)(2,1)S(1)}, u32[]{:S(2)}, u32[]{:S(2)}) %collective-permute-start.18) | collective-permute-done | bytes 720928 | tf_op jit(solution)/shard_map/ppermute | solution.py:437
  75.1 1.0 %total_step.1 = (f32[64,1408]{1,0:T(8,128)S(1)}, bf16[64,1408]{1,0:T(8,128)(2,1)S(1)}, bf16[64,1408]{1,0:T(8,128)(2,1)S(1)}, bf16[64,1408]{1,0:T(8,128)(2,1)S(1)}) custom-call(s32[12]{0:T(128)S(1)} %dynamic-slice_bitcast_fusion.pos_ref, f32[256,1408]{1,0:T(8,128)S(1)} %keep.1.kept_ref, bf16[256,1408]{1,0:T(8,128)(2,1)S(1)} %collective-permute-done.18.up_ref, ...), custom_call_target="tpu_custom_call" | custom-call | tf_op jit(solution)/shard_map/total_step/pallas_call | solution.py:393
  77.0 2.3 %collective-permute-start.21 = (bf16[64,1408]{1,0:T(8,128)(2,1)S(1)}, bf16[64,1408]{1,0:T(8,128)(2,1)S(1)}, u32[]{:S(2)}, u32[]{:S(2)}) collective-permute-start(bf16[64,1408]{1,0:T(8,128)(2,1)S(1)} %get-tuple-element.90), channel_id=1, source_target_pairs={{0,3},{1,0},{2,1},{3,2},{4,7},{5,4},{6,5},{7,6},{8,11},{9,8},{10,9... | collective-permute-start | bytes 540680 | tf_op jit(solution)/shard_map/ppermute | solution.py:437
  79.9 4.1 %collective-permute-done.20.next_ref = bf16[64,1408]{1,0:T(8,128)(2,1)S(1)} collective-permute-done((bf16[64,1408]{1,0:T(8,128)(2,1)S(1)}, bf16[64,1408]{1,0:T(8,128)(2,1)S(1)}, u32[]{:S(2)}, u32[]{:S(2)}) %collective-permute-start.20) | collective-permute-done | bytes 180256 | tf_op jit(solution)/shard_map/ppermute | solution.py:437
  84.4 2.0 %collective-permute-done.22.far_ref = bf16[64,1408]{1,0:T(8,128)(2,1)S(1)} collective-permute-done((bf16[64,1408]{1,0:T(8,128)(2,1)S(1)}, bf16[64,1408]{1,0:T(8,128)(2,1)S(1)}, u32[]{:S(2)}, u32[]{:S(2)}) %collective-permute-start.22) | collective-permute-done | bytes 180256 | tf_op jit(solution)/shard_map/ppermute | solution.py:437
  86.4 1.9 %finish.1 = bf16[64,5376]{1,0:T(8,128)(2,1)} custom-call(s32[12]{0:T(128)S(1)} %dynamic-slice_bitcast_fusion.pos_ref, f32[64,1408]{1,0:T(8,128)S(1)} %get-tuple-element.88.own_ref, bf16[64,1408]{1,0:T(8,128)(2,1)S(1)} %collective-permute-done.20.next_ref, bf16[64,1408]{1,0:T(8,128)(2,1)S(1)} %collective-permute-done.21.last_ref, ...), custom_call_target="tpu_custom_call" | custom-call | tf_op jit(solution)/shard_map/finish/pallas_call | solution.py:424
  (44 shorter events, 10.0 us)
Async XLA Ops:
  0.0 8.6 %copy-start.5 = (f32[5376]{0:T(1024)S(1)}, f32[5376]{0:T(1024)}, u32[]{:S(2)}) copy-start(f32[5376]{0:T(1024)} %param.14) | copy-start | bytes 64516
  0.0 8.6 %copy-start.4 = (f32[128]{0:T(128)S(1)}, f32[128]{0:T(128)}, u32[]{:S(2)}) copy-start(f32[128]{0:T(128)} %param.19) | copy-start | bytes 1540
  2.5 23.7 %collective-permute-start = (bf16[128,1408]{1,0:T(8,128)(2,1)S(1)}, bf16[128,1408]{1,0:T(8,128)(2,1)S(1)}, u32[]{:S(2)}, u32[]{:S(2)}) collective-permute-start(bf16[128,1408]{1,0:T(8,128)(2,1)S(1)} %get-tuple-element.55), channel_id=1, source_target_pairs={{0,1},{1,2},{2,3},{3,0},{4,5},{5,6},{6,7},{7,4},{8,9},{9,10},{10,1... | collective-permute-start | bytes 1081352 | tf_op jit(solution)/shard_map/ppermute | solution.py:437
  4.6 21.7 %collective-permute-start.1 = (bf16[128,1408]{1,0:T(8,128)(2,1)S(1)}, bf16[128,1408]{1,0:T(8,128)(2,1)S(1)}, u32[]{:S(2)}, u32[]{:S(2)}) collective-permute-start(bf16[128,1408]{1,0:T(8,128)(2,1)S(1)} %get-tuple-element.56), channel_id=1, source_target_pairs={{0,3},{1,0},{2,1},{3,2},{4,7},{5,4},{6,5},{7,6},{8,11},{9,8},{10,9... | collective-permute-start | bytes 1081352 | tf_op jit(solution)/shard_map/ppermute | solution.py:437
  6.8 19.5 %collective-permute-start.2 = (bf16[128,1408]{1,0:T(8,128)(2,1)S(1)}, bf16[128,1408]{1,0:T(8,128)(2,1)S(1)}, u32[]{:S(2)}, u32[]{:S(2)}) collective-permute-start(bf16[128,1408]{1,0:T(8,128)(2,1)S(1)} %get-tuple-element.57), channel_id=1, source_target_pairs={{0,2},{1,3},{2,0},{3,1},{4,6},{5,7},{6,4},{7,5},{8,10},{9,11},{10,... | collective-permute-start | bytes 1081352 | tf_op jit(solution)/shard_map/ppermute | solution.py:437
  8.6 12.7 %copy-start = (bf16[5376,256]{1,0:T(8,128)(2,1)S(1)}, bf16[5376,256]{1,0:T(8,128)(2,1)}, u32[]{:S(2)}) copy-start(bf16[5376,256]{1,0:T(8,128)(2,1)} %w_ref.3) | copy-start | bytes 8257540
  8.6 12.7 %copy-start.3 = (f32[128]{0:T(128)S(1)}, f32[128]{0:T(128)}, u32[]{:S(2)}) copy-start(f32[128]{0:T(128)} %param.18) | copy-start | bytes 1540
  19.9 11.1 %collective-permute-start.6 = (bf16[1024,256]{1,0:T(8,128)(2,1)S(1)}, bf16[1024,256]{1,0:T(8,128)(2,1)S(1)}, u32[]{:S(2)}, u32[]{:S(2)}) collective-permute-start(bf16[1024,256]{1,0:T(8,128)(2,1)S(1)} %get-tuple-element.63.kv_ref), channel_id=1, source_target_pairs={{0,16},{16,32},{32,48},{48,64},{64,80},{80,96},{96,112},{1,17},{17... | collective-permute-start | bytes 1572872 | tf_op jit(solution)/shard_map/ppermute | solution.py:456
  21.3 9.7 %copy-start.1 = (bf16[1024,128]{1,0:T(8,128)(2,1)S(1)}, bf16[1024,128]{1,0:T(8,128)(2,1)}, u32[]{:S(2)}) copy-start(bf16[1024,128]{1,0:T(8,128)(2,1)} %pk_ref.1) | copy-start | bytes 786436
  21.3 9.7 %copy-start.2 = (bf16[1024,128]{1,0:T(8,128)(2,1)S(1)}, bf16[1024,128]{1,0:T(8,128)(2,1)}, u32[]{:S(2)}) copy-start(bf16[1024,128]{1,0:T(8,128)(2,1)} %pv_ref.1) | copy-start | bytes 786436
  26.3 3.7 %collective-permute-start.3 = (bf16[128,1408]{1,0:T(8,128)(2,1)S(1)}, bf16[128,1408]{1,0:T(8,128)(2,1)S(1)}, u32[]{:S(2)}, u32[]{:S(2)}) collective-permute-start(bf16[128,1408]{1,0:T(8,128)(2,1)S(1)} %collective-permute-done.refs_0_), channel_id=1, source_target_pairs={{0,16},{16,0},{1,17},{17,1},{2,18},{18,2},{3,19},{19,3},{4,20},{20... | collective-permute-start | bytes 1081352 | tf_op jit(solution)/shard_map/ppermute | solution.py:459
  28.6 1.8 %collective-permute-start.4 = (bf16[128,1408]{1,0:T(8,128)(2,1)S(1)}, bf16[128,1408]{1,0:T(8,128)(2,1)S(1)}, u32[]{:S(2)}, u32[]{:S(2)}) collective-permute-start(bf16[128,1408]{1,0:T(8,128)(2,1)S(1)} %collective-permute-done.1.refs_1_), channel_id=1, source_target_pairs={{0,16},{16,0},{1,17},{17,1},{2,18},{18,2},{3,19},{19,3},{4,20},{20... | collective-permute-start | bytes 1081352 | tf_op jit(solution)/shard_map/ppermute | solution.py:459
  28.7 2.2 %collective-permute-start.5 = (bf16[128,1408]{1,0:T(8,128)(2,1)S(1)}, bf16[128,1408]{1,0:T(8,128)(2,1)S(1)}, u32[]{:S(2)}, u32[]{:S(2)}) collective-permute-start(bf16[128,1408]{1,0:T(8,128)(2,1)S(1)} %collective-permute-done.2.refs_2_), channel_id=1, source_target_pairs={{0,16},{16,0},{1,17},{17,1},{2,18},{18,2},{3,19},{19,3},{4,20},{20... | collective-permute-start | bytes 1081352 | tf_op jit(solution)/shard_map/ppermute | solution.py:459
  33.0 10.9 %collective-permute-start.7 = (bf16[256,256]{1,0:T(8,128)(2,1)S(1)}, bf16[256,256]{1,0:T(8,128)(2,1)S(1)}, u32[]{:S(2)}, u32[]{:S(2)}) collective-permute-start(bf16[256,256]{1,0:T(8,128)(2,1)S(1)} %get-tuple-element.68.refs_0_), channel_id=1, source_target_pairs={{0,1},{1,2},{2,3},{3,0},{4,5},{5,6},{6,7},{7,4},{8,9},{9,10},{10,1... | collective-permute-start | bytes 393224 | tf_op jit(solution)/shard_map/ppermute | solution.py:437
  34.1 11.7 %collective-permute-start.8 = (bf16[256,256]{1,0:T(8,128)(2,1)S(1)}, bf16[256,256]{1,0:T(8,128)(2,1)S(1)}, u32[]{:S(2)}, u32[]{:S(2)}) collective-permute-start(bf16[256,256]{1,0:T(8,128)(2,1)S(1)} %get-tuple-element.68.refs_0_), channel_id=1, source_target_pairs={{0,3},{1,0},{2,1},{3,2},{4,7},{5,4},{6,5},{7,6},{8,11},{9,8},{10,9... | collective-permute-start | bytes 393224 | tf_op jit(solution)/shard_map/ppermute | solution.py:437
  36.3 9.5 %collective-permute-start.9 = (bf16[256,256]{1,0:T(8,128)(2,1)S(1)}, bf16[256,256]{1,0:T(8,128)(2,1)S(1)}, u32[]{:S(2)}, u32[]{:S(2)}) collective-permute-start(bf16[256,256]{1,0:T(8,128)(2,1)S(1)} %get-tuple-element.68.refs_0_), channel_id=1, source_target_pairs={{0,2},{1,3},{2,0},{3,1},{4,6},{5,7},{6,4},{7,5},{8,10},{9,11},{10,... | collective-permute-start | bytes 393224 | tf_op jit(solution)/shard_map/ppermute | solution.py:437
  39.7 12.2 %collective-permute-start.15 = (bf16[512,256]{1,0:T(8,128)(2,1)S(1)}, bf16[512,256]{1,0:T(8,128)(2,1)S(1)}, u32[]{:S(2)}, u32[]{:S(2)}) collective-permute-start(bf16[512,256]{1,0:T(8,128)(2,1)S(1)} %attend.4.refs_0_), channel_id=1, source_target_pairs={{0,1},{1,2},{2,3},{3,0},{4,5},{5,6},{6,7},{7,4},{8,9},{9,10},{10,1... | collective-permute-start | bytes 786440 | tf_op jit(solution)/shard_map/ppermute | solution.py:437
  40.3 13.6 %collective-permute-start.16 = (bf16[512,256]{1,0:T(8,128)(2,1)S(1)}, bf16[512,256]{1,0:T(8,128)(2,1)S(1)}, u32[]{:S(2)}, u32[]{:S(2)}) collective-permute-start(bf16[512,256]{1,0:T(8,128)(2,1)S(1)} %attend.4.refs_0_), channel_id=1, source_target_pairs={{0,3},{1,0},{2,1},{3,2},{4,7},{5,4},{6,5},{7,6},{8,11},{9,8},{10,9... | collective-permute-start | bytes 786440 | tf_op jit(solution)/shard_map/ppermute | solution.py:437
  43.9 10.8 %collective-permute-start.17 = (bf16[512,256]{1,0:T(8,128)(2,1)S(1)}, bf16[512,256]{1,0:T(8,128)(2,1)S(1)}, u32[]{:S(2)}, u32[]{:S(2)}) collective-permute-start(bf16[512,256]{1,0:T(8,128)(2,1)S(1)} %attend.4.refs_0_), channel_id=1, source_target_pairs={{0,2},{1,3},{2,0},{3,1},{4,6},{5,7},{6,4},{7,5},{8,10},{9,11},{10,... | collective-permute-start | bytes 786440 | tf_op jit(solution)/shard_map/ppermute | solution.py:437
  46.8 10.3 %collective-permute-start.13 = (bf16[128,1408]{1,0:T(8,128)(2,1)S(1)}, bf16[128,1408]{1,0:T(8,128)(2,1)S(1)}, u32[]{:S(2)}, u32[]{:S(2)}) collective-permute-start(bf16[128,1408]{1,0:T(8,128)(2,1)S(1)} %get-tuple-element.77), channel_id=1, source_target_pairs={{0,4},{4,8},{8,12},{12,0},{1,5},{5,9},{9,13},{13,1},{2,6},{6,10},{... | collective-permute-start | bytes 1081352 | tf_op jit(solution)/shard_map/ppermute | solution.py:437
  48.3 8.8 %collective-permute-start.14 = (bf16[128,1408]{1,0:T(8,128)(2,1)S(1)}, bf16[128,1408]{1,0:T(8,128)(2,1)S(1)}, u32[]{:S(2)}, u32[]{:S(2)}) collective-permute-start(bf16[128,1408]{1,0:T(8,128)(2,1)S(1)} %get-tuple-element.79), channel_id=1, source_target_pairs={{0,12},{4,0},{8,4},{12,8},{1,13},{5,1},{9,5},{13,9},{2,14},{6,2},{... | collective-permute-start | bytes 1081352 | tf_op jit(solution)/shard_map/ppermute | solution.py:437
  57.6 17.5 %collective-permute-start.18 = (bf16[256,1408]{1,0:T(8,128)(2,1)S(1)}, bf16[256,1408]{1,0:T(8,128)(2,1)S(1)}, u32[]{:S(2)}, u32[]{:S(2)}) collective-permute-start(bf16[256,1408]{1,0:T(8,128)(2,1)S(1)} %get-tuple-element.86), channel_id=1, source_target_pairs={{0,4},{4,8},{8,12},{12,0},{1,5},{5,9},{9,13},{13,1},{2,6},{6,10},{... | collective-permute-start | bytes 2162696 | tf_op jit(solution)/shard_map/ppermute | solution.py:437
  59.2 20.7 %copy-start.6 = (f32[5376]{0:T(1024)S(1)}, f32[5376]{0:T(1024)}, u32[]{:S(2)}) copy-start(f32[5376]{0:T(1024)} %param.23) | copy-start | bytes 64516
  59.2 15.9 %collective-permute-start.19 = (bf16[256,1408]{1,0:T(8,128)(2,1)S(1)}, bf16[256,1408]{1,0:T(8,128)(2,1)S(1)}, u32[]{:S(2)}, u32[]{:S(2)}) collective-permute-start(bf16[256,1408]{1,0:T(8,128)(2,1)S(1)} %get-tuple-element.87), channel_id=1, source_target_pairs={{0,12},{4,0},{8,4},{12,8},{1,13},{5,1},{9,5},{13,9},{2,14},{6,2},{... | collective-permute-start | bytes 2162696 | tf_op jit(solution)/shard_map/ppermute | solution.py:437
  60.9 7.2 %collective-permute-start.10 = (bf16[256,256]{1,0:T(8,128)(2,1)S(1)}, bf16[256,256]{1,0:T(8,128)(2,1)S(1)}, u32[]{:S(2)}, u32[]{:S(2)}) collective-permute-start(bf16[256,256]{1,0:T(8,128)(2,1)S(1)} %attend.5.refs_0_), channel_id=1, source_target_pairs={{0,1},{1,2},{2,3},{3,0},{4,5},{5,6},{6,7},{7,4},{8,9},{9,10},{10,1... | collective-permute-start | bytes 393224 | tf_op jit(solution)/shard_map/ppermute | solution.py:437
  61.7 6.4 %collective-permute-start.11 = (bf16[256,256]{1,0:T(8,128)(2,1)S(1)}, bf16[256,256]{1,0:T(8,128)(2,1)S(1)}, u32[]{:S(2)}, u32[]{:S(2)}) collective-permute-start(bf16[256,256]{1,0:T(8,128)(2,1)S(1)} %attend.5.refs_0_), channel_id=1, source_target_pairs={{0,3},{1,0},{2,1},{3,2},{4,7},{5,4},{6,5},{7,6},{8,11},{9,8},{10,9... | collective-permute-start | bytes 393224 | tf_op jit(solution)/shard_map/ppermute | solution.py:437
  64.2 6.5 %collective-permute-start.12 = (bf16[256,256]{1,0:T(8,128)(2,1)S(1)}, bf16[256,256]{1,0:T(8,128)(2,1)S(1)}, u32[]{:S(2)}, u32[]{:S(2)}) collective-permute-start(bf16[256,256]{1,0:T(8,128)(2,1)S(1)} %attend.5.refs_0_), channel_id=1, source_target_pairs={{0,2},{1,3},{2,0},{3,1},{4,6},{5,7},{6,4},{7,5},{8,10},{9,11},{10,... | collective-permute-start | bytes 393224 | tf_op jit(solution)/shard_map/ppermute | solution.py:437
  76.1 7.9 %collective-permute-start.20 = (bf16[64,1408]{1,0:T(8,128)(2,1)S(1)}, bf16[64,1408]{1,0:T(8,128)(2,1)S(1)}, u32[]{:S(2)}, u32[]{:S(2)}) collective-permute-start(bf16[64,1408]{1,0:T(8,128)(2,1)S(1)} %get-tuple-element.89), channel_id=1, source_target_pairs={{0,1},{1,2},{2,3},{3,0},{4,5},{5,6},{6,7},{7,4},{8,9},{9,10},{10,1... | collective-permute-start | bytes 540680 | tf_op jit(solution)/shard_map/ppermute | solution.py:437
  77.0 7.3 %collective-permute-start.21 = (bf16[64,1408]{1,0:T(8,128)(2,1)S(1)}, bf16[64,1408]{1,0:T(8,128)(2,1)S(1)}, u32[]{:S(2)}, u32[]{:S(2)}) collective-permute-start(bf16[64,1408]{1,0:T(8,128)(2,1)S(1)} %get-tuple-element.90), channel_id=1, source_target_pairs={{0,3},{1,0},{2,1},{3,2},{4,7},{5,4},{6,5},{7,6},{8,11},{9,8},{10,9... | collective-permute-start | bytes 540680 | tf_op jit(solution)/shard_map/ppermute | solution.py:437
  79.4 7.0 %collective-permute-start.22 = (bf16[64,1408]{1,0:T(8,128)(2,1)S(1)}, bf16[64,1408]{1,0:T(8,128)(2,1)S(1)}, u32[]{:S(2)}, u32[]{:S(2)}) collective-permute-start(bf16[64,1408]{1,0:T(8,128)(2,1)S(1)} %get-tuple-element.91), channel_id=1, source_target_pairs={{0,2},{1,3},{2,0},{3,1},{4,6},{5,7},{6,4},{7,5},{8,10},{9,11},{10,... | collective-permute-start | bytes 540680 | tf_op jit(solution)/shard_map/ppermute | solution.py:437

commit v11 on v10

--- a/solution.py
+++ b/solution.py
@@ -79,9 +79,8 @@
     ]
     blocks = MODEL_WIDTH // 128
 
-    def norm_group(i, carry):
-        at = i * GROUP if isinstance(i, int) else pl.multiple_of(i * GROUP, GROUP)
-        rows = pl.ds(at, GROUP)
+    def norm_group(i):
+        rows = slice(i * GROUP, (i + 1) * GROUP)
         parts = [jnp.zeros((GROUP, 128), F32) for _ in range(2)]
         for b in range(blocks):
             v = tok_ref[rows, b * 128 : (b + 1) * 128].astype(F32)
@@ -92,7 +91,6 @@
             cols = slice(b * 128, (b + 1) * 128)
             v = tok_ref[rows, cols].astype(F32)
             normed[rows, cols] = (v * r * g_all[:, cols]).astype(BF16)
-        return carry
 
     def multiply_and_rotate():
         raw = jnp.dot(normed[...], w_all[...], preferred_element_type=F32)
@@ -104,7 +102,8 @@
         for copy in copies:
             copy.start()
         g_all[...] = jnp.broadcast_to(g_ref[...], g_all.shape)
-        lax.fori_loop(0, ROWS // GROUP, norm_group, 0, unroll=4)
+        for i in range(ROWS // GROUP):
+            norm_group(i)
         for copy in copies:
             copy.wait()
         multiply_and_rotate()
@@ -112,7 +111,7 @@
     @pl.when(step != 0)
     def _():
         for i in range(ROWS // GROUP):
-            norm_group(i, 0)
+            norm_group(i)
         multiply_and_rotate()
 
     @pl.when(step == pos_ref[ROW_AT + 8])

time: 88.6 us -> 88.9 us (level)
  no operation moved by 1% of the time
where the time goes in v11:
time: 88.9 us; the launch traced here: 88.5 us
  starting transfers between devices  33.4 us (38%)
  Pallas kernels  32.9 us (37%)
  waiting for transfers between devices  21.1 us (24%)
    ppermute x19, starting transfers between devices, shift_by(): return lax.ppermute(array, axis, [(i, (i + steps) % 4) for i in range(4)])  29.3 us
    ppermute x19, waiting for transfers between devices, shift_by(): return lax.ppermute(array, axis, [(i, (i + steps) % 4) for i in range(4)])  19.3 us
    pallas_call x1, Pallas kernels, key_value(): pl.pallas_call(key_value_kernel, grid_spec=pltpu.PrefetchScalarGridSpec(n...  11.7 us
    pallas_call x3, Pallas kernels, attend(): pl.pallas_call(functools.partial(kernel, first_part), in_specs=[SMEM] + [...  6.67 us
    pallas_call x1, Pallas kernels, query(): pl.pallas_call(query_kernel, in_specs=[SMEM, VMEM, VMEM, VMEM, ANY, ANY],...  4.94 us
    pallas_call x3, Pallas kernels, multiply(): pl.pallas_call(kernel, in_specs=[VMEM] * 6, out_specs=jax.tree.map(lambda...  3.77 us
    ppermute x3, starting transfers between devices, per_device(): swapped = [lax.ppermute(part, 'c', [(0, 1), (1, 0)]) for part in lines]  2.86 us
    pallas_call x1, Pallas kernels, finish(): pl.pallas_call(finish_kernel, in_specs=[SMEM] + [VMEM] * 6, out_specs=VME...  1.89 us
  transfers between devices with their start and end apart: 23, of which 12 were waited for; matrix products, arithmetic and copies ran while one was open for 0% of the time, Pallas kernels for 29%

profile of v11, /device:TPU:0, one launch (start us, length us, event | category | flops | bytes accessed | tf_op | source)
XLA Modules:
  0.0 88.5 jit_solution(8866183715550965110)
XLA Ops:
  0.7 1.8 %pick.1 = (bf16[128,1408]{1,0:T(8,128)(2,1)S(1)}, bf16[128,1408]{1,0:T(8,128)(2,1)S(1)}, bf16[128,1408]{1,0:T(8,128)(2,1)S(1)}) custom-call(s32[12]{0:T(128)S(1)} %dynamic-slice_bitcast_fusion.pos_ref, bf16[256,5376]{1,0:T(8,128)(2,1)} %w_out_ref.1), custom_call_target="tpu_custom_call" | custom-call | tf_op jit(solution)/shard_map/pick/pallas_call | solution.py:292
  2.5 2.1 %collective-permute-start = (bf16[128,1408]{1,0:T(8,128)(2,1)S(1)}, bf16[128,1408]{1,0:T(8,128)(2,1)S(1)}, u32[]{:S(2)}, u32[]{:S(2)}) collective-permute-start(bf16[128,1408]{1,0:T(8,128)(2,1)S(1)} %get-tuple-element.55), channel_id=1, source_target_pairs={{0,1},{1,2},{2,3},{3,0},{4,5},{5,6},{6,7},{7,4},{8,9},{9,10},{10,1... | collective-permute-start | bytes 1081352 | tf_op jit(solution)/shard_map/ppermute | solution.py:436
  4.6 2.2 %collective-permute-start.1 = (bf16[128,1408]{1,0:T(8,128)(2,1)S(1)}, bf16[128,1408]{1,0:T(8,128)(2,1)S(1)}, u32[]{:S(2)}, u32[]{:S(2)}) collective-permute-start(bf16[128,1408]{1,0:T(8,128)(2,1)S(1)} %get-tuple-element.56), channel_id=1, source_target_pairs={{0,3},{1,0},{2,1},{3,2},{4,7},{5,4},{6,5},{7,6},{8,11},{9,8},{10,9... | collective-permute-start | bytes 1081352 | tf_op jit(solution)/shard_map/ppermute | solution.py:436
  6.8 1.8 %collective-permute-start.2 = (bf16[128,1408]{1,0:T(8,128)(2,1)S(1)}, bf16[128,1408]{1,0:T(8,128)(2,1)S(1)}, u32[]{:S(2)}, u32[]{:S(2)}) collective-permute-start(bf16[128,1408]{1,0:T(8,128)(2,1)S(1)} %get-tuple-element.57), channel_id=1, source_target_pairs={{0,2},{1,3},{2,0},{3,1},{4,6},{5,7},{6,4},{7,5},{8,10},{9,11},{10,... | collective-permute-start | bytes 1081352 | tf_op jit(solution)/shard_map/ppermute | solution.py:436
  8.6 11.7 %key_value.1 = (bf16[1024,5376]{1,0:T(8,128)(2,1)S(1)}, bf16[1024,256]{1,0:T(8,128)(2,1)S(1)}, bf16[64,5376]{1,0:T(8,128)(2,1)S(1)}) custom-call(s32[12]{0:T(128)S(1)} %dynamic-slice_bitcast_fusion.pos_ref, bf16[1024,5376]{1,0:T(8,128)(2,1)} %tok_ref.1, f32[1,5376]{1,0:T(1,128)S(1)} %reshape.16.g_ref, bf16[5376,128]{1,0:T(8,128)(2,1)} %wk_ref.1, ...), custom_call_target="tpu_custom_call" | custom-call | flops 11274289152 | bytes 27262976 | tf_op jit(solution)/shard_map/key_value/pallas_call | solution.py:139
  20.3 1.3 %collective-permute-start.6 = (bf16[1024,256]{1,0:T(8,128)(2,1)S(1)}, bf16[1024,256]{1,0:T(8,128)(2,1)S(1)}, u32[]{:S(2)}, u32[]{:S(2)}) collective-permute-start(bf16[1024,256]{1,0:T(8,128)(2,1)S(1)} %get-tuple-element.63.kv_ref), channel_id=1, source_target_pairs={{0,16},{16,32},{32,48},{48,64},{64,80},{80,96},{96,112},{1,17},{17... | collective-permute-start | bytes 1572872 | tf_op jit(solution)/shard_map/ppermute | solution.py:455
  21.7 4.9 %query.1 = (bf16[1024,256]{1,0:T(8,128)(2,1)S(1)}, bf16[256,1408]{1,0:T(8,128)(2,1)S(1)}) custom-call(s32[12]{0:T(128)S(1)} %dynamic-slice_bitcast_fusion.pos_ref, bf16[1024,5376]{1,0:T(8,128)(2,1)S(1)} %get-tuple-element.53.normed_ref, bf16[5376,256]{1,0:T(8,128)(2,1)S(1)} %copy-done, f32[1,128]{1,0:T(1,128)S(1)} %bitcast.4, ...), custom_call_target="tpu_custom_call" | custom-call | tf_op jit(solution)/shard_map/query/pallas_call | solution.py:192
  26.7 2.4 %collective-permute-start.3 = (bf16[128,1408]{1,0:T(8,128)(2,1)S(1)}, bf16[128,1408]{1,0:T(8,128)(2,1)S(1)}, u32[]{:S(2)}, u32[]{:S(2)}) collective-permute-start(bf16[128,1408]{1,0:T(8,128)(2,1)S(1)} %collective-permute-done.refs_0_), channel_id=1, source_target_pairs={{0,16},{16,0},{1,17},{17,1},{2,18},{18,2},{3,19},{19,3},{4,20},{20... | collective-permute-start | bytes 1081352 | tf_op jit(solution)/shard_map/ppermute | solution.py:458
  31.4 2.0 %attend.3 = (bf16[256,256]{1,0:T(8,128)(2,1)S(1)}, bf16[2048,128]{1,0:T(8,128)(2,1)S(1)}, bf16[2048,256]{1,0:T(8,128)(2,1)S(1)}) custom-call(s32[12]{0:T(128)S(1)} %dynamic-slice_bitcast_fusion.pos_ref, bf16[1024,256]{1,0:T(8,128)(2,1)S(1)} %get-tuple-element.62.q_ref, bf16[1024,256]{1,0:T(8,128)(2,1)S(1)} %get-tuple-element.63.kv_ref, ...), custom_call_target="tpu_custom_call" | custom-call | tf_op jit(solution)/shard_map/attend/pallas_call | solution.py:262
  33.4 1.1 %collective-permute-start.7 = (bf16[256,256]{1,0:T(8,128)(2,1)S(1)}, bf16[256,256]{1,0:T(8,128)(2,1)S(1)}, u32[]{:S(2)}, u32[]{:S(2)}) collective-permute-start(bf16[256,256]{1,0:T(8,128)(2,1)S(1)} %get-tuple-element.68.refs_0_), channel_id=1, source_target_pairs={{0,1},{1,2},{2,3},{3,0},{4,5},{5,6},{6,7},{7,4},{8,9},{9,10},{10,1... | collective-permute-start | bytes 393224 | tf_op jit(solution)/shard_map/ppermute | solution.py:436
  34.5 2.2 %collective-permute-start.8 = (bf16[256,256]{1,0:T(8,128)(2,1)S(1)}, bf16[256,256]{1,0:T(8,128)(2,1)S(1)}, u32[]{:S(2)}, u32[]{:S(2)}) collective-permute-start(bf16[256,256]{1,0:T(8,128)(2,1)S(1)} %get-tuple-element.68.refs_0_), channel_id=1, source_target_pairs={{0,3},{1,0},{2,1},{3,2},{4,7},{5,4},{6,5},{7,6},{8,11},{9,8},{10,9... | collective-permute-start | bytes 393224 | tf_op jit(solution)/shard_map/ppermute | solution.py:436
  37.2 2.9 %attend.4.refs_0_ = bf16[512,256]{1,0:T(8,128)(2,1)S(1)} custom-call(s32[12]{0:T(128)S(1)} %dynamic-slice_bitcast_fusion.pos_ref, bf16[1024,256]{1,0:T(8,128)(2,1)S(1)} %get-tuple-element.62.q_ref, bf16[2048,128]{1,0:T(8,128)(2,1)S(1)} %get-tuple-element.66.keys, bf16[2048,256]{1,0:T(8,128)(2,1)S(1)} %get-tuple-element.67.values), custom_call_target="tpu_custom_call" | custom-call | tf_op jit(solution)/shard_map/attend/pallas_call | solution.py:262
  40.5 2.9 %collective-permute-start.16 = (bf16[512,256]{1,0:T(8,128)(2,1)S(1)}, bf16[512,256]{1,0:T(8,128)(2,1)S(1)}, u32[]{:S(2)}, u32[]{:S(2)}) collective-permute-start(bf16[512,256]{1,0:T(8,128)(2,1)S(1)} %attend.4.refs_0_), channel_id=1, source_target_pairs={{0,3},{1,0},{2,1},{3,2},{4,7},{5,4},{6,5},{7,6},{8,11},{9,8},{10,9... | collective-permute-start | bytes 786440 | tf_op jit(solution)/shard_map/ppermute | solution.py:436
  44.1 1.9 %collective-permute-start.17 = (bf16[512,256]{1,0:T(8,128)(2,1)S(1)}, bf16[512,256]{1,0:T(8,128)(2,1)S(1)}, u32[]{:S(2)}, u32[]{:S(2)}) collective-permute-start(bf16[512,256]{1,0:T(8,128)(2,1)S(1)} %attend.4.refs_0_), channel_id=1, source_target_pairs={{0,2},{1,3},{2,0},{3,1},{4,6},{5,7},{6,4},{7,5},{8,10},{9,11},{10,... | collective-permute-start | bytes 786440 | tf_op jit(solution)/shard_map/ppermute | solution.py:436
  46.0 1.0 %far.1 = (bf16[128,1408]{1,0:T(8,128)(2,1)S(1)}, bf16[128,1408]{1,0:T(8,128)(2,1)S(1)}) custom-call(bf16[256,256]{1,0:T(8,128)(2,1)S(1)} %get-tuple-element.68.refs_0_, bf16[256,256]{1,0:T(8,128)(2,1)S(1)} %collective-permute-done.7.refs_1_, bf16[256,256]{1,0:T(8,128)(2,1)S(1)} %collective-permute-done.8.refs_2_, ...), custom_call_target="tpu_custom_call" | custom-call | tf_op jit(solution)/shard_map/far/pallas_call | solution.py:366
  47.0 1.6 %collective-permute-start.13 = (bf16[128,1408]{1,0:T(8,128)(2,1)S(1)}, bf16[128,1408]{1,0:T(8,128)(2,1)S(1)}, u32[]{:S(2)}, u32[]{:S(2)}) collective-permute-start(bf16[128,1408]{1,0:T(8,128)(2,1)S(1)} %get-tuple-element.77), channel_id=1, source_target_pairs={{0,4},{4,8},{8,12},{12,0},{1,5},{5,9},{9,13},{13,1},{2,6},{6,10},{... | collective-permute-start | bytes 1081352 | tf_op jit(solution)/shard_map/ppermute | solution.py:436
  48.6 1.7 %collective-permute-start.14 = (bf16[128,1408]{1,0:T(8,128)(2,1)S(1)}, bf16[128,1408]{1,0:T(8,128)(2,1)S(1)}, u32[]{:S(2)}, u32[]{:S(2)}) collective-permute-start(bf16[128,1408]{1,0:T(8,128)(2,1)S(1)} %get-tuple-element.79), channel_id=1, source_target_pairs={{0,12},{4,0},{8,4},{12,8},{1,13},{5,1},{9,5},{13,9},{2,14},{6,2},{... | collective-permute-start | bytes 1081352 | tf_op jit(solution)/shard_map/ppermute | solution.py:436
  50.3 1.8 %attend.5.refs_0_ = bf16[256,256]{1,0:T(8,128)(2,1)S(1)} custom-call(s32[12]{0:T(128)S(1)} %dynamic-slice_bitcast_fusion.pos_ref, bf16[1024,256]{1,0:T(8,128)(2,1)S(1)} %get-tuple-element.62.q_ref, bf16[2048,128]{1,0:T(8,128)(2,1)S(1)} %get-tuple-element.66.keys, bf16[2048,256]{1,0:T(8,128)(2,1)S(1)} %get-tuple-element.67.values), custom_call_target="tpu_custom_call" | custom-call | flops 4000000000 | tf_op jit(solution)/shard_map/attend/pallas_call | solution.py:262
  52.1 2.0 %collective-permute-done.16.refs_2_ = bf16[512,256]{1,0:T(8,128)(2,1)S(1)} collective-permute-done((bf16[512,256]{1,0:T(8,128)(2,1)S(1)}, bf16[512,256]{1,0:T(8,128)(2,1)S(1)}, u32[]{:S(2)}, u32[]{:S(2)}) %collective-permute-start.16) | collective-permute-done | bytes 262176 | tf_op jit(solution)/shard_map/ppermute | solution.py:436
  55.0 1.8 %near.1 = (bf16[256,1408]{1,0:T(8,128)(2,1)S(1)}, bf16[256,1408]{1,0:T(8,128)(2,1)S(1)}) custom-call(bf16[512,256]{1,0:T(8,128)(2,1)S(1)} %attend.4.refs_0_, bf16[512,256]{1,0:T(8,128)(2,1)S(1)} %collective-permute-done.15.refs_1_, bf16[512,256]{1,0:T(8,128)(2,1)S(1)} %collective-permute-done.16.refs_2_, ...), custom_call_target="tpu_custom_call" | custom-call | flops 30000001024 | tf_op jit(solution)/shard_map/near/pallas_call | solution.py:366
  57.8 1.6 %collective-permute-start.18 = (bf16[256,1408]{1,0:T(8,128)(2,1)S(1)}, bf16[256,1408]{1,0:T(8,128)(2,1)S(1)}, u32[]{:S(2)}, u32[]{:S(2)}) collective-permute-start(bf16[256,1408]{1,0:T(8,128)(2,1)S(1)} %get-tuple-element.86), channel_id=1, source_target_pairs={{0,4},{4,8},{8,12},{12,0},{1,5},{5,9},{9,13},{13,1},{2,6},{6,10},{... | collective-permute-start | bytes 2162696 | tf_op jit(solution)/shard_map/ppermute | solution.py:436
  59.4 1.7 %collective-permute-start.19 = (bf16[256,1408]{1,0:T(8,128)(2,1)S(1)}, bf16[256,1408]{1,0:T(8,128)(2,1)S(1)}, u32[]{:S(2)}, u32[]{:S(2)}) collective-permute-start(bf16[256,1408]{1,0:T(8,128)(2,1)S(1)} %get-tuple-element.87), channel_id=1, source_target_pairs={{0,12},{4,0},{8,4},{12,8},{1,13},{5,1},{9,5},{13,9},{2,14},{6,2},{... | collective-permute-start | bytes 2162696 | tf_op jit(solution)/shard_map/ppermute | solution.py:436
  61.9 2.5 %collective-permute-start.11 = (bf16[256,256]{1,0:T(8,128)(2,1)S(1)}, bf16[256,256]{1,0:T(8,128)(2,1)S(1)}, u32[]{:S(2)}, u32[]{:S(2)}) collective-permute-start(bf16[256,256]{1,0:T(8,128)(2,1)S(1)} %attend.5.refs_0_), channel_id=1, source_target_pairs={{0,3},{1,0},{2,1},{3,2},{4,7},{5,4},{6,5},{7,6},{8,11},{9,8},{10,9... | collective-permute-start | bytes 393224 | tf_op jit(solution)/shard_map/ppermute | solution.py:436
  64.9 3.4 %collective-permute-done.10.refs_1_ = bf16[256,256]{1,0:T(8,128)(2,1)S(1)} collective-permute-done((bf16[256,256]{1,0:T(8,128)(2,1)S(1)}, bf16[256,256]{1,0:T(8,128)(2,1)S(1)}, u32[]{:S(2)}, u32[]{:S(2)}) %collective-permute-start.10) | collective-permute-done | bytes 131104 | tf_op jit(solution)/shard_map/ppermute | solution.py:436
  68.3 2.5 %collective-permute-done.12.refs_3_ = bf16[256,256]{1,0:T(8,128)(2,1)S(1)} collective-permute-done((bf16[256,256]{1,0:T(8,128)(2,1)S(1)}, bf16[256,256]{1,0:T(8,128)(2,1)S(1)}, u32[]{:S(2)}, u32[]{:S(2)}) %collective-permute-start.12) | collective-permute-done | bytes 131104 | tf_op jit(solution)/shard_map/ppermute | solution.py:436
  70.9 1.0 %keep.1.kept_ref = f32[256,1408]{1,0:T(8,128)S(1)} custom-call(bf16[256,256]{1,0:T(8,128)(2,1)S(1)} %attend.5.refs_0_, bf16[256,256]{1,0:T(8,128)(2,1)S(1)} %collective-permute-done.10.refs_1_, bf16[256,256]{1,0:T(8,128)(2,1)S(1)} %collective-permute-done.11.refs_2_, bf16[256,256]{1,0:T(8,128)(2,1)S(1)} %collective-permute-done.12.refs_3_, ...), custom_call_target="tpu_custom_call" | custom-call | tf_op jit(solution)/shard_map/keep/pallas_call | solution.py:366
  71.8 3.5 %collective-permute-done.18.up_ref = bf16[256,1408]{1,0:T(8,128)(2,1)S(1)} collective-permute-done((bf16[256,1408]{1,0:T(8,128)(2,1)S(1)}, bf16[256,1408]{1,0:T(8,128)(2,1)S(1)}, u32[]{:S(2)}, u32[]{:S(2)}) %collective-permute-start.18) | collective-permute-done | bytes 720928 | tf_op jit(solution)/shard_map/ppermute | solution.py:436
  75.3 1.0 %total_step.1 = (f32[64,1408]{1,0:T(8,128)S(1)}, bf16[64,1408]{1,0:T(8,128)(2,1)S(1)}, bf16[64,1408]{1,0:T(8,128)(2,1)S(1)}, bf16[64,1408]{1,0:T(8,128)(2,1)S(1)}) custom-call(s32[12]{0:T(128)S(1)} %dynamic-slice_bitcast_fusion.pos_ref, f32[256,1408]{1,0:T(8,128)S(1)} %keep.1.kept_ref, bf16[256,1408]{1,0:T(8,128)(2,1)S(1)} %collective-permute-done.18.up_ref, ...), custom_call_target="tpu_custom_call" | custom-call | tf_op jit(solution)/shard_map/total_step/pallas_call | solution.py:392
  77.3 2.3 %collective-permute-start.21 = (bf16[64,1408]{1,0:T(8,128)(2,1)S(1)}, bf16[64,1408]{1,0:T(8,128)(2,1)S(1)}, u32[]{:S(2)}, u32[]{:S(2)}) collective-permute-start(bf16[64,1408]{1,0:T(8,128)(2,1)S(1)} %get-tuple-element.90), channel_id=1, source_target_pairs={{0,3},{1,0},{2,1},{3,2},{4,7},{5,4},{6,5},{7,6},{8,11},{9,8},{10,9... | collective-permute-start | bytes 540680 | tf_op jit(solution)/shard_map/ppermute | solution.py:436
  80.1 4.1 %collective-permute-done.20.next_ref = bf16[64,1408]{1,0:T(8,128)(2,1)S(1)} collective-permute-done((bf16[64,1408]{1,0:T(8,128)(2,1)S(1)}, bf16[64,1408]{1,0:T(8,128)(2,1)S(1)}, u32[]{:S(2)}, u32[]{:S(2)}) %collective-permute-start.20) | collective-permute-done | bytes 180256 | tf_op jit(solution)/shard_map/ppermute | solution.py:436
  84.6 2.0 %collective-permute-done.22.far_ref = bf16[64,1408]{1,0:T(8,128)(2,1)S(1)} collective-permute-done((bf16[64,1408]{1,0:T(8,128)(2,1)S(1)}, bf16[64,1408]{1,0:T(8,128)(2,1)S(1)}, u32[]{:S(2)}, u32[]{:S(2)}) %collective-permute-start.22) | collective-permute-done | bytes 180256 | tf_op jit(solution)/shard_map/ppermute | solution.py:436
  86.6 1.9 %finish.1 = bf16[64,5376]{1,0:T(8,128)(2,1)} custom-call(s32[12]{0:T(128)S(1)} %dynamic-slice_bitcast_fusion.pos_ref, f32[64,1408]{1,0:T(8,128)S(1)} %get-tuple-element.88.own_ref, bf16[64,1408]{1,0:T(8,128)(2,1)S(1)} %collective-permute-done.20.next_ref, bf16[64,1408]{1,0:T(8,128)(2,1)S(1)} %collective-permute-done.21.last_ref, ...), custom_call_target="tpu_custom_call" | custom-call | tf_op jit(solution)/shard_map/finish/pallas_call | solution.py:423
  (44 shorter events, 9.8 us)
Async XLA Ops:
  0.0 8.6 %copy-start.5 = (f32[5376]{0:T(1024)S(1)}, f32[5376]{0:T(1024)}, u32[]{:S(2)}) copy-start(f32[5376]{0:T(1024)} %param.14) | copy-start | bytes 64516
  0.0 8.6 %copy-start.4 = (f32[128]{0:T(128)S(1)}, f32[128]{0:T(128)}, u32[]{:S(2)}) copy-start(f32[128]{0:T(128)} %param.19) | copy-start | bytes 1540
  2.5 24.2 %collective-permute-start = (bf16[128,1408]{1,0:T(8,128)(2,1)S(1)}, bf16[128,1408]{1,0:T(8,128)(2,1)S(1)}, u32[]{:S(2)}, u32[]{:S(2)}) collective-permute-start(bf16[128,1408]{1,0:T(8,128)(2,1)S(1)} %get-tuple-element.55), channel_id=1, source_target_pairs={{0,1},{1,2},{2,3},{3,0},{4,5},{5,6},{6,7},{7,4},{8,9},{9,10},{10,1... | collective-permute-start | bytes 1081352 | tf_op jit(solution)/shard_map/ppermute | solution.py:436
  4.6 22.1 %collective-permute-start.1 = (bf16[128,1408]{1,0:T(8,128)(2,1)S(1)}, bf16[128,1408]{1,0:T(8,128)(2,1)S(1)}, u32[]{:S(2)}, u32[]{:S(2)}) collective-permute-start(bf16[128,1408]{1,0:T(8,128)(2,1)S(1)} %get-tuple-element.56), channel_id=1, source_target_pairs={{0,3},{1,0},{2,1},{3,2},{4,7},{5,4},{6,5},{7,6},{8,11},{9,8},{10,9... | collective-permute-start | bytes 1081352 | tf_op jit(solution)/shard_map/ppermute | solution.py:436
  6.8 19.9 %collective-permute-start.2 = (bf16[128,1408]{1,0:T(8,128)(2,1)S(1)}, bf16[128,1408]{1,0:T(8,128)(2,1)S(1)}, u32[]{:S(2)}, u32[]{:S(2)}) collective-permute-start(bf16[128,1408]{1,0:T(8,128)(2,1)S(1)} %get-tuple-element.57), channel_id=1, source_target_pairs={{0,2},{1,3},{2,0},{3,1},{4,6},{5,7},{6,4},{7,5},{8,10},{9,11},{10,... | collective-permute-start | bytes 1081352 | tf_op jit(solution)/shard_map/ppermute | solution.py:436
  8.6 13.1 %copy-start = (bf16[5376,256]{1,0:T(8,128)(2,1)S(1)}, bf16[5376,256]{1,0:T(8,128)(2,1)}, u32[]{:S(2)}) copy-start(bf16[5376,256]{1,0:T(8,128)(2,1)} %w_ref.3) | copy-start | bytes 8257540
  8.6 13.1 %copy-start.3 = (f32[128]{0:T(128)S(1)}, f32[128]{0:T(128)}, u32[]{:S(2)}) copy-start(f32[128]{0:T(128)} %param.18) | copy-start | bytes 1540
  20.3 11.0 %collective-permute-start.6 = (bf16[1024,256]{1,0:T(8,128)(2,1)S(1)}, bf16[1024,256]{1,0:T(8,128)(2,1)S(1)}, u32[]{:S(2)}, u32[]{:S(2)}) collective-permute-start(bf16[1024,256]{1,0:T(8,128)(2,1)S(1)} %get-tuple-element.63.kv_ref), channel_id=1, source_target_pairs={{0,16},{16,32},{32,48},{48,64},{64,80},{80,96},{96,112},{1,17},{17... | collective-permute-start | bytes 1572872 | tf_op jit(solution)/shard_map/ppermute | solution.py:455
  21.7 9.7 %copy-start.1 = (bf16[1024,128]{1,0:T(8,128)(2,1)S(1)}, bf16[1024,128]{1,0:T(8,128)(2,1)}, u32[]{:S(2)}) copy-start(bf16[1024,128]{1,0:T(8,128)(2,1)} %pk_ref.1) | copy-start | bytes 786436
  21.7 9.7 %copy-start.2 = (bf16[1024,128]{1,0:T(8,128)(2,1)S(1)}, bf16[1024,128]{1,0:T(8,128)(2,1)}, u32[]{:S(2)}) copy-start(bf16[1024,128]{1,0:T(8,128)(2,1)} %pv_ref.1) | copy-start | bytes 786436
  26.7 3.7 %collective-permute-start.3 = (bf16[128,1408]{1,0:T(8,128)(2,1)S(1)}, bf16[128,1408]{1,0:T(8,128)(2,1)S(1)}, u32[]{:S(2)}, u32[]{:S(2)}) collective-permute-start(bf16[128,1408]{1,0:T(8,128)(2,1)S(1)} %collective-permute-done.refs_0_), channel_id=1, source_target_pairs={{0,16},{16,0},{1,17},{17,1},{2,18},{18,2},{3,19},{19,3},{4,20},{20... | collective-permute-start | bytes 1081352 | tf_op jit(solution)/shard_map/ppermute | solution.py:458
  29.0 1.8 %collective-permute-start.4 = (bf16[128,1408]{1,0:T(8,128)(2,1)S(1)}, bf16[128,1408]{1,0:T(8,128)(2,1)S(1)}, u32[]{:S(2)}, u32[]{:S(2)}) collective-permute-start(bf16[128,1408]{1,0:T(8,128)(2,1)S(1)} %collective-permute-done.1.refs_1_), channel_id=1, source_target_pairs={{0,16},{16,0},{1,17},{17,1},{2,18},{18,2},{3,19},{19,3},{4,20},{20... | collective-permute-start | bytes 1081352 | tf_op jit(solution)/shard_map/ppermute | solution.py:458
  29.1 2.2 %collective-permute-start.5 = (bf16[128,1408]{1,0:T(8,128)(2,1)S(1)}, bf16[128,1408]{1,0:T(8,128)(2,1)S(1)}, u32[]{:S(2)}, u32[]{:S(2)}) collective-permute-start(bf16[128,1408]{1,0:T(8,128)(2,1)S(1)} %collective-permute-done.2.refs_2_), channel_id=1, source_target_pairs={{0,16},{16,0},{1,17},{17,1},{2,18},{18,2},{3,19},{19,3},{4,20},{20... | collective-permute-start | bytes 1081352 | tf_op jit(solution)/shard_map/ppermute | solution.py:458
  33.4 10.7 %collective-permute-start.7 = (bf16[256,256]{1,0:T(8,128)(2,1)S(1)}, bf16[256,256]{1,0:T(8,128)(2,1)S(1)}, u32[]{:S(2)}, u32[]{:S(2)}) collective-permute-start(bf16[256,256]{1,0:T(8,128)(2,1)S(1)} %get-tuple-element.68.refs_0_), channel_id=1, source_target_pairs={{0,1},{1,2},{2,3},{3,0},{4,5},{5,6},{6,7},{7,4},{8,9},{9,10},{10,1... | collective-permute-start | bytes 393224 | tf_op jit(solution)/shard_map/ppermute | solution.py:436
  34.5 11.5 %collective-permute-start.8 = (bf16[256,256]{1,0:T(8,128)(2,1)S(1)}, bf16[256,256]{1,0:T(8,128)(2,1)S(1)}, u32[]{:S(2)}, u32[]{:S(2)}) collective-permute-start(bf16[256,256]{1,0:T(8,128)(2,1)S(1)} %get-tuple-element.68.refs_0_), channel_id=1, source_target_pairs={{0,3},{1,0},{2,1},{3,2},{4,7},{5,4},{6,5},{7,6},{8,11},{9,8},{10,9... | collective-permute-start | bytes 393224 | tf_op jit(solution)/shard_map/ppermute | solution.py:436
  36.7 9.3 %collective-permute-start.9 = (bf16[256,256]{1,0:T(8,128)(2,1)S(1)}, bf16[256,256]{1,0:T(8,128)(2,1)S(1)}, u32[]{:S(2)}, u32[]{:S(2)}) collective-permute-start(bf16[256,256]{1,0:T(8,128)(2,1)S(1)} %get-tuple-element.68.refs_0_), channel_id=1, source_target_pairs={{0,2},{1,3},{2,0},{3,1},{4,6},{5,7},{6,4},{7,5},{8,10},{9,11},{10,... | collective-permute-start | bytes 393224 | tf_op jit(solution)/shard_map/ppermute | solution.py:436
  40.1 12.0 %collective-permute-start.15 = (bf16[512,256]{1,0:T(8,128)(2,1)S(1)}, bf16[512,256]{1,0:T(8,128)(2,1)S(1)}, u32[]{:S(2)}, u32[]{:S(2)}) collective-permute-start(bf16[512,256]{1,0:T(8,128)(2,1)S(1)} %attend.4.refs_0_), channel_id=1, source_target_pairs={{0,1},{1,2},{2,3},{3,0},{4,5},{5,6},{6,7},{7,4},{8,9},{9,10},{10,1... | collective-permute-start | bytes 786440 | tf_op jit(solution)/shard_map/ppermute | solution.py:436
  40.5 13.6 %collective-permute-start.16 = (bf16[512,256]{1,0:T(8,128)(2,1)S(1)}, bf16[512,256]{1,0:T(8,128)(2,1)S(1)}, u32[]{:S(2)}, u32[]{:S(2)}) collective-permute-start(bf16[512,256]{1,0:T(8,128)(2,1)S(1)} %attend.4.refs_0_), channel_id=1, source_target_pairs={{0,3},{1,0},{2,1},{3,2},{4,7},{5,4},{6,5},{7,6},{8,11},{9,8},{10,9... | collective-permute-start | bytes 786440 | tf_op jit(solution)/shard_map/ppermute | solution.py:436
  44.1 10.8 %collective-permute-start.17 = (bf16[512,256]{1,0:T(8,128)(2,1)S(1)}, bf16[512,256]{1,0:T(8,128)(2,1)S(1)}, u32[]{:S(2)}, u32[]{:S(2)}) collective-permute-start(bf16[512,256]{1,0:T(8,128)(2,1)S(1)} %attend.4.refs_0_), channel_id=1, source_target_pairs={{0,2},{1,3},{2,0},{3,1},{4,6},{5,7},{6,4},{7,5},{8,10},{9,11},{10,... | collective-permute-start | bytes 786440 | tf_op jit(solution)/shard_map/ppermute | solution.py:436
  47.0 10.3 %collective-permute-start.13 = (bf16[128,1408]{1,0:T(8,128)(2,1)S(1)}, bf16[128,1408]{1,0:T(8,128)(2,1)S(1)}, u32[]{:S(2)}, u32[]{:S(2)}) collective-permute-start(bf16[128,1408]{1,0:T(8,128)(2,1)S(1)} %get-tuple-element.77), channel_id=1, source_target_pairs={{0,4},{4,8},{8,12},{12,0},{1,5},{5,9},{9,13},{13,1},{2,6},{6,10},{... | collective-permute-start | bytes 1081352 | tf_op jit(solution)/shard_map/ppermute | solution.py:436
  48.6 8.8 %collective-permute-start.14 = (bf16[128,1408]{1,0:T(8,128)(2,1)S(1)}, bf16[128,1408]{1,0:T(8,128)(2,1)S(1)}, u32[]{:S(2)}, u32[]{:S(2)}) collective-permute-start(bf16[128,1408]{1,0:T(8,128)(2,1)S(1)} %get-tuple-element.79), channel_id=1, source_target_pairs={{0,12},{4,0},{8,4},{12,8},{1,13},{5,1},{9,5},{13,9},{2,14},{6,2},{... | collective-permute-start | bytes 1081352 | tf_op jit(solution)/shard_map/ppermute | solution.py:436
  57.8 17.5 %collective-permute-start.18 = (bf16[256,1408]{1,0:T(8,128)(2,1)S(1)}, bf16[256,1408]{1,0:T(8,128)(2,1)S(1)}, u32[]{:S(2)}, u32[]{:S(2)}) collective-permute-start(bf16[256,1408]{1,0:T(8,128)(2,1)S(1)} %get-tuple-element.86), channel_id=1, source_target_pairs={{0,4},{4,8},{8,12},{12,0},{1,5},{5,9},{9,13},{13,1},{2,6},{6,10},{... | collective-permute-start | bytes 2162696 | tf_op jit(solution)/shard_map/ppermute | solution.py:436
  59.4 20.7 %copy-start.6 = (f32[5376]{0:T(1024)S(1)}, f32[5376]{0:T(1024)}, u32[]{:S(2)}) copy-start(f32[5376]{0:T(1024)} %param.23) | copy-start | bytes 64516
  59.4 15.9 %collective-permute-start.19 = (bf16[256,1408]{1,0:T(8,128)(2,1)S(1)}, bf16[256,1408]{1,0:T(8,128)(2,1)S(1)}, u32[]{:S(2)}, u32[]{:S(2)}) collective-permute-start(bf16[256,1408]{1,0:T(8,128)(2,1)S(1)} %get-tuple-element.87), channel_id=1, source_target_pairs={{0,12},{4,0},{8,4},{12,8},{1,13},{5,1},{9,5},{13,9},{2,14},{6,2},{... | collective-permute-start | bytes 2162696 | tf_op jit(solution)/shard_map/ppermute | solution.py:436
  61.1 7.2 %collective-permute-start.10 = (bf16[256,256]{1,0:T(8,128)(2,1)S(1)}, bf16[256,256]{1,0:T(8,128)(2,1)S(1)}, u32[]{:S(2)}, u32[]{:S(2)}) collective-permute-start(bf16[256,256]{1,0:T(8,128)(2,1)S(1)} %attend.5.refs_0_), channel_id=1, source_target_pairs={{0,1},{1,2},{2,3},{3,0},{4,5},{5,6},{6,7},{7,4},{8,9},{9,10},{10,1... | collective-permute-start | bytes 393224 | tf_op jit(solution)/shard_map/ppermute | solution.py:436
  61.9 6.4 %collective-permute-start.11 = (bf16[256,256]{1,0:T(8,128)(2,1)S(1)}, bf16[256,256]{1,0:T(8,128)(2,1)S(1)}, u32[]{:S(2)}, u32[]{:S(2)}) collective-permute-start(bf16[256,256]{1,0:T(8,128)(2,1)S(1)} %attend.5.refs_0_), channel_id=1, source_target_pairs={{0,3},{1,0},{2,1},{3,2},{4,7},{5,4},{6,5},{7,6},{8,11},{9,8},{10,9... | collective-permute-start | bytes 393224 | tf_op jit(solution)/shard_map/ppermute | solution.py:436
  64.4 6.5 %collective-permute-start.12 = (bf16[256,256]{1,0:T(8,128)(2,1)S(1)}, bf16[256,256]{1,0:T(8,128)(2,1)S(1)}, u32[]{:S(2)}, u32[]{:S(2)}) collective-permute-start(bf16[256,256]{1,0:T(8,128)(2,1)S(1)} %attend.5.refs_0_), channel_id=1, source_target_pairs={{0,2},{1,3},{2,0},{3,1},{4,6},{5,7},{6,4},{7,5},{8,10},{9,11},{10,... | collective-permute-start | bytes 393224 | tf_op jit(solution)/shard_map/ppermute | solution.py:436
  76.3 7.9 %collective-permute-start.20 = (bf16[64,1408]{1,0:T(8,128)(2,1)S(1)}, bf16[64,1408]{1,0:T(8,128)(2,1)S(1)}, u32[]{:S(2)}, u32[]{:S(2)}) collective-permute-start(bf16[64,1408]{1,0:T(8,128)(2,1)S(1)} %get-tuple-element.89), channel_id=1, source_target_pairs={{0,1},{1,2},{2,3},{3,0},{4,5},{5,6},{6,7},{7,4},{8,9},{9,10},{10,1... | collective-permute-start | bytes 540680 | tf_op jit(solution)/shard_map/ppermute | solution.py:436
  77.3 7.3 %collective-permute-start.21 = (bf16[64,1408]{1,0:T(8,128)(2,1)S(1)}, bf16[64,1408]{1,0:T(8,128)(2,1)S(1)}, u32[]{:S(2)}, u32[]{:S(2)}) collective-permute-start(bf16[64,1408]{1,0:T(8,128)(2,1)S(1)} %get-tuple-element.90), channel_id=1, source_target_pairs={{0,3},{1,0},{2,1},{3,2},{4,7},{5,4},{6,5},{7,6},{8,11},{9,8},{10,9... | collective-permute-start | bytes 540680 | tf_op jit(solution)/shard_map/ppermute | solution.py:436
  79.6 7.0 %collective-permute-start.22 = (bf16[64,1408]{1,0:T(8,128)(2,1)S(1)}, bf16[64,1408]{1,0:T(8,128)(2,1)S(1)}, u32[]{:S(2)}, u32[]{:S(2)}) collective-permute-start(bf16[64,1408]{1,0:T(8,128)(2,1)S(1)} %get-tuple-element.91), channel_id=1, source_target_pairs={{0,2},{1,3},{2,0},{3,1},{4,6},{5,7},{6,4},{7,5},{8,10},{9,11},{10,... | collective-permute-start | bytes 540680 | tf_op jit(solution)/shard_map/ppermute | solution.py:436

commit v12 on v10

--- a/solution.py
+++ b/solution.py
@@ -375,12 +375,12 @@
     )(*pieces, *weights)
 
 
-def total_kernel(pos_ref, kept_ref, up_ref, down_ref, own_ref, next_ref, last_ref, far_ref, total):
+def total_kernel(pos_ref, kept_ref, up_ref, down_ref, own_ref, next_ref, last_ref, far_ref):
     z = pos_ref[1]
-    total[...] = kept_ref[...] + up_ref[...].astype(F32) + down_ref[...].astype(F32)
 
     def rows(shift):
-        return total[pl.ds(pl.multiple_of(((z + shift) % 4) * 64, 64), 64), :]
+        at = pl.ds(pl.multiple_of(((z + shift) % 4) * 64, 64), 64)
+        return kept_ref[at, :] + up_ref[at, :].astype(F32) + down_ref[at, :].astype(F32)
 
     next_ref[...] = rows(1).astype(BF16)
     last_ref[...] = rows(3).astype(BF16)
@@ -395,7 +395,6 @@
         in_specs=[SMEM] + [VMEM] * 3,
         out_specs=[VMEM] * 4,
         out_shape=[jax.ShapeDtypeStruct((64, QUARTER), F32), part, part, part],
-        scratch_shapes=[pltpu.VMEM((256, QUARTER), F32)],
         compiler_params=pltpu.CompilerParams(vmem_limit_bytes=32 << 20),
         cost_estimate=SMALL,
         name="total_step",

time: 88.6 us -> 88.4 us (level)
  no operation moved by 1% of the time
where the time goes in v12:
time: 88.4 us; the launch traced here: 88.1 us
  starting transfers between devices  33.6 us (38%)
  Pallas kernels  32.3 us (37%)
  waiting for transfers between devices  21.1 us (24%)
    ppermute x19, starting transfers between devices, shift_by(): return lax.ppermute(array, axis, [(i, (i + steps) % 4) for i in range(4)])  29.4 us
    ppermute x19, waiting for transfers between devices, shift_by(): return lax.ppermute(array, axis, [(i, (i + steps) % 4) for i in range(4)])  19.3 us
    pallas_call x1, Pallas kernels, key_value(): pl.pallas_call(key_value_kernel, grid_spec=pltpu.PrefetchScalarGridSpec(n...  11.3 us
    pallas_call x3, Pallas kernels, attend(): pl.pallas_call(functools.partial(kernel, first_part), in_specs=[SMEM] + [...  6.68 us
    pallas_call x1, Pallas kernels, query(): pl.pallas_call(query_kernel, in_specs=[SMEM, VMEM, VMEM, VMEM, ANY, ANY],...  4.94 us
    pallas_call x3, Pallas kernels, multiply(): pl.pallas_call(kernel, in_specs=[VMEM] * 6, out_specs=jax.tree.map(lambda...  3.77 us
    ppermute x3, starting transfers between devices, per_device(): swapped = [lax.ppermute(part, 'c', [(0, 1), (1, 0)]) for part in lines]  2.87 us
    pallas_call x1, Pallas kernels, finish(): pl.pallas_call(finish_kernel, in_specs=[SMEM] + [VMEM] * 6, out_specs=VME...  1.89 us
  transfers between devices with their start and end apart: 23, of which 12 were waited for; matrix products, arithmetic and copies ran while one was open for 0% of the time, Pallas kernels for 29%

profile of v12, /device:TPU:0, one launch (start us, length us, event | category | flops | bytes accessed | tf_op | source)
XLA Modules:
  0.0 88.1 jit_solution(9256417534476695363)
XLA Ops:
  0.7 1.8 %pick.1 = (bf16[128,1408]{1,0:T(8,128)(2,1)S(1)}, bf16[128,1408]{1,0:T(8,128)(2,1)S(1)}, bf16[128,1408]{1,0:T(8,128)(2,1)S(1)}) custom-call(s32[12]{0:T(128)S(1)} %dynamic-slice_bitcast_fusion.pos_ref, bf16[256,5376]{1,0:T(8,128)(2,1)} %w_out_ref.1), custom_call_target="tpu_custom_call" | custom-call | tf_op jit(solution)/shard_map/pick/pallas_call | solution.py:293
  2.5 2.1 %collective-permute-start = (bf16[128,1408]{1,0:T(8,128)(2,1)S(1)}, bf16[128,1408]{1,0:T(8,128)(2,1)S(1)}, u32[]{:S(2)}, u32[]{:S(2)}) collective-permute-start(bf16[128,1408]{1,0:T(8,128)(2,1)S(1)} %get-tuple-element.55), channel_id=1, source_target_pairs={{0,1},{1,2},{2,3},{3,0},{4,5},{5,6},{6,7},{7,4},{8,9},{9,10},{10,1... | collective-permute-start | bytes 1081352 | tf_op jit(solution)/shard_map/ppermute | solution.py:436
  4.6 2.2 %collective-permute-start.1 = (bf16[128,1408]{1,0:T(8,128)(2,1)S(1)}, bf16[128,1408]{1,0:T(8,128)(2,1)S(1)}, u32[]{:S(2)}, u32[]{:S(2)}) collective-permute-start(bf16[128,1408]{1,0:T(8,128)(2,1)S(1)} %get-tuple-element.56), channel_id=1, source_target_pairs={{0,3},{1,0},{2,1},{3,2},{4,7},{5,4},{6,5},{7,6},{8,11},{9,8},{10,9... | collective-permute-start | bytes 1081352 | tf_op jit(solution)/shard_map/ppermute | solution.py:436
  6.8 1.8 %collective-permute-start.2 = (bf16[128,1408]{1,0:T(8,128)(2,1)S(1)}, bf16[128,1408]{1,0:T(8,128)(2,1)S(1)}, u32[]{:S(2)}, u32[]{:S(2)}) collective-permute-start(bf16[128,1408]{1,0:T(8,128)(2,1)S(1)} %get-tuple-element.57), channel_id=1, source_target_pairs={{0,2},{1,3},{2,0},{3,1},{4,6},{5,7},{6,4},{7,5},{8,10},{9,11},{10,... | collective-permute-start | bytes 1081352 | tf_op jit(solution)/shard_map/ppermute | solution.py:436
  8.6 11.3 %key_value.1 = (bf16[1024,5376]{1,0:T(8,128)(2,1)S(1)}, bf16[1024,256]{1,0:T(8,128)(2,1)S(1)}, bf16[64,5376]{1,0:T(8,128)(2,1)S(1)}) custom-call(s32[12]{0:T(128)S(1)} %dynamic-slice_bitcast_fusion.pos_ref, bf16[1024,5376]{1,0:T(8,128)(2,1)} %tok_ref.1, f32[1,5376]{1,0:T(1,128)S(1)} %reshape.16.g_ref, bf16[5376,128]{1,0:T(8,128)(2,1)} %wk_ref.1, ...), custom_call_target="tpu_custom_call" | custom-call | flops 11274289152 | bytes 27262976 | tf_op jit(solution)/shard_map/key_value/pallas_call | solution.py:140
  19.9 1.3 %collective-permute-start.6 = (bf16[1024,256]{1,0:T(8,128)(2,1)S(1)}, bf16[1024,256]{1,0:T(8,128)(2,1)S(1)}, u32[]{:S(2)}, u32[]{:S(2)}) collective-permute-start(bf16[1024,256]{1,0:T(8,128)(2,1)S(1)} %get-tuple-element.63.kv_ref), channel_id=1, source_target_pairs={{0,16},{16,32},{32,48},{48,64},{64,80},{80,96},{96,112},{1,17},{17... | collective-permute-start | bytes 1572872 | tf_op jit(solution)/shard_map/ppermute | solution.py:455
  21.3 4.9 %query.1 = (bf16[1024,256]{1,0:T(8,128)(2,1)S(1)}, bf16[256,1408]{1,0:T(8,128)(2,1)S(1)}) custom-call(s32[12]{0:T(128)S(1)} %dynamic-slice_bitcast_fusion.pos_ref, bf16[1024,5376]{1,0:T(8,128)(2,1)S(1)} %get-tuple-element.53.normed_ref, bf16[5376,256]{1,0:T(8,128)(2,1)S(1)} %copy-done, f32[1,128]{1,0:T(1,128)S(1)} %bitcast.4, ...), custom_call_target="tpu_custom_call" | custom-call | tf_op jit(solution)/shard_map/query/pallas_call | solution.py:193
  26.3 2.4 %collective-permute-start.3 = (bf16[128,1408]{1,0:T(8,128)(2,1)S(1)}, bf16[128,1408]{1,0:T(8,128)(2,1)S(1)}, u32[]{:S(2)}, u32[]{:S(2)}) collective-permute-start(bf16[128,1408]{1,0:T(8,128)(2,1)S(1)} %collective-permute-done.refs_0_), channel_id=1, source_target_pairs={{0,16},{16,0},{1,17},{17,1},{2,18},{18,2},{3,19},{19,3},{4,20},{20... | collective-permute-start | bytes 1081352 | tf_op jit(solution)/shard_map/ppermute | solution.py:458
  31.0 2.0 %attend.3 = (bf16[256,256]{1,0:T(8,128)(2,1)S(1)}, bf16[2048,128]{1,0:T(8,128)(2,1)S(1)}, bf16[2048,256]{1,0:T(8,128)(2,1)S(1)}) custom-call(s32[12]{0:T(128)S(1)} %dynamic-slice_bitcast_fusion.pos_ref, bf16[1024,256]{1,0:T(8,128)(2,1)S(1)} %get-tuple-element.62.q_ref, bf16[1024,256]{1,0:T(8,128)(2,1)S(1)} %get-tuple-element.63.kv_ref, ...), custom_call_target="tpu_custom_call" | custom-call | tf_op jit(solution)/shard_map/attend/pallas_call | solution.py:263
  33.0 1.1 %collective-permute-start.7 = (bf16[256,256]{1,0:T(8,128)(2,1)S(1)}, bf16[256,256]{1,0:T(8,128)(2,1)S(1)}, u32[]{:S(2)}, u32[]{:S(2)}) collective-permute-start(bf16[256,256]{1,0:T(8,128)(2,1)S(1)} %get-tuple-element.68.refs_0_), channel_id=1, source_target_pairs={{0,1},{1,2},{2,3},{3,0},{4,5},{5,6},{6,7},{7,4},{8,9},{9,10},{10,1... | collective-permute-start | bytes 393224 | tf_op jit(solution)/shard_map/ppermute | solution.py:436
  34.1 2.2 %collective-permute-start.8 = (bf16[256,256]{1,0:T(8,128)(2,1)S(1)}, bf16[256,256]{1,0:T(8,128)(2,1)S(1)}, u32[]{:S(2)}, u32[]{:S(2)}) collective-permute-start(bf16[256,256]{1,0:T(8,128)(2,1)S(1)} %get-tuple-element.68.refs_0_), channel_id=1, source_target_pairs={{0,3},{1,0},{2,1},{3,2},{4,7},{5,4},{6,5},{7,6},{8,11},{9,8},{10,9... | collective-permute-start | bytes 393224 | tf_op jit(solution)/shard_map/ppermute | solution.py:436
  36.8 2.9 %attend.4.refs_0_ = bf16[512,256]{1,0:T(8,128)(2,1)S(1)} custom-call(s32[12]{0:T(128)S(1)} %dynamic-slice_bitcast_fusion.pos_ref, bf16[1024,256]{1,0:T(8,128)(2,1)S(1)} %get-tuple-element.62.q_ref, bf16[2048,128]{1,0:T(8,128)(2,1)S(1)} %get-tuple-element.66.keys, bf16[2048,256]{1,0:T(8,128)(2,1)S(1)} %get-tuple-element.67.values), custom_call_target="tpu_custom_call" | custom-call | tf_op jit(solution)/shard_map/attend/pallas_call | solution.py:263
  40.3 2.9 %collective-permute-start.16 = (bf16[512,256]{1,0:T(8,128)(2,1)S(1)}, bf16[512,256]{1,0:T(8,128)(2,1)S(1)}, u32[]{:S(2)}, u32[]{:S(2)}) collective-permute-start(bf16[512,256]{1,0:T(8,128)(2,1)S(1)} %attend.4.refs_0_), channel_id=1, source_target_pairs={{0,3},{1,0},{2,1},{3,2},{4,7},{5,4},{6,5},{7,6},{8,11},{9,8},{10,9... | collective-permute-start | bytes 786440 | tf_op jit(solution)/shard_map/ppermute | solution.py:436
  43.9 1.9 %collective-permute-start.17 = (bf16[512,256]{1,0:T(8,128)(2,1)S(1)}, bf16[512,256]{1,0:T(8,128)(2,1)S(1)}, u32[]{:S(2)}, u32[]{:S(2)}) collective-permute-start(bf16[512,256]{1,0:T(8,128)(2,1)S(1)} %attend.4.refs_0_), channel_id=1, source_target_pairs={{0,2},{1,3},{2,0},{3,1},{4,6},{5,7},{6,4},{7,5},{8,10},{9,11},{10,... | collective-permute-start | bytes 786440 | tf_op jit(solution)/shard_map/ppermute | solution.py:436
  45.8 1.0 %far.1 = (bf16[128,1408]{1,0:T(8,128)(2,1)S(1)}, bf16[128,1408]{1,0:T(8,128)(2,1)S(1)}) custom-call(bf16[256,256]{1,0:T(8,128)(2,1)S(1)} %get-tuple-element.68.refs_0_, bf16[256,256]{1,0:T(8,128)(2,1)S(1)} %collective-permute-done.7.refs_1_, bf16[256,256]{1,0:T(8,128)(2,1)S(1)} %collective-permute-done.8.refs_2_, ...), custom_call_target="tpu_custom_call" | custom-call | tf_op jit(solution)/shard_map/far/pallas_call | solution.py:367
  46.8 1.6 %collective-permute-start.13 = (bf16[128,1408]{1,0:T(8,128)(2,1)S(1)}, bf16[128,1408]{1,0:T(8,128)(2,1)S(1)}, u32[]{:S(2)}, u32[]{:S(2)}) collective-permute-start(bf16[128,1408]{1,0:T(8,128)(2,1)S(1)} %get-tuple-element.77), channel_id=1, source_target_pairs={{0,4},{4,8},{8,12},{12,0},{1,5},{5,9},{9,13},{13,1},{2,6},{6,10},{... | collective-permute-start | bytes 1081352 | tf_op jit(solution)/shard_map/ppermute | solution.py:436
  48.3 1.7 %collective-permute-start.14 = (bf16[128,1408]{1,0:T(8,128)(2,1)S(1)}, bf16[128,1408]{1,0:T(8,128)(2,1)S(1)}, u32[]{:S(2)}, u32[]{:S(2)}) collective-permute-start(bf16[128,1408]{1,0:T(8,128)(2,1)S(1)} %get-tuple-element.79), channel_id=1, source_target_pairs={{0,12},{4,0},{8,4},{12,8},{1,13},{5,1},{9,5},{13,9},{2,14},{6,2},{... | collective-permute-start | bytes 1081352 | tf_op jit(solution)/shard_map/ppermute | solution.py:436
  50.1 1.8 %attend.5.refs_0_ = bf16[256,256]{1,0:T(8,128)(2,1)S(1)} custom-call(s32[12]{0:T(128)S(1)} %dynamic-slice_bitcast_fusion.pos_ref, bf16[1024,256]{1,0:T(8,128)(2,1)S(1)} %get-tuple-element.62.q_ref, bf16[2048,128]{1,0:T(8,128)(2,1)S(1)} %get-tuple-element.66.keys, bf16[2048,256]{1,0:T(8,128)(2,1)S(1)} %get-tuple-element.67.values), custom_call_target="tpu_custom_call" | custom-call | flops 4000000000 | tf_op jit(solution)/shard_map/attend/pallas_call | solution.py:263
  51.9 2.0 %collective-permute-done.16.refs_2_ = bf16[512,256]{1,0:T(8,128)(2,1)S(1)} collective-permute-done((bf16[512,256]{1,0:T(8,128)(2,1)S(1)}, bf16[512,256]{1,0:T(8,128)(2,1)S(1)}, u32[]{:S(2)}, u32[]{:S(2)}) %collective-permute-start.16) | collective-permute-done | bytes 262176 | tf_op jit(solution)/shard_map/ppermute | solution.py:436
  54.8 1.8 %near.1 = (bf16[256,1408]{1,0:T(8,128)(2,1)S(1)}, bf16[256,1408]{1,0:T(8,128)(2,1)S(1)}) custom-call(bf16[512,256]{1,0:T(8,128)(2,1)S(1)} %attend.4.refs_0_, bf16[512,256]{1,0:T(8,128)(2,1)S(1)} %collective-permute-done.15.refs_1_, bf16[512,256]{1,0:T(8,128)(2,1)S(1)} %collective-permute-done.16.refs_2_, ...), custom_call_target="tpu_custom_call" | custom-call | flops 30000001024 | tf_op jit(solution)/shard_map/near/pallas_call | solution.py:367
  57.6 1.6 %collective-permute-start.18 = (bf16[256,1408]{1,0:T(8,128)(2,1)S(1)}, bf16[256,1408]{1,0:T(8,128)(2,1)S(1)}, u32[]{:S(2)}, u32[]{:S(2)}) collective-permute-start(bf16[256,1408]{1,0:T(8,128)(2,1)S(1)} %get-tuple-element.86), channel_id=1, source_target_pairs={{0,4},{4,8},{8,12},{12,0},{1,5},{5,9},{9,13},{13,1},{2,6},{6,10},{... | collective-permute-start | bytes 2162696 | tf_op jit(solution)/shard_map/ppermute | solution.py:436
  59.2 1.7 %collective-permute-start.19 = (bf16[256,1408]{1,0:T(8,128)(2,1)S(1)}, bf16[256,1408]{1,0:T(8,128)(2,1)S(1)}, u32[]{:S(2)}, u32[]{:S(2)}) collective-permute-start(bf16[256,1408]{1,0:T(8,128)(2,1)S(1)} %get-tuple-element.87), channel_id=1, source_target_pairs={{0,12},{4,0},{8,4},{12,8},{1,13},{5,1},{9,5},{13,9},{2,14},{6,2},{... | collective-permute-start | bytes 2162696 | tf_op jit(solution)/shard_map/ppermute | solution.py:436
  61.7 2.5 %collective-permute-start.11 = (bf16[256,256]{1,0:T(8,128)(2,1)S(1)}, bf16[256,256]{1,0:T(8,128)(2,1)S(1)}, u32[]{:S(2)}, u32[]{:S(2)}) collective-permute-start(bf16[256,256]{1,0:T(8,128)(2,1)S(1)} %attend.5.refs_0_), channel_id=1, source_target_pairs={{0,3},{1,0},{2,1},{3,2},{4,7},{5,4},{6,5},{7,6},{8,11},{9,8},{10,9... | collective-permute-start | bytes 393224 | tf_op jit(solution)/shard_map/ppermute | solution.py:436
  64.7 3.4 %collective-permute-done.10.refs_1_ = bf16[256,256]{1,0:T(8,128)(2,1)S(1)} collective-permute-done((bf16[256,256]{1,0:T(8,128)(2,1)S(1)}, bf16[256,256]{1,0:T(8,128)(2,1)S(1)}, u32[]{:S(2)}, u32[]{:S(2)}) %collective-permute-start.10) | collective-permute-done | bytes 131104 | tf_op jit(solution)/shard_map/ppermute | solution.py:436
  68.1 2.5 %collective-permute-done.12.refs_3_ = bf16[256,256]{1,0:T(8,128)(2,1)S(1)} collective-permute-done((bf16[256,256]{1,0:T(8,128)(2,1)S(1)}, bf16[256,256]{1,0:T(8,128)(2,1)S(1)}, u32[]{:S(2)}, u32[]{:S(2)}) %collective-permute-start.12) | collective-permute-done | bytes 131104 | tf_op jit(solution)/shard_map/ppermute | solution.py:436
  70.6 1.0 %keep.1.kept_ref = f32[256,1408]{1,0:T(8,128)S(1)} custom-call(bf16[256,256]{1,0:T(8,128)(2,1)S(1)} %attend.5.refs_0_, bf16[256,256]{1,0:T(8,128)(2,1)S(1)} %collective-permute-done.10.refs_1_, bf16[256,256]{1,0:T(8,128)(2,1)S(1)} %collective-permute-done.11.refs_2_, bf16[256,256]{1,0:T(8,128)(2,1)S(1)} %collective-permute-done.12.refs_3_, ...), custom_call_target="tpu_custom_call" | custom-call | tf_op jit(solution)/shard_map/keep/pallas_call | solution.py:367
  71.6 3.5 %collective-permute-done.18.up_ref = bf16[256,1408]{1,0:T(8,128)(2,1)S(1)} collective-permute-done((bf16[256,1408]{1,0:T(8,128)(2,1)S(1)}, bf16[256,1408]{1,0:T(8,128)(2,1)S(1)}, u32[]{:S(2)}, u32[]{:S(2)}) %collective-permute-start.18) | collective-permute-done | bytes 720928 | tf_op jit(solution)/shard_map/ppermute | solution.py:436
  75.9 1.0 %collective-permute-start.20 = (bf16[64,1408]{1,0:T(8,128)(2,1)S(1)}, bf16[64,1408]{1,0:T(8,128)(2,1)S(1)}, u32[]{:S(2)}, u32[]{:S(2)}) collective-permute-start(bf16[64,1408]{1,0:T(8,128)(2,1)S(1)} %get-tuple-element.89), channel_id=1, source_target_pairs={{0,1},{1,2},{2,3},{3,0},{4,5},{5,6},{6,7},{7,4},{8,9},{9,10},{10,1... | collective-permute-start | bytes 540680 | tf_op jit(solution)/shard_map/ppermute | solution.py:436
  76.8 2.3 %collective-permute-start.21 = (bf16[64,1408]{1,0:T(8,128)(2,1)S(1)}, bf16[64,1408]{1,0:T(8,128)(2,1)S(1)}, u32[]{:S(2)}, u32[]{:S(2)}) collective-permute-start(bf16[64,1408]{1,0:T(8,128)(2,1)S(1)} %get-tuple-element.90), channel_id=1, source_target_pairs={{0,3},{1,0},{2,1},{3,2},{4,7},{5,4},{6,5},{7,6},{8,11},{9,8},{10,9... | collective-permute-start | bytes 540680 | tf_op jit(solution)/shard_map/ppermute | solution.py:436
  79.7 4.1 %collective-permute-done.20.next_ref = bf16[64,1408]{1,0:T(8,128)(2,1)S(1)} collective-permute-done((bf16[64,1408]{1,0:T(8,128)(2,1)S(1)}, bf16[64,1408]{1,0:T(8,128)(2,1)S(1)}, u32[]{:S(2)}, u32[]{:S(2)}) %collective-permute-start.20) | collective-permute-done | bytes 180256 | tf_op jit(solution)/shard_map/ppermute | solution.py:436
  84.1 2.0 %collective-permute-done.22.far_ref = bf16[64,1408]{1,0:T(8,128)(2,1)S(1)} collective-permute-done((bf16[64,1408]{1,0:T(8,128)(2,1)S(1)}, bf16[64,1408]{1,0:T(8,128)(2,1)S(1)}, u32[]{:S(2)}, u32[]{:S(2)}) %collective-permute-start.22) | collective-permute-done | bytes 180256 | tf_op jit(solution)/shard_map/ppermute | solution.py:436
  86.2 1.9 %finish.1 = bf16[64,5376]{1,0:T(8,128)(2,1)} custom-call(s32[12]{0:T(128)S(1)} %dynamic-slice_bitcast_fusion.pos_ref, f32[64,1408]{1,0:T(8,128)S(1)} %get-tuple-element.88.own_ref, bf16[64,1408]{1,0:T(8,128)(2,1)S(1)} %collective-permute-done.20.next_ref, bf16[64,1408]{1,0:T(8,128)(2,1)S(1)} %collective-permute-done.21.last_ref, ...), custom_call_target="tpu_custom_call" | custom-call | tf_op jit(solution)/shard_map/finish/pallas_call | solution.py:423
  (44 shorter events, 9.8 us)
Async XLA Ops:
  0.0 8.6 %copy-start.5 = (f32[5376]{0:T(1024)S(1)}, f32[5376]{0:T(1024)}, u32[]{:S(2)}) copy-start(f32[5376]{0:T(1024)} %param.14) | copy-start | bytes 64516
  0.0 8.6 %copy-start.4 = (f32[128]{0:T(128)S(1)}, f32[128]{0:T(128)}, u32[]{:S(2)}) copy-start(f32[128]{0:T(128)} %param.19) | copy-start | bytes 1540
  2.5 23.7 %collective-permute-start = (bf16[128,1408]{1,0:T(8,128)(2,1)S(1)}, bf16[128,1408]{1,0:T(8,128)(2,1)S(1)}, u32[]{:S(2)}, u32[]{:S(2)}) collective-permute-start(bf16[128,1408]{1,0:T(8,128)(2,1)S(1)} %get-tuple-element.55), channel_id=1, source_target_pairs={{0,1},{1,2},{2,3},{3,0},{4,5},{5,6},{6,7},{7,4},{8,9},{9,10},{10,1... | collective-permute-start | bytes 1081352 | tf_op jit(solution)/shard_map/ppermute | solution.py:436
  4.6 21.7 %collective-permute-start.1 = (bf16[128,1408]{1,0:T(8,128)(2,1)S(1)}, bf16[128,1408]{1,0:T(8,128)(2,1)S(1)}, u32[]{:S(2)}, u32[]{:S(2)}) collective-permute-start(bf16[128,1408]{1,0:T(8,128)(2,1)S(1)} %get-tuple-element.56), channel_id=1, source_target_pairs={{0,3},{1,0},{2,1},{3,2},{4,7},{5,4},{6,5},{7,6},{8,11},{9,8},{10,9... | collective-permute-start | bytes 1081352 | tf_op jit(solution)/shard_map/ppermute | solution.py:436
  6.8 19.5 %collective-permute-start.2 = (bf16[128,1408]{1,0:T(8,128)(2,1)S(1)}, bf16[128,1408]{1,0:T(8,128)(2,1)S(1)}, u32[]{:S(2)}, u32[]{:S(2)}) collective-permute-start(bf16[128,1408]{1,0:T(8,128)(2,1)S(1)} %get-tuple-element.57), channel_id=1, source_target_pairs={{0,2},{1,3},{2,0},{3,1},{4,6},{5,7},{6,4},{7,5},{8,10},{9,11},{10,... | collective-permute-start | bytes 1081352 | tf_op jit(solution)/shard_map/ppermute | solution.py:436
  8.6 12.7 %copy-start = (bf16[5376,256]{1,0:T(8,128)(2,1)S(1)}, bf16[5376,256]{1,0:T(8,128)(2,1)}, u32[]{:S(2)}) copy-start(bf16[5376,256]{1,0:T(8,128)(2,1)} %w_ref.3) | copy-start | bytes 8257540
  8.6 12.7 %copy-start.3 = (f32[128]{0:T(128)S(1)}, f32[128]{0:T(128)}, u32[]{:S(2)}) copy-start(f32[128]{0:T(128)} %param.18) | copy-start | bytes 1540
  19.9 11.1 %collective-permute-start.6 = (bf16[1024,256]{1,0:T(8,128)(2,1)S(1)}, bf16[1024,256]{1,0:T(8,128)(2,1)S(1)}, u32[]{:S(2)}, u32[]{:S(2)}) collective-permute-start(bf16[1024,256]{1,0:T(8,128)(2,1)S(1)} %get-tuple-element.63.kv_ref), channel_id=1, source_target_pairs={{0,16},{16,32},{32,48},{48,64},{64,80},{80,96},{96,112},{1,17},{17... | collective-permute-start | bytes 1572872 | tf_op jit(solution)/shard_map/ppermute | solution.py:455
  21.3 9.7 %copy-start.1 = (bf16[1024,128]{1,0:T(8,128)(2,1)S(1)}, bf16[1024,128]{1,0:T(8,128)(2,1)}, u32[]{:S(2)}) copy-start(bf16[1024,128]{1,0:T(8,128)(2,1)} %pk_ref.1) | copy-start | bytes 786436
  21.3 9.7 %copy-start.2 = (bf16[1024,128]{1,0:T(8,128)(2,1)S(1)}, bf16[1024,128]{1,0:T(8,128)(2,1)}, u32[]{:S(2)}) copy-start(bf16[1024,128]{1,0:T(8,128)(2,1)} %pv_ref.1) | copy-start | bytes 786436
  26.3 3.7 %collective-permute-start.3 = (bf16[128,1408]{1,0:T(8,128)(2,1)S(1)}, bf16[128,1408]{1,0:T(8,128)(2,1)S(1)}, u32[]{:S(2)}, u32[]{:S(2)}) collective-permute-start(bf16[128,1408]{1,0:T(8,128)(2,1)S(1)} %collective-permute-done.refs_0_), channel_id=1, source_target_pairs={{0,16},{16,0},{1,17},{17,1},{2,18},{18,2},{3,19},{19,3},{4,20},{20... | collective-permute-start | bytes 1081352 | tf_op jit(solution)/shard_map/ppermute | solution.py:458
  28.6 1.8 %collective-permute-start.4 = (bf16[128,1408]{1,0:T(8,128)(2,1)S(1)}, bf16[128,1408]{1,0:T(8,128)(2,1)S(1)}, u32[]{:S(2)}, u32[]{:S(2)}) collective-permute-start(bf16[128,1408]{1,0:T(8,128)(2,1)S(1)} %collective-permute-done.1.refs_1_), channel_id=1, source_target_pairs={{0,16},{16,0},{1,17},{17,1},{2,18},{18,2},{3,19},{19,3},{4,20},{20... | collective-permute-start | bytes 1081352 | tf_op jit(solution)/shard_map/ppermute | solution.py:458
  28.7 2.2 %collective-permute-start.5 = (bf16[128,1408]{1,0:T(8,128)(2,1)S(1)}, bf16[128,1408]{1,0:T(8,128)(2,1)S(1)}, u32[]{:S(2)}, u32[]{:S(2)}) collective-permute-start(bf16[128,1408]{1,0:T(8,128)(2,1)S(1)} %collective-permute-done.2.refs_2_), channel_id=1, source_target_pairs={{0,16},{16,0},{1,17},{17,1},{2,18},{18,2},{3,19},{19,3},{4,20},{20... | collective-permute-start | bytes 1081352 | tf_op jit(solution)/shard_map/ppermute | solution.py:458
  33.0 10.9 %collective-permute-start.7 = (bf16[256,256]{1,0:T(8,128)(2,1)S(1)}, bf16[256,256]{1,0:T(8,128)(2,1)S(1)}, u32[]{:S(2)}, u32[]{:S(2)}) collective-permute-start(bf16[256,256]{1,0:T(8,128)(2,1)S(1)} %get-tuple-element.68.refs_0_), channel_id=1, source_target_pairs={{0,1},{1,2},{2,3},{3,0},{4,5},{5,6},{6,7},{7,4},{8,9},{9,10},{10,1... | collective-permute-start | bytes 393224 | tf_op jit(solution)/shard_map/ppermute | solution.py:436
  34.1 11.7 %collective-permute-start.8 = (bf16[256,256]{1,0:T(8,128)(2,1)S(1)}, bf16[256,256]{1,0:T(8,128)(2,1)S(1)}, u32[]{:S(2)}, u32[]{:S(2)}) collective-permute-start(bf16[256,256]{1,0:T(8,128)(2,1)S(1)} %get-tuple-element.68.refs_0_), channel_id=1, source_target_pairs={{0,3},{1,0},{2,1},{3,2},{4,7},{5,4},{6,5},{7,6},{8,11},{9,8},{10,9... | collective-permute-start | bytes 393224 | tf_op jit(solution)/shard_map/ppermute | solution.py:436
  36.3 9.5 %collective-permute-start.9 = (bf16[256,256]{1,0:T(8,128)(2,1)S(1)}, bf16[256,256]{1,0:T(8,128)(2,1)S(1)}, u32[]{:S(2)}, u32[]{:S(2)}) collective-permute-start(bf16[256,256]{1,0:T(8,128)(2,1)S(1)} %get-tuple-element.68.refs_0_), channel_id=1, source_target_pairs={{0,2},{1,3},{2,0},{3,1},{4,6},{5,7},{6,4},{7,5},{8,10},{9,11},{10,... | collective-permute-start | bytes 393224 | tf_op jit(solution)/shard_map/ppermute | solution.py:436
  39.7 12.2 %collective-permute-start.15 = (bf16[512,256]{1,0:T(8,128)(2,1)S(1)}, bf16[512,256]{1,0:T(8,128)(2,1)S(1)}, u32[]{:S(2)}, u32[]{:S(2)}) collective-permute-start(bf16[512,256]{1,0:T(8,128)(2,1)S(1)} %attend.4.refs_0_), channel_id=1, source_target_pairs={{0,1},{1,2},{2,3},{3,0},{4,5},{5,6},{6,7},{7,4},{8,9},{9,10},{10,1... | collective-permute-start | bytes 786440 | tf_op jit(solution)/shard_map/ppermute | solution.py:436
  40.3 13.6 %collective-permute-start.16 = (bf16[512,256]{1,0:T(8,128)(2,1)S(1)}, bf16[512,256]{1,0:T(8,128)(2,1)S(1)}, u32[]{:S(2)}, u32[]{:S(2)}) collective-permute-start(bf16[512,256]{1,0:T(8,128)(2,1)S(1)} %attend.4.refs_0_), channel_id=1, source_target_pairs={{0,3},{1,0},{2,1},{3,2},{4,7},{5,4},{6,5},{7,6},{8,11},{9,8},{10,9... | collective-permute-start | bytes 786440 | tf_op jit(solution)/shard_map/ppermute | solution.py:436
  43.9 10.8 %collective-permute-start.17 = (bf16[512,256]{1,0:T(8,128)(2,1)S(1)}, bf16[512,256]{1,0:T(8,128)(2,1)S(1)}, u32[]{:S(2)}, u32[]{:S(2)}) collective-permute-start(bf16[512,256]{1,0:T(8,128)(2,1)S(1)} %attend.4.refs_0_), channel_id=1, source_target_pairs={{0,2},{1,3},{2,0},{3,1},{4,6},{5,7},{6,4},{7,5},{8,10},{9,11},{10,... | collective-permute-start | bytes 786440 | tf_op jit(solution)/shard_map/ppermute | solution.py:436
  46.8 10.3 %collective-permute-start.13 = (bf16[128,1408]{1,0:T(8,128)(2,1)S(1)}, bf16[128,1408]{1,0:T(8,128)(2,1)S(1)}, u32[]{:S(2)}, u32[]{:S(2)}) collective-permute-start(bf16[128,1408]{1,0:T(8,128)(2,1)S(1)} %get-tuple-element.77), channel_id=1, source_target_pairs={{0,4},{4,8},{8,12},{12,0},{1,5},{5,9},{9,13},{13,1},{2,6},{6,10},{... | collective-permute-start | bytes 1081352 | tf_op jit(solution)/shard_map/ppermute | solution.py:436
  48.3 8.8 %collective-permute-start.14 = (bf16[128,1408]{1,0:T(8,128)(2,1)S(1)}, bf16[128,1408]{1,0:T(8,128)(2,1)S(1)}, u32[]{:S(2)}, u32[]{:S(2)}) collective-permute-start(bf16[128,1408]{1,0:T(8,128)(2,1)S(1)} %get-tuple-element.79), channel_id=1, source_target_pairs={{0,12},{4,0},{8,4},{12,8},{1,13},{5,1},{9,5},{13,9},{2,14},{6,2},{... | collective-permute-start | bytes 1081352 | tf_op jit(solution)/shard_map/ppermute | solution.py:436
  57.6 17.5 %collective-permute-start.18 = (bf16[256,1408]{1,0:T(8,128)(2,1)S(1)}, bf16[256,1408]{1,0:T(8,128)(2,1)S(1)}, u32[]{:S(2)}, u32[]{:S(2)}) collective-permute-start(bf16[256,1408]{1,0:T(8,128)(2,1)S(1)} %get-tuple-element.86), channel_id=1, source_target_pairs={{0,4},{4,8},{8,12},{12,0},{1,5},{5,9},{9,13},{13,1},{2,6},{6,10},{... | collective-permute-start | bytes 2162696 | tf_op jit(solution)/shard_map/ppermute | solution.py:436
  59.2 20.5 %copy-start.6 = (f32[5376]{0:T(1024)S(1)}, f32[5376]{0:T(1024)}, u32[]{:S(2)}) copy-start(f32[5376]{0:T(1024)} %param.23) | copy-start | bytes 64516
  59.2 15.9 %collective-permute-start.19 = (bf16[256,1408]{1,0:T(8,128)(2,1)S(1)}, bf16[256,1408]{1,0:T(8,128)(2,1)S(1)}, u32[]{:S(2)}, u32[]{:S(2)}) collective-permute-start(bf16[256,1408]{1,0:T(8,128)(2,1)S(1)} %get-tuple-element.87), channel_id=1, source_target_pairs={{0,12},{4,0},{8,4},{12,8},{1,13},{5,1},{9,5},{13,9},{2,14},{6,2},{... | collective-permute-start | bytes 2162696 | tf_op jit(solution)/shard_map/ppermute | solution.py:436
  60.9 7.2 %collective-permute-start.10 = (bf16[256,256]{1,0:T(8,128)(2,1)S(1)}, bf16[256,256]{1,0:T(8,128)(2,1)S(1)}, u32[]{:S(2)}, u32[]{:S(2)}) collective-permute-start(bf16[256,256]{1,0:T(8,128)(2,1)S(1)} %attend.5.refs_0_), channel_id=1, source_target_pairs={{0,1},{1,2},{2,3},{3,0},{4,5},{5,6},{6,7},{7,4},{8,9},{9,10},{10,1... | collective-permute-start | bytes 393224 | tf_op jit(solution)/shard_map/ppermute | solution.py:436
  61.7 6.4 %collective-permute-start.11 = (bf16[256,256]{1,0:T(8,128)(2,1)S(1)}, bf16[256,256]{1,0:T(8,128)(2,1)S(1)}, u32[]{:S(2)}, u32[]{:S(2)}) collective-permute-start(bf16[256,256]{1,0:T(8,128)(2,1)S(1)} %attend.5.refs_0_), channel_id=1, source_target_pairs={{0,3},{1,0},{2,1},{3,2},{4,7},{5,4},{6,5},{7,6},{8,11},{9,8},{10,9... | collective-permute-start | bytes 393224 | tf_op jit(solution)/shard_map/ppermute | solution.py:436
  64.2 6.5 %collective-permute-start.12 = (bf16[256,256]{1,0:T(8,128)(2,1)S(1)}, bf16[256,256]{1,0:T(8,128)(2,1)S(1)}, u32[]{:S(2)}, u32[]{:S(2)}) collective-permute-start(bf16[256,256]{1,0:T(8,128)(2,1)S(1)} %attend.5.refs_0_), channel_id=1, source_target_pairs={{0,2},{1,3},{2,0},{3,1},{4,6},{5,7},{6,4},{7,5},{8,10},{9,11},{10,... | collective-permute-start | bytes 393224 | tf_op jit(solution)/shard_map/ppermute | solution.py:436
  75.9 7.9 %collective-permute-start.20 = (bf16[64,1408]{1,0:T(8,128)(2,1)S(1)}, bf16[64,1408]{1,0:T(8,128)(2,1)S(1)}, u32[]{:S(2)}, u32[]{:S(2)}) collective-permute-start(bf16[64,1408]{1,0:T(8,128)(2,1)S(1)} %get-tuple-element.89), channel_id=1, source_target_pairs={{0,1},{1,2},{2,3},{3,0},{4,5},{5,6},{6,7},{7,4},{8,9},{9,10},{10,1... | collective-permute-start | bytes 540680 | tf_op jit(solution)/shard_map/ppermute | solution.py:436
  76.8 7.3 %collective-permute-start.21 = (bf16[64,1408]{1,0:T(8,128)(2,1)S(1)}, bf16[64,1408]{1,0:T(8,128)(2,1)S(1)}, u32[]{:S(2)}, u32[]{:S(2)}) collective-permute-start(bf16[64,1408]{1,0:T(8,128)(2,1)S(1)} %get-tuple-element.90), channel_id=1, source_target_pairs={{0,3},{1,0},{2,1},{3,2},{4,7},{5,4},{6,5},{7,6},{8,11},{9,8},{10,9... | collective-permute-start | bytes 540680 | tf_op jit(solution)/shard_map/ppermute | solution.py:436
  79.2 7.0 %collective-permute-start.22 = (bf16[64,1408]{1,0:T(8,128)(2,1)S(1)}, bf16[64,1408]{1,0:T(8,128)(2,1)S(1)}, u32[]{:S(2)}, u32[]{:S(2)}) collective-permute-start(bf16[64,1408]{1,0:T(8,128)(2,1)S(1)} %get-tuple-element.91), channel_id=1, source_target_pairs={{0,2},{1,3},{2,0},{3,1},{4,6},{5,7},{6,4},{7,5},{8,10},{9,11},{10,... | collective-permute-start | bytes 540680 | tf_op jit(solution)/shard_map/ppermute | solution.py:436
